TPU v7x, 256 devices: a whole 4x4x8 slice. The times are simulated.
256 devices in a mesh: dp: 8 (over z), seq: 16 (over x_lo, y, core), tensor: 2 (over x_hi).
Axes of the slice: x: 4 (x_hi: 2, x_lo: 2; x = x_hi * 2 + x_lo), y: 4, z: 8, core: 2. Of those that a mesh axis runs over, the one named last changes fastest.
Arguments:
- latent: bfloat16 [8, 16, 256, 1152], P('dp', 'seq'), may hold values from -6 to 6
- mod_shift: float32 [8, 1152], P('dp'), may hold values from -3 to 3
- mod_scale: float32 [8, 1152], P('dp'), may hold values from -2.5 to 2.5
- w_qkv: bfloat16 [1152, 3, 1152], P(None, None, 'tensor'), may hold values from -0.1875 to 0.1875
- q_gain: float32 [72], replicated, may hold values from 0.1 to 1.9
- k_gain: float32 [72], replicated, may hold values from 0.1 to 1.9
- cotangent: bfloat16 [8, 16, 256, 1152], P('dp', 'seq', None, 'tensor'), may hold values from -6 to 6
Outputs:
- attended: bfloat16 [8, 16, 256, 1152], P('dp', 'seq', None, 'tensor')
- grad_latent: bfloat16 [8, 16, 256, 1152], P('dp', 'seq', None, 'tensor')
- grad_qkv: bfloat16 [1152, 3, 1152], P(None, None, 'tensor')
All inputs are finite; a program needn't handle non-finite values.
Results may differ from a plain program's by a relative error of at most 0.02.
Values may be sent and summed in bfloat16 or wider, within the bound.
No kernel may reach another device: no remote copies, remote signals or barrier semaphores. Data moves between devices by JAX's collectives and lax.ppermute only.
A program may use at most 128 MiB of HBM per device.

v0:
```python
from functools import partial
import math

import jax
import jax.numpy as jnp
from jax import lax
from jax.sharding import PartitionSpec as P


def head_norm(values, gain_row):
    return values * lax.rsqrt(jnp.mean(values * values, axis=-1, keepdims=True) + 1e-06) * gain_row


def temporal(queries, key_rows, values, q_gain, k_gain):
    queries = head_norm(queries, q_gain)
    key_rows = head_norm(key_rows, k_gain)
    scores = jnp.einsum("...fphd,...gphd->...phfg", queries, key_rows) / math.sqrt(
        queries.shape[-1]
    )
    weights = jnp.exp(scores)
    weights = weights / jnp.sum(weights, axis=-1, keepdims=True)
    return jnp.einsum("...phfg,...gphd->...fphd", weights, values)


def body(latent, mod_shift, mod_scale, w_qkv, q_gain, k_gain, cotangent):
    clip_count, local_frames, patches, model_width = latent.shape
    heads_width = w_qkv.shape[2]
    head_size = q_gain.shape[0]
    local_heads = heads_width // head_size
    seq_count = lax.axis_size("seq")
    frames = local_frames * seq_count
    local_patches = patches // seq_count
    half_width = model_width // lax.axis_size("tensor")
    flat_w = w_qkv.reshape(model_width, 3 * heads_width)
    values = latent.astype(jnp.float32)
    centred = values - jnp.mean(values, axis=-1, keepdims=True)
    inverse = lax.rsqrt(jnp.mean(centred * centred, axis=-1, keepdims=True) + 1e-06)
    unit_rows = centred * inverse
    factor = 1.0 + mod_scale[:, None, None, :]
    modulated = (unit_rows * factor + mod_shift[:, None, None, :]).astype(jnp.bfloat16)
    attend = partial(temporal, q_gain=q_gain, k_gain=k_gain)
    qkv_frames = jnp.einsum(
        "cfpd,dk->cfpk", modulated, flat_w, preferred_element_type=jnp.float32
    ).astype(jnp.bfloat16)
    qkv_patches = lax.all_to_all(qkv_frames, "seq", split_axis=2, concat_axis=1, tiled=True)
    pieces = qkv_patches.reshape(
        clip_count, frames, local_patches, 3, local_heads, head_size
    ).astype(jnp.float32)
    attended_float, attend_back = jax.vjp(
        attend, pieces[:, :, :, 0], pieces[:, :, :, 1], pieces[:, :, :, 2]
    )
    attended_patches = attended_float.astype(jnp.bfloat16).reshape(
        clip_count, frames, local_patches, heads_width
    )
    attended = lax.all_to_all(attended_patches, "seq", split_axis=1, concat_axis=2, tiled=True)
    cot_patches = lax.all_to_all(cotangent, "seq", split_axis=2, concat_axis=1, tiled=True)
    cotangents = attend_back(
        cot_patches.reshape(clip_count, frames, local_patches, local_heads, head_size).astype(
            jnp.float32
        )
    )
    grad_proj = (
        jnp.stack(cotangents, axis=3)
        .reshape(clip_count, frames, local_patches, 3 * heads_width)
        .astype(jnp.bfloat16)
    )
    grad_frames = lax.all_to_all(grad_proj, "seq", split_axis=1, concat_axis=2, tiled=True)
    grad_w = jnp.einsum("cfpd,cfpk->dk", modulated, grad_frames, preferred_element_type=jnp.float32)
    partials = jnp.einsum("cfpk,dk->cfpd", grad_frames, flat_w, preferred_element_type=jnp.float32)
    grad_mod = lax.psum_scatter(partials, "tensor", scatter_dimension=3, tiled=True)
    rows_all = clip_count * lax.axis_size("dp") * frames * patches
    summed = lax.psum(grad_w, ("dp", "seq"))
    grad_qkv = (
        (summed / math.sqrt(rows_all)).astype(jnp.bfloat16).reshape(model_width, 3, heads_width)
    )
    offset = lax.axis_index("tensor") * half_width
    unit_half = lax.dynamic_slice_in_dim(unit_rows, offset, half_width, 3)
    factor_half = lax.dynamic_slice_in_dim(factor, offset, half_width, 3)
    scaled = grad_mod * factor_half
    row_sums = lax.psum(
        (
            jnp.sum(scaled, axis=-1, keepdims=True),
            jnp.sum(scaled * unit_half, axis=-1, keepdims=True),
        ),
        "tensor",
    )
    grad_latent = (
        inverse * (scaled - row_sums[0] / model_width - unit_half * (row_sums[1] / model_width))
    ).astype(jnp.bfloat16)
    return (attended, grad_latent, grad_qkv)


def solution(mesh):
    in_specs = (
        P("dp", "seq", None, None),
        P("dp", None),
        P("dp", None),
        P(None, None, "tensor"),
        P(),
        P(),
        P("dp", "seq", None, "tensor"),
    )
    out_specs = (
        P("dp", "seq", None, "tensor"),
        P("dp", "seq", None, "tensor"),
        P(None, None, "tensor"),
    )
    return jax.shard_map(body, mesh=mesh, in_specs=in_specs, out_specs=out_specs, check_vma=False)
```

profile of v0, /device:TPU:1, one launch (start us, length us, event | category | flops | bytes accessed | tf_op | source)
XLA Modules:
  0.0 1278.2 jit_solution(1305078413589260385)
XLA Ops:
  9.2 2.7 reduce.22
  13.0 7.6 all-to-all-start.2
  21.2 3.6 fusion
  24.8 2.8 copy.41
  27.6 6.5 reduce.21
  34.1 1.9 reshape.335
  36.0 5.8 all-to-all-start
  42.4 2.6 reshape.338
  44.9 1.8 bitcast_reduce_fusion.1
  48.1 7.7 all-to-all-done
  57.5 5.1 bitcast_reduce_fusion
  62.7 1.9 reshape.322
  64.6 1.9 copy_convert_fusion
  73.3 1.9 convert_element_type.59
  75.2 18.4 %all_to_all.19 = bf16[1,16,16,1728]{3,2,0,1:T(8,128)(2,1)S(1)} all-to-all(bf16[1,16,16,1728]{3,2,0,1:T(8,128)(2,1)} %bitcast.138), channel_id=1, replica_groups=mesh['dp'=8,'seq'=16,'tensor'=2] {'seq'}, dimensions={1} | all-to-all | bytes 1769472 | tf_op jit(solution)/shard_map/all_to_all | solution.py:67
  93.6 4.5 convolution_bitcast_fusion
  98.0 3.8 copy.52
  102.1 4.7 fusion.45
  111.4 4.5 all-to-all-start.1
  116.2 11.7 all-to-all-done.1
  128.8 33.4 %all-reduce.7.cloned.1.call-done = f32[1,1,256,1152]{2,1,0,3:T(1,128)} async-done(((f32[1,1,256,1152]{2,1,0,3:T(1,128)}), f32[1,1,256,1152]{2,1,0,3:T(1,128)}) %all-reduce.7.cloned.1.call-update) | async-done | bytes 1179664
  164.8 5.3 all-reduce.1
  171.5 1093.6 %all-reduce.5.cloned.1.call-done = f32[1152,1728]{0,1:T(8,128)} async-done(((f32[1152,1728]{0,1:T(8,128)}), f32[1152,1728]{0,1:T(8,128)}) %all-reduce.5.cloned.1.call-update) | async-done | bytes 7962640 | tf_op jit(solution)/shard_map/psum | solution.py:72
  1265.1 6.0 multiply_convert_fusion
  (60 shorter events, 23.2 us)
Async XLA Ops:
  7.2 13.4 %copy-start = (bf16[1,1,256,1152]{3,2,1,0:T(8,128)(2,1)S(1)}, bf16[1,1,256,1152]{3,2,1,0:T(8,128)(2,1)}, u32[]{:S(2)}) copy-start(bf16[1,1,256,1152]{3,2,1,0:T(8,128)(2,1)} %param.7) | copy-start | bytes 1769476
  9.2 11.9 copy-start.4
  9.2 12.0 copy-start.3
  13.0 23.0 %all-to-all-start.2 = ((bf16[16,2,4608]{2,1,0:T(2,128)(2,1)}), bf16[16,2,4608]{2,1,0:T(2,128)(2,1)}, u32[]{:S(2)}, u32[]{:S(2)}) async-start(bf16[16,2,4608]{2,1,0:T(2,128)(2,1)} %reshape.337), calls=%async_computation.2 | async-start | bytes 589824 | tf_op jit(solution)/shard_map/all_to_all | solution.py:56
  36.0 19.8 %all-to-all-start = ((bf16[16,2,13824]{2,1,0:T(2,128)(2,1)}), bf16[16,2,13824]{2,1,0:T(2,128)(2,1)S(1)}, u32[]{:S(2)}, u32[]{:S(2)}) async-start(bf16[16,2,13824]{2,1,0:T(2,128)(2,1)} %reshape.335), calls=%async_computation | async-start | bytes 1769472 | tf_op jit(solution)/shard_map/all_to_all | solution.py:45
  41.8 120.4 %all-reduce.7.cloned.1.call-start = ((), (), s32[]{:S(2)}) async-start(), calls=%async_computation.5 | async-start | bytes 2359296
  66.5 2.3 copy-start.1
  66.5 0.7 copy-start.5
  66.5 0.7 copy-start.6
  67.2 1.0 copy-start.2
  101.8 1163.3 %all-reduce.5.cloned.1.call-start = ((), (), s32[]{:S(2)}) async-start(), calls=%async_computation.4 | async-start | bytes 15925248 | tf_op jit(solution)/shard_map/psum | solution.py:72
  106.8 0.7 copy-start.7
  111.4 16.5 %all-to-all-start.1 = ((bf16[1,16,16,576]{3,2,0,1:T(8,128)(2,1)}), bf16[1,16,16,576]{3,2,0,1:T(8,128)(2,1)S(1)}, u32[]{:S(2)}, u32[]{:S(2)}) async-start(bf16[1,16,16,576]{3,2,0,1:T(8,128)(2,1)} %bitcast.10), calls=%async_computation.1 | async-start | bytes 655360 | tf_op jit(solution)/shard_map/all_to_all | solution.py:55
Sparse Core Ops, SparseCore 0:
  102.0 60.2 all-reduce.6
  165.1 1100.0 all-reduce.4
where the time goes:
time: 1280 us
  waiting for transfers between devices  1150 us (90%)
  local copies, waits for them, and re-layouts  35.2 us (3%)
  blocking collectives  23.7 us (2%)
  other arithmetic  21 us (2%)
  starting transfers between devices  18.7 us (1%)
  matrix products  17.8 us (1%)
  between operations  15.2 us (1%)
    psum x1, waiting for transfers between devices, body(): summed = lax.psum(grad_w, ('dp', 'seq'))  1090 us
    unnamed x3, waiting for transfers between devices  33.5 us
  transfers between devices with their start and end apart: 5, of which 4 were waited for; matrix products, arithmetic and copies ran while one was open for 3% of the time, Pallas kernels for 0%

commit v1 on v0

v1 whole, which is shorter than its diff:
```python
import functools
import math

import jax
import jax.numpy as jnp
from jax import lax
from jax.experimental import pallas as pl
from jax.experimental.pallas import tpu as pltpu
from jax.sharding import Mesh, PartitionSpec as P

BF = jnp.bfloat16
F32 = jnp.float32
EPS = 1e-06
NN = (((1,), (0,)), ((), ()))
NT = (((1,), (1,)), ((), ()))
ROWS, LANES = 16, 128
SEQ = ("xlo", "y", "core")


def mm(a, b, dims):
    return lax.dot_general(a, b, dims, preferred_element_type=F32)


def eye(n):
    rows = lax.broadcasted_iota(jnp.int32, (n, n), 0)
    cols = lax.broadcasted_iota(jnp.int32, (n, n), 1)
    return jnp.where(rows == cols, 1.0, 0.0).astype(BF)


def unit_of(x_ref, width):
    values = x_ref[:, :width].astype(F32)
    centred = values - jnp.sum(values, axis=1, keepdims=True) * (1.0 / width)
    inverse = lax.rsqrt(jnp.sum(centred * centred, axis=1, keepdims=True) * (1.0 / width) + EPS)
    return centred * inverse, inverse


def attend_kernel(x_ref, shift_ref, scale_ref, wt_ref, qg_ref, kg_ref,
                  gw_ref, gp_ref, att_ref, mod_s, gpt_s, ot_s, *, patches, heads, hd):
    tokens, total = x_ref.shape
    width = scale_ref.shape[1]
    hw = heads * hd
    unit, _ = unit_of(x_ref, width)
    mod_s[...] = (unit * (1.0 + scale_ref[...]) + shift_ref[...]).astype(BF)
    mod = mod_s[...]
    root = 1.0 / math.sqrt(hd)
    ident = eye(tokens)
    cot_t = mm(eye(hw), x_ref[:, width:], NT).reshape(heads, hd, tokens)

    def project(part):
        rows = mm(wt_ref[part * hw : (part + 1) * hw, :], mod, NT)
        return rows.astype(BF).astype(F32).reshape(heads, hd, tokens)

    def norm(part, gain_ref):
        rows = project(part)
        inverse = lax.rsqrt(jnp.sum(rows * rows, axis=1, keepdims=True) * (1.0 / hd) + EPS)
        return rows * inverse, inverse, gain_ref[...]

    q_hat, q_inv, q_gain = norm(0, qg_ref)
    k_hat, k_inv, k_gain = norm(1, kg_ref)
    values = project(2)
    row_id = lax.broadcasted_iota(jnp.int32, (tokens, tokens), 0)
    col_id = lax.broadcasted_iota(jnp.int32, (tokens, tokens), 1)
    same = lax.rem(row_id, patches) == lax.rem(col_id, patches)

    def back(hat, inverse, gain, grad):
        weighted = grad * gain
        mean = jnp.sum(hat * weighted, axis=0, keepdims=True) * (1.0 / hd)
        return inverse * (weighted - hat * mean)

    for h in range(heads):
        qn = q_hat[h] * q_gain
        kn = k_hat[h] * k_gain
        q_b = qn.astype(BF)
        k_b = kn.astype(BF)
        v_b = values[h].astype(BF)
        o_b = cot_t[h].astype(BF)
        k_rows = mm(ident, k_b, NT).astype(BF)
        v_rows = mm(ident, v_b, NT).astype(BF)
        scores = mm(k_rows, q_b, NN) * root
        weights = jnp.where(same, jnp.exp(scores), 0.0)
        probs = weights * (1.0 / jnp.sum(weights, axis=0, keepdims=True))
        probs_b = probs.astype(BF)
        ot_s[h * hd : (h + 1) * hd, :] = mm(v_b, probs_b, NN)
        grad_v = mm(o_b, probs_b, NT)
        grad_p = mm(v_rows, o_b, NN)
        terms = probs * grad_p
        grad_s = (terms - probs * jnp.sum(terms, axis=0, keepdims=True)) * root
        grad_s = grad_s.astype(BF)
        grad_q = back(q_hat[h], q_inv[h], q_gain, mm(k_b, grad_s, NN))
        grad_k = back(k_hat[h], k_inv[h], k_gain, mm(q_b, grad_s, NT))
        for part, rows in enumerate((grad_q, grad_k, grad_v)):
            start = part * hw + h * hd
            gpt_s[start : start + hd, :] = rows
    for part in range(3):
        lo, hi = part * hw, (part + 1) * hw
        block = gpt_s[lo:hi, :].astype(BF)
        gp_ref[:, lo:hi] = mm(ident, block, NT).astype(BF)
        tiles, base = hw // ROWS, part * (hw // ROWS)
        all_tiles = 3 * tiles
        for j in range(width // LANES):
            cols = slice(j * LANES, (j + 1) * LANES)
            found = mm(block, mod_s[:, cols], NN).astype(BF).reshape(tiles, ROWS, LANES)
            gw_ref[j * all_tiles + base : j * all_tiles + base + tiles] = found
    used = 3 * (hw // ROWS) * (width // LANES)
    gw_ref[used:] = jnp.zeros((gw_ref.shape[0] - used, ROWS, LANES), BF)
    att_ref[...] = mm(ident, ot_s[...].astype(BF), NT).astype(BF)


def attend(x, shift, scale, wt, qg, kg, patches, heads, hd, padded):
    tokens = x.shape[0]
    width = wt.shape[1]
    hw = heads * hd
    return pl.pallas_call(
        functools.partial(attend_kernel, patches=patches, heads=heads, hd=hd),
        out_shape=(
            jax.ShapeDtypeStruct((padded, ROWS, LANES), BF),
            jax.ShapeDtypeStruct((tokens, 3 * hw), BF),
            jax.ShapeDtypeStruct((tokens, hw), BF),
        ),
        scratch_shapes=[
            pltpu.VMEM((tokens, width), BF),
            pltpu.VMEM((3 * hw, tokens), F32),
            pltpu.VMEM((hw, tokens), F32),
        ],
        compiler_params=pltpu.CompilerParams(vmem_limit_bytes=48 * 2**20),
        name="attend",
    )(x, shift, scale, wt, qg, kg)


def window_of(half):
    return -(-half // LANES) * LANES


def split_kernel(which_ref, x_ref, scale_ref, wt_ref, gp_ref, send_ref, keep_ref, unit_ref):
    width = wt_ref.shape[1]
    half = width // 2
    win = window_of(half)
    grad = mm(gp_ref[...], wt_ref[...], NN)
    unit, inverse = unit_of(x_ref, width)
    scaled = grad * (1.0 + scale_ref[...])
    first = jnp.sum(scaled, axis=1, keepdims=True)
    second = jnp.sum(scaled * unit, axis=1, keepdims=True)
    mine_low = which_ref[0] == 0
    col = lax.broadcasted_iota(jnp.int32, (grad.shape[0], win), 1)
    here = jnp.where(mine_low, half, 0)
    there = jnp.where(mine_low, 0, half)
    low, high = scaled[:, :win], scaled[:, width - win :]
    send = jnp.where(mine_low, high, low)
    keep = jnp.where(mine_low, low, high)
    for place, term in enumerate((first, second)):
        coarse = term.astype(BF).astype(F32)
        send = jnp.where(col == there + 2 * place, coarse, send)
        send = jnp.where(col == there + 2 * place + 1, term - coarse, send)
    for place, term in enumerate((first, second, inverse)):
        keep = jnp.where(col == here + place, term, keep)
    send_ref[...] = send.astype(BF)
    keep_ref[...] = keep
    unit_ref[...] = jnp.where(mine_low, unit[:, :win], unit[:, width - win :])


def split(which, x, scale, wt, gp):
    tokens = x.shape[0]
    win = window_of(wt.shape[1] // 2)
    smem = pl.BlockSpec(memory_space=pltpu.SMEM)
    vmem = pl.BlockSpec(memory_space=pltpu.VMEM)
    return pl.pallas_call(
        split_kernel,
        in_specs=[smem, vmem, vmem, vmem, vmem],
        out_shape=(
            jax.ShapeDtypeStruct((tokens, win), BF),
            jax.ShapeDtypeStruct((tokens, win), F32),
            jax.ShapeDtypeStruct((tokens, win), F32),
        ),
        compiler_params=pltpu.CompilerParams(vmem_limit_bytes=40 * 2**20),
        name="split",
    )(which, x, scale, wt, gp)


def finish_kernel(which_ref, recv_ref, keep_ref, unit_ref, out_ref, *, width):
    half = width // 2
    win = recv_ref.shape[1]
    mine_low = which_ref[0] == 0
    recv = recv_ref[...].astype(F32)
    keep = keep_ref[...]

    def column(block, place):
        return jnp.where(mine_low, block[:, half + place : half + place + 1], block[:, place : place + 1])

    first = column(keep, 0) + (column(recv, 0) + column(recv, 1))
    second = column(keep, 1) + (column(recv, 2) + column(recv, 3))
    inverse = column(keep, 2)
    grad = keep + recv
    out = inverse * (grad - first * (1.0 / width) - unit_ref[...] * (second * (1.0 / width)))
    moved = pltpu.roll(out, win - (win - half), 1)
    out_ref[...] = jnp.where(mine_low, out, moved)[:, :half].astype(BF)


def finish(which, recv, keep, unit, width):
    tokens = recv.shape[0]
    smem = pl.BlockSpec(memory_space=pltpu.SMEM)
    vmem = pl.BlockSpec(memory_space=pltpu.VMEM)
    return pl.pallas_call(
        functools.partial(finish_kernel, width=width),
        in_specs=[smem, vmem, vmem, vmem],
        out_shape=jax.ShapeDtypeStruct((tokens, width // 2), BF),
        compiler_params=pltpu.CompilerParams(vmem_limit_bytes=24 * 2**20),
        name="finish",
    )(which, recv, keep, unit)


def untile_kernel(tiles_ref, out_ref, *, factor):
    rows = out_ref.shape[0] // ROWS
    for j in range(out_ref.shape[1] // LANES):
        block = tiles_ref[j * rows : (j + 1) * rows].astype(F32) * factor
        out_ref[:, j * LANES : (j + 1) * LANES] = block.reshape(rows * ROWS, LANES).astype(BF)


def untile(tiles, rows, width, factor):
    return pl.pallas_call(
        functools.partial(untile_kernel, factor=factor),
        out_shape=jax.ShapeDtypeStruct((rows, width), BF),
        compiler_params=pltpu.CompilerParams(vmem_limit_bytes=40 * 2**20),
        name="untile",
    )(tiles)


def exchange(x, axes):
    count = math.prod(lax.axis_size(a) for a in axes)
    parts = x.reshape((count, x.shape[0] // count) + x.shape[1:])
    return lax.all_to_all(parts, axes, split_axis=0, concat_axis=0, tiled=True)


def scatter_sum(x, axes):
    return jnp.sum(exchange(x, axes).astype(F32), axis=0).astype(BF)


def total_of(tiles):
    own = scatter_sum(scatter_sum(scatter_sum(tiles, ("core",)), ("xlo", "y")), ("dp",))
    own = lax.all_gather(own, "dp", axis=0, tiled=True)
    own = lax.all_gather(own, ("xlo", "y"), axis=0, tiled=True)
    return lax.all_gather(own, "core", axis=0, tiled=True)


def body(latent, mod_shift, mod_scale, w_qkv, q_gain, k_gain, cotangent):
    _, _, patches, width = latent.shape
    hw = w_qkv.shape[2]
    hd = q_gain.shape[0]
    heads = hw // hd
    frames = 1
    for a in SEQ:
        frames *= lax.axis_size(a)
    own_patches = patches // frames
    clips = lax.axis_size("dp")
    wt = w_qkv.transpose(1, 2, 0).reshape(3 * hw, width)
    x = jnp.concatenate([latent[0, 0], cotangent[0, 0]], axis=1)
    x = x.reshape(frames, own_patches, width + hw)
    x = lax.all_to_all(x, SEQ, split_axis=0, concat_axis=0, tiled=True).reshape(patches, width + hw)
    group = 2
    for a in ("dp",) + SEQ:
        group *= lax.axis_size(a)
    used = (3 * hw // ROWS) * (width // LANES)
    padded = -(-used // group) * group
    gw, gp, attended = attend(
        x, mod_shift, mod_scale, wt, q_gain[:, None], k_gain[:, None], own_patches, heads, hd, padded
    )
    which = lax.axis_index("tensor").astype(jnp.int32).reshape(1)

    def home(rows):
        rows = rows.reshape(frames, own_patches, hw)
        rows = lax.all_to_all(rows, SEQ, split_axis=0, concat_axis=0, tiled=True)
        return rows.reshape(1, 1, patches, hw)

    send, keep, unit = split(which, x, mod_scale, wt, gp)
    recv = lax.ppermute(send, "tensor", [(0, 1), (1, 0)])
    grad_latent = home(finish(which, recv, keep, unit, width))
    factor = 1.0 / math.sqrt(clips * frames * patches)
    grad_qkv = untile(total_of(gw), 3 * hw, width, factor)
    grad_qkv = grad_qkv.reshape(3, hw, width).transpose(2, 0, 1)
    return (home(attended), grad_latent, grad_qkv)


def solution(mesh):
    fine = Mesh(mesh.devices.reshape(mesh.shape["dp"], 2, 4, 2, 2), ("dp",) + SEQ + ("tensor",))
    in_specs = (
        P("dp", SEQ, None, None),
        P("dp", None),
        P("dp", None),
        P(None, None, "tensor"),
        P(),
        P(),
        P("dp", SEQ, None, "tensor"),
    )
    out_specs = (
        P("dp", SEQ, None, "tensor"),
        P("dp", SEQ, None, "tensor"),
        P(None, None, "tensor"),
    )
    return jax.shard_map(body, mesh=fine, in_specs=in_specs, out_specs=out_specs, check_vma=False)
```

time: 1280 us -> 226 us (0.18)
  waiting for transfers between devices: 1150 us -> 70.7 us
  blocking collectives: 23.7 us -> 80.8 us
  local copies, waits for them, and re-layouts: 35.2 us -> 7.46 us
  Pallas kernels: 0 us -> 20.1 us
  matrix products: 17.8 us -> 0 us
    psum x1 -> x0, waiting for transfers between devices: 1090 us -> none  [body(): summed = lax.psum(grad_w, ('dp', 'seq'))]
    all_gather x0 -> x2, waiting for transfers between devices: none -> 43.2 us  [the longest x1 43.2 us: total_of(): own = lax.all_gather(own, ('xlo', 'y'), axis=0, tiled=True)]
    all_to_all x1 -> x3, blocking collectives: 18.4 us -> 59.8 us  [exchange(): return lax.all_to_all(parts, axes, split_axis=0, concat_axis=0, tiled=True)]
    unnamed x3 -> x2, waiting for transfers between devices: 33.5 us -> 0.03 us
    all_gather x0 -> x1, blocking collectives: none -> 21 us  [total_of(): own = lax.all_gather(own, 'dp', axis=0, tiled=True)]
    pallas_call x0 -> x4, Pallas kernels: none -> 20.1 us  [the longest x1 14.1 us: attend(): pl.pallas_call(functools.partial(attend_kernel, patches=patches, heads=he...]
    dot_general x9 -> x0, matrix products: 17.8 us -> none  [the longest x1 4.69 us: body(): jnp.einsum('cfpd,cfpk->dk', modulated, grad_frames, preferred_element_typ...]
  transfers between devices with their start and end apart: 5 -> 6, of which waited for: 4 -> 4; matrix products, arithmetic and copies ran while one was open for 3% -> 1% of each run, Pallas kernels for 0% -> 1%
where the time goes in v1:
time: 226 us
  blocking collectives  80.8 us (36%)
  waiting for transfers between devices  70.7 us (31%)
  starting transfers between devices  23.5 us (10%)
  Pallas kernels  20.1 us (9%)
  between operations  14.1 us (6%)
  other arithmetic  8.97 us (4%)
  local copies, waits for them, and re-layouts  7.46 us (3%)
    all_to_all x3, blocking collectives, exchange(): return lax.all_to_all(parts, axes, split_axis=0, concat_axis=0, tiled=True)  59.8 us
    all_gather x1, waiting for transfers between devices, total_of(): own = lax.all_gather(own, ('xlo', 'y'), axis=0, tiled=True)  43.2 us
    all_gather x1, blocking collectives, total_of(): own = lax.all_gather(own, 'dp', axis=0, tiled=True)  21 us
    all_to_all x1, waiting for transfers between devices, body(): lax.all_to_all(x, SEQ, split_axis=0, concat_axis=0, tiled=True)  14.1 us
    pallas_call x1, Pallas kernels, attend(): pl.pallas_call(functools.partial(attend_kernel, patches=patches, heads=he...  14.1 us
    all_to_all x2, starting transfers between devices, home(): rows = lax.all_to_all(rows, SEQ, split_axis=0, concat_axis=0, tiled=True)  13.8 us
    all_to_all x2, waiting for transfers between devices, home(): rows = lax.all_to_all(rows, SEQ, split_axis=0, concat_axis=0, tiled=True)  13.3 us
    unnamed x15, local copies, waits for them, and re-layouts  7.27 us
  transfers between devices with their start and end apart: 6, of which 4 were waited for; matrix products, arithmetic and copies ran while one was open for 1% of the time, Pallas kernels for 1%

profile of v1, /device:TPU:1, one launch (start us, length us, event | category | flops | bytes accessed | tf_op | source)
XLA Modules:
  0.0 225.6 jit_solution(4722748884847686432)
XLA Ops:
  7.2 1.2 copy.25
  8.4 2.1 pad_maximum_fusion
  10.5 6.9 %all-to-all-start = ((bf16[16,16,1728]{2,1,0:T(8,128)(2,1)}), bf16[16,16,1728]{2,1,0:T(8,128)(2,1)S(1)}, u32[]{:S(2)}, u32[]{:S(2)}) async-start(bf16[16,16,1728]{2,1,0:T(8,128)(2,1)} %pad_maximum_fusion), calls=%async_computation | async-start | bytes 1835008 | tf_op jit(solution)/shard_map/all_to_all | solution.py:257
  17.6 14.1 %all-to-all-done = bf16[16,16,1728]{2,1,0:T(8,128)(2,1)S(1)} async-done(((bf16[16,16,1728]{2,1,0:T(8,128)(2,1)}), bf16[16,16,1728]{2,1,0:T(8,128)(2,1)S(1)}, u32[]{:S(2)}, u32[]{:S(2)}) %all-to-all-start) | async-done | bytes 884768 | tf_op jit(solution)/shard_map/all_to_all | solution.py:257
  31.8 14.1 %attend.1 = (bf16[1024,16,128]{2,1,0:T(8,128)(2,1)}, bf16[256,1728]{1,0:T(8,128)(2,1)S(1)}, bf16[256,576]{1,0:T(8,128)(2,1)}) custom-call(bf16[256,1728]{1,0:T(8,128)(2,1)S(1)} %bitcast.21, f32[1,1152]{1,0:T(1,128)S(1)} %copy-done.3, f32[1,1152]{1,0:T(1,128)S(1)} %copy-done.2, bf16[1728,1152]{1,0:T(8,128)(2,1)} %bitcast.19, f32[72,1]{1,0:T(8,128)S(1)} %copy.26.qg_ref, ...), custom_call_target="tpu_custom_call" | custom-call | tf_op jit(solution)/shard_map/attend/pallas_call | solution.py:113
  45.8 12.3 %all_to_all.30 = bf16[2,512,16,128]{3,2,1,0:T(8,128)(2,1)} all-to-all(bf16[2,512,16,128]{3,2,1,0:T(8,128)(2,1)} %bitcast.24), channel_id=1, replica_groups=mesh['dp'=8,'xlo'=2,'y'=4,'core'=2,'tensor'=2] {'core'}, dimensions={0} | all-to-all | bytes 8388608 | tf_op jit(solution)/shard_map/all_to_all | solution.py:230
  58.2 4.9 %reduce_sum.36 = bf16[512,16,128]{2,1,0:T(8,128)(2,1)} reduce(bf16[2,512,16,128]{3,2,1,0:T(8,128)(2,1)} %all_to_all.30, bf16[]{:T(256)} %constant.8.clone.1), dimensions={0}, to_apply=%region_0.0 | reduce | flops 1048576 | bytes 6291458 | tf_op jit(solution)/shard_map/reduce_sum | solution.py:234
  63.1 30.0 %all_to_all.31 = bf16[8,64,16,128]{3,2,1,0:T(8,128)(2,1)} all-to-all(bf16[8,64,16,128]{3,2,1,0:T(8,128)(2,1)} %bitcast.23), channel_id=1, replica_groups=mesh['dp'=8,'xlo'=2,'y'=4,'core'=2,'tensor'=2] {'xlo','y'}, dimensions={0} | all-to-all | bytes 4194304 | tf_op jit(solution)/shard_map/all_to_all | solution.py:230
  93.1 2.0 reduce_sum.37
  95.1 17.4 %all_to_all.32 = bf16[8,8,16,128]{3,2,1,0:T(8,128)(2,1)S(1)} all-to-all(bf16[8,8,16,128]{3,2,1,0:T(8,128)(2,1)S(1)} %bitcast.29), channel_id=1, replica_groups=mesh['dp'=8,'xlo'=2,'y'=4,'core'=2,'tensor'=2] {'dp'}, dimensions={0} | all-to-all | bytes 524288 | tf_op jit(solution)/shard_map/all_to_all | solution.py:230
  112.6 21.0 %all_gather.9 = bf16[64,16,128]{2,1,0:T(8,128)(2,1)} all-gather(bf16[8,16,128]{2,1,0:T(8,128)(2,1)S(1)} %reduce_sum.38), channel_id=1, replica_groups=mesh['dp'=8,'xlo'=2,'y'=4,'core'=2,'tensor'=2] {'dp'}, dimensions={0}, use_global_device_ids=true | all-gather | bytes 294912 | tf_op jit(solution)/shard_map/all_gather | solution.py:239
  133.8 43.2 %all-gather.3.cloned.1.call-done = bf16[512,16,128]{2,1,0:T(8,128)(2,1)} async-done(((bf16[64,16,128]{2,1,0:T(8,128)(2,1)}), bf16[512,16,128]{2,1,0:T(8,128)(2,1)}) %all-gather.3.cloned.1.call-update) | async-done | bytes 2097168 | tf_op jit(solution)/shard_map/all_gather | solution.py:240
  177.1 2.1 copy-done
  179.2 1.9 split.1
  181.1 2.6 %collective-permute-start = (bf16[256,640]{1,0:T(8,128)(2,1)S(1)}, bf16[256,640]{1,0:T(8,128)(2,1)S(1)}, u32[]{:S(2)}, u32[]{:S(2)}) collective-permute-start(bf16[256,640]{1,0:T(8,128)(2,1)S(1)} %get-tuple-element.11), channel_id=1, source_target_pairs={{0,1},{1,0},{2,3},{3,2},{4,5},{5,4},{6,7},{7,6},{8,9},{9,8},{10,11... | collective-permute-start | bytes 983048 | tf_op jit(solution)/shard_map/ppermute | solution.py:274
  183.7 9.3 %all-to-all-start.1 = ((bf16[16,16,576]{2,1,0:T(8,128)(2,1)}), bf16[16,16,576]{2,1,0:T(8,128)(2,1)S(1)}, u32[]{:S(2)}, u32[]{:S(2)}) async-start(bf16[16,16,576]{2,1,0:T(8,128)(2,1)} %bitcast.7), calls=%async_computation.1 | async-start | bytes 655360 | tf_op jit(solution)/shard_map/all_to_all | solution.py:270
  193.0 1.4 finish.1
  194.3 6.4 %all-to-all-done.1 = bf16[16,16,576]{2,1,0:T(8,128)(2,1)S(1)} async-done(((bf16[16,16,576]{2,1,0:T(8,128)(2,1)}), bf16[16,16,576]{2,1,0:T(8,128)(2,1)S(1)}, u32[]{:S(2)}, u32[]{:S(2)}) %all-to-all-start.1) | async-done | bytes 294944 | tf_op jit(solution)/shard_map/all_to_all | solution.py:270
  200.7 4.5 %all-to-all-start.2 = ((bf16[16,16,576]{2,1,0:T(8,128)(2,1)}), bf16[16,16,576]{2,1,0:T(8,128)(2,1)S(1)}, u32[]{:S(2)}, u32[]{:S(2)}) async-start(bf16[16,16,576]{2,1,0:T(8,128)(2,1)} %bitcast.11), calls=%async_computation.2 | async-start | bytes 655360 | tf_op jit(solution)/shard_map/all_to_all | solution.py:270
  205.2 0.9 copy.28
  206.1 6.9 %all-to-all-done.2 = bf16[16,16,576]{2,1,0:T(8,128)(2,1)S(1)} async-done(((bf16[16,16,576]{2,1,0:T(8,128)(2,1)}), bf16[16,16,576]{2,1,0:T(8,128)(2,1)S(1)}, u32[]{:S(2)}, u32[]{:S(2)}) %all-to-all-start.2) | async-done | bytes 294944 | tf_op jit(solution)/shard_map/all_to_all | solution.py:270
  213.0 0.9 copy.29
  213.9 2.2 copy-done.1
  216.1 2.7 %untile.1 = bf16[1728,1152]{1,0:T(8,128)(2,1)} custom-call(bf16[1024,16,128]{2,1,0:T(8,128)(2,1)S(1)} %copy-done.1), custom_call_target="tpu_custom_call" | custom-call | tf_op jit(solution)/shard_map/untile/pallas_call | solution.py:219
  (19 shorter events, 0.6 us)
Async XLA Ops:
  7.2 10.3 %copy-start.4 = (f32[72]{0:T(128)S(1)}, f32[72]{0:T(128)}, u32[]{:S(2)}) copy-start(f32[72]{0:T(128)} %param.11) | copy-start | bytes 868
  7.2 10.4 %copy-start.5 = (f32[72]{0:T(128)S(1)}, f32[72]{0:T(128)}, u32[]{:S(2)}) copy-start(f32[72]{0:T(128)} %param.12) | copy-start | bytes 868
  7.2 24.6 %copy-start.3 = (f32[1,1152]{1,0:T(1,128)S(1)}, f32[1,1152]{1,0:T(1,128)}, u32[]{:S(2)}) copy-start(f32[1,1152]{1,0:T(1,128)} %shift_ref.1) | copy-start | bytes 13828
  7.2 24.6 %copy-start.2 = (f32[1,1152]{1,0:T(1,128)S(1)}, f32[1,1152]{1,0:T(1,128)}, u32[]{:S(2)}) copy-start(f32[1,1152]{1,0:T(1,128)} %scale_ref.3) | copy-start | bytes 13828
  10.5 21.3 %all-to-all-start = ((bf16[16,16,1728]{2,1,0:T(8,128)(2,1)}), bf16[16,16,1728]{2,1,0:T(8,128)(2,1)S(1)}, u32[]{:S(2)}, u32[]{:S(2)}) async-start(bf16[16,16,1728]{2,1,0:T(8,128)(2,1)} %pad_maximum_fusion), calls=%async_computation | async-start | bytes 1835008 | tf_op jit(solution)/shard_map/all_to_all | solution.py:257
  17.4 159.7 %all-gather.3.cloned.1.call-start = ((), (), s32[]{:S(2)}) async-start(), calls=%async_computation.6 | async-start | bytes 2359296 | tf_op jit(solution)/shard_map/all_gather | solution.py:240
  133.6 80.3 %all-gather.5.cloned.1.call-start = ((), (), s32[]{:S(2)}) async-start(), calls=%async_computation.7 | async-start | bytes 6291456 | tf_op jit(solution)/shard_map/all_gather | solution.py:241
  177.1 2.1 copy-start
  181.1 11.9 %collective-permute-start = (bf16[256,640]{1,0:T(8,128)(2,1)S(1)}, bf16[256,640]{1,0:T(8,128)(2,1)S(1)}, u32[]{:S(2)}, u32[]{:S(2)}) collective-permute-start(bf16[256,640]{1,0:T(8,128)(2,1)S(1)} %get-tuple-element.11), channel_id=1, source_target_pairs={{0,1},{1,0},{2,3},{3,2},{4,5},{5,4},{6,7},{7,6},{8,9},{9,8},{10,11... | collective-permute-start | bytes 983048 | tf_op jit(solution)/shard_map/ppermute | solution.py:274
  183.7 17.0 %all-to-all-start.1 = ((bf16[16,16,576]{2,1,0:T(8,128)(2,1)}), bf16[16,16,576]{2,1,0:T(8,128)(2,1)S(1)}, u32[]{:S(2)}, u32[]{:S(2)}) async-start(bf16[16,16,576]{2,1,0:T(8,128)(2,1)} %bitcast.7), calls=%async_computation.1 | async-start | bytes 655360 | tf_op jit(solution)/shard_map/all_to_all | solution.py:270
  200.7 12.3 %all-to-all-start.2 = ((bf16[16,16,576]{2,1,0:T(8,128)(2,1)}), bf16[16,16,576]{2,1,0:T(8,128)(2,1)S(1)}, u32[]{:S(2)}, u32[]{:S(2)}) async-start(bf16[16,16,576]{2,1,0:T(8,128)(2,1)} %bitcast.11), calls=%async_computation.2 | async-start | bytes 655360 | tf_op jit(solution)/shard_map/all_to_all | solution.py:270
  213.9 2.2 copy-start.1
Sparse Core Ops, SparseCore 0:
  133.7 43.2 all-gather.2
  178.8 24.2 all-gather.4

commit v2 on v1

--- a/solution.py
+++ b/solution.py
@@ -14,7 +14,8 @@
 NN = (((1,), (0,)), ((), ()))
 NT = (((1,), (1,)), ((), ()))
 ROWS, LANES = 16, 128
-SEQ = ("xlo", "y", "core")
+PLANE = ("xlo", "y")
+SEQ = PLANE + ("core",)
 
 
 def mm(a, b, dims):
@@ -34,8 +35,8 @@
     return centred * inverse, inverse
 
 
-def attend_kernel(x_ref, shift_ref, scale_ref, wt_ref, qg_ref, kg_ref,
-                  gw_ref, gp_ref, att_ref, mod_s, gpt_s, ot_s, *, patches, heads, hd):
+def attend_kernel(core_ref, x_ref, shift_ref, scale_ref, wt_ref, qg_ref, kg_ref,
+                  keep_ref, send_ref, gp_ref, att_ref, mod_s, gpt_s, ot_s, gw_ref, *, patches, heads, hd):
     tokens, total = x_ref.shape
     width = scale_ref.shape[1]
     hw = heads * hd
@@ -103,17 +104,24 @@
             gw_ref[j * all_tiles + base : j * all_tiles + base + tiles] = found
     used = 3 * (hw // ROWS) * (width // LANES)
     gw_ref[used:] = jnp.zeros((gw_ref.shape[0] - used, ROWS, LANES), BF)
+    size = keep_ref.shape[0]
+    keep_ref[...] = gw_ref[pl.ds(core_ref[0] * size, size)]
+    send_ref[...] = gw_ref[pl.ds((1 - core_ref[0]) * size, size)]
     att_ref[...] = mm(ident, ot_s[...].astype(BF), NT).astype(BF)
 
 
-def attend(x, shift, scale, wt, qg, kg, patches, heads, hd, padded):
+def attend(core, x, shift, scale, wt, qg, kg, patches, heads, hd, padded):
     tokens = x.shape[0]
     width = wt.shape[1]
     hw = heads * hd
+    smem = pl.BlockSpec(memory_space=pltpu.SMEM)
+    vmem = pl.BlockSpec(memory_space=pltpu.VMEM)
     return pl.pallas_call(
         functools.partial(attend_kernel, patches=patches, heads=heads, hd=hd),
+        in_specs=[smem] + [vmem] * 6,
         out_shape=(
-            jax.ShapeDtypeStruct((padded, ROWS, LANES), BF),
+            jax.ShapeDtypeStruct((padded // 2, ROWS, LANES), BF),
+            jax.ShapeDtypeStruct((padded // 2, ROWS, LANES), BF),
             jax.ShapeDtypeStruct((tokens, 3 * hw), BF),
             jax.ShapeDtypeStruct((tokens, hw), BF),
         ),
@@ -121,10 +129,11 @@
             pltpu.VMEM((tokens, width), BF),
             pltpu.VMEM((3 * hw, tokens), F32),
             pltpu.VMEM((hw, tokens), F32),
+            pltpu.VMEM((padded, ROWS, LANES), BF),
         ],
-        compiler_params=pltpu.CompilerParams(vmem_limit_bytes=48 * 2**20),
+        compiler_params=pltpu.CompilerParams(vmem_limit_bytes=24 * 2**20),
         name="attend",
-    )(x, shift, scale, wt, qg, kg)
+    )(core, x, shift, scale, wt, qg, kg)
 
 
 def window_of(half):
@@ -171,7 +180,7 @@
             jax.ShapeDtypeStruct((tokens, win), F32),
             jax.ShapeDtypeStruct((tokens, win), F32),
         ),
-        compiler_params=pltpu.CompilerParams(vmem_limit_bytes=40 * 2**20),
+        compiler_params=pltpu.CompilerParams(vmem_limit_bytes=16 * 2**20),
         name="split",
     )(which, x, scale, wt, gp)
 
@@ -208,37 +217,120 @@
     )(which, recv, keep, unit)
 
 
-def untile_kernel(tiles_ref, out_ref, *, factor):
+def merge_kernel(where_ref, keep_ref, got_ref, *out_refs):
+    count = len(out_refs)
+    size = keep_ref.shape[0] // count
+    for k, out_ref in enumerate(out_refs):
+        rows = pl.ds((where_ref[0] ^ k) * size, size)
+        out_ref[...] = (keep_ref[rows].astype(F32) + got_ref[rows].astype(F32)).astype(BF)
+
+
+def merge(where, keep, got, count):
+    smem = pl.BlockSpec(memory_space=pltpu.SMEM)
+    vmem = pl.BlockSpec(memory_space=pltpu.VMEM)
+    shape = (keep.shape[0] // count,) + keep.shape[1:]
+    return pl.pallas_call(
+        merge_kernel,
+        in_specs=[smem, vmem, vmem],
+        out_shape=tuple(jax.ShapeDtypeStruct(shape, BF) for _ in range(count)),
+        compiler_params=pltpu.CompilerParams(vmem_limit_bytes=24 * 2**20),
+        name="merge",
+    )(where, keep, got)
+
+
+def sum_kernel(*refs):
+    total = refs[0][...].astype(F32)
+    for ref in refs[1:-1]:
+        total = total + ref[...].astype(F32)
+    refs[-1][...] = total.astype(BF)
+
+
+def sum_of(parts):
+    return pl.pallas_call(
+        sum_kernel,
+        out_shape=jax.ShapeDtypeStruct(parts[0].shape, BF),
+        compiler_params=pltpu.CompilerParams(vmem_limit_bytes=8 * 2**20),
+        name="sum_of",
+    )(*parts)
+
+
+def spread_kernel(parts_ref, out_ref, *, factor):
+    total = jnp.sum(parts_ref[...].astype(F32), axis=0) * factor
+    total = total.astype(BF)
+    for k in range(out_ref.shape[0]):
+        out_ref[k] = total
+
+
+def spread(parts, factor):
+    return pl.pallas_call(
+        functools.partial(spread_kernel, factor=factor),
+        out_shape=jax.ShapeDtypeStruct(parts.shape, BF),
+        compiler_params=pltpu.CompilerParams(vmem_limit_bytes=8 * 2**20),
+        name="spread",
+    )(parts)
+
+
+def untile_kernel(where_ref, half_ref, *refs):
+    pieces, (out_ref, tiles_s) = refs[:-2], refs[-2:]
+    count = len(pieces) // 2
+    size = pieces[0].shape[0]
+    for side in range(2):
+        half = half_ref[0] ^ side
+        for k in range(count):
+            base = (half * count + (where_ref[0] ^ k)) * size
+            tiles_s[pl.ds(base, size)] = pieces[side * count + k][...]
     rows = out_ref.shape[0] // ROWS
     for j in range(out_ref.shape[1] // LANES):
-        block = tiles_ref[j * rows : (j + 1) * rows].astype(F32) * factor
-        out_ref[:, j * LANES : (j + 1) * LANES] = block.reshape(rows * ROWS, LANES).astype(BF)
-
-
-def untile(tiles, rows, width, factor):
-    return pl.pallas_call(
-        functools.partial(untile_kernel, factor=factor),
+        block = tiles_s[j * rows : (j + 1) * rows]
+        out_ref[:, j * LANES : (j + 1) * LANES] = block.reshape(rows * ROWS, LANES)
+
+
+def untile(where, half, pieces, rows, width):
+    smem = pl.BlockSpec(memory_space=pltpu.SMEM)
+    vmem = pl.BlockSpec(memory_space=pltpu.VMEM)
+    tiles = len(pieces) * pieces[0].shape[0]
+    return pl.pallas_call(
+        untile_kernel,
+        in_specs=[smem, smem] + [vmem] * len(pieces),
         out_shape=jax.ShapeDtypeStruct((rows, width), BF),
-        compiler_params=pltpu.CompilerParams(vmem_limit_bytes=40 * 2**20),
+        scratch_shapes=[pltpu.VMEM((tiles, ROWS, LANES), BF)],
+        compiler_params=pltpu.CompilerParams(vmem_limit_bytes=16 * 2**20),
         name="untile",
-    )(tiles)
-
-
-def exchange(x, axes):
+    )(where, half, *pieces)
+
+
+def swap(x, axes, k):
     count = math.prod(lax.axis_size(a) for a in axes)
-    parts = x.reshape((count, x.shape[0] // count) + x.shape[1:])
-    return lax.all_to_all(parts, axes, split_axis=0, concat_axis=0, tiled=True)
-
-
-def scatter_sum(x, axes):
-    return jnp.sum(exchange(x, axes).astype(F32), axis=0).astype(BF)
-
-
-def total_of(tiles):
-    own = scatter_sum(scatter_sum(scatter_sum(tiles, ("core",)), ("xlo", "y")), ("dp",))
-    own = lax.all_gather(own, "dp", axis=0, tiled=True)
-    own = lax.all_gather(own, ("xlo", "y"), axis=0, tiled=True)
-    return lax.all_gather(own, "core", axis=0, tiled=True)
+    return lax.ppermute(x, axes, [(i, i ^ k) for i in range(count)])
+
+
+def exchange(x, axis):
+    parts = x.reshape((-1,) + x.shape[-3:])
+    return lax.all_to_all(parts, axis, split_axis=0, concat_axis=0, tiled=True)
+
+
+def plane_size():
+    return lax.axis_size("xlo") * lax.axis_size("y")
+
+
+def scatter_plane(keep, send):
+    where = lax.axis_index(PLANE).astype(jnp.int32).reshape(1)
+    parts = merge(where, keep, swap(send, ("core",), 1), plane_size())
+    return [parts[0]] + [swap(part, PLANE, k + 1) for k, part in enumerate(parts[1:])]
+
+
+def sum_clips(own, factor):
+    clips = lax.axis_size("dp")
+    parts = own.reshape((clips, own.shape[0] // clips) + own.shape[1:])
+    return exchange(spread(exchange(parts, "dp"), factor), "dp").reshape(own.shape)
+
+
+def gather_plane(own, rows, width):
+    where = lax.axis_index(PLANE).astype(jnp.int32).reshape(1)
+    half = lax.axis_index("core").astype(jnp.int32).reshape(1)
+    pieces = [own] + [swap(own, PLANE, k) for k in range(1, plane_size())]
+    pieces = pieces + [swap(piece, ("core",), 1) for piece in pieces]
+    return untile(where, half, pieces, rows, width)
 
 
 def body(latent, mod_shift, mod_scale, w_qkv, q_gain, k_gain, cotangent):
@@ -260,8 +352,8 @@
         group *= lax.axis_size(a)
     used = (3 * hw // ROWS) * (width // LANES)
     padded = -(-used // group) * group
-    gw, gp, attended = attend(
-        x, mod_shift, mod_scale, wt, q_gain[:, None], k_gain[:, None], own_patches, heads, hd, padded
+    keep_w, send_w, gp, attended = attend(
+        lax.axis_index("core").astype(jnp.int32).reshape(1), x, mod_shift, mod_scale, wt, q_gain[:, None], k_gain[:, None], own_patches, heads, hd, padded
     )
     which = lax.axis_index("tensor").astype(jnp.int32).reshape(1)
 
@@ -270,13 +362,18 @@
         rows = lax.all_to_all(rows, SEQ, split_axis=0, concat_axis=0, tiled=True)
         return rows.reshape(1, 1, patches, hw)
 
+    attended = home(attended)
     send, keep, unit = split(which, x, mod_scale, wt, gp)
     recv = lax.ppermute(send, "tensor", [(0, 1), (1, 0)])
-    grad_latent = home(finish(which, recv, keep, unit, width))
+    parts = scatter_plane(keep_w, send_w)
+    parts, recv, attended = lax.optimization_barrier((parts, recv, attended))
+    grad_latent = finish(which, recv, keep, unit, width)
+    own, grad_latent = lax.optimization_barrier((sum_of(parts), grad_latent))
+    grad_latent = home(grad_latent)
     factor = 1.0 / math.sqrt(clips * frames * patches)
-    grad_qkv = untile(total_of(gw), 3 * hw, width, factor)
+    grad_qkv = gather_plane(sum_clips(own, factor), 3 * hw, width)
     grad_qkv = grad_qkv.reshape(3, hw, width).transpose(2, 0, 1)
-    return (home(attended), grad_latent, grad_qkv)
+    return (attended, grad_latent, grad_qkv)
 
 
 def solution(mesh):

time: 226 us -> 176 us (0.78)
  blocking collectives: 80.8 us -> 30.2 us
  starting transfers between devices: 23.5 us -> 43.3 us
  between operations: 14.1 us -> 0.76 us
  waiting for transfers between devices: 70.7 us -> 58.9 us
  local copies, waits for them, and re-layouts: 7.46 us -> 17.7 us
  other arithmetic: 8.97 us -> 2.06 us
  Pallas kernels: 20.1 us -> 22.8 us
    all_gather x2 -> x0, waiting for transfers between devices: 43.2 us -> none  [the longest x1 43.2 us: total_of(): own = lax.all_gather(own, ('xlo', 'y'), axis=0, tiled=True)]
    ppermute x0 -> x23, waiting for transfers between devices: none -> 39.1 us  [swap(): return lax.ppermute(x, axes, [(i, i ^ k) for i in range(count)])]
    all_to_all x3 -> x2, blocking collectives: 59.8 us -> 30.2 us  [exchange(): return lax.all_to_all(parts, axis, split_axis=0, concat_axis=0, tiled=True)]
    ppermute x0 -> x23, starting transfers between devices: none -> 24.8 us  [swap(): return lax.ppermute(x, axes, [(i, i ^ k) for i in range(count)])]
    all_gather x1 -> x0, blocking collectives: 21 us -> none  [total_of(): own = lax.all_gather(own, 'dp', axis=0, tiled=True)]
    unnamed x15 -> x37, local copies, waits for them, and re-layouts: 7.27 us -> 17.5 us
    all_to_all x2, waiting for transfers between devices: 13.3 us -> 5.59 us  [home(): rows = lax.all_to_all(rows, SEQ, split_axis=0, concat_axis=0, tiled=True)]
    reduce_sum x3 -> x0, other arithmetic: 6.9 us -> none  [scatter_sum(): return jnp.sum(exchange(x, axes).astype(F32), axis=0).astype(BF)]
  transfers between devices with their start and end apart: 6 -> 27, of which waited for: 4 -> 13; matrix products, arithmetic and copies ran while one was open for 1% -> 2% of each run, Pallas kernels for 1% -> 3%
where the time goes in v2:
time: 176 us
  waiting for transfers between devices  58.9 us (33%)
  starting transfers between devices  43.3 us (25%)
  blocking collectives  30.2 us (17%)
  Pallas kernels  22.8 us (13%)
  local copies, waits for them, and re-layouts  17.7 us (10%)
  other arithmetic  2.06 us (1%)
    ppermute x23, waiting for transfers between devices, swap(): return lax.ppermute(x, axes, [(i, i ^ k) for i in range(count)])  39.1 us
    all_to_all x2, blocking collectives, exchange(): return lax.all_to_all(parts, axis, split_axis=0, concat_axis=0, tiled=True)  30.2 us
    ppermute x23, starting transfers between devices, swap(): return lax.ppermute(x, axes, [(i, i ^ k) for i in range(count)])  24.8 us
    unnamed x37, local copies, waits for them, and re-layouts  17.5 us
    all_to_all x1, waiting for transfers between devices, body(): lax.all_to_all(x, SEQ, split_axis=0, concat_axis=0, tiled=True)  14.2 us
    pallas_call x1, Pallas kernels, attend(): pl.pallas_call(functools.partial(attend_kernel, patches=patches, heads=he...  11.6 us
    all_to_all x2, starting transfers between devices, home(): rows = lax.all_to_all(rows, SEQ, split_axis=0, concat_axis=0, tiled=True)  9.16 us
    all_to_all x1, starting transfers between devices, body(): lax.all_to_all(x, SEQ, split_axis=0, concat_axis=0, tiled=True)  6.91 us
  transfers between devices with their start and end apart: 27, of which 13 were waited for; matrix products, arithmetic and copies ran while one was open for 2% of the time, Pallas kernels for 3%

profile of v2, /device:TPU:1, one launch (start us, length us, event | category | flops | bytes accessed | tf_op | source)
XLA Modules:
  0.0 175.6 jit_solution(14221524550647244452)
XLA Ops:
  3.9 6.9 %all-to-all-start = ((bf16[16,16,1728]{2,1,0:T(8,128)(2,1)}), bf16[16,16,1728]{2,1,0:T(8,128)(2,1)S(1)}, u32[]{:S(2)}, u32[]{:S(2)}) async-start(bf16[16,16,1728]{2,1,0:T(8,128)(2,1)} %pad_maximum_fusion), calls=%async_computation | async-start | bytes 1835008 | tf_op jit(solution)/shard_map/all_to_all | solution.py:349
  11.0 14.2 %all-to-all-done = bf16[16,16,1728]{2,1,0:T(8,128)(2,1)S(1)} async-done(((bf16[16,16,1728]{2,1,0:T(8,128)(2,1)}), bf16[16,16,1728]{2,1,0:T(8,128)(2,1)S(1)}, u32[]{:S(2)}, u32[]{:S(2)}) %all-to-all-start) | async-done | bytes 884768 | tf_op jit(solution)/shard_map/all_to_all | solution.py:349
  27.4 11.6 %attend.1 = (bf16[512,16,128]{2,1,0:T(8,128)(2,1)S(1)}, bf16[512,16,128]{2,1,0:T(8,128)(2,1)}, bf16[256,1728]{1,0:T(8,128)(2,1)S(1)}, bf16[256,576]{1,0:T(8,128)(2,1)}) custom-call(s32[1]{0:T(128)} %bitcast.1.core_ref.half_ref, bf16[256,1728]{1,0:T(8,128)(2,1)S(1)} %bitcast.22, f32[1,1152]{1,0:T(1,128)S(1)} %copy-done.9, f32[1,1152]{1,0:T(1,128)S(1)} %copy-done.8, ...), custom_call_target="tpu_custom_call" | custom-call | tf_op jit(solution)/shard_map/attend/pallas_call | solution.py:119
  44.0 2.7 %split.1 = (bf16[256,640]{1,0:T(8,128)(2,1)}, f32[256,640]{1,0:T(8,128)S(1)}, f32[256,640]{1,0:T(8,128)S(1)}) custom-call(s32[1]{0:T(128)} %bitcast.9.which_ref, bf16[256,1728]{1,0:T(8,128)(2,1)S(1)} %bitcast.23, f32[1,1152]{1,0:T(1,128)S(1)} %copy-done.8, bf16[1728,1152]{1,0:T(8,128)(2,1)S(1)} %bitcast.21, bf16[256,1728]{1,0:T(8,128)(2,1)S(1)} %copy-done.3), custom_call_target="tpu_custom_call" | custom-call | tf_op jit(solution)/shard_map/split/pallas_call | solution.py:175
  48.4 2.5 %collective-permute-start.8 = (bf16[256,640]{1,0:T(8,128)(2,1)}, bf16[256,640]{1,0:T(8,128)(2,1)S(1)}, u32[]{:S(2)}, u32[]{:S(2)}) collective-permute-start(bf16[256,640]{1,0:T(8,128)(2,1)} %get-tuple-element.41), channel_id=1, source_target_pairs={{0,1},{1,0},{2,3},{3,2},{4,5},{5,4},{6,7},{7,6},{8,9},{9,8},{10,11... | collective-permute-start | bytes 983048 | tf_op jit(solution)/shard_map/ppermute | solution.py:367
  50.9 2.8 %merge.1 = (bf16[64,16,128]{2,1,0:T(8,128)(2,1)S(1)}, bf16[64,16,128]{2,1,0:T(8,128)(2,1)}, bf16[64,16,128]{2,1,0:T(8,128)(2,1)}, bf16[64,16,128]{2,1,0:T(8,128)...) custom-call(s32[1]{0:T(128)} %bitcast.where_ref, ...), custom_call_target="tpu_custom_call" | custom-call | tf_op jit(solution)/shard_map/merge/pallas_call | solution.py:232
  57.2 2.2 %collective-permute-start.2 = (bf16[64,16,128]{2,1,0:T(8,128)(2,1)}, bf16[64,16,128]{2,1,0:T(8,128)(2,1)S(1)}, u32[]{:S(2)}, u32[]{:S(2)}) collective-permute-start(bf16[64,16,128]{2,1,0:T(8,128)(2,1)} %get-tuple-element.34), channel_id=1, source_target_pairs={{0,8},{4,12},{8,0},{12,4},{16,24},{20,28},{24,16},{28,20},{1,9},{5... | collective-permute-start | bytes 786440 | tf_op jit(solution)/shard_map/ppermute | solution.py:304
  59.4 5.1 %all-to-all-start.1 = ((bf16[16,16,576]{2,1,0:T(8,128)(2,1)}), bf16[16,16,576]{2,1,0:T(8,128)(2,1)}, u32[]{:S(2)}, u32[]{:S(2)}) async-start(bf16[16,16,576]{2,1,0:T(8,128)(2,1)} %bitcast.11), calls=%async_computation.1 | async-start | bytes 655360 | tf_op jit(solution)/shard_map/all_to_all | solution.py:362
  64.4 2.6 %collective-permute-start.3 = (bf16[64,16,128]{2,1,0:T(8,128)(2,1)}, bf16[64,16,128]{2,1,0:T(8,128)(2,1)S(1)}, u32[]{:S(2)}, u32[]{:S(2)}) collective-permute-start(bf16[64,16,128]{2,1,0:T(8,128)(2,1)} %copy-done.14), channel_id=1, source_target_pairs={{0,12},{4,8},{8,4},{12,0},{16,28},{20,24},{24,20},{28,16},{1,13},{... | collective-permute-start | bytes 786440 | tf_op jit(solution)/shard_map/ppermute | solution.py:304
  68.3 2.3 %collective-permute-start.6 = (bf16[64,16,128]{2,1,0:T(8,128)(2,1)}, bf16[64,16,128]{2,1,0:T(8,128)(2,1)S(1)}, u32[]{:S(2)}, u32[]{:S(2)}) collective-permute-start(bf16[64,16,128]{2,1,0:T(8,128)(2,1)} %copy-done.11), channel_id=1, source_target_pairs={{0,24},{4,28},{8,16},{12,20},{16,8},{20,12},{24,0},{28,4},{1,25},{... | collective-permute-start | bytes 786440 | tf_op jit(solution)/shard_map/ppermute | solution.py:304
  75.6 5.5 %collective-permute-done.3.refs_3_ = bf16[64,16,128]{2,1,0:T(8,128)(2,1)S(1)} collective-permute-done((bf16[64,16,128]{2,1,0:T(8,128)(2,1)}, bf16[64,16,128]{2,1,0:T(8,128)(2,1)S(1)}, u32[]{:S(2)}, u32[]{:S(2)}) %collective-permute-start.3) | collective-permute-done | bytes 262176 | tf_op jit(solution)/shard_map/ppermute | solution.py:304
  82.5 7.1 %collective-permute-done.6.refs_6_ = bf16[64,16,128]{2,1,0:T(8,128)(2,1)S(1)} collective-permute-done((bf16[64,16,128]{2,1,0:T(8,128)(2,1)}, bf16[64,16,128]{2,1,0:T(8,128)(2,1)S(1)}, u32[]{:S(2)}, u32[]{:S(2)}) %collective-permute-start.6) | collective-permute-done | bytes 262176 | tf_op jit(solution)/shard_map/ppermute | solution.py:304
  89.6 5.6 %collective-permute-done.7.refs_7_ = bf16[64,16,128]{2,1,0:T(8,128)(2,1)S(1)} collective-permute-done((bf16[64,16,128]{2,1,0:T(8,128)(2,1)}, bf16[64,16,128]{2,1,0:T(8,128)(2,1)S(1)}, u32[]{:S(2)}, u32[]{:S(2)}) %collective-permute-start.7) | collective-permute-done | bytes 262176 | tf_op jit(solution)/shard_map/ppermute | solution.py:304
  97.9 18.1 %all_to_all.25.parts_ref = bf16[8,8,16,128]{3,2,1,0:T(8,128)(2,1)S(1)} all-to-all(bf16[8,8,16,128]{3,2,1,0:T(8,128)(2,1)S(1)} %bitcast.33), channel_id=1, replica_groups=mesh['dp'=8,'xlo'=2,'y'=4,'core'=2,'tensor'=2] {'dp'}, dimensions={0} | all-to-all | bytes 524288 | tf_op jit(solution)/shard_map/all_to_all | solution.py:309
  116.0 12.1 %all_to_all.26 = bf16[8,8,16,128]{3,2,1,0:T(8,128)(2,1)S(1)} all-to-all(bf16[8,8,16,128]{3,2,1,0:T(8,128)(2,1)S(1)} %spread.1), channel_id=1, replica_groups=mesh['dp'=8,'xlo'=2,'y'=4,'core'=2,'tensor'=2] {'dp'}, dimensions={0} | all-to-all | bytes 524288 | tf_op jit(solution)/shard_map/all_to_all | solution.py:309
  128.1 3.5 %collective-permute-start.16 = (bf16[64,16,128]{2,1,0:T(8,128)(2,1)S(1)}, bf16[64,16,128]{2,1,0:T(8,128)(2,1)S(1)}, u32[]{:S(2)}, u32[]{:S(2)}) collective-permute-start(bf16[64,16,128]{2,1,0:T(8,128)(2,1)S(1)} %bitcast.24), channel_id=1, source_target_pairs={{0,2},{2,0},{1,3},{3,1},{4,6},{6,4},{5,7},{7,5},{8,10},{10,8},{9,1... | collective-permute-start | bytes 786440 | tf_op jit(solution)/shard_map/ppermute | solution.py:304
  131.8 2.8 %collective-permute-start.14 = (bf16[64,16,128]{2,1,0:T(8,128)(2,1)S(1)}, bf16[64,16,128]{2,1,0:T(8,128)(2,1)S(1)}, u32[]{:S(2)}, u32[]{:S(2)}) collective-permute-start(bf16[64,16,128]{2,1,0:T(8,128)(2,1)S(1)} %bitcast.26), channel_id=1, source_target_pairs={{0,24},{4,28},{8,16},{12,20},{16,8},{20,12},{24,0},{28,4},{1,25},{... | collective-permute-start | bytes 786440 | tf_op jit(solution)/shard_map/ppermute | solution.py:304
  137.9 3.9 %collective-permute-done.15.refs_7_ = bf16[64,16,128]{2,1,0:T(8,128)(2,1)S(1)} collective-permute-done((bf16[64,16,128]{2,1,0:T(8,128)(2,1)S(1)}, bf16[64,16,128]{2,1,0:T(8,128)(2,1)S(1)}, u32[]{:S(2)}, u32[]{:S(2)}) %collective-permute-start.15) | collective-permute-done | bytes 262176 | tf_op jit(solution)/shard_map/ppermute | solution.py:304
  141.8 5.5 %collective-permute-done.14.refs_6_ = bf16[64,16,128]{2,1,0:T(8,128)(2,1)S(1)} collective-permute-done((bf16[64,16,128]{2,1,0:T(8,128)(2,1)S(1)}, bf16[64,16,128]{2,1,0:T(8,128)(2,1)S(1)}, u32[]{:S(2)}, u32[]{:S(2)}) %collective-permute-start.14) | collective-permute-done | bytes 262176 | tf_op jit(solution)/shard_map/ppermute | solution.py:304
  148.0 3.5 %collective-permute-done.13.refs_5_ = bf16[64,16,128]{2,1,0:T(8,128)(2,1)S(1)} collective-permute-done((bf16[64,16,128]{2,1,0:T(8,128)(2,1)S(1)}, bf16[64,16,128]{2,1,0:T(8,128)(2,1)S(1)}, u32[]{:S(2)}, u32[]{:S(2)}) %collective-permute-start.13) | collective-permute-done | bytes 262176 | tf_op jit(solution)/shard_map/ppermute | solution.py:304
  152.7 4.5 %collective-permute-done.12.refs_4_ = bf16[64,16,128]{2,1,0:T(8,128)(2,1)S(1)} collective-permute-done((bf16[64,16,128]{2,1,0:T(8,128)(2,1)S(1)}, bf16[64,16,128]{2,1,0:T(8,128)(2,1)S(1)}, u32[]{:S(2)}, u32[]{:S(2)}) %collective-permute-start.12) | collective-permute-done | bytes 262176 | tf_op jit(solution)/shard_map/ppermute | solution.py:304
  157.9 4.1 %all-to-all-start.2 = ((bf16[16,16,576]{2,1,0:T(8,128)(2,1)}), bf16[16,16,576]{2,1,0:T(8,128)(2,1)}, u32[]{:S(2)}, u32[]{:S(2)}) async-start(bf16[16,16,576]{2,1,0:T(8,128)(2,1)} %bitcast.13), calls=%async_computation.2 | async-start | bytes 655360 | tf_op jit(solution)/shard_map/all_to_all | solution.py:362
  165.8 3.9 %all-to-all-done.2 = bf16[16,16,576]{2,1,0:T(8,128)(2,1)} async-done(((bf16[16,16,576]{2,1,0:T(8,128)(2,1)}), bf16[16,16,576]{2,1,0:T(8,128)(2,1)}, u32[]{:S(2)}, u32[]{:S(2)}) %all-to-all-start.2) | async-done | bytes 294944 | tf_op jit(solution)/shard_map/all_to_all | solution.py:362
  171.6 4.0 %untile.1 = bf16[1728,1152]{1,0:T(8,128)(2,1)} custom-call(s32[1]{0:T(128)} %bitcast.where_ref, s32[1]{0:T(128)} %bitcast.1.core_ref.half_ref, bf16[64,16,128]{2,1,0:T(8,128)(2,1)S(1)} %bitcast.32, bf16[64,16,128]{2,1,0:T(8,128)(2,1)S(1)} %collective-permute-done.9.refs_1_, bf16[64,16,128]{2,1,0:T(8,128)(2,1)S(1)} %collective-permute-done.10.refs_2_, ...), custom_call_target="tpu_custom_call" | custom-call | tf_op jit(solution)/shard_map/untile/pallas_call | solution.py:292
  (79 shorter events, 37.9 us)
Async XLA Ops:
  3.9 21.3 %all-to-all-start = ((bf16[16,16,1728]{2,1,0:T(8,128)(2,1)}), bf16[16,16,1728]{2,1,0:T(8,128)(2,1)S(1)}, u32[]{:S(2)}, u32[]{:S(2)}) async-start(bf16[16,16,1728]{2,1,0:T(8,128)(2,1)} %pad_maximum_fusion), calls=%async_computation | async-start | bytes 1835008 | tf_op jit(solution)/shard_map/all_to_all | solution.py:349
  39.9 11.0 %collective-permute-start = (bf16[512,16,128]{2,1,0:T(8,128)(2,1)}, bf16[512,16,128]{2,1,0:T(8,128)(2,1)}, u32[]{:S(2)}, u32[]{:S(2)}) collective-permute-start(bf16[512,16,128]{2,1,0:T(8,128)(2,1)} %get-tuple-element.31), channel_id=1, source_target_pairs={{0,2},{2,0},{1,3},{3,1},{4,6},{6,4},{5,7},{7,5},{8,10},{10,8},{9,1... | collective-permute-start | bytes 6291464 | tf_op jit(solution)/shard_map/ppermute | solution.py:304
  48.4 19.9 %collective-permute-start.8 = (bf16[256,640]{1,0:T(8,128)(2,1)}, bf16[256,640]{1,0:T(8,128)(2,1)S(1)}, u32[]{:S(2)}, u32[]{:S(2)}) collective-permute-start(bf16[256,640]{1,0:T(8,128)(2,1)} %get-tuple-element.41), channel_id=1, source_target_pairs={{0,1},{1,0},{2,3},{3,2},{4,5},{5,4},{6,7},{7,6},{8,9},{9,8},{10,11... | collective-permute-start | bytes 983048 | tf_op jit(solution)/shard_map/ppermute | solution.py:367
  57.2 11.1 %collective-permute-start.1 = (bf16[64,16,128]{2,1,0:T(8,128)(2,1)}, bf16[64,16,128]{2,1,0:T(8,128)(2,1)S(1)}, u32[]{:S(2)}, u32[]{:S(2)}) collective-permute-start(bf16[64,16,128]{2,1,0:T(8,128)(2,1)} %get-tuple-element.33), channel_id=1, source_target_pairs={{0,4},{4,0},{8,12},{12,8},{16,20},{20,16},{24,28},{28,24},{1,5},{5... | collective-permute-start | bytes 786440 | tf_op jit(solution)/shard_map/ppermute | solution.py:304
  57.2 15.1 %collective-permute-start.2 = (bf16[64,16,128]{2,1,0:T(8,128)(2,1)}, bf16[64,16,128]{2,1,0:T(8,128)(2,1)S(1)}, u32[]{:S(2)}, u32[]{:S(2)}) collective-permute-start(bf16[64,16,128]{2,1,0:T(8,128)(2,1)} %get-tuple-element.34), channel_id=1, source_target_pairs={{0,8},{4,12},{8,0},{12,4},{16,24},{20,28},{24,16},{28,20},{1,9},{5... | collective-permute-start | bytes 786440 | tf_op jit(solution)/shard_map/ppermute | solution.py:304
  59.4 16.3 %all-to-all-start.1 = ((bf16[16,16,576]{2,1,0:T(8,128)(2,1)}), bf16[16,16,576]{2,1,0:T(8,128)(2,1)}, u32[]{:S(2)}, u32[]{:S(2)}) async-start(bf16[16,16,576]{2,1,0:T(8,128)(2,1)} %bitcast.11), calls=%async_computation.1 | async-start | bytes 655360 | tf_op jit(solution)/shard_map/all_to_all | solution.py:362
  64.4 16.7 %collective-permute-start.3 = (bf16[64,16,128]{2,1,0:T(8,128)(2,1)}, bf16[64,16,128]{2,1,0:T(8,128)(2,1)S(1)}, u32[]{:S(2)}, u32[]{:S(2)}) collective-permute-start(bf16[64,16,128]{2,1,0:T(8,128)(2,1)} %copy-done.14), channel_id=1, source_target_pairs={{0,12},{4,8},{8,4},{12,0},{16,28},{20,24},{24,20},{28,16},{1,13},{... | collective-permute-start | bytes 786440 | tf_op jit(solution)/shard_map/ppermute | solution.py:304
  67.0 14.1 %collective-permute-start.4 = (bf16[64,16,128]{2,1,0:T(8,128)(2,1)}, bf16[64,16,128]{2,1,0:T(8,128)(2,1)S(1)}, u32[]{:S(2)}, u32[]{:S(2)}) collective-permute-start(bf16[64,16,128]{2,1,0:T(8,128)(2,1)} %copy-done.13), channel_id=1, source_target_pairs={{0,16},{4,20},{8,24},{12,28},{16,0},{20,4},{24,8},{28,12},{1,17},{... | collective-permute-start | bytes 786440 | tf_op jit(solution)/shard_map/ppermute | solution.py:304
  68.3 14.2 %collective-permute-start.5 = (bf16[64,16,128]{2,1,0:T(8,128)(2,1)}, bf16[64,16,128]{2,1,0:T(8,128)(2,1)S(1)}, u32[]{:S(2)}, u32[]{:S(2)}) collective-permute-start(bf16[64,16,128]{2,1,0:T(8,128)(2,1)} %copy-done.12), channel_id=1, source_target_pairs={{0,20},{4,16},{8,28},{12,24},{16,4},{20,0},{24,12},{28,8},{1,21},{... | collective-permute-start | bytes 786440 | tf_op jit(solution)/shard_map/ppermute | solution.py:304
  68.3 21.3 %collective-permute-start.6 = (bf16[64,16,128]{2,1,0:T(8,128)(2,1)}, bf16[64,16,128]{2,1,0:T(8,128)(2,1)S(1)}, u32[]{:S(2)}, u32[]{:S(2)}) collective-permute-start(bf16[64,16,128]{2,1,0:T(8,128)(2,1)} %copy-done.11), channel_id=1, source_target_pairs={{0,24},{4,28},{8,16},{12,20},{16,8},{20,12},{24,0},{28,4},{1,25},{... | collective-permute-start | bytes 786440 | tf_op jit(solution)/shard_map/ppermute | solution.py:304
  72.3 22.9 %collective-permute-start.7 = (bf16[64,16,128]{2,1,0:T(8,128)(2,1)}, bf16[64,16,128]{2,1,0:T(8,128)(2,1)S(1)}, u32[]{:S(2)}, u32[]{:S(2)}) collective-permute-start(bf16[64,16,128]{2,1,0:T(8,128)(2,1)} %copy-done.10), channel_id=1, source_target_pairs={{0,28},{4,24},{8,20},{12,16},{16,12},{20,8},{24,4},{28,0},{1,29},{... | collective-permute-start | bytes 786440 | tf_op jit(solution)/shard_map/ppermute | solution.py:304
  128.1 8.8 %collective-permute-start.16 = (bf16[64,16,128]{2,1,0:T(8,128)(2,1)S(1)}, bf16[64,16,128]{2,1,0:T(8,128)(2,1)S(1)}, u32[]{:S(2)}, u32[]{:S(2)}) collective-permute-start(bf16[64,16,128]{2,1,0:T(8,128)(2,1)S(1)} %bitcast.24), channel_id=1, source_target_pairs={{0,2},{2,0},{1,3},{3,1},{4,6},{6,4},{5,7},{7,5},{8,10},{10,8},{9,1... | collective-permute-start | bytes 786440 | tf_op jit(solution)/shard_map/ppermute | solution.py:304
  131.6 10.1 %collective-permute-start.15 = (bf16[64,16,128]{2,1,0:T(8,128)(2,1)S(1)}, bf16[64,16,128]{2,1,0:T(8,128)(2,1)S(1)}, u32[]{:S(2)}, u32[]{:S(2)}) collective-permute-start(bf16[64,16,128]{2,1,0:T(8,128)(2,1)S(1)} %bitcast.25), channel_id=1, source_target_pairs={{0,28},{4,24},{8,20},{12,16},{16,12},{20,8},{24,4},{28,0},{1,29},{... | collective-permute-start | bytes 786440 | tf_op jit(solution)/shard_map/ppermute | solution.py:304
  131.8 15.5 %collective-permute-start.14 = (bf16[64,16,128]{2,1,0:T(8,128)(2,1)S(1)}, bf16[64,16,128]{2,1,0:T(8,128)(2,1)S(1)}, u32[]{:S(2)}, u32[]{:S(2)}) collective-permute-start(bf16[64,16,128]{2,1,0:T(8,128)(2,1)S(1)} %bitcast.26), channel_id=1, source_target_pairs={{0,24},{4,28},{8,16},{12,20},{16,8},{20,12},{24,0},{28,4},{1,25},{... | collective-permute-start | bytes 786440 | tf_op jit(solution)/shard_map/ppermute | solution.py:304
  134.6 16.9 %collective-permute-start.13 = (bf16[64,16,128]{2,1,0:T(8,128)(2,1)S(1)}, bf16[64,16,128]{2,1,0:T(8,128)(2,1)S(1)}, u32[]{:S(2)}, u32[]{:S(2)}) collective-permute-start(bf16[64,16,128]{2,1,0:T(8,128)(2,1)S(1)} %bitcast.27), channel_id=1, source_target_pairs={{0,20},{4,16},{8,28},{12,24},{16,4},{20,0},{24,12},{28,8},{1,21},{... | collective-permute-start | bytes 786440 | tf_op jit(solution)/shard_map/ppermute | solution.py:304
  135.7 21.4 %collective-permute-start.12 = (bf16[64,16,128]{2,1,0:T(8,128)(2,1)S(1)}, bf16[64,16,128]{2,1,0:T(8,128)(2,1)S(1)}, u32[]{:S(2)}, u32[]{:S(2)}) collective-permute-start(bf16[64,16,128]{2,1,0:T(8,128)(2,1)S(1)} %bitcast.28), channel_id=1, source_target_pairs={{0,16},{4,20},{8,24},{12,28},{16,0},{20,4},{24,8},{28,12},{1,17},{... | collective-permute-start | bytes 786440 | tf_op jit(solution)/shard_map/ppermute | solution.py:304
  137.0 25.1 %collective-permute-start.11 = (bf16[64,16,128]{2,1,0:T(8,128)(2,1)S(1)}, bf16[64,16,128]{2,1,0:T(8,128)(2,1)S(1)}, u32[]{:S(2)}, u32[]{:S(2)}) collective-permute-start(bf16[64,16,128]{2,1,0:T(8,128)(2,1)S(1)} %bitcast.29), channel_id=1, source_target_pairs={{0,12},{4,8},{8,4},{12,0},{16,28},{20,24},{24,20},{28,16},{1,13},{... | collective-permute-start | bytes 786440 | tf_op jit(solution)/shard_map/ppermute | solution.py:304
  141.8 20.5 %collective-permute-start.10 = (bf16[64,16,128]{2,1,0:T(8,128)(2,1)S(1)}, bf16[64,16,128]{2,1,0:T(8,128)(2,1)S(1)}, u32[]{:S(2)}, u32[]{:S(2)}) collective-permute-start(bf16[64,16,128]{2,1,0:T(8,128)(2,1)S(1)} %bitcast.30), channel_id=1, source_target_pairs={{0,8},{4,12},{8,0},{12,4},{16,24},{20,28},{24,16},{28,20},{1,9},{5... | collective-permute-start | bytes 786440 | tf_op jit(solution)/shard_map/ppermute | solution.py:304
  147.3 15.6 %collective-permute-start.9 = (bf16[64,16,128]{2,1,0:T(8,128)(2,1)S(1)}, bf16[64,16,128]{2,1,0:T(8,128)(2,1)S(1)}, u32[]{:S(2)}, u32[]{:S(2)}) collective-permute-start(bf16[64,16,128]{2,1,0:T(8,128)(2,1)S(1)} %bitcast.31), channel_id=1, source_target_pairs={{0,4},{4,0},{8,12},{12,8},{16,20},{20,16},{24,28},{28,24},{1,5},{5... | collective-permute-start | bytes 786440 | tf_op jit(solution)/shard_map/ppermute | solution.py:304
  151.5 12.0 %collective-permute-start.23 = (bf16[64,16,128]{2,1,0:T(8,128)(2,1)S(1)}, bf16[64,16,128]{2,1,0:T(8,128)(2,1)S(1)}, u32[]{:S(2)}, u32[]{:S(2)}) collective-permute-start(bf16[64,16,128]{2,1,0:T(8,128)(2,1)S(1)} %collective-permute-done.15.refs_7_), channel_id=1, source_target_pairs={{0,2},{2,0},{1,3},{3,1},{4,6},{6,4},{5,7},{7,5},{8,10},{10,8},{9,1... | collective-permute-start | bytes 786440 | tf_op jit(solution)/shard_map/ppermute | solution.py:304
  157.9 11.8 %all-to-all-start.2 = ((bf16[16,16,576]{2,1,0:T(8,128)(2,1)}), bf16[16,16,576]{2,1,0:T(8,128)(2,1)}, u32[]{:S(2)}, u32[]{:S(2)}) async-start(bf16[16,16,576]{2,1,0:T(8,128)(2,1)} %bitcast.13), calls=%async_computation.2 | async-start | bytes 655360 | tf_op jit(solution)/shard_map/all_to_all | solution.py:362
  162.1 9.5 %collective-permute-start.21 = (bf16[64,16,128]{2,1,0:T(8,128)(2,1)S(1)}, bf16[64,16,128]{2,1,0:T(8,128)(2,1)S(1)}, u32[]{:S(2)}, u32[]{:S(2)}) collective-permute-start(bf16[64,16,128]{2,1,0:T(8,128)(2,1)S(1)} %collective-permute-done.13.refs_5_), channel_id=1, source_target_pairs={{0,2},{2,0},{1,3},{3,1},{4,6},{6,4},{5,7},{7,5},{8,10},{10,8},{9,1... | collective-permute-start | bytes 786440 | tf_op jit(solution)/shard_map/ppermute | solution.py:304
  162.3 9.3 %collective-permute-start.20 = (bf16[64,16,128]{2,1,0:T(8,128)(2,1)S(1)}, bf16[64,16,128]{2,1,0:T(8,128)(2,1)S(1)}, u32[]{:S(2)}, u32[]{:S(2)}) collective-permute-start(bf16[64,16,128]{2,1,0:T(8,128)(2,1)S(1)} %collective-permute-done.12.refs_4_), channel_id=1, source_target_pairs={{0,2},{2,0},{1,3},{3,1},{4,6},{6,4},{5,7},{7,5},{8,10},{10,8},{9,1... | collective-permute-start | bytes 786440 | tf_op jit(solution)/shard_map/ppermute | solution.py:304
  163.0 8.6 %collective-permute-start.19 = (bf16[64,16,128]{2,1,0:T(8,128)(2,1)S(1)}, bf16[64,16,128]{2,1,0:T(8,128)(2,1)}, u32[]{:S(2)}, u32[]{:S(2)}) collective-permute-start(bf16[64,16,128]{2,1,0:T(8,128)(2,1)S(1)} %collective-permute-done.11.refs_3_), channel_id=1, source_target_pairs={{0,2},{2,0},{1,3},{3,1},{4,6},{6,4},{5,7},{7,5},{8,10},{10,8},{9,1... | collective-permute-start | bytes 786440 | tf_op jit(solution)/shard_map/ppermute | solution.py:304
  (20 other events, 149.2 us)

commit v3 on v2

v3 whole, which is shorter than its diff:
```python
import functools
import math

import jax
import jax.numpy as jnp
from jax import lax
from jax.experimental import pallas as pl
from jax.experimental.pallas import tpu as pltpu
from jax.sharding import Mesh, PartitionSpec as P

BF = jnp.bfloat16
F32 = jnp.float32
EPS = 1e-06
NN = (((1,), (0,)), ((), ()))
NT = (((1,), (1,)), ((), ()))
LOG2E = math.log2(math.e)
ROWS, LANES = 16, 128
PLANE = ("xlo", "y")
SEQ = PLANE + ("core",)


def mm(a, b, dims):
    return lax.dot_general(a, b, dims, preferred_element_type=F32)


def eye(n):
    rows = lax.broadcasted_iota(jnp.int32, (n, n), 0)
    cols = lax.broadcasted_iota(jnp.int32, (n, n), 1)
    return jnp.where(rows == cols, 1.0, 0.0).astype(BF)


def pack_kernel(latent_ref, cot_ref, out_ref):
    width = latent_ref.shape[1]
    out_ref[:, :width] = latent_ref[...]
    out_ref[:, width:] = mm(eye(latent_ref.shape[0]), cot_ref[...], NT).astype(BF)


def pack(latent, cot_t):
    tokens, width = latent.shape
    return pl.pallas_call(
        pack_kernel,
        out_shape=jax.ShapeDtypeStruct((tokens, width + cot_t.shape[0]), BF),
        compiler_params=pltpu.CompilerParams(vmem_limit_bytes=8 * 2**20),
        name="pack",
    )(latent, cot_t)


def unpack_kernel(rows_ref, first_ref, second_ref):
    ident = eye(LANES)
    half = first_ref.shape[0]
    for start in range(0, 2 * half, LANES):
        found = mm(ident, rows_ref[:, start : start + LANES], NT).astype(BF)
        cut = min(max(half - start, 0), LANES)
        if cut:
            first_ref[start : start + cut] = found[:cut]
        if cut < LANES:
            second_ref[start + cut - half : start + LANES - half] = found[cut:]


def unpack(rows):
    tokens, width = rows.shape
    shape = jax.ShapeDtypeStruct((width // 2, tokens), BF)
    return pl.pallas_call(
        unpack_kernel,
        out_shape=(shape, shape),
        compiler_params=pltpu.CompilerParams(vmem_limit_bytes=8 * 2**20),
        name="unpack",
    )(rows)


def unit_of(values):
    width = values.shape[1]
    centred = values - jnp.sum(values, axis=1, keepdims=True) * (1.0 / width)
    inverse = lax.rsqrt(jnp.sum(centred * centred, axis=1, keepdims=True) * (1.0 / width) + EPS)
    return centred * inverse, inverse


def attend_kernel(core_ref, which_ref, x_ref, shift_ref, scale_ref, wt_hbm, qg_ref, kg_ref,
                  mod_ref, gp_keep_ref, gp_send_ref, att_ref, send_ref, keep_ref, unit_ref,
                  wt_s, gp_s, ot_s, rows_s, sems, *, patches, heads, hd):
    tokens, _ = x_ref.shape
    width = scale_ref.shape[1]
    hw = heads * hd
    copies = []
    for part in range(3):
        rows = pl.ds(part * hw, hw)
        copy = pltpu.make_async_copy(wt_hbm.at[rows], wt_s.at[rows], sems.at[part])
        copy.start()
        copies.append(copy)
    unit, inverse = unit_of(x_ref[:, :width].astype(F32))
    factor = 1.0 + scale_ref[...]
    mod_ref[...] = (unit * factor + shift_ref[...]).astype(BF)
    mod = mod_ref[...]
    ident = eye(tokens)
    cot_t = mm(eye(hw), x_ref[:, width:], NT)

    def project(part):
        copies[part].wait()
        rows = mm(wt_s[part * hw : (part + 1) * hw, :], mod, NT)
        return rows.astype(BF).astype(F32)

    def norm(rows):
        inv = lax.rsqrt(jnp.sum(rows * rows, axis=0, keepdims=True) * (1.0 / hd) + EPS)
        return rows * inv, inv

    root = 1.0 / math.sqrt(hd)
    q_gain = qg_ref[...] * (root * LOG2E)
    k_gain = kg_ref[...]
    q_back = qg_ref[...] * root
    k_back = kg_ref[...] * (1.0 / LOG2E)
    q_all, k_all, v_all = project(0), project(1), project(2)

    spot = lax.broadcasted_iota(jnp.int32, (patches, tokens), 0)
    token = lax.broadcasted_iota(jnp.int32, (patches, tokens), 1)
    spots = jnp.where(lax.rem(token, patches) == spot, 16.0, 0.0)
    top = lax.broadcasted_iota(jnp.int32, (8, tokens), 0) == 0
    spare = -(hd + patches + 8) % LANES
    zeros = jnp.zeros((spare, tokens), F32)
    q_tail = [spots, jnp.where(top, 16.0, 0.0), zeros]
    k_tail = [spots, jnp.where(top, -16.0, 0.0), zeros]
    ones = jnp.where(top, 1.0, 0.0)
    blank = jnp.zeros((-hd % LANES, tokens), F32)

    def back(hat, inv, gain, grad):
        weighted = grad * gain
        mean = jnp.sum(hat * weighted, axis=0, keepdims=True) * (1.0 / hd)
        return inv * (weighted - hat * mean)

    def put(part, h, rows):
        start = part * hw + h * hd
        rows_s[start : start + hd, :] = rows

    for pair in range(heads // 2):
        hats, tall = [], []
        for h in (2 * pair, 2 * pair + 1):
            at = slice(h * hd, (h + 1) * hd)
            hats.append((norm(q_all[at]), norm(k_all[at])))
            kn = hats[-1][1][0] * k_gain
            tall.append((jnp.concatenate([kn] + k_tail), jnp.concatenate([v_all[at], blank])))
        k_rows = mm(ident, jnp.concatenate([t[0] for t in tall]).astype(BF), NT).astype(BF)
        v_rows = mm(ident, jnp.concatenate([t[1] for t in tall]).astype(BF), NT).astype(BF)
        for i, h in enumerate((2 * pair, 2 * pair + 1)):
            at = slice(h * hd, (h + 1) * hd)
            lanes = slice(i * LANES, (i + 1) * LANES)
            (q_hat, q_inv), (k_hat, k_inv) = hats[i]
            q_b = jnp.concatenate([q_hat * q_gain] + q_tail).astype(BF)
            k_b = (k_hat * k_gain).astype(BF)
            weights = jnp.exp2(mm(k_rows[:, lanes], q_b, NN))
            w_b = weights.astype(BF)
            v_b = jnp.concatenate([v_all[at], ones]).astype(BF)
            summed = mm(v_b, w_b, NN)
            share = 1.0 / summed[hd : hd + 1]
            out = summed[:hd] * share
            ot_s[at, :] = out
            cot = cot_t[at]
            cot_share = cot * share
            cot_b = jnp.concatenate([cot_share, blank]).astype(BF)
            delta = jnp.sum(out * cot_share, axis=0, keepdims=True)
            grad_s = (weights * (mm(v_rows[:, lanes], cot_b, NN) - delta)).astype(BF)
            put(2, h, mm(cot_b, w_b, NT)[:hd])
            put(0, h, back(q_hat, q_inv, q_back, mm(k_b, grad_s, NN)))
            put(1, h, back(k_hat, k_inv, k_back, mm(q_b, grad_s, NT)[:hd]))

    grad = jnp.zeros((tokens, width), F32)
    size = gp_keep_ref.shape[0]
    for part in range(3):
        at = slice(part * hw, (part + 1) * hw)
        block = rows_s[at, :].astype(BF)
        gp_s[at, :] = block
        grad = grad + mm(mm(ident, block, NT).astype(BF), wt_s[at, :], NN)
    gp_keep_ref[...] = gp_s[pl.ds(pl.multiple_of(core_ref[0] * size, ROWS), size), :]
    gp_send_ref[...] = gp_s[pl.ds(pl.multiple_of((1 - core_ref[0]) * size, ROWS), size), :]
    att_ref[...] = mm(ident, ot_s[...].astype(BF), NT).astype(BF)

    half = width // 2
    win = send_ref.shape[1]
    scaled = grad * factor
    first = jnp.sum(scaled, axis=1, keepdims=True)
    second = jnp.sum(scaled * unit, axis=1, keepdims=True)
    mine_low = which_ref[0] == 0
    col = lax.broadcasted_iota(jnp.int32, (tokens, win), 1)
    here = jnp.where(mine_low, half, 0)
    there = jnp.where(mine_low, 0, half)
    low, high = scaled[:, :win], scaled[:, width - win :]
    send = jnp.where(mine_low, high, low)
    keep = jnp.where(mine_low, low, high)
    for place, term in enumerate((first, second)):
        coarse = term.astype(BF).astype(F32)
        send = jnp.where(col == there + 2 * place, coarse, send)
        send = jnp.where(col == there + 2 * place + 1, term - coarse, send)
    for place, term in enumerate((first, second, inverse)):
        keep = jnp.where(col == here + place, term, keep)
    send_ref[...] = send.astype(BF)
    keep_ref[...] = keep
    unit_ref[...] = jnp.where(mine_low, unit[:, :win], unit[:, width - win :]).astype(BF)


def attend(core, which, x, shift, scale, wt, qg, kg, patches, heads, hd):
    tokens = x.shape[0]
    width = wt.shape[1]
    hw = heads * hd
    win = window_of(width // 2)
    smem = pl.BlockSpec(memory_space=pltpu.SMEM)
    vmem = pl.BlockSpec(memory_space=pltpu.VMEM)
    shapes = [
        ((tokens, width), BF),
        ((3 * hw // 2, tokens), BF),
        ((3 * hw // 2, tokens), BF),
        ((tokens, hw), BF),
        ((tokens, win), BF),
        ((tokens, win), F32),
        ((tokens, win), BF),
    ]
    return pl.pallas_call(
        functools.partial(attend_kernel, patches=patches, heads=heads, hd=hd),
        in_specs=[smem, smem, vmem, vmem, vmem, pl.BlockSpec(memory_space=pl.ANY), vmem, vmem],
        out_shape=tuple(jax.ShapeDtypeStruct(*shape) for shape in shapes),
        scratch_shapes=[
            pltpu.VMEM((3 * hw, width), BF),
            pltpu.VMEM((3 * hw, tokens), BF),
            pltpu.VMEM((hw, tokens), F32),
            pltpu.VMEM((3 * hw, tokens), F32),
            pltpu.SemaphoreType.DMA((3,)),
        ],
        compiler_params=pltpu.CompilerParams(vmem_limit_bytes=32 * 2**20),
        name="attend",
    )(core, which, x, shift, scale, wt, qg, kg)


def outer_kernel(where_ref, gp_a, gp_b, mod_a, mod_b, *refs):
    out_refs, tiles_s = refs[:-1], refs[-1]
    rows, width = gp_a.shape[0], mod_a.shape[1]
    tiles = rows // ROWS
    used = tiles * (width // LANES)
    tiles_s[used:] = jnp.zeros((tiles_s.shape[0] - used, ROWS, LANES), BF)
    gp = jnp.concatenate([gp_a[...], gp_b[...]], axis=1)
    for start in range(0, width, 2 * LANES):
        stop = min(start + 2 * LANES, width)
        mod = jnp.concatenate([mod_a[:, start:stop], mod_b[:, start:stop]], axis=0)
        found = mm(gp, mod, NN).astype(BF)
        for at in range(0, stop - start, LANES):
            j = (start + at) // LANES
            tiles_s[j * tiles : (j + 1) * tiles] = found[:, at : at + LANES].reshape(tiles, ROWS, LANES)
    size = out_refs[0].shape[0]
    for k, out_ref in enumerate(out_refs):
        out_ref[...] = tiles_s[pl.ds((where_ref[0] ^ k) * size, size)]


def outer(where, gp_a, gp_b, mod_a, mod_b, count, padded):
    smem = pl.BlockSpec(memory_space=pltpu.SMEM)
    vmem = pl.BlockSpec(memory_space=pltpu.VMEM)
    shape = jax.ShapeDtypeStruct((padded // count, ROWS, LANES), BF)
    return pl.pallas_call(
        outer_kernel,
        in_specs=[smem] + [vmem] * 4,
        out_shape=(shape,) * count,
        scratch_shapes=[pltpu.VMEM((padded, ROWS, LANES), BF)],
        compiler_params=pltpu.CompilerParams(vmem_limit_bytes=16 * 2**20),
        name="outer",
    )(where, gp_a, gp_b, mod_a, mod_b)


def window_of(half):
    return -(-half // LANES) * LANES


def finish_kernel(which_ref, recv_ref, keep_ref, unit_ref, att_ref, out_ref, *, width):
    half = width // 2
    win = recv_ref.shape[1]
    mine_low = which_ref[0] == 0
    recv = recv_ref[...].astype(F32)
    keep = keep_ref[...]

    def column(block, place):
        return jnp.where(mine_low, block[:, half + place : half + place + 1], block[:, place : place + 1])

    first = column(keep, 0) + (column(recv, 0) + column(recv, 1))
    second = column(keep, 1) + (column(recv, 2) + column(recv, 3))
    inverse = column(keep, 2)
    grad = keep + recv
    out = inverse * (grad - first * (1.0 / width) - unit_ref[...].astype(F32) * (second * (1.0 / width)))
    moved = pltpu.roll(out, win - (win - half), 1)
    out_ref[:, :half] = jnp.where(mine_low, out, moved)[:, :half].astype(BF)
    out_ref[:, half:] = att_ref[...]


def finish(which, recv, keep, unit, att, width):
    tokens = recv.shape[0]
    smem = pl.BlockSpec(memory_space=pltpu.SMEM)
    vmem = pl.BlockSpec(memory_space=pltpu.VMEM)
    return pl.pallas_call(
        functools.partial(finish_kernel, width=width),
        in_specs=[smem, vmem, vmem, vmem, vmem],
        out_shape=jax.ShapeDtypeStruct((tokens, width), BF),
        compiler_params=pltpu.CompilerParams(vmem_limit_bytes=24 * 2**20),
        name="finish",
    )(which, recv, keep, unit, att)


def sum_kernel(*refs):
    total = refs[0][...].astype(F32)
    for ref in refs[1:-1]:
        total = total + ref[...].astype(F32)
    refs[-1][...] = total.astype(BF)


def sum_of(parts):
    return pl.pallas_call(
        sum_kernel,
        out_shape=jax.ShapeDtypeStruct(parts[0].shape, BF),
        compiler_params=pltpu.CompilerParams(vmem_limit_bytes=8 * 2**20),
        name="sum_of",
    )(*parts)


def spread_kernel(parts_ref, out_ref, *, factor):
    total = jnp.sum(parts_ref[...].astype(F32), axis=0) * factor
    total = total.astype(BF)
    for k in range(out_ref.shape[0]):
        out_ref[k] = total


def spread(parts, factor):
    return pl.pallas_call(
        functools.partial(spread_kernel, factor=factor),
        out_shape=jax.ShapeDtypeStruct(parts.shape, BF),
        compiler_params=pltpu.CompilerParams(vmem_limit_bytes=8 * 2**20),
        name="spread",
    )(parts)


def untile_kernel(where_ref, half_ref, *refs):
    pieces, (out_ref, tiles_s) = refs[:-2], refs[-2:]
    count = len(pieces) // 2
    size = pieces[0].shape[0]
    for side in range(2):
        half = half_ref[0] ^ side
        for k in range(count):
            base = (half * count + (where_ref[0] ^ k)) * size
            tiles_s[pl.ds(base, size)] = pieces[side * count + k][...]
    rows = out_ref.shape[0] // 2
    tiles = rows // ROWS
    for half in range(2):
        for j in range(out_ref.shape[1] // LANES):
            start = half * count * size + j * tiles
            block = tiles_s[start : start + tiles].reshape(rows, LANES)
            out_ref[half * rows : (half + 1) * rows, j * LANES : (j + 1) * LANES] = block


def untile(where, half, pieces, rows, width):
    smem = pl.BlockSpec(memory_space=pltpu.SMEM)
    vmem = pl.BlockSpec(memory_space=pltpu.VMEM)
    tiles = len(pieces) * pieces[0].shape[0]
    return pl.pallas_call(
        untile_kernel,
        in_specs=[smem, smem] + [vmem] * len(pieces),
        out_shape=jax.ShapeDtypeStruct((rows, width), BF),
        scratch_shapes=[pltpu.VMEM((tiles, ROWS, LANES), BF)],
        compiler_params=pltpu.CompilerParams(vmem_limit_bytes=16 * 2**20),
        name="untile",
    )(where, half, *pieces)


def swap(x, axes, k):
    count = math.prod(lax.axis_size(a) for a in axes)
    return lax.ppermute(x, axes, [(i, i ^ k) for i in range(count)])


def exchange(x, axis):
    parts = x.reshape((-1,) + x.shape[-3:])
    return lax.all_to_all(parts, axis, split_axis=0, concat_axis=0, tiled=True)


def plane_size():
    return lax.axis_size("xlo") * lax.axis_size("y")


ORDER = (6, 2, 5, 7, 4, 1, 3)


def scatter_plane(parts):
    return [parts[0]] + [swap(parts[k], PLANE, k) for k in ORDER]


def sum_clips(own, factor):
    clips = lax.axis_size("dp")
    parts = own.reshape((clips, own.shape[0] // clips) + own.shape[1:])
    return exchange(spread(exchange(parts, "dp"), factor), "dp").reshape(own.shape)


def gather_plane(own, rows, width):
    where = lax.axis_index(PLANE).astype(jnp.int32).reshape(1)
    half = lax.axis_index("core").astype(jnp.int32).reshape(1)
    found = {k: swap(own, PLANE, k) for k in ORDER}
    pieces = [own] + [found[k] for k in range(1, plane_size())]
    pieces = pieces + [swap(piece, ("core",), 1) for piece in pieces]
    return untile(where, half, pieces, rows, width)


def body(latent, mod_shift, mod_scale, w_qkv, q_gain, k_gain, cotangent):
    _, _, patches, width = latent.shape
    hw = w_qkv.shape[2]
    hd = q_gain.shape[0]
    heads = hw // hd
    frames = 1
    for a in SEQ:
        frames *= lax.axis_size(a)
    own_patches = patches // frames
    clips = lax.axis_size("dp")
    wt = w_qkv.transpose(1, 2, 0).reshape(3 * hw, width)
    x = pack(latent[0, 0], cotangent[0, 0].T).reshape(frames, own_patches, width + hw)
    x = lax.all_to_all(x, SEQ, split_axis=0, concat_axis=0, tiled=True).reshape(patches, width + hw)
    core = lax.axis_index("core").astype(jnp.int32).reshape(1)
    which = lax.axis_index("tensor").astype(jnp.int32).reshape(1)
    where = lax.axis_index(PLANE).astype(jnp.int32).reshape(1)
    mod, gp_keep, gp_send, att, send, keep, unit = attend(
        core, which, x, mod_shift, mod_scale, wt, q_gain[:, None], k_gain[:, None], own_patches, heads, hd
    )
    recv = lax.ppermute(send, "tensor", [(0, 1), (1, 0)])
    used = (3 * hw // 2 // ROWS) * (width // LANES)
    group = plane_size() * clips
    padded = -(-used // group) * group
    gp_other, mod_other = swap(gp_send, ("core",), 1), swap(mod, ("core",), 1)
    parts = scatter_plane(outer(where, gp_keep, gp_other, mod, mod_other, plane_size(), padded))
    parts, recv = lax.optimization_barrier((parts, recv))
    home = finish(which, recv, keep, unit, att, width)
    own, home = lax.optimization_barrier((sum_of(parts), home))
    home = home.reshape(frames, own_patches, width)
    home = lax.all_to_all(home, SEQ, split_axis=0, concat_axis=0, tiled=True)
    grad_t, att_t = unpack(home.reshape(patches, width))
    factor = 1.0 / math.sqrt(clips * frames * patches)
    grad_qkv = gather_plane(sum_clips(own, factor), 3 * hw, width)
    grad_qkv = grad_qkv.reshape(3, hw, width).transpose(2, 0, 1)
    return (att_t.T[None, None], grad_t.T[None, None], grad_qkv)


def solution(mesh):
    fine = Mesh(mesh.devices.reshape(mesh.shape["dp"], 2, 4, 2, 2), ("dp",) + SEQ + ("tensor",))
    in_specs = (
        P("dp", SEQ, None, None),
        P("dp", None),
        P("dp", None),
        P(None, None, "tensor"),
        P(),
        P(),
        P("dp", SEQ, None, "tensor"),
    )
    out_specs = (
        P("dp", SEQ, None, "tensor"),
        P("dp", SEQ, None, "tensor"),
        P(None, None, "tensor"),
    )
    return jax.shard_map(body, mesh=fine, in_specs=in_specs, out_specs=out_specs, check_vma=False)
```

time: 176 us -> 160 us (0.909)
  local copies, waits for them, and re-layouts: 17.7 us -> 8.72 us
  starting transfers between devices: 43.3 us -> 40.7 us
  other arithmetic: 2.06 us -> 0 us
    unnamed x37 -> x14, local copies, waits for them, and re-layouts: 17.5 us -> 7.23 us
    all_to_all x2 -> x1, waiting for transfers between devices: 5.59 us -> 0.01 us  [body(): home = lax.all_to_all(home, SEQ, split_axis=0, concat_axis=0, tiled=True)]
    ppermute x23 -> x24, waiting for transfers between devices: 39.1 us -> 43.4 us  [swap(): return lax.ppermute(x, axes, [(i, i ^ k) for i in range(count)])]
    all_to_all x2 -> x1, starting transfers between devices: 9.16 us -> 4.98 us  [body(): home = lax.all_to_all(home, SEQ, split_axis=0, concat_axis=0, tiled=True)]
    concatenate x1 -> x0, other arithmetic: 2.06 us -> none  [body(): x = jnp.concatenate([latent[0, 0], cotangent[0, 0]], axis=1)]
    pallas_call x2 -> x3, Pallas kernels: 5.51 us -> 3.72 us  [the longest x1 1.44 us: outer(): pl.pallas_call(outer_kernel, in_specs=[smem] + [vmem] * 4, out_shape=(sha...]
    ppermute x23 -> x24, starting transfers between devices: 24.8 us -> 26.4 us  [swap(): return lax.ppermute(x, axes, [(i, i ^ k) for i in range(count)])]
  transfers between devices with their start and end apart: 27 -> 27, of which waited for: 13 -> 13; matrix products, arithmetic and copies ran while one was open for 2% -> 1% of each run, Pallas kernels for 3% -> 2%
where the time goes in v3:
time: 160 us; the launch traced here: 159 us
  waiting for transfers between devices  57.5 us (36%)
  starting transfers between devices  40.7 us (25%)
  blocking collectives  29.1 us (18%)
  Pallas kernels  22.1 us (14%)
  local copies, waits for them, and re-layouts  8.72 us (5%)
    ppermute x24, waiting for transfers between devices, swap(): return lax.ppermute(x, axes, [(i, i ^ k) for i in range(count)])  43.4 us
    all_to_all x2, blocking collectives, exchange(): return lax.all_to_all(parts, axis, split_axis=0, concat_axis=0, tiled=True)  29.1 us
    ppermute x24, starting transfers between devices, swap(): return lax.ppermute(x, axes, [(i, i ^ k) for i in range(count)])  26.4 us
    all_to_all x1, waiting for transfers between devices, body(): lax.all_to_all(x, SEQ, split_axis=0, concat_axis=0, tiled=True)  12.9 us
    pallas_call x1, Pallas kernels, attend(): pl.pallas_call(functools.partial(attend_kernel, patches=patches, heads=he...  12.4 us
    unnamed x14, local copies, waits for them, and re-layouts  7.23 us
    all_to_all x1, starting transfers between devices, body(): lax.all_to_all(x, SEQ, split_axis=0, concat_axis=0, tiled=True)  6.92 us
    all_to_all x1, starting transfers between devices, body(): home = lax.all_to_all(home, SEQ, split_axis=0, concat_axis=0, tiled=True)  4.98 us
  transfers between devices with their start and end apart: 27, of which 13 were waited for; matrix products, arithmetic and copies ran while one was open for 1% of the time, Pallas kernels for 2%

profile of v3, /device:TPU:1, one launch (start us, length us, event | category | flops | bytes accessed | tf_op | source)
XLA Modules:
  0.0 158.9 jit_solution(13560179013034225535)
XLA Ops:
  3.9 6.9 %all-to-all-start = ((bf16[16,16,1728]{2,1,0:T(8,128)(2,1)}), bf16[16,16,1728]{2,1,0:T(8,128)(2,1)S(1)}, u32[]{:S(2)}, u32[]{:S(2)}) async-start(bf16[16,16,1728]{2,1,0:T(8,128)(2,1)} %bitcast.6), calls=%async_computation | async-start | bytes 1835008 | tf_op jit(solution)/shard_map/all_to_all | solution.py:412
  12.3 12.9 %all-to-all-done = bf16[16,16,1728]{2,1,0:T(8,128)(2,1)S(1)} async-done(((bf16[16,16,1728]{2,1,0:T(8,128)(2,1)}), bf16[16,16,1728]{2,1,0:T(8,128)(2,1)S(1)}, u32[]{:S(2)}, u32[]{:S(2)}) %all-to-all-start) | async-done | bytes 884768 | tf_op jit(solution)/shard_map/all_to_all | solution.py:412
  25.2 2.1 %copy-done = bf16[1152,3,576]{0,2,1:T(8,128)(2,1)S(1)} copy-done((bf16[1152,3,576]{0,2,1:T(8,128)(2,1)S(1)}, bf16[1152,3,576]{0,2,1:T(8,128)(2,1)}, u32[]{:S(2)}) %copy-start) | copy-done | bytes 3981336
  28.7 12.4 %attend.1 = (bf16[256,1152]{1,0:T(8,128)(2,1)S(1)}, bf16[864,256]{1,0:T(8,128)(2,1)S(1)}, bf16[864,256]{1,0:T(8,128)(2,1)}, bf16[256,576]{1,0:T(8,128)(2,1)S(1)}...) custom-call(s32[1]{0:T(128)} %bitcast.1.core_ref.half_ref, s32[1]{0:T(128)} %bitcast.2.which_ref, ...), custom_call_target="tpu_custom_call" | custom-call | tf_op jit(solution)/shard_map/attend/pallas_call | solution.py:214
  42.7 2.4 %collective-permute-start.9 = (bf16[256,640]{1,0:T(8,128)(2,1)}, bf16[256,640]{1,0:T(8,128)(2,1)S(1)}, u32[]{:S(2)}, u32[]{:S(2)}) collective-permute-start(bf16[256,640]{1,0:T(8,128)(2,1)} %get-tuple-element.42), channel_id=1, source_target_pairs={{0,1},{1,0},{2,3},{3,2},{4,5},{5,4},{6,7},{7,6},{8,9},{9,8},{10,11... | collective-permute-start | bytes 983048 | tf_op jit(solution)/shard_map/ppermute | solution.py:419
  47.8 1.7 %collective-permute-start.3 = (bf16[64,16,128]{2,1,0:T(8,128)(2,1)S(1)}, bf16[64,16,128]{2,1,0:T(8,128)(2,1)S(1)}, u32[]{:S(2)}, u32[]{:S(2)}) collective-permute-start(bf16[64,16,128]{2,1,0:T(8,128)(2,1)S(1)} %get-tuple-element.36), channel_id=1, source_target_pairs={{0,8},{4,12},{8,0},{12,4},{16,24},{20,28},{24,16},{28,20},{1,9},{5... | collective-permute-start | bytes 786440 | tf_op jit(solution)/shard_map/ppermute | solution.py:366
  49.5 2.4 %collective-permute-start.5 = (bf16[64,16,128]{2,1,0:T(8,128)(2,1)S(1)}, bf16[64,16,128]{2,1,0:T(8,128)(2,1)S(1)}, u32[]{:S(2)}, u32[]{:S(2)}) collective-permute-start(bf16[64,16,128]{2,1,0:T(8,128)(2,1)S(1)} %get-tuple-element.38), channel_id=1, source_target_pairs={{0,28},{4,24},{8,20},{12,16},{16,12},{20,8},{24,4},{28,0},{1,29},{... | collective-permute-start | bytes 786440 | tf_op jit(solution)/shard_map/ppermute | solution.py:366
  53.5 5.6 %collective-permute-done.2.refs_1_ = bf16[64,16,128]{2,1,0:T(8,128)(2,1)S(1)} collective-permute-done((bf16[64,16,128]{2,1,0:T(8,128)(2,1)S(1)}, bf16[64,16,128]{2,1,0:T(8,128)(2,1)S(1)}, u32[]{:S(2)}, u32[]{:S(2)}) %collective-permute-start.2) | collective-permute-done | bytes 262176 | tf_op jit(solution)/shard_map/ppermute | solution.py:366
  59.8 9.2 %collective-permute-done.3.refs_2_ = bf16[64,16,128]{2,1,0:T(8,128)(2,1)S(1)} collective-permute-done((bf16[64,16,128]{2,1,0:T(8,128)(2,1)S(1)}, bf16[64,16,128]{2,1,0:T(8,128)(2,1)S(1)}, u32[]{:S(2)}, u32[]{:S(2)}) %collective-permute-start.3) | collective-permute-done | bytes 262176 | tf_op jit(solution)/shard_map/ppermute | solution.py:366
  69.9 3.2 %collective-permute-done.5.refs_4_ = bf16[64,16,128]{2,1,0:T(8,128)(2,1)S(1)} collective-permute-done((bf16[64,16,128]{2,1,0:T(8,128)(2,1)S(1)}, bf16[64,16,128]{2,1,0:T(8,128)(2,1)S(1)}, u32[]{:S(2)}, u32[]{:S(2)}) %collective-permute-start.5) | collective-permute-done | bytes 262176 | tf_op jit(solution)/shard_map/ppermute | solution.py:366
  73.0 4.0 %collective-permute-done.6.refs_5_ = bf16[64,16,128]{2,1,0:T(8,128)(2,1)S(1)} collective-permute-done((bf16[64,16,128]{2,1,0:T(8,128)(2,1)S(1)}, bf16[64,16,128]{2,1,0:T(8,128)(2,1)S(1)}, u32[]{:S(2)}, u32[]{:S(2)}) %collective-permute-start.6) | collective-permute-done | bytes 262176 | tf_op jit(solution)/shard_map/ppermute | solution.py:366
  79.8 17.4 %all_to_all.20.parts_ref = bf16[8,8,16,128]{3,2,1,0:T(8,128)(2,1)S(1)} all-to-all(bf16[8,8,16,128]{3,2,1,0:T(8,128)(2,1)S(1)} %bitcast.39), channel_id=1, replica_groups=mesh['dp'=8,'xlo'=2,'y'=4,'core'=2,'tensor'=2] {'dp'}, dimensions={0} | all-to-all | bytes 524288 | tf_op jit(solution)/shard_map/all_to_all | solution.py:371
  97.2 11.7 %all_to_all.21 = bf16[8,8,16,128]{3,2,1,0:T(8,128)(2,1)S(1)} all-to-all(bf16[8,8,16,128]{3,2,1,0:T(8,128)(2,1)S(1)} %spread.1), channel_id=1, replica_groups=mesh['dp'=8,'xlo'=2,'y'=4,'core'=2,'tensor'=2] {'dp'}, dimensions={0} | all-to-all | bytes 524288 | tf_op jit(solution)/shard_map/all_to_all | solution.py:371
  109.0 5.2 %collective-permute-start.17 = (bf16[64,16,128]{2,1,0:T(8,128)(2,1)S(1)}, bf16[64,16,128]{2,1,0:T(8,128)(2,1)S(1)}, u32[]{:S(2)}, u32[]{:S(2)}) collective-permute-start(bf16[64,16,128]{2,1,0:T(8,128)(2,1)S(1)} %bitcast.30), channel_id=1, source_target_pairs={{0,2},{2,0},{1,3},{3,1},{4,6},{6,4},{5,7},{7,5},{8,10},{10,8},{9,1... | collective-permute-start | bytes 786440 | tf_op jit(solution)/shard_map/ppermute | solution.py:366
  114.2 2.3 %collective-permute-start.16 = (bf16[64,16,128]{2,1,0:T(8,128)(2,1)S(1)}, bf16[64,16,128]{2,1,0:T(8,128)(2,1)S(1)}, u32[]{:S(2)}, u32[]{:S(2)}) collective-permute-start(bf16[64,16,128]{2,1,0:T(8,128)(2,1)S(1)} %bitcast.31), channel_id=1, source_target_pairs={{0,28},{4,24},{8,20},{12,16},{16,12},{20,8},{24,4},{28,0},{1,29},{... | collective-permute-start | bytes 786440 | tf_op jit(solution)/shard_map/ppermute | solution.py:366
  117.0 2.2 %collective-permute-start.14 = (bf16[64,16,128]{2,1,0:T(8,128)(2,1)S(1)}, bf16[64,16,128]{2,1,0:T(8,128)(2,1)S(1)}, u32[]{:S(2)}, u32[]{:S(2)}) collective-permute-start(bf16[64,16,128]{2,1,0:T(8,128)(2,1)S(1)} %bitcast.33), channel_id=1, source_target_pairs={{0,20},{4,16},{8,28},{12,24},{16,4},{20,0},{24,12},{28,8},{1,21},{... | collective-permute-start | bytes 786440 | tf_op jit(solution)/shard_map/ppermute | solution.py:366
  119.5 5.0 %all-to-all-start.1 = ((bf16[16,16,1152]{2,1,0:T(8,128)(2,1)}), bf16[16,16,1152]{2,1,0:T(8,128)(2,1)S(1)}, u32[]{:S(2)}, u32[]{:S(2)}) async-start(bf16[16,16,1152]{2,1,0:T(8,128)(2,1)} %bitcast.12), calls=%async_computation.1 | async-start | bytes 1179648 | tf_op jit(solution)/shard_map/all_to_all | solution.py:429
  124.5 2.7 %collective-permute-start.12 = (bf16[64,16,128]{2,1,0:T(8,128)(2,1)S(1)}, bf16[64,16,128]{2,1,0:T(8,128)(2,1)S(1)}, u32[]{:S(2)}, u32[]{:S(2)}) collective-permute-start(bf16[64,16,128]{2,1,0:T(8,128)(2,1)S(1)} %bitcast.35), channel_id=1, source_target_pairs={{0,12},{4,8},{8,4},{12,0},{16,28},{20,24},{24,20},{28,16},{1,13},{... | collective-permute-start | bytes 786440 | tf_op jit(solution)/shard_map/ppermute | solution.py:366
  127.7 2.0 %collective-permute-done.15.refs_6_ = bf16[64,16,128]{2,1,0:T(8,128)(2,1)S(1)} collective-permute-done((bf16[64,16,128]{2,1,0:T(8,128)(2,1)S(1)}, bf16[64,16,128]{2,1,0:T(8,128)(2,1)S(1)}, u32[]{:S(2)}, u32[]{:S(2)}) %collective-permute-start.15) | collective-permute-done | bytes 262176 | tf_op jit(solution)/shard_map/ppermute | solution.py:366
  130.4 4.0 %collective-permute-done.14.refs_5_ = bf16[64,16,128]{2,1,0:T(8,128)(2,1)S(1)} collective-permute-done((bf16[64,16,128]{2,1,0:T(8,128)(2,1)S(1)}, bf16[64,16,128]{2,1,0:T(8,128)(2,1)S(1)}, u32[]{:S(2)}, u32[]{:S(2)}) %collective-permute-start.14) | collective-permute-done | bytes 262176 | tf_op jit(solution)/shard_map/ppermute | solution.py:366
  135.6 4.4 %collective-permute-done.13.refs_4_ = bf16[64,16,128]{2,1,0:T(8,128)(2,1)S(1)} collective-permute-done((bf16[64,16,128]{2,1,0:T(8,128)(2,1)S(1)}, bf16[64,16,128]{2,1,0:T(8,128)(2,1)S(1)}, u32[]{:S(2)}, u32[]{:S(2)}) %collective-permute-start.13) | collective-permute-done | bytes 262176 | tf_op jit(solution)/shard_map/ppermute | solution.py:366
  141.2 6.0 %collective-permute-done.11.refs_2_ = bf16[64,16,128]{2,1,0:T(8,128)(2,1)S(1)} collective-permute-done((bf16[64,16,128]{2,1,0:T(8,128)(2,1)S(1)}, bf16[64,16,128]{2,1,0:T(8,128)(2,1)S(1)}, u32[]{:S(2)}, u32[]{:S(2)}) %collective-permute-start.11) | collective-permute-done | bytes 262176 | tf_op jit(solution)/shard_map/ppermute | solution.py:366
  147.8 4.5 %collective-permute-done.10.refs_1_ = bf16[64,16,128]{2,1,0:T(8,128)(2,1)S(1)} collective-permute-done((bf16[64,16,128]{2,1,0:T(8,128)(2,1)S(1)}, bf16[64,16,128]{2,1,0:T(8,128)(2,1)S(1)}, u32[]{:S(2)}, u32[]{:S(2)}) %collective-permute-start.10) | collective-permute-done | bytes 262176 | tf_op jit(solution)/shard_map/ppermute | solution.py:366
  154.8 4.2 %untile.1 = bf16[1728,1152]{1,0:T(8,128)(2,1)} custom-call(s32[1]{0:T(128)} %bitcast.where_ref, s32[1]{0:T(128)} %bitcast.1.core_ref.half_ref, bf16[64,16,128]{2,1,0:T(8,128)(2,1)S(1)} %bitcast.38, bf16[64,16,128]{2,1,0:T(8,128)(2,1)S(1)} %collective-permute-done.10.refs_1_, bf16[64,16,128]{2,1,0:T(8,128)(2,1)S(1)} %collective-permute-done.11.refs_2_, ...), custom_call_target="tpu_custom_call" | custom-call | tf_op jit(solution)/shard_map/untile/pallas_call | solution.py:354
  (56 shorter events, 23.7 us)
Async XLA Ops:
  3.9 21.3 %all-to-all-start = ((bf16[16,16,1728]{2,1,0:T(8,128)(2,1)}), bf16[16,16,1728]{2,1,0:T(8,128)(2,1)S(1)}, u32[]{:S(2)}, u32[]{:S(2)}) async-start(bf16[16,16,1728]{2,1,0:T(8,128)(2,1)} %bitcast.6), calls=%async_computation | async-start | bytes 1835008 | tf_op jit(solution)/shard_map/all_to_all | solution.py:412
  41.8 3.3 %collective-permute-start.1 = (bf16[256,1152]{1,0:T(8,128)(2,1)S(1)}, bf16[256,1152]{1,0:T(8,128)(2,1)S(1)}, u32[]{:S(2)}, u32[]{:S(2)}) collective-permute-start(bf16[256,1152]{1,0:T(8,128)(2,1)S(1)} %get-tuple-element.33.mod_a), channel_id=1, source_target_pairs={{0,2},{2,0},{1,3},{3,1},{4,6},{6,4},{5,7},{7,5},{8,10},{10,8},{9,1... | collective-permute-start | bytes 1769480 | tf_op jit(solution)/shard_map/ppermute | solution.py:366
  42.7 2.5 %collective-permute-start = (bf16[864,256]{1,0:T(8,128)(2,1)}, bf16[864,256]{1,0:T(8,128)(2,1)S(1)}, u32[]{:S(2)}, u32[]{:S(2)}) collective-permute-start(bf16[864,256]{1,0:T(8,128)(2,1)} %get-tuple-element.32), channel_id=1, source_target_pairs={{0,2},{2,0},{1,3},{3,1},{4,6},{6,4},{5,7},{7,5},{8,10},{10,8},{9,1... | collective-permute-start | bytes 1327112 | tf_op jit(solution)/shard_map/ppermute | solution.py:366
  42.7 10.5 %collective-permute-start.9 = (bf16[256,640]{1,0:T(8,128)(2,1)}, bf16[256,640]{1,0:T(8,128)(2,1)S(1)}, u32[]{:S(2)}, u32[]{:S(2)}) collective-permute-start(bf16[256,640]{1,0:T(8,128)(2,1)} %get-tuple-element.42), channel_id=1, source_target_pairs={{0,1},{1,0},{2,3},{3,2},{4,5},{5,4},{6,7},{7,6},{8,9},{9,8},{10,11... | collective-permute-start | bytes 983048 | tf_op jit(solution)/shard_map/ppermute | solution.py:419
  46.6 12.4 %collective-permute-start.2 = (bf16[64,16,128]{2,1,0:T(8,128)(2,1)S(1)}, bf16[64,16,128]{2,1,0:T(8,128)(2,1)S(1)}, u32[]{:S(2)}, u32[]{:S(2)}) collective-permute-start(bf16[64,16,128]{2,1,0:T(8,128)(2,1)S(1)} %get-tuple-element.35), channel_id=1, source_target_pairs={{0,24},{4,28},{8,16},{12,20},{16,8},{20,12},{24,0},{28,4},{1,25},{... | collective-permute-start | bytes 786440 | tf_op jit(solution)/shard_map/ppermute | solution.py:366
  47.8 21.2 %collective-permute-start.3 = (bf16[64,16,128]{2,1,0:T(8,128)(2,1)S(1)}, bf16[64,16,128]{2,1,0:T(8,128)(2,1)S(1)}, u32[]{:S(2)}, u32[]{:S(2)}) collective-permute-start(bf16[64,16,128]{2,1,0:T(8,128)(2,1)S(1)} %get-tuple-element.36), channel_id=1, source_target_pairs={{0,8},{4,12},{8,0},{12,4},{16,24},{20,28},{24,16},{28,20},{1,9},{5... | collective-permute-start | bytes 786440 | tf_op jit(solution)/shard_map/ppermute | solution.py:366
  49.5 20.3 %collective-permute-start.4 = (bf16[64,16,128]{2,1,0:T(8,128)(2,1)S(1)}, bf16[64,16,128]{2,1,0:T(8,128)(2,1)S(1)}, u32[]{:S(2)}, u32[]{:S(2)}) collective-permute-start(bf16[64,16,128]{2,1,0:T(8,128)(2,1)S(1)} %get-tuple-element.37), channel_id=1, source_target_pairs={{0,20},{4,16},{8,28},{12,24},{16,4},{20,0},{24,12},{28,8},{1,21},{... | collective-permute-start | bytes 786440 | tf_op jit(solution)/shard_map/ppermute | solution.py:366
  49.5 23.5 %collective-permute-start.5 = (bf16[64,16,128]{2,1,0:T(8,128)(2,1)S(1)}, bf16[64,16,128]{2,1,0:T(8,128)(2,1)S(1)}, u32[]{:S(2)}, u32[]{:S(2)}) collective-permute-start(bf16[64,16,128]{2,1,0:T(8,128)(2,1)S(1)} %get-tuple-element.38), channel_id=1, source_target_pairs={{0,28},{4,24},{8,20},{12,16},{16,12},{20,8},{24,4},{28,0},{1,29},{... | collective-permute-start | bytes 786440 | tf_op jit(solution)/shard_map/ppermute | solution.py:366
  53.2 23.9 %collective-permute-start.6 = (bf16[64,16,128]{2,1,0:T(8,128)(2,1)S(1)}, bf16[64,16,128]{2,1,0:T(8,128)(2,1)S(1)}, u32[]{:S(2)}, u32[]{:S(2)}) collective-permute-start(bf16[64,16,128]{2,1,0:T(8,128)(2,1)S(1)} %get-tuple-element.39), channel_id=1, source_target_pairs={{0,16},{4,20},{8,24},{12,28},{16,0},{20,4},{24,8},{28,12},{1,17},{... | collective-permute-start | bytes 786440 | tf_op jit(solution)/shard_map/ppermute | solution.py:366
  59.0 18.0 %collective-permute-start.7 = (bf16[64,16,128]{2,1,0:T(8,128)(2,1)S(1)}, bf16[64,16,128]{2,1,0:T(8,128)(2,1)S(1)}, u32[]{:S(2)}, u32[]{:S(2)}) collective-permute-start(bf16[64,16,128]{2,1,0:T(8,128)(2,1)S(1)} %get-tuple-element.40), channel_id=1, source_target_pairs={{0,4},{4,0},{8,12},{12,8},{16,20},{20,16},{24,28},{28,24},{1,5},{5... | collective-permute-start | bytes 786440 | tf_op jit(solution)/shard_map/ppermute | solution.py:366
  69.0 8.1 %collective-permute-start.8 = (bf16[64,16,128]{2,1,0:T(8,128)(2,1)S(1)}, bf16[64,16,128]{2,1,0:T(8,128)(2,1)S(1)}, u32[]{:S(2)}, u32[]{:S(2)}) collective-permute-start(bf16[64,16,128]{2,1,0:T(8,128)(2,1)S(1)} %get-tuple-element.41), channel_id=1, source_target_pairs={{0,12},{4,8},{8,4},{12,0},{16,28},{20,24},{24,20},{28,16},{1,13},{... | collective-permute-start | bytes 786440 | tf_op jit(solution)/shard_map/ppermute | solution.py:366
  109.0 15.5 %collective-permute-start.17 = (bf16[64,16,128]{2,1,0:T(8,128)(2,1)S(1)}, bf16[64,16,128]{2,1,0:T(8,128)(2,1)S(1)}, u32[]{:S(2)}, u32[]{:S(2)}) collective-permute-start(bf16[64,16,128]{2,1,0:T(8,128)(2,1)S(1)} %bitcast.30), channel_id=1, source_target_pairs={{0,2},{2,0},{1,3},{3,1},{4,6},{6,4},{5,7},{7,5},{8,10},{10,8},{9,1... | collective-permute-start | bytes 786440 | tf_op jit(solution)/shard_map/ppermute | solution.py:366
  114.2 13.0 %collective-permute-start.16 = (bf16[64,16,128]{2,1,0:T(8,128)(2,1)S(1)}, bf16[64,16,128]{2,1,0:T(8,128)(2,1)S(1)}, u32[]{:S(2)}, u32[]{:S(2)}) collective-permute-start(bf16[64,16,128]{2,1,0:T(8,128)(2,1)S(1)} %bitcast.31), channel_id=1, source_target_pairs={{0,28},{4,24},{8,20},{12,16},{16,12},{20,8},{24,4},{28,0},{1,29},{... | collective-permute-start | bytes 786440 | tf_op jit(solution)/shard_map/ppermute | solution.py:366
  116.4 13.3 %collective-permute-start.15 = (bf16[64,16,128]{2,1,0:T(8,128)(2,1)S(1)}, bf16[64,16,128]{2,1,0:T(8,128)(2,1)S(1)}, u32[]{:S(2)}, u32[]{:S(2)}) collective-permute-start(bf16[64,16,128]{2,1,0:T(8,128)(2,1)S(1)} %bitcast.32), channel_id=1, source_target_pairs={{0,24},{4,28},{8,16},{12,20},{16,8},{20,12},{24,0},{28,4},{1,25},{... | collective-permute-start | bytes 786440 | tf_op jit(solution)/shard_map/ppermute | solution.py:366
  117.0 17.5 %collective-permute-start.14 = (bf16[64,16,128]{2,1,0:T(8,128)(2,1)S(1)}, bf16[64,16,128]{2,1,0:T(8,128)(2,1)S(1)}, u32[]{:S(2)}, u32[]{:S(2)}) collective-permute-start(bf16[64,16,128]{2,1,0:T(8,128)(2,1)S(1)} %bitcast.33), channel_id=1, source_target_pairs={{0,20},{4,16},{8,28},{12,24},{16,4},{20,0},{24,12},{28,8},{1,21},{... | collective-permute-start | bytes 786440 | tf_op jit(solution)/shard_map/ppermute | solution.py:366
  119.2 20.9 %collective-permute-start.13 = (bf16[64,16,128]{2,1,0:T(8,128)(2,1)S(1)}, bf16[64,16,128]{2,1,0:T(8,128)(2,1)S(1)}, u32[]{:S(2)}, u32[]{:S(2)}) collective-permute-start(bf16[64,16,128]{2,1,0:T(8,128)(2,1)S(1)} %bitcast.34), channel_id=1, source_target_pairs={{0,16},{4,20},{8,24},{12,28},{16,0},{20,4},{24,8},{28,12},{1,17},{... | collective-permute-start | bytes 786440 | tf_op jit(solution)/shard_map/ppermute | solution.py:366
  119.5 33.7 %all-to-all-start.1 = ((bf16[16,16,1152]{2,1,0:T(8,128)(2,1)}), bf16[16,16,1152]{2,1,0:T(8,128)(2,1)S(1)}, u32[]{:S(2)}, u32[]{:S(2)}) async-start(bf16[16,16,1152]{2,1,0:T(8,128)(2,1)} %bitcast.12), calls=%async_computation.1 | async-start | bytes 1179648 | tf_op jit(solution)/shard_map/all_to_all | solution.py:429
  124.5 16.7 %collective-permute-start.12 = (bf16[64,16,128]{2,1,0:T(8,128)(2,1)S(1)}, bf16[64,16,128]{2,1,0:T(8,128)(2,1)S(1)}, u32[]{:S(2)}, u32[]{:S(2)}) collective-permute-start(bf16[64,16,128]{2,1,0:T(8,128)(2,1)S(1)} %bitcast.35), channel_id=1, source_target_pairs={{0,12},{4,8},{8,4},{12,0},{16,28},{20,24},{24,20},{28,16},{1,13},{... | collective-permute-start | bytes 786440 | tf_op jit(solution)/shard_map/ppermute | solution.py:366
  127.2 20.0 %collective-permute-start.11 = (bf16[64,16,128]{2,1,0:T(8,128)(2,1)S(1)}, bf16[64,16,128]{2,1,0:T(8,128)(2,1)S(1)}, u32[]{:S(2)}, u32[]{:S(2)}) collective-permute-start(bf16[64,16,128]{2,1,0:T(8,128)(2,1)S(1)} %bitcast.36), channel_id=1, source_target_pairs={{0,8},{4,12},{8,0},{12,4},{16,24},{20,28},{24,16},{28,20},{1,9},{5... | collective-permute-start | bytes 786440 | tf_op jit(solution)/shard_map/ppermute | solution.py:366
  129.7 22.5 %collective-permute-start.10 = (bf16[64,16,128]{2,1,0:T(8,128)(2,1)S(1)}, bf16[64,16,128]{2,1,0:T(8,128)(2,1)S(1)}, u32[]{:S(2)}, u32[]{:S(2)}) collective-permute-start(bf16[64,16,128]{2,1,0:T(8,128)(2,1)S(1)} %bitcast.37), channel_id=1, source_target_pairs={{0,4},{4,0},{8,12},{12,8},{16,20},{20,16},{24,28},{28,24},{1,5},{5... | collective-permute-start | bytes 786440 | tf_op jit(solution)/shard_map/ppermute | solution.py:366
  134.4 18.3 %collective-permute-start.24 = (bf16[64,16,128]{2,1,0:T(8,128)(2,1)S(1)}, bf16[64,16,128]{2,1,0:T(8,128)(2,1)S(1)}, u32[]{:S(2)}, u32[]{:S(2)}) collective-permute-start(bf16[64,16,128]{2,1,0:T(8,128)(2,1)S(1)} %collective-permute-done.16.refs_7_), channel_id=1, source_target_pairs={{0,2},{2,0},{1,3},{3,1},{4,6},{6,4},{5,7},{7,5},{8,10},{10,8},{9,1... | collective-permute-start | bytes 786440 | tf_op jit(solution)/shard_map/ppermute | solution.py:366
  140.0 12.8 %collective-permute-start.23 = (bf16[64,16,128]{2,1,0:T(8,128)(2,1)S(1)}, bf16[64,16,128]{2,1,0:T(8,128)(2,1)S(1)}, u32[]{:S(2)}, u32[]{:S(2)}) collective-permute-start(bf16[64,16,128]{2,1,0:T(8,128)(2,1)S(1)} %collective-permute-done.15.refs_6_), channel_id=1, source_target_pairs={{0,2},{2,0},{1,3},{3,1},{4,6},{6,4},{5,7},{7,5},{8,10},{10,8},{9,1... | collective-permute-start | bytes 786440 | tf_op jit(solution)/shard_map/ppermute | solution.py:366
  141.2 13.1 %collective-permute-start.22 = (bf16[64,16,128]{2,1,0:T(8,128)(2,1)S(1)}, bf16[64,16,128]{2,1,0:T(8,128)(2,1)}, u32[]{:S(2)}, u32[]{:S(2)}) collective-permute-start(bf16[64,16,128]{2,1,0:T(8,128)(2,1)S(1)} %collective-permute-done.14.refs_5_), channel_id=1, source_target_pairs={{0,2},{2,0},{1,3},{3,1},{4,6},{6,4},{5,7},{7,5},{8,10},{10,8},{9,1... | collective-permute-start | bytes 786440 | tf_op jit(solution)/shard_map/ppermute | solution.py:366
  147.2 7.1 %collective-permute-start.21 = (bf16[64,16,128]{2,1,0:T(8,128)(2,1)S(1)}, bf16[64,16,128]{2,1,0:T(8,128)(2,1)}, u32[]{:S(2)}, u32[]{:S(2)}) collective-permute-start(bf16[64,16,128]{2,1,0:T(8,128)(2,1)S(1)} %collective-permute-done.13.refs_4_), channel_id=1, source_target_pairs={{0,2},{2,0},{1,3},{3,1},{4,6},{6,4},{5,7},{7,5},{8,10},{10,8},{9,1... | collective-permute-start | bytes 786440 | tf_op jit(solution)/shard_map/ppermute | solution.py:366
  (10 other events, 12.9 us)

commit v4 on v3

--- a/solution.py
+++ b/solution.py
@@ -241,23 +241,40 @@
         for at in range(0, stop - start, LANES):
             j = (start + at) // LANES
             tiles_s[j * tiles : (j + 1) * tiles] = found[:, at : at + LANES].reshape(tiles, ROWS, LANES)
-    size = out_refs[0].shape[0]
-    for k, out_ref in enumerate(out_refs):
-        out_ref[...] = tiles_s[pl.ds((where_ref[0] ^ k) * size, size)]
-
-
-def outer(where, gp_a, gp_b, mod_a, mod_b, count, padded):
+    size = tiles_s.shape[0] // 8
+    for (lo, hi), order, send_ref, keep_ref in zip(bounds(size), ORDERS, out_refs[::2], out_refs[1::2]):
+        for q in range(4):
+            k = picked(q, order[1:])
+            at = (where_ref[0] ^ k) * size + lo
+            keep_ref[q] = tiles_s[pl.ds(at, hi - lo)]
+            at = (where_ref[0] ^ (k ^ order[0])) * size + lo
+            send_ref[q] = tiles_s[pl.ds(at, hi - lo)]
+
+
+def outer(where, gp_a, gp_b, mod_a, mod_b, padded):
     smem = pl.BlockSpec(memory_space=pltpu.SMEM)
     vmem = pl.BlockSpec(memory_space=pltpu.VMEM)
-    shape = jax.ShapeDtypeStruct((padded // count, ROWS, LANES), BF)
+    shapes = [jax.ShapeDtypeStruct((4, hi - lo, ROWS, LANES), BF) for lo, hi in bounds(padded // 8)]
     return pl.pallas_call(
         outer_kernel,
         in_specs=[smem] + [vmem] * 4,
-        out_shape=(shape,) * count,
+        out_shape=tuple(shape for shape in shapes for _ in range(2)),
         scratch_shapes=[pltpu.VMEM((padded, ROWS, LANES), BF)],
         compiler_params=pltpu.CompilerParams(vmem_limit_bytes=16 * 2**20),
         name="outer",
     )(where, gp_a, gp_b, mod_a, mod_b)
+
+
+ORDERS = ((1, 3, 4), (3, 4, 1), (4, 1, 3))
+
+
+def bounds(size):
+    cuts = [0, -(-size // 3), -(-2 * size // 3), size]
+    return list(zip(cuts[:-1], cuts[1:]))
+
+
+def picked(q, masks):
+    return (masks[0] if q % 2 else 0) ^ (masks[1] if q // 2 else 0)
 
 
 def window_of(half):
@@ -297,52 +314,124 @@
     )(which, recv, keep, unit, att)
 
 
-def sum_kernel(*refs):
-    total = refs[0][...].astype(F32)
-    for ref in refs[1:-1]:
-        total = total + ref[...].astype(F32)
-    refs[-1][...] = total.astype(BF)
-
-
-def sum_of(parts):
-    return pl.pallas_call(
-        sum_kernel,
-        out_shape=jax.ShapeDtypeStruct(parts[0].shape, BF),
+def fold_kernel(*refs):
+    count = len(refs) // 4
+    for i in range(count):
+        keep_ref, got_ref = refs[2 * i : 2 * i + 2]
+        send_ref, left_ref = refs[2 * count + 2 * i : 2 * count + 2 * i + 2]
+        for q in range(keep_ref.shape[0]):
+            total = (keep_ref[q].astype(F32) + got_ref[q].astype(F32)).astype(BF)
+            if q % 2:
+                send_ref[q // 2] = total
+            else:
+                left_ref[q // 2] = total
+
+
+def fold(pairs):
+    shapes = []
+    for keep, _ in pairs:
+        shapes += [jax.ShapeDtypeStruct((keep.shape[0] // 2,) + keep.shape[1:], BF)] * 2
+    found = pl.pallas_call(
+        fold_kernel,
+        out_shape=tuple(shapes),
         compiler_params=pltpu.CompilerParams(vmem_limit_bytes=8 * 2**20),
-        name="sum_of",
-    )(*parts)
-
-
-def spread_kernel(parts_ref, out_ref, *, factor):
-    total = jnp.sum(parts_ref[...].astype(F32), axis=0) * factor
-    total = total.astype(BF)
-    for k in range(out_ref.shape[0]):
-        out_ref[k] = total
-
-
-def spread(parts, factor):
-    return pl.pallas_call(
-        functools.partial(spread_kernel, factor=factor),
-        out_shape=jax.ShapeDtypeStruct(parts.shape, BF),
+        name="fold",
+    )(*[x for pair in pairs for x in pair])
+    return found[::2], found[1::2]
+
+
+def close_kernel(*refs):
+    out_ref, at = refs[-1], 0
+    for keep_ref, got_ref in zip(refs[:-1:2], refs[1:-1:2]):
+        count = keep_ref.shape[1]
+        out_ref[at : at + count] = (keep_ref[0].astype(F32) + got_ref[0].astype(F32)).astype(BF)
+        at += count
+
+
+def close(pairs):
+    count = sum(keep.shape[1] for keep, _ in pairs)
+    return pl.pallas_call(
+        close_kernel,
+        out_shape=jax.ShapeDtypeStruct((count, ROWS, LANES), BF),
         compiler_params=pltpu.CompilerParams(vmem_limit_bytes=8 * 2**20),
-        name="spread",
+        name="close",
+    )(*[x for pair in pairs for x in pair])
+
+
+def join_kernel(*refs):
+    count = len(refs) // 3
+    for i in range(count):
+        have_ref, got_ref, out_ref = refs[2 * i], refs[2 * i + 1], refs[2 * count + i]
+        size = have_ref.shape[0]
+        out_ref[:size] = have_ref[...]
+        out_ref[size:] = got_ref[...]
+
+
+def join(pairs):
+    shapes = [jax.ShapeDtypeStruct((2 * have.shape[0],) + have.shape[1:], BF) for have, _ in pairs]
+    return pl.pallas_call(
+        join_kernel,
+        out_shape=tuple(shapes),
+        compiler_params=pltpu.CompilerParams(vmem_limit_bytes=8 * 2**20),
+        name="join",
+    )(*[x for pair in pairs for x in pair])
+
+
+def reduce_kernel(parts_ref, out_ref, *, factor):
+    out_ref[...] = (jnp.sum(parts_ref[...].astype(F32), axis=0) * factor).astype(BF)
+
+
+def reduce(parts, factor):
+    return pl.pallas_call(
+        functools.partial(reduce_kernel, factor=factor),
+        out_shape=jax.ShapeDtypeStruct(parts.shape[1:], BF),
+        compiler_params=pltpu.CompilerParams(vmem_limit_bytes=4 * 2**20),
+        name="reduce",
     )(parts)
+
+
+def place_kernel(clip_ref, *refs):
+    clips = len(refs) - 4
+    pieces, out_refs, all_s = refs[:clips], refs[clips:-1], refs[-1]
+    size = pieces[0].shape[0]
+    for shift, piece in enumerate(pieces):
+        all_s[pl.ds(lax.rem(clip_ref[0] + shift, clips) * size, size)] = piece[...]
+    for (lo, hi), out_ref in zip(bounds(clips * size), out_refs):
+        out_ref[0] = all_s[lo:hi]
+
+
+def place(clip, pieces):
+    total = len(pieces) * pieces[0].shape[0]
+    smem = pl.BlockSpec(memory_space=pltpu.SMEM)
+    vmem = pl.BlockSpec(memory_space=pltpu.VMEM)
+    return pl.pallas_call(
+        place_kernel,
+        in_specs=[smem] + [vmem] * len(pieces),
+        out_shape=tuple(jax.ShapeDtypeStruct((1, hi - lo, ROWS, LANES), BF) for lo, hi in bounds(total)),
+        scratch_shapes=[pltpu.VMEM((total, ROWS, LANES), BF)],
+        compiler_params=pltpu.CompilerParams(vmem_limit_bytes=4 * 2**20),
+        name="place",
+    )(clip, *pieces)
 
 
 def untile_kernel(where_ref, half_ref, *refs):
     pieces, (out_ref, tiles_s) = refs[:-2], refs[-2:]
-    count = len(pieces) // 2
-    size = pieces[0].shape[0]
+    size = tiles_s.shape[0] // 16
+    pieces = iter(pieces)
     for side in range(2):
         half = half_ref[0] ^ side
-        for k in range(count):
-            base = (half * count + (where_ref[0] ^ k)) * size
-            tiles_s[pl.ds(base, size)] = pieces[side * count + k][...]
+        for far in range(2):
+            for (lo, hi), order in zip(bounds(size), ORDERS):
+                piece = next(pieces)
+                for q in range(4):
+                    k = picked(q, (order[2], order[1])) ^ (order[0] * far)
+                    at = (half * 8 + (where_ref[0] ^ k)) * size + lo
+                    tiles_s[pl.ds(at, hi - lo)] = piece[q]
     rows = out_ref.shape[0] // 2
     tiles = rows // ROWS
     for half in range(2):
         for j in range(out_ref.shape[1] // LANES):
-            start = half * count * size + j * tiles
+            start = half * 8 * size + j * tiles
             block = tiles_s[start : start + tiles].reshape(rows, LANES)
             out_ref[half * rows : (half + 1) * rows, j * LANES : (j + 1) * LANES] = block
 
@@ -350,7 +439,7 @@
 def untile(where, half, pieces, rows, width):
     smem = pl.BlockSpec(memory_space=pltpu.SMEM)
     vmem = pl.BlockSpec(memory_space=pltpu.VMEM)
-    tiles = len(pieces) * pieces[0].shape[0]
+    tiles = sum(4 * piece.shape[1] for piece in pieces)
     return pl.pallas_call(
         untile_kernel,
         in_specs=[smem, smem] + [vmem] * len(pieces),
@@ -371,28 +460,34 @@
     return lax.all_to_all(parts, axis, split_axis=0, concat_axis=0, tiled=True)
 
 
-def plane_size():
-    return lax.axis_size("xlo") * lax.axis_size("y")
-
-
-ORDER = (6, 2, 5, 7, 4, 1, 3)
-
-
-def scatter_plane(parts):
-    return [parts[0]] + [swap(parts[k], PLANE, k) for k in ORDER]
-
-
-def sum_clips(own, factor):
-    clips = lax.axis_size("dp")
-    parts = own.reshape((clips, own.shape[0] // clips) + own.shape[1:])
-    return exchange(spread(exchange(parts, "dp"), factor), "dp").reshape(own.shape)
-
-
-def gather_plane(own, rows, width):
-    where = lax.axis_index(PLANE).astype(jnp.int32).reshape(1)
-    half = lax.axis_index("core").astype(jnp.int32).reshape(1)
-    found = {k: swap(own, PLANE, k) for k in ORDER}
-    pieces = [own] + [found[k] for k in range(1, plane_size())]
+def meet(blocks, level):
+    return [swap(block, PLANE, order[level]) for block, order in zip(blocks, ORDERS)]
+
+
+def sum_plane(found):
+    send, keep = found[::2], found[1::2]
+    send, keep = fold(list(zip(keep, meet(send, 0))))
+    send, keep = fold(list(zip(keep, meet(send, 1))))
+    return close(list(zip(keep, meet(send, 2))))
+
+
+def ring(own, axis):
+    count = lax.axis_size(axis)
+    pieces = [own] * count
+    up = down = own
+    for step in range(1, count // 2 + 1):
+        up = lax.ppermute(up, axis, [(i, (i + 1) % count) for i in range(count)])
+        pieces[count - step] = up
+        if step < count - step:
+            down = lax.ppermute(down, axis, [(i, (i - 1) % count) for i in range(count)])
+            pieces[step] = down
+    return pieces
+
+
+def gather_plane(have, where, half, rows, width):
+    have = join(list(zip(have, meet(have, 2))))
+    have = join(list(zip(have, meet(have, 1))))
+    pieces = list(have) + meet(have, 0)
     pieces = pieces + [swap(piece, ("core",), 1) for piece in pieces]
     return untile(where, half, pieces, rows, width)
 
@@ -416,20 +511,22 @@
     mod, gp_keep, gp_send, att, send, keep, unit = attend(
         core, which, x, mod_shift, mod_scale, wt, q_gain[:, None], k_gain[:, None], own_patches, heads, hd
     )
-    recv = lax.ppermute(send, "tensor", [(0, 1), (1, 0)])
     used = (3 * hw // 2 // ROWS) * (width // LANES)
-    group = plane_size() * clips
+    group = 8 * clips
     padded = -(-used // group) * group
     gp_other, mod_other = swap(gp_send, ("core",), 1), swap(mod, ("core",), 1)
-    parts = scatter_plane(outer(where, gp_keep, gp_other, mod, mod_other, plane_size(), padded))
-    parts, recv = lax.optimization_barrier((parts, recv))
-    home = finish(which, recv, keep, unit, att, width)
-    own, home = lax.optimization_barrier((sum_of(parts), home))
-    home = home.reshape(frames, own_patches, width)
+    own = sum_plane(outer(where, gp_keep, gp_other, mod, mod_other, padded))
+    own, send = lax.optimization_barrier((own, send))
+    recv = lax.ppermute(send, "tensor", [(0, 1), (1, 0)])
+    own = exchange(own.reshape((clips, own.shape[0] // clips) + own.shape[1:]), "dp")
+    own, recv = lax.optimization_barrier((own, recv))
+    own = reduce(own, 1.0 / math.sqrt(clips * frames * patches))
+    home = finish(which, recv, keep, unit, att, width).reshape(frames, own_patches, width)
     home = lax.all_to_all(home, SEQ, split_axis=0, concat_axis=0, tiled=True)
+    pieces, home = lax.optimization_barrier((ring(own, "dp"), home))
     grad_t, att_t = unpack(home.reshape(patches, width))
-    factor = 1.0 / math.sqrt(clips * frames * patches)
-    grad_qkv = gather_plane(sum_clips(own, factor), 3 * hw, width)
+    have = place(lax.axis_index("dp").astype(jnp.int32).reshape(1), pieces)
+    grad_qkv = gather_plane(have, where, core, 3 * hw, width)
     grad_qkv = grad_qkv.reshape(3, hw, width).transpose(2, 0, 1)
     return (att_t.T[None, None], grad_t.T[None, None], grad_qkv)
 

time: 160 us -> 156 us (0.975)
  blocking collectives: 29.1 us -> 0 us
  starting transfers between devices: 40.7 us -> 65.9 us
    all_to_all x2 -> x0, blocking collectives: 29.1 us -> none  [exchange(): return lax.all_to_all(parts, axis, split_axis=0, concat_axis=0, tiled=True)]
    ppermute x24 -> x26, waiting for transfers between devices: 43.4 us -> 31.2 us  [swap(): return lax.ppermute(x, axes, [(i, i ^ k) for i in range(count)])]
    ppermute x0 -> x7, starting transfers between devices: none -> 8.39 us  [the longest x3 8.3 us: ring(): lax.ppermute(down, axis, [(i, (i - 1) % count) for i in range(count)])]
    all_to_all x0 -> x1, starting transfers between devices: none -> 8.18 us  [exchange(): return lax.all_to_all(parts, axis, split_axis=0, concat_axis=0, tiled=True)]
    ppermute x0 -> x7, waiting for transfers between devices: none -> 7.87 us  [the longest x4 7.86 us: ring(): up = lax.ppermute(up, axis, [(i, (i + 1) % count) for i in range(count)])]
    ppermute x24 -> x26, starting transfers between devices: 26.4 us -> 30.7 us  [swap(): return lax.ppermute(x, axes, [(i, i ^ k) for i in range(count)])]
    all_to_all x1, starting transfers between devices: 4.98 us -> 9.17 us  [body(): home = lax.all_to_all(home, SEQ, split_axis=0, concat_axis=0, tiled=True)]
    ppermute x1, waiting for transfers between devices: 1.23 us -> 4.98 us  [body(): recv = lax.ppermute(send, 'tensor', [(0, 1), (1, 0)])]
  transfers between devices with their start and end apart: 27 -> 37, of which waited for: 13 -> 20; matrix products, arithmetic and copies ran while one was open for 1% -> 1% of each run, Pallas kernels for 2% -> 1%
where the time goes in v4:
time: 156 us; the launch traced here: 155 us
  starting transfers between devices  65.9 us (42%)
  waiting for transfers between devices  58.9 us (38%)
  Pallas kernels  21.1 us (14%)
  local copies, waits for them, and re-layouts  8.5 us (5%)
    ppermute x26, waiting for transfers between devices, swap(): return lax.ppermute(x, axes, [(i, i ^ k) for i in range(count)])  31.2 us
    ppermute x26, starting transfers between devices, swap(): return lax.ppermute(x, axes, [(i, i ^ k) for i in range(count)])  30.7 us
    all_to_all x1, waiting for transfers between devices, body(): lax.all_to_all(x, SEQ, split_axis=0, concat_axis=0, tiled=True)  12.9 us
    pallas_call x1, Pallas kernels, attend(): pl.pallas_call(functools.partial(attend_kernel, patches=patches, heads=he...  11.7 us
    all_to_all x1, starting transfers between devices, body(): home = lax.all_to_all(home, SEQ, split_axis=0, concat_axis=0, tiled=True)  9.17 us
    ppermute x3, starting transfers between devices, ring(): lax.ppermute(down, axis, [(i, (i - 1) % count) for i in range(count)])  8.3 us
    all_to_all x1, starting transfers between devices, exchange(): return lax.all_to_all(parts, axis, split_axis=0, concat_axis=0, tiled=True)  8.18 us
    ppermute x4, waiting for transfers between devices, ring(): up = lax.ppermute(up, axis, [(i, (i + 1) % count) for i in range(count)])  7.86 us
  transfers between devices with their start and end apart: 37, of which 20 were waited for; matrix products, arithmetic and copies ran while one was open for 1% of the time, Pallas kernels for 1%

profile of v4, /device:TPU:1, one launch (start us, length us, event | category | flops | bytes accessed | tf_op | source)
XLA Modules:
  0.0 155.2 jit_solution(8916013641210019032)
XLA Ops:
  3.9 6.9 %all-to-all-start = ((bf16[16,16,1728]{2,1,0:T(8,128)(2,1)}), bf16[16,16,1728]{2,1,0:T(8,128)(2,1)S(1)}, u32[]{:S(2)}, u32[]{:S(2)}) async-start(bf16[16,16,1728]{2,1,0:T(8,128)(2,1)} %bitcast.6), calls=%async_computation | async-start | bytes 1835008 | tf_op jit(solution)/shard_map/all_to_all | solution.py:507
  12.3 12.9 %all-to-all-done = bf16[16,16,1728]{2,1,0:T(8,128)(2,1)S(1)} async-done(((bf16[16,16,1728]{2,1,0:T(8,128)(2,1)}), bf16[16,16,1728]{2,1,0:T(8,128)(2,1)S(1)}, u32[]{:S(2)}, u32[]{:S(2)}) %all-to-all-start) | async-done | bytes 884768 | tf_op jit(solution)/shard_map/all_to_all | solution.py:507
  25.2 2.1 %copy-done = bf16[1152,3,576]{0,2,1:T(8,128)(2,1)S(1)} copy-done((bf16[1152,3,576]{0,2,1:T(8,128)(2,1)S(1)}, bf16[1152,3,576]{0,2,1:T(8,128)(2,1)}, u32[]{:S(2)}) %copy-start) | copy-done | bytes 3981336
  28.7 11.7 %attend.1 = (bf16[256,1152]{1,0:T(8,128)(2,1)S(1)}, bf16[864,256]{1,0:T(8,128)(2,1)S(1)}, bf16[864,256]{1,0:T(8,128)(2,1)}, bf16[256,576]{1,0:T(8,128)(2,1)S(1)}...) custom-call(s32[1]{0:T(128)} %bitcast.1.core_ref.half_ref, ...), custom_call_target="tpu_custom_call" | custom-call | tf_op jit(solution)/shard_map/attend/pallas_call | solution.py:214
  42.7 2.3 %collective-permute-done.gp_b = bf16[864,256]{1,0:T(8,128)(2,1)S(1)} collective-permute-done((bf16[864,256]{1,0:T(8,128)(2,1)}, bf16[864,256]{1,0:T(8,128)(2,1)S(1)}, u32[]{:S(2)}, u32[]{:S(2)}) %collective-permute-start) | collective-permute-done | bytes 442400 | tf_op jit(solution)/shard_map/ppermute | solution.py:455
  48.4 8.9 %collective-permute-done.3.refs_3_ = bf16[4,21,16,128]{3,2,1,0:T(8,128)(2,1)S(1)} collective-permute-done((bf16[4,21,16,128]{3,2,1,0:T(8,128)(2,1)S(1)}, bf16[4,21,16,128]{3,2,1,0:T(8,128)(2,1)S(1)}, u32[]{:S(2)}, u32[]{:S(2)}) %collective-permute-start.3) | collective-permute-done | bytes 344096 | tf_op jit(solution)/shard_map/ppermute | solution.py:455
  59.0 4.5 %collective-permute-done.6.refs_3_ = bf16[2,21,16,128]{3,2,1,0:T(8,128)(2,1)S(1)} collective-permute-done((bf16[2,21,16,128]{3,2,1,0:T(8,128)(2,1)S(1)}, bf16[2,21,16,128]{3,2,1,0:T(8,128)(2,1)S(1)}, u32[]{:S(2)}, u32[]{:S(2)}) %collective-permute-start.6) | collective-permute-done | bytes 172064 | tf_op jit(solution)/shard_map/ppermute | solution.py:455
  66.5 2.1 %collective-permute-done.9.refs_3_ = bf16[1,21,16,128]{3,2,1,0:T(8,128)(2,1)S(1)} collective-permute-done((bf16[1,21,16,128]{3,2,1,0:T(8,128)(2,1)S(1)}, bf16[1,21,16,128]{3,2,1,0:T(8,128)(2,1)S(1)}, u32[]{:S(2)}, u32[]{:S(2)}) %collective-permute-start.9) | collective-permute-done | bytes 86048 | tf_op jit(solution)/shard_map/ppermute | solution.py:455
  70.6 8.2 %all-to-all-start.1 = ((bf16[8,8,16,128]{3,2,1,0:T(8,128)(2,1)}), bf16[8,8,16,128]{3,2,1,0:T(8,128)(2,1)S(1)}, u32[]{:S(2)}, u32[]{:S(2)}) async-start(bf16[8,8,16,128]{3,2,1,0:T(8,128)(2,1)} %bitcast.12), calls=%async_computation.1 | async-start | bytes 524288 | tf_op jit(solution)/shard_map/all_to_all | solution.py:460
  78.8 2.5 %collective-permute-start.11 = (bf16[256,640]{1,0:T(8,128)(2,1)S(1)}, bf16[256,640]{1,0:T(8,128)(2,1)S(1)}, u32[]{:S(2)}, u32[]{:S(2)}) collective-permute-start(bf16[256,640]{1,0:T(8,128)(2,1)S(1)} %copy-done.8), channel_id=1, source_target_pairs={{0,1},{1,0},{2,3},{3,2},{4,5},{5,4},{6,7},{7,6},{8,9},{9,8},{10,11... | collective-permute-start | bytes 983048 | tf_op jit(solution)/shard_map/ppermute | solution.py:520
  81.3 5.0 %collective-permute-done.11.recv_ref = bf16[256,640]{1,0:T(8,128)(2,1)S(1)} collective-permute-done((bf16[256,640]{1,0:T(8,128)(2,1)S(1)}, bf16[256,640]{1,0:T(8,128)(2,1)S(1)}, u32[]{:S(2)}, u32[]{:S(2)}) %collective-permute-start.11) | collective-permute-done | bytes 327712 | tf_op jit(solution)/shard_map/ppermute | solution.py:520
  86.3 1.9 %all-to-all-done.1.parts_ref = bf16[8,8,16,128]{3,2,1,0:T(8,128)(2,1)S(1)} async-done(((bf16[8,8,16,128]{3,2,1,0:T(8,128)(2,1)}), bf16[8,8,16,128]{3,2,1,0:T(8,128)(2,1)S(1)}, u32[]{:S(2)}, u32[]{:S(2)}) %all-to-all-start.1) | async-done | bytes 262176 | tf_op jit(solution)/shard_map/all_to_all | solution.py:460
  89.7 9.2 %all-to-all-start.2 = ((bf16[16,16,1152]{2,1,0:T(8,128)(2,1)}), bf16[16,16,1152]{2,1,0:T(8,128)(2,1)S(1)}, u32[]{:S(2)}, u32[]{:S(2)}) async-start(bf16[16,16,1152]{2,1,0:T(8,128)(2,1)} %bitcast.13), calls=%async_computation.2 | async-start | bytes 1179648 | tf_op jit(solution)/shard_map/all_to_all | solution.py:525
  99.0 2.7 %collective-permute-start.12 = (bf16[8,16,128]{2,1,0:T(8,128)(2,1)S(1)}, bf16[8,16,128]{2,1,0:T(8,128)(2,1)S(1)}, u32[]{:S(2)}, u32[]{:S(2)}) collective-permute-start(bf16[8,16,128]{2,1,0:T(8,128)(2,1)S(1)} %reduce.1.refs_0_), channel_id=1, source_target_pairs={{0,224},{32,0},{64,32},{96,64},{128,96},{160,128},{192,160},{224,1... | collective-permute-start | bytes 98312 | tf_op jit(solution)/shard_map/ppermute | solution.py:482
  103.0 3.0 %collective-permute-start.13 = (bf16[8,16,128]{2,1,0:T(8,128)(2,1)S(1)}, bf16[8,16,128]{2,1,0:T(8,128)(2,1)S(1)}, u32[]{:S(2)}, u32[]{:S(2)}) collective-permute-start(bf16[8,16,128]{2,1,0:T(8,128)(2,1)S(1)} %collective-permute-done.12.refs_1_), channel_id=1, source_target_pairs={{0,224},{32,0},{64,32},{96,64},{128,96},{160,128},{192,160},{224,1... | collective-permute-start | bytes 98312 | tf_op jit(solution)/shard_map/ppermute | solution.py:482
  107.3 2.7 %collective-permute-start.14 = (bf16[8,16,128]{2,1,0:T(8,128)(2,1)S(1)}, bf16[8,16,128]{2,1,0:T(8,128)(2,1)S(1)}, u32[]{:S(2)}, u32[]{:S(2)}) collective-permute-start(bf16[8,16,128]{2,1,0:T(8,128)(2,1)S(1)} %collective-permute-done.13.refs_2_), channel_id=1, source_target_pairs={{0,224},{32,0},{64,32},{96,64},{128,96},{160,128},{192,160},{224,1... | collective-permute-start | bytes 98312 | tf_op jit(solution)/shard_map/ppermute | solution.py:482
  111.2 4.0 %collective-permute-done.18.refs_4_ = bf16[8,16,128]{2,1,0:T(8,128)(2,1)S(1)} collective-permute-done((bf16[8,16,128]{2,1,0:T(8,128)(2,1)S(1)}, bf16[8,16,128]{2,1,0:T(8,128)(2,1)S(1)}, u32[]{:S(2)}, u32[]{:S(2)}) %collective-permute-start.18) | collective-permute-done | bytes 32800 | tf_op jit(solution)/shard_map/ppermute | solution.py:479
  120.1 2.5 %collective-permute-done.21.refs_5_ = bf16[1,21,16,128]{3,2,1,0:T(8,128)(2,1)S(1)} collective-permute-done((bf16[1,21,16,128]{3,2,1,0:T(8,128)(2,1)S(1)}, bf16[1,21,16,128]{3,2,1,0:T(8,128)(2,1)S(1)}, u32[]{:S(2)}, u32[]{:S(2)}) %collective-permute-start.21) | collective-permute-done | bytes 86048 | tf_op jit(solution)/shard_map/ppermute | solution.py:455
  122.7 1.6 %collective-permute-start.22 = (bf16[2,22,16,128]{3,2,1,0:T(8,128)(2,1)S(1)}, bf16[2,22,16,128]{3,2,1,0:T(8,128)(2,1)S(1)}, u32[]{:S(2)}, u32[]{:S(2)}) collective-permute-start(bf16[2,22,16,128]{3,2,1,0:T(8,128)(2,1)S(1)} %get-tuple-element.95.refs_0_), channel_id=1, source_target_pairs={{0,12},{4,8},{8,4},{12,0},{16,28},{20,24},{24,20},{28,16},{1,13},{... | collective-permute-start | bytes 540680 | tf_op jit(solution)/shard_map/ppermute | solution.py:455
  124.5 4.3 %collective-permute-done.23.refs_3_ = bf16[2,21,16,128]{3,2,1,0:T(8,128)(2,1)S(1)} collective-permute-done((bf16[2,21,16,128]{3,2,1,0:T(8,128)(2,1)S(1)}, bf16[2,21,16,128]{3,2,1,0:T(8,128)(2,1)S(1)}, u32[]{:S(2)}, u32[]{:S(2)}) %collective-permute-start.23) | collective-permute-done | bytes 172064 | tf_op jit(solution)/shard_map/ppermute | solution.py:455
  129.6 9.2 %collective-permute-start.29 = (bf16[4,21,16,128]{3,2,1,0:T(8,128)(2,1)S(1)}, bf16[4,21,16,128]{3,2,1,0:T(8,128)(2,1)S(1)}, u32[]{:S(2)}, u32[]{:S(2)}) collective-permute-start(bf16[4,21,16,128]{3,2,1,0:T(8,128)(2,1)S(1)} %get-tuple-element.99.refs_1_), channel_id=1, source_target_pairs={{0,2},{2,0},{1,3},{3,1},{4,6},{6,4},{5,7},{7,5},{8,10},{10,8},{9,1... | collective-permute-start | bytes 1032200 | tf_op jit(solution)/shard_map/ppermute | solution.py:455
  141.3 4.7 %collective-permute-start.31 = (bf16[4,22,16,128]{3,2,1,0:T(8,128)(2,1)S(1)}, bf16[4,22,16,128]{3,2,1,0:T(8,128)(2,1)S(1)}, u32[]{:S(2)}, u32[]{:S(2)}) collective-permute-start(bf16[4,22,16,128]{3,2,1,0:T(8,128)(2,1)S(1)} %collective-permute-done.25.refs_3_), channel_id=1, source_target_pairs={{0,2},{2,0},{1,3},{3,1},{4,6},{6,4},{5,7},{7,5},{8,10},{10,8},{9,1... | collective-permute-start | bytes 1081352 | tf_op jit(solution)/shard_map/ppermute | solution.py:455
  146.0 3.8 %collective-permute-done.26.refs_4_ = bf16[4,21,16,128]{3,2,1,0:T(8,128)(2,1)S(1)} collective-permute-done((bf16[4,21,16,128]{3,2,1,0:T(8,128)(2,1)S(1)}, bf16[4,21,16,128]{3,2,1,0:T(8,128)(2,1)S(1)}, u32[]{:S(2)}, u32[]{:S(2)}) %collective-permute-start.26) | collective-permute-done | bytes 344096 | tf_op jit(solution)/shard_map/ppermute | solution.py:455
  152.3 2.9 %untile.1 = bf16[1728,1152]{1,0:T(8,128)(2,1)} custom-call(s32[1]{0:T(128)} %bitcast.where_ref, s32[1]{0:T(128)} %bitcast.1.core_ref.half_ref, bf16[4,22,16,128]{3,2,1,0:T(8,128)(2,1)S(1)} %get-tuple-element.98.refs_0_, bf16[4,21,16,128]{3,2,1,0:T(8,128)(2,1)S(1)} %get-tuple-element.99.refs_1_, bf16[4,21,16,128]{3,2,1,0:T(8,128)(2,1)S(1)} %get-tuple-element.100.refs_2_, ...), custom_call_target="tpu_custom_call" | custom-call | tf_op jit(solution)/shard_map/untile/pallas_call | solution.py:443
  (83 shorter events, 34.9 us)
Async XLA Ops:
  3.9 21.3 %all-to-all-start = ((bf16[16,16,1728]{2,1,0:T(8,128)(2,1)}), bf16[16,16,1728]{2,1,0:T(8,128)(2,1)S(1)}, u32[]{:S(2)}, u32[]{:S(2)}) async-start(bf16[16,16,1728]{2,1,0:T(8,128)(2,1)} %bitcast.6), calls=%async_computation | async-start | bytes 1835008 | tf_op jit(solution)/shard_map/all_to_all | solution.py:507
  46.6 10.7 %collective-permute-start.2 = (bf16[4,22,16,128]{3,2,1,0:T(8,128)(2,1)S(1)}, bf16[4,22,16,128]{3,2,1,0:T(8,128)(2,1)S(1)}, u32[]{:S(2)}, u32[]{:S(2)}) collective-permute-start(bf16[4,22,16,128]{3,2,1,0:T(8,128)(2,1)S(1)} %get-tuple-element.56), channel_id=1, source_target_pairs={{0,4},{4,0},{8,12},{12,8},{16,20},{20,16},{24,28},{28,24},{1,5},{5... | collective-permute-start | bytes 1081352 | tf_op jit(solution)/shard_map/ppermute | solution.py:455
  46.7 10.6 %collective-permute-start.3 = (bf16[4,21,16,128]{3,2,1,0:T(8,128)(2,1)S(1)}, bf16[4,21,16,128]{3,2,1,0:T(8,128)(2,1)S(1)}, u32[]{:S(2)}, u32[]{:S(2)}) collective-permute-start(bf16[4,21,16,128]{3,2,1,0:T(8,128)(2,1)S(1)} %get-tuple-element.58), channel_id=1, source_target_pairs={{0,12},{4,8},{8,4},{12,0},{16,28},{20,24},{24,20},{28,16},{1,13},{... | collective-permute-start | bytes 1032200 | tf_op jit(solution)/shard_map/ppermute | solution.py:455
  48.0 9.3 %collective-permute-start.4 = (bf16[4,21,16,128]{3,2,1,0:T(8,128)(2,1)S(1)}, bf16[4,21,16,128]{3,2,1,0:T(8,128)(2,1)S(1)}, u32[]{:S(2)}, u32[]{:S(2)}) collective-permute-start(bf16[4,21,16,128]{3,2,1,0:T(8,128)(2,1)S(1)} %get-tuple-element.60), channel_id=1, source_target_pairs={{0,16},{4,20},{8,24},{12,28},{16,0},{20,4},{24,8},{28,12},{1,17},{... | collective-permute-start | bytes 1032200 | tf_op jit(solution)/shard_map/ppermute | solution.py:455
  57.5 6.1 %collective-permute-start.5 = (bf16[2,22,16,128]{3,2,1,0:T(8,128)(2,1)S(1)}, bf16[2,22,16,128]{3,2,1,0:T(8,128)(2,1)S(1)}, u32[]{:S(2)}, u32[]{:S(2)}) collective-permute-start(bf16[2,22,16,128]{3,2,1,0:T(8,128)(2,1)S(1)} %get-tuple-element.62), channel_id=1, source_target_pairs={{0,12},{4,8},{8,4},{12,0},{16,28},{20,24},{24,20},{28,16},{1,13},{... | collective-permute-start | bytes 540680 | tf_op jit(solution)/shard_map/ppermute | solution.py:455
  59.0 4.6 %collective-permute-start.6 = (bf16[2,21,16,128]{3,2,1,0:T(8,128)(2,1)S(1)}, bf16[2,21,16,128]{3,2,1,0:T(8,128)(2,1)S(1)}, u32[]{:S(2)}, u32[]{:S(2)}) collective-permute-start(bf16[2,21,16,128]{3,2,1,0:T(8,128)(2,1)S(1)} %get-tuple-element.64), channel_id=1, source_target_pairs={{0,16},{4,20},{8,24},{12,28},{16,0},{20,4},{24,8},{28,12},{1,17},{... | collective-permute-start | bytes 516104 | tf_op jit(solution)/shard_map/ppermute | solution.py:455
  59.0 4.6 %collective-permute-start.7 = (bf16[2,21,16,128]{3,2,1,0:T(8,128)(2,1)S(1)}, bf16[2,21,16,128]{3,2,1,0:T(8,128)(2,1)S(1)}, u32[]{:S(2)}, u32[]{:S(2)}) collective-permute-start(bf16[2,21,16,128]{3,2,1,0:T(8,128)(2,1)S(1)} %get-tuple-element.66), channel_id=1, source_target_pairs={{0,4},{4,0},{8,12},{12,8},{16,20},{20,16},{24,28},{28,24},{1,5},{5... | collective-permute-start | bytes 516104 | tf_op jit(solution)/shard_map/ppermute | solution.py:455
  63.8 6.0 %collective-permute-start.8 = (bf16[1,22,16,128]{3,2,1,0:T(8,128)(2,1)S(1)}, bf16[1,22,16,128]{3,2,1,0:T(8,128)(2,1)S(1)}, u32[]{:S(2)}, u32[]{:S(2)}) collective-permute-start(bf16[1,22,16,128]{3,2,1,0:T(8,128)(2,1)S(1)} %get-tuple-element.68), channel_id=1, source_target_pairs={{0,16},{4,20},{8,24},{12,28},{16,0},{20,4},{24,8},{28,12},{1,17},{... | collective-permute-start | bytes 270344 | tf_op jit(solution)/shard_map/ppermute | solution.py:455
  65.3 4.5 %collective-permute-start.10 = (bf16[1,21,16,128]{3,2,1,0:T(8,128)(2,1)S(1)}, bf16[1,21,16,128]{3,2,1,0:T(8,128)(2,1)S(1)}, u32[]{:S(2)}, u32[]{:S(2)}) collective-permute-start(bf16[1,21,16,128]{3,2,1,0:T(8,128)(2,1)S(1)} %get-tuple-element.72), channel_id=1, source_target_pairs={{0,12},{4,8},{8,4},{12,0},{16,28},{20,24},{24,20},{28,16},{1,13},{... | collective-permute-start | bytes 258056 | tf_op jit(solution)/shard_map/ppermute | solution.py:455
  70.6 17.6 %all-to-all-start.1 = ((bf16[8,8,16,128]{3,2,1,0:T(8,128)(2,1)}), bf16[8,8,16,128]{3,2,1,0:T(8,128)(2,1)S(1)}, u32[]{:S(2)}, u32[]{:S(2)}) async-start(bf16[8,8,16,128]{3,2,1,0:T(8,128)(2,1)} %bitcast.12), calls=%async_computation.1 | async-start | bytes 524288 | tf_op jit(solution)/shard_map/all_to_all | solution.py:460
  78.8 7.5 %collective-permute-start.11 = (bf16[256,640]{1,0:T(8,128)(2,1)S(1)}, bf16[256,640]{1,0:T(8,128)(2,1)S(1)}, u32[]{:S(2)}, u32[]{:S(2)}) collective-permute-start(bf16[256,640]{1,0:T(8,128)(2,1)S(1)} %copy-done.8), channel_id=1, source_target_pairs={{0,1},{1,0},{2,3},{3,2},{4,5},{5,4},{6,7},{7,6},{8,9},{9,8},{10,11... | collective-permute-start | bytes 983048 | tf_op jit(solution)/shard_map/ppermute | solution.py:520
  89.7 25.5 %all-to-all-start.2 = ((bf16[16,16,1152]{2,1,0:T(8,128)(2,1)}), bf16[16,16,1152]{2,1,0:T(8,128)(2,1)S(1)}, u32[]{:S(2)}, u32[]{:S(2)}) async-start(bf16[16,16,1152]{2,1,0:T(8,128)(2,1)} %bitcast.13), calls=%async_computation.2 | async-start | bytes 1179648 | tf_op jit(solution)/shard_map/all_to_all | solution.py:525
  115.3 7.4 %collective-permute-start.19 = (bf16[1,22,16,128]{3,2,1,0:T(8,128)(2,1)S(1)}, bf16[1,22,16,128]{3,2,1,0:T(8,128)(2,1)S(1)}, u32[]{:S(2)}, u32[]{:S(2)}) collective-permute-start(bf16[1,22,16,128]{3,2,1,0:T(8,128)(2,1)S(1)} %get-tuple-element.92.refs_0_), channel_id=1, source_target_pairs={{0,16},{4,20},{8,24},{12,28},{16,0},{20,4},{24,8},{28,12},{1,17},{... | collective-permute-start | bytes 270344 | tf_op jit(solution)/shard_map/ppermute | solution.py:455
  118.1 4.5 %collective-permute-start.21 = (bf16[1,21,16,128]{3,2,1,0:T(8,128)(2,1)S(1)}, bf16[1,21,16,128]{3,2,1,0:T(8,128)(2,1)S(1)}, u32[]{:S(2)}, u32[]{:S(2)}) collective-permute-start(bf16[1,21,16,128]{3,2,1,0:T(8,128)(2,1)S(1)} %get-tuple-element.94.refs_4_), channel_id=1, source_target_pairs={{0,12},{4,8},{8,4},{12,0},{16,28},{20,24},{24,20},{28,16},{1,13},{... | collective-permute-start | bytes 258056 | tf_op jit(solution)/shard_map/ppermute | solution.py:455
  122.7 6.7 %collective-permute-start.22 = (bf16[2,22,16,128]{3,2,1,0:T(8,128)(2,1)S(1)}, bf16[2,22,16,128]{3,2,1,0:T(8,128)(2,1)S(1)}, u32[]{:S(2)}, u32[]{:S(2)}) collective-permute-start(bf16[2,22,16,128]{3,2,1,0:T(8,128)(2,1)S(1)} %get-tuple-element.95.refs_0_), channel_id=1, source_target_pairs={{0,12},{4,8},{8,4},{12,0},{16,28},{20,24},{24,20},{28,16},{1,13},{... | collective-permute-start | bytes 540680 | tf_op jit(solution)/shard_map/ppermute | solution.py:455
  124.3 4.6 %collective-permute-start.23 = (bf16[2,21,16,128]{3,2,1,0:T(8,128)(2,1)S(1)}, bf16[2,21,16,128]{3,2,1,0:T(8,128)(2,1)S(1)}, u32[]{:S(2)}, u32[]{:S(2)}) collective-permute-start(bf16[2,21,16,128]{3,2,1,0:T(8,128)(2,1)S(1)} %get-tuple-element.96.refs_2_), channel_id=1, source_target_pairs={{0,16},{4,20},{8,24},{12,28},{16,0},{20,4},{24,8},{28,12},{1,17},{... | collective-permute-start | bytes 516104 | tf_op jit(solution)/shard_map/ppermute | solution.py:455
  124.5 4.6 %collective-permute-start.24 = (bf16[2,21,16,128]{3,2,1,0:T(8,128)(2,1)S(1)}, bf16[2,21,16,128]{3,2,1,0:T(8,128)(2,1)S(1)}, u32[]{:S(2)}, u32[]{:S(2)}) collective-permute-start(bf16[2,21,16,128]{3,2,1,0:T(8,128)(2,1)S(1)} %get-tuple-element.97.refs_4_), channel_id=1, source_target_pairs={{0,4},{4,0},{8,12},{12,8},{16,20},{20,16},{24,28},{28,24},{1,5},{5... | collective-permute-start | bytes 516104 | tf_op jit(solution)/shard_map/ppermute | solution.py:455
  129.5 11.8 %collective-permute-start.25 = (bf16[4,22,16,128]{3,2,1,0:T(8,128)(2,1)S(1)}, bf16[4,22,16,128]{3,2,1,0:T(8,128)(2,1)S(1)}, u32[]{:S(2)}, u32[]{:S(2)}) collective-permute-start(bf16[4,22,16,128]{3,2,1,0:T(8,128)(2,1)S(1)} %get-tuple-element.98.refs_0_), channel_id=1, source_target_pairs={{0,4},{4,0},{8,12},{12,8},{16,20},{20,16},{24,28},{28,24},{1,5},{5... | collective-permute-start | bytes 1081352 | tf_op jit(solution)/shard_map/ppermute | solution.py:455
  129.6 16.4 %collective-permute-start.29 = (bf16[4,21,16,128]{3,2,1,0:T(8,128)(2,1)S(1)}, bf16[4,21,16,128]{3,2,1,0:T(8,128)(2,1)S(1)}, u32[]{:S(2)}, u32[]{:S(2)}) collective-permute-start(bf16[4,21,16,128]{3,2,1,0:T(8,128)(2,1)S(1)} %get-tuple-element.99.refs_1_), channel_id=1, source_target_pairs={{0,2},{2,0},{1,3},{3,1},{4,6},{6,4},{5,7},{7,5},{8,10},{10,8},{9,1... | collective-permute-start | bytes 1032200 | tf_op jit(solution)/shard_map/ppermute | solution.py:455
  138.8 10.9 %collective-permute-start.26 = (bf16[4,21,16,128]{3,2,1,0:T(8,128)(2,1)S(1)}, bf16[4,21,16,128]{3,2,1,0:T(8,128)(2,1)S(1)}, u32[]{:S(2)}, u32[]{:S(2)}) collective-permute-start(bf16[4,21,16,128]{3,2,1,0:T(8,128)(2,1)S(1)} %get-tuple-element.99.refs_1_), channel_id=1, source_target_pairs={{0,12},{4,8},{8,4},{12,0},{16,28},{20,24},{24,20},{28,16},{1,13},{... | collective-permute-start | bytes 1032200 | tf_op jit(solution)/shard_map/ppermute | solution.py:455
  140.3 10.2 %collective-permute-start.27 = (bf16[4,21,16,128]{3,2,1,0:T(8,128)(2,1)S(1)}, bf16[4,21,16,128]{3,2,1,0:T(8,128)(2,1)S(1)}, u32[]{:S(2)}, u32[]{:S(2)}) collective-permute-start(bf16[4,21,16,128]{3,2,1,0:T(8,128)(2,1)S(1)} %get-tuple-element.100.refs_2_), channel_id=1, source_target_pairs={{0,16},{4,20},{8,24},{12,28},{16,0},{20,4},{24,8},{28,12},{1,17},{... | collective-permute-start | bytes 1032200 | tf_op jit(solution)/shard_map/ppermute | solution.py:455
  140.7 11.1 %collective-permute-start.28 = (bf16[4,22,16,128]{3,2,1,0:T(8,128)(2,1)S(1)}, bf16[4,22,16,128]{3,2,1,0:T(8,128)(2,1)S(1)}, u32[]{:S(2)}, u32[]{:S(2)}) collective-permute-start(bf16[4,22,16,128]{3,2,1,0:T(8,128)(2,1)S(1)} %get-tuple-element.98.refs_0_), channel_id=1, source_target_pairs={{0,2},{2,0},{1,3},{3,1},{4,6},{6,4},{5,7},{7,5},{8,10},{10,8},{9,1... | collective-permute-start | bytes 1081352 | tf_op jit(solution)/shard_map/ppermute | solution.py:455
  141.3 11.0 %collective-permute-start.31 = (bf16[4,22,16,128]{3,2,1,0:T(8,128)(2,1)S(1)}, bf16[4,22,16,128]{3,2,1,0:T(8,128)(2,1)S(1)}, u32[]{:S(2)}, u32[]{:S(2)}) collective-permute-start(bf16[4,22,16,128]{3,2,1,0:T(8,128)(2,1)S(1)} %collective-permute-done.25.refs_3_), channel_id=1, source_target_pairs={{0,2},{2,0},{1,3},{3,1},{4,6},{6,4},{5,7},{7,5},{8,10},{10,8},{9,1... | collective-permute-start | bytes 1081352 | tf_op jit(solution)/shard_map/ppermute | solution.py:455
  146.0 5.9 %collective-permute-start.30 = (bf16[4,21,16,128]{3,2,1,0:T(8,128)(2,1)S(1)}, bf16[4,21,16,128]{3,2,1,0:T(8,128)(2,1)S(1)}, u32[]{:S(2)}, u32[]{:S(2)}) collective-permute-start(bf16[4,21,16,128]{3,2,1,0:T(8,128)(2,1)S(1)} %get-tuple-element.100.refs_2_), channel_id=1, source_target_pairs={{0,2},{2,0},{1,3},{3,1},{4,6},{6,4},{5,7},{7,5},{8,10},{10,8},{9,1... | collective-permute-start | bytes 1032200 | tf_op jit(solution)/shard_map/ppermute | solution.py:455
  (22 other events, 125.5 us)

commit v5 on v4

--- a/solution.py
+++ b/solution.py
@@ -29,18 +29,36 @@
     return jnp.where(rows == cols, 1.0, 0.0).astype(BF)
 
 
-def pack_kernel(latent_ref, cot_ref, out_ref):
-    width = latent_ref.shape[1]
-    out_ref[:, :width] = latent_ref[...]
-    out_ref[:, width:] = mm(eye(latent_ref.shape[0]), cot_ref[...], NT).astype(BF)
+def fetch(pairs, sems):
+    copies = [pltpu.make_async_copy(src, dst, sems.at[i]) for i, (src, dst) in enumerate(pairs)]
+    for copy in copies:
+        copy.start()
+    return copies
+
+
+def pack_kernel(latent_hbm, cot_hbm, out_ref, latent_s, cot_s, sems):
+    width = latent_s.shape[1]
+    first, second = fetch([(cot_hbm, cot_s), (latent_hbm, latent_s)], sems)
+    ident = eye(latent_s.shape[0])
+    first.wait()
+    out_ref[:, width:] = mm(ident, cot_s[...], NT).astype(BF)
+    second.wait()
+    out_ref[:, :width] = latent_s[...]
 
 
 def pack(latent, cot_t):
     tokens, width = latent.shape
+    hbm = pl.BlockSpec(memory_space=pltpu.HBM)
     return pl.pallas_call(
         pack_kernel,
+        in_specs=[hbm, hbm],
         out_shape=jax.ShapeDtypeStruct((tokens, width + cot_t.shape[0]), BF),
-        compiler_params=pltpu.CompilerParams(vmem_limit_bytes=8 * 2**20),
+        scratch_shapes=[
+            pltpu.VMEM(latent.shape, BF),
+            pltpu.VMEM(cot_t.shape, BF),
+            pltpu.SemaphoreType.DMA((2,)),
+        ],
+        compiler_params=pltpu.CompilerParams(vmem_limit_bytes=60 * 2**20),
         name="pack",
     )(latent, cot_t)
 
@@ -75,27 +93,34 @@
     return centred * inverse, inverse
 
 
-def attend_kernel(core_ref, which_ref, x_ref, shift_ref, scale_ref, wt_hbm, qg_ref, kg_ref,
-                  mod_ref, gp_keep_ref, gp_send_ref, att_ref, send_ref, keep_ref, unit_ref,
-                  wt_s, gp_s, ot_s, rows_s, sems, *, patches, heads, hd):
+def attend_kernel(core_ref, which_ref, x_hbm, affine_hbm, wt_hbm, qg_ref, kg_ref,
+                  mod_ref, gp_keep_ref, gp_send_ref, send_hbm, keep_hbm,
+                  x_ref, affine_ref, wt_s, gp_s, ot_s, rows_s, send_ref, keep_ref,
+                  in_sems, out_sems, *, patches, heads, hd):
     tokens, _ = x_ref.shape
-    width = scale_ref.shape[1]
+    width = affine_ref.shape[1]
     hw = heads * hd
-    copies = []
-    for part in range(3):
-        rows = pl.ds(part * hw, hw)
-        copy = pltpu.make_async_copy(wt_hbm.at[rows], wt_s.at[rows], sems.at[part])
-        copy.start()
-        copies.append(copy)
+    parts = [pl.ds(part * hw, hw) for part in range(3)]
+    copies = fetch(
+        [(x_hbm, x_ref), (affine_hbm, affine_ref)]
+        + [(wt_hbm.at[rows], wt_s.at[rows]) for rows in parts],
+        in_sems,
+    )
+    for copy in copies[:2]:
+        copy.wait()
     unit, inverse = unit_of(x_ref[:, :width].astype(F32))
-    factor = 1.0 + scale_ref[...]
-    mod_ref[...] = (unit * factor + shift_ref[...]).astype(BF)
+    half = width // 2
+    win = send_ref.shape[1]
+    mine_low = which_ref[0] == 0
+    keep_ref[:, win : 2 * win] = jnp.where(mine_low, unit[:, :win], unit[:, width - win :])
+    factor = affine_ref[1:2]
+    mod_ref[...] = (unit * factor + affine_ref[0:1]).astype(BF)
     mod = mod_ref[...]
     ident = eye(tokens)
     cot_t = mm(eye(hw), x_ref[:, width:], NT)
 
     def project(part):
-        copies[part].wait()
+        copies[2 + part].wait()
         rows = mm(wt_s[part * hw : (part + 1) * hw, :], mod, NT)
         return rows.astype(BF).astype(F32)
 
@@ -168,16 +193,9 @@
         block = rows_s[at, :].astype(BF)
         gp_s[at, :] = block
         grad = grad + mm(mm(ident, block, NT).astype(BF), wt_s[at, :], NN)
-    gp_keep_ref[...] = gp_s[pl.ds(pl.multiple_of(core_ref[0] * size, ROWS), size), :]
-    gp_send_ref[...] = gp_s[pl.ds(pl.multiple_of((1 - core_ref[0]) * size, ROWS), size), :]
-    att_ref[...] = mm(ident, ot_s[...].astype(BF), NT).astype(BF)
-
-    half = width // 2
-    win = send_ref.shape[1]
     scaled = grad * factor
     first = jnp.sum(scaled, axis=1, keepdims=True)
     second = jnp.sum(scaled * unit, axis=1, keepdims=True)
-    mine_low = which_ref[0] == 0
     col = lax.broadcasted_iota(jnp.int32, (tokens, win), 1)
     here = jnp.where(mine_low, half, 0)
     there = jnp.where(mine_low, 0, half)
@@ -191,40 +209,47 @@
     for place, term in enumerate((first, second, inverse)):
         keep = jnp.where(col == here + place, term, keep)
     send_ref[...] = send.astype(BF)
-    keep_ref[...] = keep
-    unit_ref[...] = jnp.where(mine_low, unit[:, :win], unit[:, width - win :]).astype(BF)
-
-
-def attend(core, which, x, shift, scale, wt, qg, kg, patches, heads, hd):
+    keep_ref[:, :win] = keep
+    outs = []
+    keep_ref[:, 2 * win : 2 * win + hw] = mm(ident, ot_s[...].astype(BF), NT)
+    for i, (src, dst) in enumerate(((send_ref, send_hbm), (keep_ref, keep_hbm))):
+        outs.append(pltpu.make_async_copy(src, dst, out_sems.at[i]))
+        outs[-1].start()
+    gp_keep_ref[...] = gp_s[pl.ds(pl.multiple_of(core_ref[0] * size, ROWS), size), :]
+    gp_send_ref[...] = gp_s[pl.ds(pl.multiple_of((1 - core_ref[0]) * size, ROWS), size), :]
+    for out in outs:
+        out.wait()
+
+
+def attend(core, which, x, affine, wt, qg, kg, patches, heads, hd):
     tokens = x.shape[0]
     width = wt.shape[1]
     hw = heads * hd
     win = window_of(width // 2)
     smem = pl.BlockSpec(memory_space=pltpu.SMEM)
     vmem = pl.BlockSpec(memory_space=pltpu.VMEM)
-    shapes = [
-        ((tokens, width), BF),
-        ((3 * hw // 2, tokens), BF),
-        ((3 * hw // 2, tokens), BF),
-        ((tokens, hw), BF),
-        ((tokens, win), BF),
-        ((tokens, win), F32),
-        ((tokens, win), BF),
-    ]
+    hbm = pl.BlockSpec(memory_space=pltpu.HBM)
+    outs = [((tokens, win), BF), ((tokens, 2 * win + window_of(hw)), F32)]
+    half = jax.ShapeDtypeStruct((3 * hw // 2, tokens), BF)
     return pl.pallas_call(
         functools.partial(attend_kernel, patches=patches, heads=heads, hd=hd),
-        in_specs=[smem, smem, vmem, vmem, vmem, pl.BlockSpec(memory_space=pl.ANY), vmem, vmem],
-        out_shape=tuple(jax.ShapeDtypeStruct(*shape) for shape in shapes),
+        in_specs=[smem, smem] + [hbm] * 3 + [vmem, vmem],
+        out_specs=(vmem,) * 3 + (hbm,) * 2,
+        out_shape=(jax.ShapeDtypeStruct((tokens, width), BF), half, half)
+        + tuple(jax.ShapeDtypeStruct(*out) for out in outs),
         scratch_shapes=[
+            pltpu.VMEM(x.shape, BF),
+            pltpu.VMEM(affine.shape, F32),
             pltpu.VMEM((3 * hw, width), BF),
             pltpu.VMEM((3 * hw, tokens), BF),
             pltpu.VMEM((hw, tokens), F32),
             pltpu.VMEM((3 * hw, tokens), F32),
-            pltpu.SemaphoreType.DMA((3,)),
-        ],
-        compiler_params=pltpu.CompilerParams(vmem_limit_bytes=32 * 2**20),
+        ]
+        + [pltpu.VMEM(*out) for out in outs]
+        + [pltpu.SemaphoreType.DMA((5,)), pltpu.SemaphoreType.DMA((2,))],
+        compiler_params=pltpu.CompilerParams(vmem_limit_bytes=50 * 2**20),
         name="attend",
-    )(core, which, x, shift, scale, wt, qg, kg)
+    )(core, which, x, affine, wt, qg, kg)
 
 
 def outer_kernel(where_ref, gp_a, gp_b, mod_a, mod_b, *refs):
@@ -281,12 +306,13 @@
     return -(-half // LANES) * LANES
 
 
-def finish_kernel(which_ref, recv_ref, keep_ref, unit_ref, att_ref, out_ref, *, width):
+def finish_kernel(which_ref, recv_ref, keep_ref, out_ref, *, width):
     half = width // 2
     win = recv_ref.shape[1]
     mine_low = which_ref[0] == 0
     recv = recv_ref[...].astype(F32)
-    keep = keep_ref[...]
+    keep = keep_ref[:, :win]
+    unit = keep_ref[:, win : 2 * win]
 
     def column(block, place):
         return jnp.where(mine_low, block[:, half + place : half + place + 1], block[:, place : place + 1])
@@ -295,23 +321,23 @@
     second = column(keep, 1) + (column(recv, 2) + column(recv, 3))
     inverse = column(keep, 2)
     grad = keep + recv
-    out = inverse * (grad - first * (1.0 / width) - unit_ref[...].astype(F32) * (second * (1.0 / width)))
+    out = inverse * (grad - first * (1.0 / width) - unit * (second * (1.0 / width)))
     moved = pltpu.roll(out, win - (win - half), 1)
     out_ref[:, :half] = jnp.where(mine_low, out, moved)[:, :half].astype(BF)
-    out_ref[:, half:] = att_ref[...]
-
-
-def finish(which, recv, keep, unit, att, width):
+    out_ref[:, half:] = keep_ref[:, 2 * win : 2 * win + width - half].astype(BF)
+
+
+def finish(which, recv, keep, width):
     tokens = recv.shape[0]
     smem = pl.BlockSpec(memory_space=pltpu.SMEM)
     vmem = pl.BlockSpec(memory_space=pltpu.VMEM)
     return pl.pallas_call(
         functools.partial(finish_kernel, width=width),
-        in_specs=[smem, vmem, vmem, vmem, vmem],
+        in_specs=[smem, vmem, vmem],
         out_shape=jax.ShapeDtypeStruct((tokens, width), BF),
         compiler_params=pltpu.CompilerParams(vmem_limit_bytes=24 * 2**20),
         name="finish",
-    )(which, recv, keep, unit, att)
+    )(which, recv, keep)
 
 
 def fold_kernel(*refs):
@@ -471,17 +497,19 @@
     return close(list(zip(keep, meet(send, 2))))
 
 
-def ring(own, axis):
+def ring(own, axis, home):
     count = lax.axis_size(axis)
     pieces = [own] * count
     up = down = own
     for step in range(1, count // 2 + 1):
+        if step == 2:
+            up, down, home = lax.optimization_barrier((up, down, home))
         up = lax.ppermute(up, axis, [(i, (i + 1) % count) for i in range(count)])
         pieces[count - step] = up
         if step < count - step:
             down = lax.ppermute(down, axis, [(i, (i - 1) % count) for i in range(count)])
             pieces[step] = down
-    return pieces
+    return pieces, home
 
 
 def gather_plane(have, where, half, rows, width):
@@ -505,25 +533,26 @@
     wt = w_qkv.transpose(1, 2, 0).reshape(3 * hw, width)
     x = pack(latent[0, 0], cotangent[0, 0].T).reshape(frames, own_patches, width + hw)
     x = lax.all_to_all(x, SEQ, split_axis=0, concat_axis=0, tiled=True).reshape(patches, width + hw)
+    affine = jnp.concatenate([mod_shift, 1.0 + mod_scale])
     core = lax.axis_index("core").astype(jnp.int32).reshape(1)
     which = lax.axis_index("tensor").astype(jnp.int32).reshape(1)
     where = lax.axis_index(PLANE).astype(jnp.int32).reshape(1)
-    mod, gp_keep, gp_send, att, send, keep, unit = attend(
-        core, which, x, mod_shift, mod_scale, wt, q_gain[:, None], k_gain[:, None], own_patches, heads, hd
+    mod, gp_keep, gp_send, send, keep = attend(
+        core, which, x, affine, wt, q_gain[:, None], k_gain[:, None], own_patches, heads, hd
     )
     used = (3 * hw // 2 // ROWS) * (width // LANES)
     group = 8 * clips
     padded = -(-used // group) * group
     gp_other, mod_other = swap(gp_send, ("core",), 1), swap(mod, ("core",), 1)
+    recv = lax.ppermute(send, "tensor", [(0, 1), (1, 0)])
     own = sum_plane(outer(where, gp_keep, gp_other, mod, mod_other, padded))
-    own, send = lax.optimization_barrier((own, send))
-    recv = lax.ppermute(send, "tensor", [(0, 1), (1, 0)])
+    home = finish(which, recv, keep, width).reshape(frames, own_patches, width)
+    own, home = lax.optimization_barrier((own, home))
     own = exchange(own.reshape((clips, own.shape[0] // clips) + own.shape[1:]), "dp")
-    own, recv = lax.optimization_barrier((own, recv))
     own = reduce(own, 1.0 / math.sqrt(clips * frames * patches))
-    home = finish(which, recv, keep, unit, att, width).reshape(frames, own_patches, width)
+    pieces, home = ring(own, "dp", home)
     home = lax.all_to_all(home, SEQ, split_axis=0, concat_axis=0, tiled=True)
-    pieces, home = lax.optimization_barrier((ring(own, "dp"), home))
+    pieces, home = lax.optimization_barrier((pieces, home))
     grad_t, att_t = unpack(home.reshape(patches, width))
     have = place(lax.axis_index("dp").astype(jnp.int32).reshape(1), pieces)
     grad_qkv = gather_plane(have, where, core, 3 * hw, width)

time: 156 us -> 157 us (level)
  blocking collectives: 0 us -> 17.5 us
  starting transfers between devices: 65.9 us -> 57.4 us
  waiting for transfers between devices: 58.9 us -> 51.2 us
  local copies, waits for them, and re-layouts: 8.5 us -> 3.27 us
  Pallas kernels: 21.1 us -> 25 us
    all_to_all x0 -> x1, blocking collectives: none -> 17.5 us  [exchange(): return lax.all_to_all(parts, axis, split_axis=0, concat_axis=0, tiled=True)]
    all_to_all x1 -> x0, starting transfers between devices: 8.18 us -> none  [exchange(): return lax.all_to_all(parts, axis, split_axis=0, concat_axis=0, tiled=True)]
    unnamed x18 -> x6, local copies, waits for them, and re-layouts: 7.01 us -> 1.78 us
    ppermute x1, waiting for transfers between devices: 4.98 us -> 0.01 us  [body(): recv = lax.ppermute(send, 'tensor', [(0, 1), (1, 0)])]
    pallas_call x1, Pallas kernels: 11.7 us -> 14.2 us  [attend(): pl.pallas_call(functools.partial(attend_kernel, patches=patches, heads=he...]
    all_to_all x1 -> x0, waiting for transfers between devices: 1.91 us -> none  [exchange(): return lax.all_to_all(parts, axis, split_axis=0, concat_axis=0, tiled=True)]
  transfers between devices with their start and end apart: 37 -> 36, of which waited for: 20 -> 16; matrix products, arithmetic and copies ran while one was open for 1% -> 2% of each run, Pallas kernels for 1% -> 2%
where the time goes in v5:
time: 157 us; the launch traced here: 156 us
  starting transfers between devices  57.4 us (37%)
  waiting for transfers between devices  51.2 us (33%)
  Pallas kernels  25 us (16%)
  blocking collectives  17.5 us (11%)
  local copies, waits for them, and re-layouts  3.27 us (2%)
    ppermute x26, waiting for transfers between devices, swap(): return lax.ppermute(x, axes, [(i, i ^ k) for i in range(count)])  31 us
    ppermute x26, starting transfers between devices, swap(): return lax.ppermute(x, axes, [(i, i ^ k) for i in range(count)])  29.9 us
    all_to_all x1, blocking collectives, exchange(): return lax.all_to_all(parts, axis, split_axis=0, concat_axis=0, tiled=True)  17.5 us
    pallas_call x1, Pallas kernels, attend(): pl.pallas_call(functools.partial(attend_kernel, patches=patches, heads=he...  14.2 us
    all_to_all x1, waiting for transfers between devices, body(): lax.all_to_all(x, SEQ, split_axis=0, concat_axis=0, tiled=True)  11.5 us
    all_to_all x1, starting transfers between devices, body(): home = lax.all_to_all(home, SEQ, split_axis=0, concat_axis=0, tiled=True)  9.66 us
    ppermute x4, waiting for transfers between devices, ring(): up = lax.ppermute(up, axis, [(i, (i + 1) % count) for i in range(count)])  8.7 us
    ppermute x3, starting transfers between devices, ring(): lax.ppermute(down, axis, [(i, (i - 1) % count) for i in range(count)])  8.25 us
  transfers between devices with their start and end apart: 36, of which 16 were waited for; matrix products, arithmetic and copies ran while one was open for 2% of the time, Pallas kernels for 2%

profile of v5, /device:TPU:1, one launch (start us, length us, event | category | flops | bytes accessed | tf_op | source)
XLA Modules:
  0.0 156.5 jit_solution(6029720918681494290)
XLA Ops:
  0.6 2.2 %pack.1 = bf16[256,1728]{1,0:T(8,128)(2,1)} custom-call(bf16[256,1152]{1,0:T(8,128)(2,1)} %bitcast.33, bf16[576,256]{1,0:T(8,128)(2,1)} %bitcast.34), custom_call_target="tpu_custom_call" | custom-call | tf_op jit(solution)/shard_map/pack/pallas_call | solution.py:52
  2.9 6.9 %all-to-all-start = ((bf16[16,16,1728]{2,1,0:T(8,128)(2,1)}), bf16[16,16,1728]{2,1,0:T(8,128)(2,1)S(1)}, u32[]{:S(2)}, u32[]{:S(2)}) async-start(bf16[16,16,1728]{2,1,0:T(8,128)(2,1)} %bitcast.32), calls=%async_computation | async-start | bytes 1835008 | tf_op jit(solution)/shard_map/all_to_all | solution.py:535
  12.7 11.5 %all-to-all-done = bf16[16,16,1728]{2,1,0:T(8,128)(2,1)S(1)} async-done(((bf16[16,16,1728]{2,1,0:T(8,128)(2,1)}), bf16[16,16,1728]{2,1,0:T(8,128)(2,1)S(1)}, u32[]{:S(2)}, u32[]{:S(2)}) %all-to-all-start) | async-done | bytes 884768 | tf_op jit(solution)/shard_map/all_to_all | solution.py:535
  24.2 14.2 %attend.1 = (bf16[256,1152]{1,0:T(8,128)(2,1)S(1)}, bf16[864,256]{1,0:T(8,128)(2,1)S(1)}, bf16[864,256]{1,0:T(8,128)(2,1)}, bf16[256,640]{1,0:T(8,128)(2,1)S(1)}, f32[256,1920]{1,0:T(8,128)}) custom-call(s32[1]{0:T(128)} %bitcast.1.core_ref.half_ref, s32[1]{0:T(128)} %bitcast.2.which_ref, bf16[256,1728]{1,0:T(8,128)(2,1)S(1)} %bitcast.27, ...), custom_call_target="tpu_custom_call" | custom-call | tf_op jit(solution)/shard_map/attend/pallas_call | solution.py:234
  40.0 2.5 %collective-permute-done.gp_b = bf16[864,256]{1,0:T(8,128)(2,1)} collective-permute-done((bf16[864,256]{1,0:T(8,128)(2,1)}, bf16[864,256]{1,0:T(8,128)(2,1)}, u32[]{:S(2)}, u32[]{:S(2)}) %collective-permute-start) | collective-permute-done | bytes 442400 | tf_op jit(solution)/shard_map/ppermute | solution.py:481
  43.5 2.5 %outer.1 = (bf16[4,22,16,128]{3,2,1,0:T(8,128)(2,1)S(1)}, bf16[4,22,16,128]{3,2,1,0:T(8,128)(2,1)S(1)}, bf16[4,21,16,128]{3,2,1,0:T(8,128)(2,1)S(1)}, bf16[4,21,...) custom-call(s32[1]{0:T(128)} %bitcast.where_ref, ...), custom_call_target="tpu_custom_call" | custom-call | tf_op jit(solution)/shard_map/outer/pallas_call | solution.py:283
  47.9 2.4 %collective-permute-start.11 = (bf16[256,640]{1,0:T(8,128)(2,1)S(1)}, bf16[256,640]{1,0:T(8,128)(2,1)S(1)}, u32[]{:S(2)}, u32[]{:S(2)}) collective-permute-start(bf16[256,640]{1,0:T(8,128)(2,1)S(1)} %get-tuple-element.72), channel_id=1, source_target_pairs={{0,1},{1,0},{2,3},{3,2},{4,5},{5,4},{6,7},{7,6},{8,9},{9,8},{10,11... | collective-permute-start | bytes 983048 | tf_op jit(solution)/shard_map/ppermute | solution.py:547
  50.3 6.4 %collective-permute-done.3.refs_3_ = bf16[4,21,16,128]{3,2,1,0:T(8,128)(2,1)S(1)} collective-permute-done((bf16[4,21,16,128]{3,2,1,0:T(8,128)(2,1)S(1)}, bf16[4,21,16,128]{3,2,1,0:T(8,128)(2,1)S(1)}, u32[]{:S(2)}, u32[]{:S(2)}) %collective-permute-start.3) | collective-permute-done | bytes 344096 | tf_op jit(solution)/shard_map/ppermute | solution.py:481
  58.5 8.8 %collective-permute-done.6.refs_3_ = bf16[2,21,16,128]{3,2,1,0:T(8,128)(2,1)S(1)} collective-permute-done((bf16[2,21,16,128]{3,2,1,0:T(8,128)(2,1)S(1)}, bf16[2,21,16,128]{3,2,1,0:T(8,128)(2,1)S(1)}, u32[]{:S(2)}, u32[]{:S(2)}) %collective-permute-start.6) | collective-permute-done | bytes 172064 | tf_op jit(solution)/shard_map/ppermute | solution.py:481
  72.7 17.5 %all_to_all.15.parts_ref = bf16[8,8,16,128]{3,2,1,0:T(8,128)(2,1)S(1)} all-to-all(bf16[8,8,16,128]{3,2,1,0:T(8,128)(2,1)S(1)} %bitcast.29), channel_id=1, replica_groups=mesh['dp'=8,'xlo'=2,'y'=4,'core'=2,'tensor'=2] {'dp'}, dimensions={0} | all-to-all | bytes 524288 | tf_op jit(solution)/shard_map/all_to_all | solution.py:486
  90.4 2.5 %collective-permute-start.12 = (bf16[8,16,128]{2,1,0:T(8,128)(2,1)S(1)}, bf16[8,16,128]{2,1,0:T(8,128)(2,1)S(1)}, u32[]{:S(2)}, u32[]{:S(2)}) collective-permute-start(bf16[8,16,128]{2,1,0:T(8,128)(2,1)S(1)} %reduce.1.refs_0_), channel_id=1, source_target_pairs={{0,224},{32,0},{64,32},{96,64},{128,96},{160,128},{192,160},{224,1... | collective-permute-start | bytes 98312 | tf_op jit(solution)/shard_map/ppermute | solution.py:510
  93.0 1.8 %collective-permute-done.13.refs_7_ = bf16[8,16,128]{2,1,0:T(8,128)(2,1)S(1)} collective-permute-done((bf16[8,16,128]{2,1,0:T(8,128)(2,1)S(1)}, bf16[8,16,128]{2,1,0:T(8,128)(2,1)S(1)}, u32[]{:S(2)}, u32[]{:S(2)}) %collective-permute-start.13) | collective-permute-done | bytes 32800 | tf_op jit(solution)/shard_map/ppermute | solution.py:507
  94.8 9.7 %all-to-all-start.2 = ((bf16[16,16,1152]{2,1,0:T(8,128)(2,1)}), bf16[16,16,1152]{2,1,0:T(8,128)(2,1)S(1)}, u32[]{:S(2)}, u32[]{:S(2)}) async-start(bf16[16,16,1152]{2,1,0:T(8,128)(2,1)} %bitcast.12), calls=%async_computation.2 | async-start | bytes 1179648 | tf_op jit(solution)/shard_map/all_to_all | solution.py:554
  104.4 3.0 %collective-permute-start.14 = (bf16[8,16,128]{2,1,0:T(8,128)(2,1)S(1)}, bf16[8,16,128]{2,1,0:T(8,128)(2,1)S(1)}, u32[]{:S(2)}, u32[]{:S(2)}) collective-permute-start(bf16[8,16,128]{2,1,0:T(8,128)(2,1)S(1)} %collective-permute-done.12.refs_1_), channel_id=1, source_target_pairs={{0,224},{32,0},{64,32},{96,64},{128,96},{160,128},{192,160},{224,1... | collective-permute-start | bytes 98312 | tf_op jit(solution)/shard_map/ppermute | solution.py:510
  108.8 2.7 %collective-permute-start.15 = (bf16[8,16,128]{2,1,0:T(8,128)(2,1)S(1)}, bf16[8,16,128]{2,1,0:T(8,128)(2,1)S(1)}, u32[]{:S(2)}, u32[]{:S(2)}) collective-permute-start(bf16[8,16,128]{2,1,0:T(8,128)(2,1)S(1)} %collective-permute-done.14.refs_2_), channel_id=1, source_target_pairs={{0,224},{32,0},{64,32},{96,64},{128,96},{160,128},{192,160},{224,1... | collective-permute-start | bytes 98312 | tf_op jit(solution)/shard_map/ppermute | solution.py:510
  113.1 4.0 %collective-permute-done.18.refs_4_ = bf16[8,16,128]{2,1,0:T(8,128)(2,1)S(1)} collective-permute-done((bf16[8,16,128]{2,1,0:T(8,128)(2,1)S(1)}, bf16[8,16,128]{2,1,0:T(8,128)(2,1)S(1)}, u32[]{:S(2)}, u32[]{:S(2)}) %collective-permute-start.18) | collective-permute-done | bytes 32800 | tf_op jit(solution)/shard_map/ppermute | solution.py:507
  117.1 1.6 %collective-permute-start.19 = (bf16[1,22,16,128]{3,2,1,0:T(8,128)(2,1)S(1)}, bf16[1,22,16,128]{3,2,1,0:T(8,128)(2,1)S(1)}, u32[]{:S(2)}, u32[]{:S(2)}) collective-permute-start(bf16[1,22,16,128]{3,2,1,0:T(8,128)(2,1)S(1)} %get-tuple-element.90.refs_0_), channel_id=1, source_target_pairs={{0,16},{4,20},{8,24},{12,28},{16,0},{20,4},{24,8},{28,12},{1,17},{... | collective-permute-start | bytes 270344 | tf_op jit(solution)/shard_map/ppermute | solution.py:481
  122.1 2.2 %collective-permute-done.21.refs_5_ = bf16[1,21,16,128]{3,2,1,0:T(8,128)(2,1)S(1)} collective-permute-done((bf16[1,21,16,128]{3,2,1,0:T(8,128)(2,1)S(1)}, bf16[1,21,16,128]{3,2,1,0:T(8,128)(2,1)S(1)}, u32[]{:S(2)}, u32[]{:S(2)}) %collective-permute-start.21) | collective-permute-done | bytes 86048 | tf_op jit(solution)/shard_map/ppermute | solution.py:481
  124.3 1.9 %collective-permute-start.22 = (bf16[2,22,16,128]{3,2,1,0:T(8,128)(2,1)S(1)}, bf16[2,22,16,128]{3,2,1,0:T(8,128)(2,1)S(1)}, u32[]{:S(2)}, u32[]{:S(2)}) collective-permute-start(bf16[2,22,16,128]{3,2,1,0:T(8,128)(2,1)S(1)} %get-tuple-element.93.refs_0_), channel_id=1, source_target_pairs={{0,12},{4,8},{8,4},{12,0},{16,28},{20,24},{24,20},{28,16},{1,13},{... | collective-permute-start | bytes 540680 | tf_op jit(solution)/shard_map/ppermute | solution.py:481
  126.4 4.0 %collective-permute-done.23.refs_3_ = bf16[2,21,16,128]{3,2,1,0:T(8,128)(2,1)S(1)} collective-permute-done((bf16[2,21,16,128]{3,2,1,0:T(8,128)(2,1)S(1)}, bf16[2,21,16,128]{3,2,1,0:T(8,128)(2,1)S(1)}, u32[]{:S(2)}, u32[]{:S(2)}) %collective-permute-start.23) | collective-permute-done | bytes 172064 | tf_op jit(solution)/shard_map/ppermute | solution.py:481
  130.9 9.2 %collective-permute-start.29 = (bf16[4,21,16,128]{3,2,1,0:T(8,128)(2,1)S(1)}, bf16[4,21,16,128]{3,2,1,0:T(8,128)(2,1)S(1)}, u32[]{:S(2)}, u32[]{:S(2)}) collective-permute-start(bf16[4,21,16,128]{3,2,1,0:T(8,128)(2,1)S(1)} %get-tuple-element.97.refs_1_), channel_id=1, source_target_pairs={{0,2},{2,0},{1,3},{3,1},{4,6},{6,4},{5,7},{7,5},{8,10},{10,8},{9,1... | collective-permute-start | bytes 1032200 | tf_op jit(solution)/shard_map/ppermute | solution.py:481
  142.6 4.6 %collective-permute-start.31 = (bf16[4,22,16,128]{3,2,1,0:T(8,128)(2,1)S(1)}, bf16[4,22,16,128]{3,2,1,0:T(8,128)(2,1)S(1)}, u32[]{:S(2)}, u32[]{:S(2)}) collective-permute-start(bf16[4,22,16,128]{3,2,1,0:T(8,128)(2,1)S(1)} %collective-permute-done.25.refs_3_), channel_id=1, source_target_pairs={{0,2},{2,0},{1,3},{3,1},{4,6},{6,4},{5,7},{7,5},{8,10},{10,8},{9,1... | collective-permute-start | bytes 1081352 | tf_op jit(solution)/shard_map/ppermute | solution.py:481
  147.3 3.7 %collective-permute-done.26.refs_4_ = bf16[4,21,16,128]{3,2,1,0:T(8,128)(2,1)S(1)} collective-permute-done((bf16[4,21,16,128]{3,2,1,0:T(8,128)(2,1)S(1)}, bf16[4,21,16,128]{3,2,1,0:T(8,128)(2,1)S(1)}, u32[]{:S(2)}, u32[]{:S(2)}) %collective-permute-start.26) | collective-permute-done | bytes 344096 | tf_op jit(solution)/shard_map/ppermute | solution.py:481
  153.6 2.9 %untile.1 = bf16[1728,1152]{1,0:T(8,128)(2,1)} custom-call(s32[1]{0:T(128)} %bitcast.where_ref, s32[1]{0:T(128)} %bitcast.1.core_ref.half_ref, bf16[4,22,16,128]{3,2,1,0:T(8,128)(2,1)S(1)} %get-tuple-element.96.refs_0_, bf16[4,21,16,128]{3,2,1,0:T(8,128)(2,1)S(1)} %get-tuple-element.97.refs_1_, bf16[4,21,16,128]{3,2,1,0:T(8,128)(2,1)S(1)} %get-tuple-element.98.refs_2_, ...), custom_call_target="tpu_custom_call" | custom-call | tf_op jit(solution)/shard_map/untile/pallas_call | solution.py:469
  (72 shorter events, 27.0 us)
Async XLA Ops:
  2.9 21.3 %all-to-all-start = ((bf16[16,16,1728]{2,1,0:T(8,128)(2,1)}), bf16[16,16,1728]{2,1,0:T(8,128)(2,1)S(1)}, u32[]{:S(2)}, u32[]{:S(2)}) async-start(bf16[16,16,1728]{2,1,0:T(8,128)(2,1)} %bitcast.32), calls=%async_computation | async-start | bytes 1835008 | tf_op jit(solution)/shard_map/all_to_all | solution.py:535
  46.0 10.7 %collective-permute-start.2 = (bf16[4,22,16,128]{3,2,1,0:T(8,128)(2,1)S(1)}, bf16[4,22,16,128]{3,2,1,0:T(8,128)(2,1)S(1)}, u32[]{:S(2)}, u32[]{:S(2)}) collective-permute-start(bf16[4,22,16,128]{3,2,1,0:T(8,128)(2,1)S(1)} %get-tuple-element.55), channel_id=1, source_target_pairs={{0,4},{4,0},{8,12},{12,8},{16,20},{20,16},{24,28},{28,24},{1,5},{5... | collective-permute-start | bytes 1081352 | tf_op jit(solution)/shard_map/ppermute | solution.py:481
  46.1 10.6 %collective-permute-start.3 = (bf16[4,21,16,128]{3,2,1,0:T(8,128)(2,1)S(1)}, bf16[4,21,16,128]{3,2,1,0:T(8,128)(2,1)S(1)}, u32[]{:S(2)}, u32[]{:S(2)}) collective-permute-start(bf16[4,21,16,128]{3,2,1,0:T(8,128)(2,1)S(1)} %get-tuple-element.57), channel_id=1, source_target_pairs={{0,12},{4,8},{8,4},{12,0},{16,28},{20,24},{24,20},{28,16},{1,13},{... | collective-permute-start | bytes 1032200 | tf_op jit(solution)/shard_map/ppermute | solution.py:481
  47.4 9.2 %collective-permute-start.4 = (bf16[4,21,16,128]{3,2,1,0:T(8,128)(2,1)S(1)}, bf16[4,21,16,128]{3,2,1,0:T(8,128)(2,1)S(1)}, u32[]{:S(2)}, u32[]{:S(2)}) collective-permute-start(bf16[4,21,16,128]{3,2,1,0:T(8,128)(2,1)S(1)} %get-tuple-element.59), channel_id=1, source_target_pairs={{0,16},{4,20},{8,24},{12,28},{16,0},{20,4},{24,8},{28,12},{1,17},{... | collective-permute-start | bytes 1032200 | tf_op jit(solution)/shard_map/ppermute | solution.py:481
  47.9 21.6 %collective-permute-start.11 = (bf16[256,640]{1,0:T(8,128)(2,1)S(1)}, bf16[256,640]{1,0:T(8,128)(2,1)S(1)}, u32[]{:S(2)}, u32[]{:S(2)}) collective-permute-start(bf16[256,640]{1,0:T(8,128)(2,1)S(1)} %get-tuple-element.72), channel_id=1, source_target_pairs={{0,1},{1,0},{2,3},{3,2},{4,5},{5,4},{6,7},{7,6},{8,9},{9,8},{10,11... | collective-permute-start | bytes 983048 | tf_op jit(solution)/shard_map/ppermute | solution.py:547
  56.9 10.4 %collective-permute-start.5 = (bf16[2,22,16,128]{3,2,1,0:T(8,128)(2,1)S(1)}, bf16[2,22,16,128]{3,2,1,0:T(8,128)(2,1)S(1)}, u32[]{:S(2)}, u32[]{:S(2)}) collective-permute-start(bf16[2,22,16,128]{3,2,1,0:T(8,128)(2,1)S(1)} %get-tuple-element.61), channel_id=1, source_target_pairs={{0,12},{4,8},{8,4},{12,0},{16,28},{20,24},{24,20},{28,16},{1,13},{... | collective-permute-start | bytes 540680 | tf_op jit(solution)/shard_map/ppermute | solution.py:481
  58.5 8.8 %collective-permute-start.6 = (bf16[2,21,16,128]{3,2,1,0:T(8,128)(2,1)S(1)}, bf16[2,21,16,128]{3,2,1,0:T(8,128)(2,1)S(1)}, u32[]{:S(2)}, u32[]{:S(2)}) collective-permute-start(bf16[2,21,16,128]{3,2,1,0:T(8,128)(2,1)S(1)} %get-tuple-element.63), channel_id=1, source_target_pairs={{0,16},{4,20},{8,24},{12,28},{16,0},{20,4},{24,8},{28,12},{1,17},{... | collective-permute-start | bytes 516104 | tf_op jit(solution)/shard_map/ppermute | solution.py:481
  58.5 8.8 %collective-permute-start.7 = (bf16[2,21,16,128]{3,2,1,0:T(8,128)(2,1)S(1)}, bf16[2,21,16,128]{3,2,1,0:T(8,128)(2,1)S(1)}, u32[]{:S(2)}, u32[]{:S(2)}) collective-permute-start(bf16[2,21,16,128]{3,2,1,0:T(8,128)(2,1)S(1)} %get-tuple-element.65), channel_id=1, source_target_pairs={{0,4},{4,0},{8,12},{12,8},{16,20},{20,16},{24,28},{28,24},{1,5},{5... | collective-permute-start | bytes 516104 | tf_op jit(solution)/shard_map/ppermute | solution.py:481
  67.4 5.2 %collective-permute-start.8 = (bf16[1,22,16,128]{3,2,1,0:T(8,128)(2,1)S(1)}, bf16[1,22,16,128]{3,2,1,0:T(8,128)(2,1)S(1)}, u32[]{:S(2)}, u32[]{:S(2)}) collective-permute-start(bf16[1,22,16,128]{3,2,1,0:T(8,128)(2,1)S(1)} %get-tuple-element.67), channel_id=1, source_target_pairs={{0,16},{4,20},{8,24},{12,28},{16,0},{20,4},{24,8},{28,12},{1,17},{... | collective-permute-start | bytes 270344 | tf_op jit(solution)/shard_map/ppermute | solution.py:481
  68.1 4.5 %collective-permute-start.10 = (bf16[1,21,16,128]{3,2,1,0:T(8,128)(2,1)S(1)}, bf16[1,21,16,128]{3,2,1,0:T(8,128)(2,1)S(1)}, u32[]{:S(2)}, u32[]{:S(2)}) collective-permute-start(bf16[1,21,16,128]{3,2,1,0:T(8,128)(2,1)S(1)} %get-tuple-element.71), channel_id=1, source_target_pairs={{0,12},{4,8},{8,4},{12,0},{16,28},{20,24},{24,20},{28,16},{1,13},{... | collective-permute-start | bytes 258056 | tf_op jit(solution)/shard_map/ppermute | solution.py:481
  90.2 4.5 %collective-permute-start.13 = (bf16[8,16,128]{2,1,0:T(8,128)(2,1)S(1)}, bf16[8,16,128]{2,1,0:T(8,128)(2,1)S(1)}, u32[]{:S(2)}, u32[]{:S(2)}) collective-permute-start(bf16[8,16,128]{2,1,0:T(8,128)(2,1)S(1)} %reduce.1.refs_0_), channel_id=1, source_target_pairs={{0,32},{32,64},{64,96},{96,128},{128,160},{160,192},{192,224},{224... | collective-permute-start | bytes 98312 | tf_op jit(solution)/shard_map/ppermute | solution.py:507
  94.8 22.3 %all-to-all-start.2 = ((bf16[16,16,1152]{2,1,0:T(8,128)(2,1)}), bf16[16,16,1152]{2,1,0:T(8,128)(2,1)S(1)}, u32[]{:S(2)}, u32[]{:S(2)}) async-start(bf16[16,16,1152]{2,1,0:T(8,128)(2,1)} %bitcast.12), calls=%async_computation.2 | async-start | bytes 1179648 | tf_op jit(solution)/shard_map/all_to_all | solution.py:554
  104.4 4.4 %collective-permute-start.16 = (bf16[8,16,128]{2,1,0:T(8,128)(2,1)S(1)}, bf16[8,16,128]{2,1,0:T(8,128)(2,1)S(1)}, u32[]{:S(2)}, u32[]{:S(2)}) collective-permute-start(bf16[8,16,128]{2,1,0:T(8,128)(2,1)S(1)} %collective-permute-done.13.refs_7_), channel_id=1, source_target_pairs={{0,32},{32,64},{64,96},{96,128},{128,160},{160,192},{192,224},{224... | collective-permute-start | bytes 98312 | tf_op jit(solution)/shard_map/ppermute | solution.py:507
  104.4 4.4 %collective-permute-start.14 = (bf16[8,16,128]{2,1,0:T(8,128)(2,1)S(1)}, bf16[8,16,128]{2,1,0:T(8,128)(2,1)S(1)}, u32[]{:S(2)}, u32[]{:S(2)}) collective-permute-start(bf16[8,16,128]{2,1,0:T(8,128)(2,1)S(1)} %collective-permute-done.12.refs_1_), channel_id=1, source_target_pairs={{0,224},{32,0},{64,32},{96,64},{128,96},{160,128},{192,160},{224,1... | collective-permute-start | bytes 98312 | tf_op jit(solution)/shard_map/ppermute | solution.py:510
  117.1 7.2 %collective-permute-start.19 = (bf16[1,22,16,128]{3,2,1,0:T(8,128)(2,1)S(1)}, bf16[1,22,16,128]{3,2,1,0:T(8,128)(2,1)S(1)}, u32[]{:S(2)}, u32[]{:S(2)}) collective-permute-start(bf16[1,22,16,128]{3,2,1,0:T(8,128)(2,1)S(1)} %get-tuple-element.90.refs_0_), channel_id=1, source_target_pairs={{0,16},{4,20},{8,24},{12,28},{16,0},{20,4},{24,8},{28,12},{1,17},{... | collective-permute-start | bytes 270344 | tf_op jit(solution)/shard_map/ppermute | solution.py:481
  119.7 4.5 %collective-permute-start.21 = (bf16[1,21,16,128]{3,2,1,0:T(8,128)(2,1)S(1)}, bf16[1,21,16,128]{3,2,1,0:T(8,128)(2,1)S(1)}, u32[]{:S(2)}, u32[]{:S(2)}) collective-permute-start(bf16[1,21,16,128]{3,2,1,0:T(8,128)(2,1)S(1)} %get-tuple-element.92.refs_4_), channel_id=1, source_target_pairs={{0,12},{4,8},{8,4},{12,0},{16,28},{20,24},{24,20},{28,16},{1,13},{... | collective-permute-start | bytes 258056 | tf_op jit(solution)/shard_map/ppermute | solution.py:481
  124.3 6.4 %collective-permute-start.22 = (bf16[2,22,16,128]{3,2,1,0:T(8,128)(2,1)S(1)}, bf16[2,22,16,128]{3,2,1,0:T(8,128)(2,1)S(1)}, u32[]{:S(2)}, u32[]{:S(2)}) collective-permute-start(bf16[2,22,16,128]{3,2,1,0:T(8,128)(2,1)S(1)} %get-tuple-element.93.refs_0_), channel_id=1, source_target_pairs={{0,12},{4,8},{8,4},{12,0},{16,28},{20,24},{24,20},{28,16},{1,13},{... | collective-permute-start | bytes 540680 | tf_op jit(solution)/shard_map/ppermute | solution.py:481
  130.8 11.9 %collective-permute-start.25 = (bf16[4,22,16,128]{3,2,1,0:T(8,128)(2,1)S(1)}, bf16[4,22,16,128]{3,2,1,0:T(8,128)(2,1)S(1)}, u32[]{:S(2)}, u32[]{:S(2)}) collective-permute-start(bf16[4,22,16,128]{3,2,1,0:T(8,128)(2,1)S(1)} %get-tuple-element.96.refs_0_), channel_id=1, source_target_pairs={{0,4},{4,0},{8,12},{12,8},{16,20},{20,16},{24,28},{28,24},{1,5},{5... | collective-permute-start | bytes 1081352 | tf_op jit(solution)/shard_map/ppermute | solution.py:481
  130.9 16.4 %collective-permute-start.29 = (bf16[4,21,16,128]{3,2,1,0:T(8,128)(2,1)S(1)}, bf16[4,21,16,128]{3,2,1,0:T(8,128)(2,1)S(1)}, u32[]{:S(2)}, u32[]{:S(2)}) collective-permute-start(bf16[4,21,16,128]{3,2,1,0:T(8,128)(2,1)S(1)} %get-tuple-element.97.refs_1_), channel_id=1, source_target_pairs={{0,2},{2,0},{1,3},{3,1},{4,6},{6,4},{5,7},{7,5},{8,10},{10,8},{9,1... | collective-permute-start | bytes 1032200 | tf_op jit(solution)/shard_map/ppermute | solution.py:481
  140.1 10.9 %collective-permute-start.26 = (bf16[4,21,16,128]{3,2,1,0:T(8,128)(2,1)S(1)}, bf16[4,21,16,128]{3,2,1,0:T(8,128)(2,1)S(1)}, u32[]{:S(2)}, u32[]{:S(2)}) collective-permute-start(bf16[4,21,16,128]{3,2,1,0:T(8,128)(2,1)S(1)} %get-tuple-element.97.refs_1_), channel_id=1, source_target_pairs={{0,12},{4,8},{8,4},{12,0},{16,28},{20,24},{24,20},{28,16},{1,13},{... | collective-permute-start | bytes 1032200 | tf_op jit(solution)/shard_map/ppermute | solution.py:481
  141.0 10.8 %collective-permute-start.27 = (bf16[4,21,16,128]{3,2,1,0:T(8,128)(2,1)S(1)}, bf16[4,21,16,128]{3,2,1,0:T(8,128)(2,1)S(1)}, u32[]{:S(2)}, u32[]{:S(2)}) collective-permute-start(bf16[4,21,16,128]{3,2,1,0:T(8,128)(2,1)S(1)} %get-tuple-element.98.refs_2_), channel_id=1, source_target_pairs={{0,16},{4,20},{8,24},{12,28},{16,0},{20,4},{24,8},{28,12},{1,17},{... | collective-permute-start | bytes 1032200 | tf_op jit(solution)/shard_map/ppermute | solution.py:481
  142.0 10.8 %collective-permute-start.28 = (bf16[4,22,16,128]{3,2,1,0:T(8,128)(2,1)S(1)}, bf16[4,22,16,128]{3,2,1,0:T(8,128)(2,1)S(1)}, u32[]{:S(2)}, u32[]{:S(2)}) collective-permute-start(bf16[4,22,16,128]{3,2,1,0:T(8,128)(2,1)S(1)} %get-tuple-element.96.refs_0_), channel_id=1, source_target_pairs={{0,2},{2,0},{1,3},{3,1},{4,6},{6,4},{5,7},{7,5},{8,10},{10,8},{9,1... | collective-permute-start | bytes 1081352 | tf_op jit(solution)/shard_map/ppermute | solution.py:481
  142.6 10.9 %collective-permute-start.31 = (bf16[4,22,16,128]{3,2,1,0:T(8,128)(2,1)S(1)}, bf16[4,22,16,128]{3,2,1,0:T(8,128)(2,1)S(1)}, u32[]{:S(2)}, u32[]{:S(2)}) collective-permute-start(bf16[4,22,16,128]{3,2,1,0:T(8,128)(2,1)S(1)} %collective-permute-done.25.refs_3_), channel_id=1, source_target_pairs={{0,2},{2,0},{1,3},{3,1},{4,6},{6,4},{5,7},{7,5},{8,10},{10,8},{9,1... | collective-permute-start | bytes 1081352 | tf_op jit(solution)/shard_map/ppermute | solution.py:481
  147.3 5.6 %collective-permute-start.30 = (bf16[4,21,16,128]{3,2,1,0:T(8,128)(2,1)S(1)}, bf16[4,21,16,128]{3,2,1,0:T(8,128)(2,1)S(1)}, u32[]{:S(2)}, u32[]{:S(2)}) collective-permute-start(bf16[4,21,16,128]{3,2,1,0:T(8,128)(2,1)S(1)} %get-tuple-element.98.refs_2_), channel_id=1, source_target_pairs={{0,2},{2,0},{1,3},{3,1},{4,6},{6,4},{5,7},{7,5},{8,10},{10,8},{9,1... | collective-permute-start | bytes 1032200 | tf_op jit(solution)/shard_map/ppermute | solution.py:481
  (15 other events, 74.0 us)

commit v6 on v5

--- a/solution.py
+++ b/solution.py
@@ -93,107 +93,161 @@
     return centred * inverse, inverse
 
 
-def attend_kernel(core_ref, which_ref, x_hbm, affine_hbm, wt_hbm, qg_ref, kg_ref,
-                  mod_ref, gp_keep_ref, gp_send_ref, send_hbm, keep_hbm,
-                  x_ref, affine_ref, wt_s, gp_s, ot_s, rows_s, send_ref, keep_ref,
-                  in_sems, out_sems, *, patches, heads, hd):
+def attend_kernel(core_ref, x_ref, affine_ref, wt_hbm, qg_ref, kg_ref,
+                  mod_ref, gp_keep_ref, gp_send_ref, att_ref,
+                  wt_s, rows_s, weights_s, w_s, grad_s, q_s, k_s, v_s, cot_s, sems, *, patches, heads, hd):
     tokens, _ = x_ref.shape
     width = affine_ref.shape[1]
     hw = heads * hd
     parts = [pl.ds(part * hw, hw) for part in range(3)]
-    copies = fetch(
-        [(x_hbm, x_ref), (affine_hbm, affine_ref)]
-        + [(wt_hbm.at[rows], wt_s.at[rows]) for rows in parts],
-        in_sems,
-    )
-    for copy in copies[:2]:
-        copy.wait()
-    unit, inverse = unit_of(x_ref[:, :width].astype(F32))
-    half = width // 2
-    win = send_ref.shape[1]
-    mine_low = which_ref[0] == 0
-    keep_ref[:, win : 2 * win] = jnp.where(mine_low, unit[:, :win], unit[:, width - win :])
-    factor = affine_ref[1:2]
-    mod_ref[...] = (unit * factor + affine_ref[0:1]).astype(BF)
+    copies = fetch([(wt_hbm.at[rows], wt_s.at[rows]) for rows in parts], sems)
+    unit, _ = unit_of(x_ref[:, :width].astype(F32))
+    mod_ref[...] = (unit * affine_ref[1:2] + affine_ref[0:1]).astype(BF)
     mod = mod_ref[...]
     ident = eye(tokens)
-    cot_t = mm(eye(hw), x_ref[:, width:], NT)
+    for start in range(0, hw, tokens):
+        size = min(tokens, hw - start)
+        block = x_ref[:, width + start : width + start + size]
+        cot_s[start : start + size, :] = mm(ident[:size, :size], block, NT)
 
     def project(part):
-        copies[2 + part].wait()
-        rows = mm(wt_s[part * hw : (part + 1) * hw, :], mod, NT)
-        return rows.astype(BF).astype(F32)
+        copies[part].wait()
+        return mm(wt_s[part * hw : (part + 1) * hw, :], mod, NT).astype(BF).astype(F32)
 
     def norm(rows):
         inv = lax.rsqrt(jnp.sum(rows * rows, axis=0, keepdims=True) * (1.0 / hd) + EPS)
         return rows * inv, inv
+
+    def back(hat, inv, gain, grad):
+        weighted = grad * gain
+        mean = jnp.sum(hat * weighted, axis=0, keepdims=True) * (1.0 / hd)
+        return inv * (weighted - hat * mean)
+
+    def put(part, h, rows):
+        start = part * hw + h * hd
+        rows_s[start : start + hd, :] = rows
 
     root = 1.0 / math.sqrt(hd)
     q_gain = qg_ref[...] * (root * LOG2E)
     k_gain = kg_ref[...]
     q_back = qg_ref[...] * root
     k_back = kg_ref[...] * (1.0 / LOG2E)
-    q_all, k_all, v_all = project(0), project(1), project(2)
+    each = [slice(h * hd, (h + 1) * hd) for h in range(heads)]
 
     spot = lax.broadcasted_iota(jnp.int32, (patches, tokens), 0)
     token = lax.broadcasted_iota(jnp.int32, (patches, tokens), 1)
     spots = jnp.where(lax.rem(token, patches) == spot, 16.0, 0.0)
     top = lax.broadcasted_iota(jnp.int32, (8, tokens), 0) == 0
-    spare = -(hd + patches + 8) % LANES
-    zeros = jnp.zeros((spare, tokens), F32)
+    zeros = jnp.zeros((-(hd + patches + 8) % LANES, tokens), F32)
     q_tail = [spots, jnp.where(top, 16.0, 0.0), zeros]
     k_tail = [spots, jnp.where(top, -16.0, 0.0), zeros]
-    ones = jnp.where(top, 1.0, 0.0)
+    v_tail = [jnp.where(top, 1.0, 0.0), jnp.zeros((-(hd + 8) % LANES, tokens), F32)]
     blank = jnp.zeros((-hd % LANES, tokens), F32)
 
-    def back(hat, inv, gain, grad):
-        weighted = grad * gain
-        mean = jnp.sum(hat * weighted, axis=0, keepdims=True) * (1.0 / hd)
-        return inv * (weighted - hat * mean)
-
-    def put(part, h, rows):
-        start = part * hw + h * hd
-        rows_s[start : start + hd, :] = rows
-
-    for pair in range(heads // 2):
-        hats, tall = [], []
-        for h in (2 * pair, 2 * pair + 1):
-            at = slice(h * hd, (h + 1) * hd)
-            hats.append((norm(q_all[at]), norm(k_all[at])))
-            kn = hats[-1][1][0] * k_gain
-            tall.append((jnp.concatenate([kn] + k_tail), jnp.concatenate([v_all[at], blank])))
-        k_rows = mm(ident, jnp.concatenate([t[0] for t in tall]).astype(BF), NT).astype(BF)
-        v_rows = mm(ident, jnp.concatenate([t[1] for t in tall]).astype(BF), NT).astype(BF)
-        for i, h in enumerate((2 * pair, 2 * pair + 1)):
-            at = slice(h * hd, (h + 1) * hd)
-            lanes = slice(i * LANES, (i + 1) * LANES)
-            (q_hat, q_inv), (k_hat, k_inv) = hats[i]
-            q_b = jnp.concatenate([q_hat * q_gain] + q_tail).astype(BF)
-            k_b = (k_hat * k_gain).astype(BF)
-            weights = jnp.exp2(mm(k_rows[:, lanes], q_b, NN))
-            w_b = weights.astype(BF)
-            v_b = jnp.concatenate([v_all[at], ones]).astype(BF)
-            summed = mm(v_b, w_b, NN)
-            share = 1.0 / summed[hd : hd + 1]
-            out = summed[:hd] * share
-            ot_s[at, :] = out
-            cot = cot_t[at]
-            cot_share = cot * share
-            cot_b = jnp.concatenate([cot_share, blank]).astype(BF)
-            delta = jnp.sum(out * cot_share, axis=0, keepdims=True)
-            grad_s = (weights * (mm(v_rows[:, lanes], cot_b, NN) - delta)).astype(BF)
-            put(2, h, mm(cot_b, w_b, NT)[:hd])
-            put(0, h, back(q_hat, q_inv, q_back, mm(k_b, grad_s, NN)))
-            put(1, h, back(k_hat, k_inv, k_back, mm(q_b, grad_s, NT)[:hd]))
-
+    def rows_of(ref):
+        found = []
+        for h in range(0, heads, 2):
+            both = mm(ident, ref[h : h + 2].reshape(2 * LANES, tokens), NT).astype(BF)
+            found += [both[:, :LANES], both[:, LANES:]]
+        return found
+
+    q_all = project(0)
+    q_inv = []
+    for h, at in enumerate(each):
+        hat, inv = norm(q_all[at])
+        q_inv.append(inv)
+        q_s[h] = jnp.concatenate([hat * q_gain] + q_tail).astype(BF)
+    k_all = project(1)
+    k_inv = []
+    for h, at in enumerate(each):
+        hat, inv = norm(k_all[at])
+        k_inv.append(inv)
+        k_s[h] = jnp.concatenate([hat * k_gain] + k_tail).astype(BF)
+    v_all = project(2)
+    for h, at in enumerate(each):
+        v_s[h] = jnp.concatenate([v_all[at]] + v_tail).astype(BF)
+    k_rows = rows_of(k_s)
+    for h in range(heads):
+        weights = jnp.exp2(mm(k_rows[h], q_s[h], NN))
+        weights_s[h] = weights
+        w_s[h] = weights.astype(BF)
+    v_rows = rows_of(v_s)
+    deltas, cots = [], []
+    for h, at in enumerate(each):
+        summed = mm(v_s[h], w_s[h], NN)
+        share = 1.0 / summed[hd : hd + 1]
+        out = summed[:hd] * share
+        att_ref[at, :] = out.astype(BF)
+        cot_share = cot_s[at, :] * share
+        cots.append(jnp.concatenate([cot_share, blank]).astype(BF))
+        deltas.append(jnp.sum(out * cot_share, axis=0, keepdims=True))
+    for h in range(heads):
+        grad_s[h] = (weights_s[h] * (mm(v_rows[h], cots[h], NN) - deltas[h])).astype(BF)
+        put(2, h, mm(cots[h], w_s[h], NT)[:hd])
+    for h, at in enumerate(each):
+        put(0, h, back(q_all[at] * q_inv[h], q_inv[h], q_back, mm(k_s[h], grad_s[h], NN)[:hd]))
+        put(1, h, back(k_all[at] * k_inv[h], k_inv[h], k_back, mm(q_s[h], grad_s[h], NT)[:hd]))
+    size = gp_keep_ref.shape[0]
+    gp_keep_ref[...] = rows_s[pl.ds(pl.multiple_of(core_ref[0] * size, ROWS), size), :].astype(BF)
+    gp_send_ref[...] = rows_s[pl.ds(pl.multiple_of((1 - core_ref[0]) * size, ROWS), size), :].astype(BF)
+
+
+def attend(core, x, affine, wt, qg, kg, patches, heads, hd):
+    tokens = x.shape[0]
+    width = wt.shape[1]
+    hw = heads * hd
+    smem = pl.BlockSpec(memory_space=pltpu.SMEM)
+    vmem = pl.BlockSpec(memory_space=pltpu.VMEM)
+    half = jax.ShapeDtypeStruct((3 * hw // 2, tokens), BF)
+    tall = pltpu.VMEM((heads, LANES, tokens), BF)
+    return pl.pallas_call(
+        functools.partial(attend_kernel, patches=patches, heads=heads, hd=hd),
+        in_specs=[smem, vmem, vmem, pl.BlockSpec(memory_space=pltpu.HBM), vmem, vmem],
+        out_shape=(
+            jax.ShapeDtypeStruct((tokens, width), BF),
+            half,
+            half,
+            jax.ShapeDtypeStruct((hw, tokens), BF),
+        ),
+        scratch_shapes=[
+            pltpu.VMEM((3 * hw, width), BF),
+            pltpu.VMEM((3 * hw, tokens), F32),
+            pltpu.VMEM((heads, tokens, tokens), F32),
+            pltpu.VMEM((heads, tokens, tokens), BF),
+            pltpu.VMEM((heads, tokens, tokens), BF),
+            tall,
+            tall,
+            tall,
+            pltpu.VMEM((hw, tokens), F32),
+            pltpu.SemaphoreType.DMA((3,)),
+        ],
+        compiler_params=pltpu.CompilerParams(vmem_limit_bytes=50 * 2**20),
+        name="attend",
+    )(core, x, affine, wt, qg, kg)
+
+
+def split_kernel(core_ref, which_ref, x_ref, affine_ref, wt_hbm, gp_keep_ref, gp_send_ref, att_ref,
+                 send_ref, keep_ref, wt_s, gp_s, sems):
+    tokens, _ = x_ref.shape
+    width = affine_ref.shape[1]
+    hw = att_ref.shape[0]
+    parts = [pl.ds(part * hw, hw) for part in range(3)]
+    copies = fetch([(wt_hbm.at[rows], wt_s.at[rows]) for rows in parts], sems)
+    unit, inverse = unit_of(x_ref[:, :width].astype(F32))
+    ident = eye(tokens)
+    size = gp_keep_ref.shape[0]
+    gp_s[pl.ds(pl.multiple_of(core_ref[0] * size, ROWS), size), :] = gp_keep_ref[...]
+    gp_s[pl.ds(pl.multiple_of((1 - core_ref[0]) * size, ROWS), size), :] = gp_send_ref[...]
     grad = jnp.zeros((tokens, width), F32)
-    size = gp_keep_ref.shape[0]
     for part in range(3):
         at = slice(part * hw, (part + 1) * hw)
-        block = rows_s[at, :].astype(BF)
-        gp_s[at, :] = block
-        grad = grad + mm(mm(ident, block, NT).astype(BF), wt_s[at, :], NN)
-    scaled = grad * factor
+        rows = mm(ident, gp_s[at, :], NT).astype(BF)
+        copies[part].wait()
+        grad = grad + mm(rows, wt_s[at, :], NN)
+    half = width // 2
+    win = send_ref.shape[1]
+    mine_low = which_ref[0] == 0
+    scaled = grad * affine_ref[1:2]
     first = jnp.sum(scaled, axis=1, keepdims=True)
     second = jnp.sum(scaled * unit, axis=1, keepdims=True)
     col = lax.broadcasted_iota(jnp.int32, (tokens, win), 1)
@@ -210,46 +264,31 @@
         keep = jnp.where(col == here + place, term, keep)
     send_ref[...] = send.astype(BF)
     keep_ref[:, :win] = keep
-    outs = []
-    keep_ref[:, 2 * win : 2 * win + hw] = mm(ident, ot_s[...].astype(BF), NT)
-    for i, (src, dst) in enumerate(((send_ref, send_hbm), (keep_ref, keep_hbm))):
-        outs.append(pltpu.make_async_copy(src, dst, out_sems.at[i]))
-        outs[-1].start()
-    gp_keep_ref[...] = gp_s[pl.ds(pl.multiple_of(core_ref[0] * size, ROWS), size), :]
-    gp_send_ref[...] = gp_s[pl.ds(pl.multiple_of((1 - core_ref[0]) * size, ROWS), size), :]
-    for out in outs:
-        out.wait()
-
-
-def attend(core, which, x, affine, wt, qg, kg, patches, heads, hd):
+    keep_ref[:, win : 2 * win] = jnp.where(mine_low, unit[:, :win], unit[:, width - win :])
+    keep_ref[:, 2 * win : 2 * win + hw] = mm(ident, att_ref[...], NT)
+
+
+def split(core, which, x, affine, wt, gp_keep, gp_send, att):
     tokens = x.shape[0]
-    width = wt.shape[1]
-    hw = heads * hd
-    win = window_of(width // 2)
+    hw = att.shape[0]
+    win = window_of(wt.shape[1] // 2)
     smem = pl.BlockSpec(memory_space=pltpu.SMEM)
     vmem = pl.BlockSpec(memory_space=pltpu.VMEM)
-    hbm = pl.BlockSpec(memory_space=pltpu.HBM)
-    outs = [((tokens, win), BF), ((tokens, 2 * win + window_of(hw)), F32)]
-    half = jax.ShapeDtypeStruct((3 * hw // 2, tokens), BF)
-    return pl.pallas_call(
-        functools.partial(attend_kernel, patches=patches, heads=heads, hd=hd),
-        in_specs=[smem, smem] + [hbm] * 3 + [vmem, vmem],
-        out_specs=(vmem,) * 3 + (hbm,) * 2,
-        out_shape=(jax.ShapeDtypeStruct((tokens, width), BF), half, half)
-        + tuple(jax.ShapeDtypeStruct(*out) for out in outs),
+    return pl.pallas_call(
+        split_kernel,
+        in_specs=[smem, smem, vmem, vmem, pl.BlockSpec(memory_space=pltpu.HBM), vmem, vmem, vmem],
+        out_shape=(
+            jax.ShapeDtypeStruct((tokens, win), BF),
+            jax.ShapeDtypeStruct((tokens, 2 * win + window_of(hw)), F32),
+        ),
         scratch_shapes=[
-            pltpu.VMEM(x.shape, BF),
-            pltpu.VMEM(affine.shape, F32),
-            pltpu.VMEM((3 * hw, width), BF),
-            pltpu.VMEM((3 * hw, tokens), BF),
-            pltpu.VMEM((hw, tokens), F32),
-            pltpu.VMEM((3 * hw, tokens), F32),
-        ]
-        + [pltpu.VMEM(*out) for out in outs]
-        + [pltpu.SemaphoreType.DMA((5,)), pltpu.SemaphoreType.DMA((2,))],
-        compiler_params=pltpu.CompilerParams(vmem_limit_bytes=50 * 2**20),
-        name="attend",
-    )(core, which, x, affine, wt, qg, kg)
+            pltpu.VMEM(wt.shape, BF),
+            pltpu.VMEM((wt.shape[0], tokens), BF),
+            pltpu.SemaphoreType.DMA((3,)),
+        ],
+        compiler_params=pltpu.CompilerParams(vmem_limit_bytes=18 * 2**20),
+        name="split",
+    )(core, which, x, affine, wt, gp_keep, gp_send, att)
 
 
 def outer_kernel(where_ref, gp_a, gp_b, mod_a, mod_b, *refs):
@@ -267,11 +306,12 @@
             j = (start + at) // LANES
             tiles_s[j * tiles : (j + 1) * tiles] = found[:, at : at + LANES].reshape(tiles, ROWS, LANES)
     size = tiles_s.shape[0] // 8
-    for (lo, hi), order, send_ref, keep_ref in zip(bounds(size), ORDERS, out_refs[::2], out_refs[1::2]):
+    keep_ref = out_refs[-1]
+    for (lo, hi), order, send_ref in zip(bounds(size), ORDERS, out_refs):
         for q in range(4):
             k = picked(q, order[1:])
             at = (where_ref[0] ^ k) * size + lo
-            keep_ref[q] = tiles_s[pl.ds(at, hi - lo)]
+            keep_ref[q, lo:hi] = tiles_s[pl.ds(at, hi - lo)]
             at = (where_ref[0] ^ (k ^ order[0])) * size + lo
             send_ref[q] = tiles_s[pl.ds(at, hi - lo)]
 
@@ -279,11 +319,12 @@
 def outer(where, gp_a, gp_b, mod_a, mod_b, padded):
     smem = pl.BlockSpec(memory_space=pltpu.SMEM)
     vmem = pl.BlockSpec(memory_space=pltpu.VMEM)
-    shapes = [jax.ShapeDtypeStruct((4, hi - lo, ROWS, LANES), BF) for lo, hi in bounds(padded // 8)]
+    size = padded // 8
+    shapes = [jax.ShapeDtypeStruct((4, n, ROWS, LANES), BF) for n in [hi - lo for lo, hi in bounds(size)] + [size]]
     return pl.pallas_call(
         outer_kernel,
         in_specs=[smem] + [vmem] * 4,
-        out_shape=tuple(shape for shape in shapes for _ in range(2)),
+        out_shape=tuple(shapes),
         scratch_shapes=[pltpu.VMEM((padded, ROWS, LANES), BF)],
         compiler_params=pltpu.CompilerParams(vmem_limit_bytes=16 * 2**20),
         name="outer",
@@ -340,48 +381,42 @@
     )(which, recv, keep)
 
 
-def fold_kernel(*refs):
-    count = len(refs) // 4
-    for i in range(count):
-        keep_ref, got_ref = refs[2 * i : 2 * i + 2]
-        send_ref, left_ref = refs[2 * count + 2 * i : 2 * count + 2 * i + 2]
+def fold_kernel(keep_ref, *refs):
+    count = (len(refs) - 1) // 2
+    got_refs, send_refs, left_ref = refs[:count], refs[count:-1], refs[-1]
+    for (lo, hi), got_ref, send_ref in zip(bounds(keep_ref.shape[1]), got_refs, send_refs):
         for q in range(keep_ref.shape[0]):
-            total = (keep_ref[q].astype(F32) + got_ref[q].astype(F32)).astype(BF)
+            total = (keep_ref[q, lo:hi].astype(F32) + got_ref[q].astype(F32)).astype(BF)
             if q % 2:
                 send_ref[q // 2] = total
             else:
-                left_ref[q // 2] = total
-
-
-def fold(pairs):
-    shapes = []
-    for keep, _ in pairs:
-        shapes += [jax.ShapeDtypeStruct((keep.shape[0] // 2,) + keep.shape[1:], BF)] * 2
+                left_ref[q // 2, lo:hi] = total
+
+
+def fold(keep, got):
+    shapes = [jax.ShapeDtypeStruct((x.shape[0] // 2,) + x.shape[1:], BF) for x in (*got, keep)]
     found = pl.pallas_call(
         fold_kernel,
         out_shape=tuple(shapes),
         compiler_params=pltpu.CompilerParams(vmem_limit_bytes=8 * 2**20),
         name="fold",
-    )(*[x for pair in pairs for x in pair])
-    return found[::2], found[1::2]
-
-
-def close_kernel(*refs):
-    out_ref, at = refs[-1], 0
-    for keep_ref, got_ref in zip(refs[:-1:2], refs[1:-1:2]):
-        count = keep_ref.shape[1]
-        out_ref[at : at + count] = (keep_ref[0].astype(F32) + got_ref[0].astype(F32)).astype(BF)
-        at += count
-
-
-def close(pairs):
-    count = sum(keep.shape[1] for keep, _ in pairs)
+    )(keep, *got)
+    return found[:-1], found[-1]
+
+
+def close_kernel(keep_ref, *refs):
+    out_ref = refs[-1]
+    for (lo, hi), got_ref in zip(bounds(keep_ref.shape[1]), refs):
+        out_ref[lo:hi] = (keep_ref[0, lo:hi].astype(F32) + got_ref[0].astype(F32)).astype(BF)
+
+
+def close(keep, got):
     return pl.pallas_call(
         close_kernel,
-        out_shape=jax.ShapeDtypeStruct((count, ROWS, LANES), BF),
+        out_shape=jax.ShapeDtypeStruct(keep.shape[1:], BF),
         compiler_params=pltpu.CompilerParams(vmem_limit_bytes=8 * 2**20),
         name="close",
-    )(*[x for pair in pairs for x in pair])
+    )(keep, *got)
 
 
 def join_kernel(*refs):
@@ -490,11 +525,12 @@
     return [swap(block, PLANE, order[level]) for block, order in zip(blocks, ORDERS)]
 
 
-def sum_plane(found):
-    send, keep = found[::2], found[1::2]
-    send, keep = fold(list(zip(keep, meet(send, 0))))
-    send, keep = fold(list(zip(keep, meet(send, 1))))
-    return close(list(zip(keep, meet(send, 2))))
+def sum_plane(found, beside):
+    send, keep = found[:-1], found[-1]
+    got, beside = lax.optimization_barrier((meet(send, 0), beside))
+    send, keep = fold(keep, got)
+    send, keep = fold(keep, meet(send, 1))
+    return close(keep, meet(send, 2)), beside
 
 
 def ring(own, axis, home):
@@ -537,15 +573,17 @@
     core = lax.axis_index("core").astype(jnp.int32).reshape(1)
     which = lax.axis_index("tensor").astype(jnp.int32).reshape(1)
     where = lax.axis_index(PLANE).astype(jnp.int32).reshape(1)
-    mod, gp_keep, gp_send, send, keep = attend(
-        core, which, x, affine, wt, q_gain[:, None], k_gain[:, None], own_patches, heads, hd
+    mod, gp_keep, gp_send, att_t = attend(
+        core, x, affine, wt, q_gain[:, None], k_gain[:, None], own_patches, heads, hd
     )
     used = (3 * hw // 2 // ROWS) * (width // LANES)
     group = 8 * clips
     padded = -(-used // group) * group
     gp_other, mod_other = swap(gp_send, ("core",), 1), swap(mod, ("core",), 1)
+    found = outer(where, gp_keep, gp_other, mod, mod_other, padded)
+    send, keep = split(core, which, x, affine, wt, gp_keep, gp_send, att_t)
+    own, send = sum_plane(found, send)
     recv = lax.ppermute(send, "tensor", [(0, 1), (1, 0)])
-    own = sum_plane(outer(where, gp_keep, gp_other, mod, mod_other, padded))
     home = finish(which, recv, keep, width).reshape(frames, own_patches, width)
     own, home = lax.optimization_barrier((own, home))
     own = exchange(own.reshape((clips, own.shape[0] // clips) + own.shape[1:]), "dp")

time: 157 us -> 154 us (0.981)
  local copies, waits for them, and re-layouts: 3.27 us -> 8.95 us
  waiting for transfers between devices: 51.2 us -> 46 us
  Pallas kernels: 25 us -> 20.4 us
    pallas_call x1, Pallas kernels: 14.2 us -> 5.95 us  [attend(): pl.pallas_call(functools.partial(attend_kernel, patches=patches, heads=he...]
    unnamed x6 -> x14, local copies, waits for them, and re-layouts: 1.78 us -> 7.46 us
    ppermute x26, waiting for transfers between devices: 31 us -> 25.9 us  [swap(): return lax.ppermute(x, axes, [(i, i ^ k) for i in range(count)])]
    pallas_call x1 -> x2, Pallas kernels: 0.06 us -> 3.81 us  [the longest x1 3.74 us: split(): pl.pallas_call(split_kernel, in_specs=[smem, smem, vmem, vmem, pl.BlockSp...]
  transfers between devices with their start and end apart: 36 -> 36, of which waited for: 16 -> 17; matrix products, arithmetic and copies ran while one was open for 2% -> 2% of each run, Pallas kernels for 2% -> 3%
where the time goes in v6:
time: 154 us; the launch traced here: 153 us
  starting transfers between devices  58.2 us (38%)
  waiting for transfers between devices  46 us (30%)
  Pallas kernels  20.4 us (13%)
  blocking collectives  17.4 us (11%)
  local copies, waits for them, and re-layouts  8.95 us (6%)
    ppermute x26, starting transfers between devices, swap(): return lax.ppermute(x, axes, [(i, i ^ k) for i in range(count)])  30.6 us
    ppermute x26, waiting for transfers between devices, swap(): return lax.ppermute(x, axes, [(i, i ^ k) for i in range(count)])  25.9 us
    all_to_all x1, blocking collectives, exchange(): return lax.all_to_all(parts, axis, split_axis=0, concat_axis=0, tiled=True)  17.4 us
    all_to_all x1, waiting for transfers between devices, body(): lax.all_to_all(x, SEQ, split_axis=0, concat_axis=0, tiled=True)  11.5 us
    all_to_all x1, starting transfers between devices, body(): home = lax.all_to_all(home, SEQ, split_axis=0, concat_axis=0, tiled=True)  9.76 us
    ppermute x4, waiting for transfers between devices, ring(): up = lax.ppermute(up, axis, [(i, (i + 1) % count) for i in range(count)])  8.56 us
    ppermute x3, starting transfers between devices, ring(): lax.ppermute(down, axis, [(i, (i - 1) % count) for i in range(count)])  8.19 us
    unnamed x14, local copies, waits for them, and re-layouts  7.46 us
  transfers between devices with their start and end apart: 36, of which 17 were waited for; matrix products, arithmetic and copies ran while one was open for 2% of the time, Pallas kernels for 3%

profile of v6, /device:TPU:1, one launch (start us, length us, event | category | flops | bytes accessed | tf_op | source)
XLA Modules:
  0.0 153.1 jit_solution(15542736373726187480)
XLA Ops:
  0.6 2.2 %pack.1 = bf16[256,1728]{1,0:T(8,128)(2,1)} custom-call(bf16[256,1152]{1,0:T(8,128)(2,1)} %bitcast.35, bf16[576,256]{1,0:T(8,128)(2,1)} %bitcast.36), custom_call_target="tpu_custom_call" | custom-call | tf_op jit(solution)/shard_map/pack/pallas_call | solution.py:52
  2.9 6.9 %all-to-all-start = ((bf16[16,16,1728]{2,1,0:T(8,128)(2,1)}), bf16[16,16,1728]{2,1,0:T(8,128)(2,1)S(1)}, u32[]{:S(2)}, u32[]{:S(2)}) async-start(bf16[16,16,1728]{2,1,0:T(8,128)(2,1)} %bitcast.34), calls=%async_computation | async-start | bytes 1835008 | tf_op jit(solution)/shard_map/all_to_all | solution.py:571
  12.7 11.5 %all-to-all-done = bf16[16,16,1728]{2,1,0:T(8,128)(2,1)S(1)} async-done(((bf16[16,16,1728]{2,1,0:T(8,128)(2,1)}), bf16[16,16,1728]{2,1,0:T(8,128)(2,1)S(1)}, u32[]{:S(2)}, u32[]{:S(2)}) %all-to-all-start) | async-done | bytes 884768 | tf_op jit(solution)/shard_map/all_to_all | solution.py:571
  24.2 6.0 %attend.1 = (bf16[256,1152]{1,0:T(8,128)(2,1)S(1)}, bf16[864,256]{1,0:T(8,128)(2,1)S(1)}, bf16[864,256]{1,0:T(8,128)(2,1)S(1)}, bf16[576,256]{1,0:T(8,128)(2,1)S(1)}) custom-call(s32[1]{0:T(128)} %bitcast.1.core_ref.half_ref, bf16[256,1728]{1,0:T(8,128)(2,1)S(1)} %bitcast.29, f32[2,1152]{1,0:T(2,128)S(1)} %pad_maximum_fusion.affine_ref, ...), custom_call_target="tpu_custom_call" | custom-call | tf_op jit(solution)/shard_map/attend/pallas_call | solution.py:203
  35.9 2.3 %outer.1 = (bf16[4,22,16,128]{3,2,1,0:T(8,128)(2,1)}, bf16[4,21,16,128]{3,2,1,0:T(8,128)(2,1)}, bf16[4,21,16,128]{3,2,1,0:T(8,128)(2,1)}, bf16[4,64,16,128]{3,2,1,0:T(8,128)(2,1)S(1)}) custom-call(s32[1]{0:T(128)} %bitcast.where_ref, bf16[864,256]{1,0:T(8,128)(2,1)S(1)} %get-tuple-element.50.gp_a.gp_keep_ref, ...), custom_call_target="tpu_custom_call" | custom-call | tf_op jit(solution)/shard_map/outer/pallas_call | solution.py:324
  39.9 2.1 %copy-done = bf16[1152,3,576]{0,2,1:T(8,128)(2,1)S(1)} copy-done((bf16[1152,3,576]{0,2,1:T(8,128)(2,1)S(1)}, bf16[1152,3,576]{0,2,1:T(8,128)(2,1)}, u32[]{:S(2)}) %copy-start) | copy-done | bytes 3981336
  44.0 3.7 %split.1 = (bf16[256,640]{1,0:T(8,128)(2,1)S(1)}, f32[256,1920]{1,0:T(8,128)S(1)}) custom-call(s32[1]{0:T(128)} %bitcast.1.core_ref.half_ref, s32[1]{0:T(128)} %bitcast.11.which_ref, bf16[256,1728]{1,0:T(8,128)(2,1)S(1)} %bitcast.30, f32[2,1152]{1,0:T(2,128)S(1)} %pad_maximum_fusion.affine_ref, bf16[1728,1152]{1,0:T(8,128)(2,1)S(1)} %bitcast.28, ...), custom_call_target="tpu_custom_call" | custom-call | tf_op jit(solution)/shard_map/split/pallas_call | solution.py:277
  48.9 2.4 %collective-permute-start.11 = (bf16[256,640]{1,0:T(8,128)(2,1)S(1)}, bf16[256,640]{1,0:T(8,128)(2,1)S(1)}, u32[]{:S(2)}, u32[]{:S(2)}) collective-permute-start(bf16[256,640]{1,0:T(8,128)(2,1)S(1)} %get-tuple-element.70), channel_id=1, source_target_pairs={{0,1},{1,0},{2,3},{3,2},{4,5},{5,4},{6,7},{7,6},{8,9},{9,8},{10,11... | collective-permute-start | bytes 983048 | tf_op jit(solution)/shard_map/ppermute | solution.py:586
  53.0 8.1 %collective-permute-done.6.refs_1_ = bf16[2,21,16,128]{3,2,1,0:T(8,128)(2,1)S(1)} collective-permute-done((bf16[2,21,16,128]{3,2,1,0:T(8,128)(2,1)S(1)}, bf16[2,21,16,128]{3,2,1,0:T(8,128)(2,1)S(1)}, u32[]{:S(2)}, u32[]{:S(2)}) %collective-permute-start.6) | collective-permute-done | bytes 172064 | tf_op jit(solution)/shard_map/ppermute | solution.py:516
  61.2 2.0 %collective-permute-start.8 = (bf16[1,22,16,128]{3,2,1,0:T(8,128)(2,1)S(1)}, bf16[1,22,16,128]{3,2,1,0:T(8,128)(2,1)S(1)}, u32[]{:S(2)}, u32[]{:S(2)}) collective-permute-start(bf16[1,22,16,128]{3,2,1,0:T(8,128)(2,1)S(1)} %get-tuple-element.67), channel_id=1, source_target_pairs={{0,16},{4,20},{8,24},{12,28},{16,0},{20,4},{24,8},{28,12},{1,17},{... | collective-permute-start | bytes 270344 | tf_op jit(solution)/shard_map/ppermute | solution.py:516
  64.3 2.6 %collective-permute-done.9.refs_1_ = bf16[1,21,16,128]{3,2,1,0:T(8,128)(2,1)S(1)} collective-permute-done((bf16[1,21,16,128]{3,2,1,0:T(8,128)(2,1)S(1)}, bf16[1,21,16,128]{3,2,1,0:T(8,128)(2,1)S(1)}, u32[]{:S(2)}, u32[]{:S(2)}) %collective-permute-start.9) | collective-permute-done | bytes 86048 | tf_op jit(solution)/shard_map/ppermute | solution.py:516
  69.4 17.4 %all_to_all.15.parts_ref = bf16[8,8,16,128]{3,2,1,0:T(8,128)(2,1)S(1)} all-to-all(bf16[8,8,16,128]{3,2,1,0:T(8,128)(2,1)S(1)} %bitcast.32), channel_id=1, replica_groups=mesh['dp'=8,'xlo'=2,'y'=4,'core'=2,'tensor'=2] {'dp'}, dimensions={0} | all-to-all | bytes 524288 | tf_op jit(solution)/shard_map/all_to_all | solution.py:521
  87.2 2.5 %collective-permute-start.12 = (bf16[8,16,128]{2,1,0:T(8,128)(2,1)S(1)}, bf16[8,16,128]{2,1,0:T(8,128)(2,1)S(1)}, u32[]{:S(2)}, u32[]{:S(2)}) collective-permute-start(bf16[8,16,128]{2,1,0:T(8,128)(2,1)S(1)} %reduce.1.refs_0_), channel_id=1, source_target_pairs={{0,224},{32,0},{64,32},{96,64},{128,96},{160,128},{192,160},{224,1... | collective-permute-start | bytes 98312 | tf_op jit(solution)/shard_map/ppermute | solution.py:546
  91.3 9.8 %all-to-all-start.2 = ((bf16[16,16,1152]{2,1,0:T(8,128)(2,1)}), bf16[16,16,1152]{2,1,0:T(8,128)(2,1)S(1)}, u32[]{:S(2)}, u32[]{:S(2)}) async-start(bf16[16,16,1152]{2,1,0:T(8,128)(2,1)} %bitcast.13), calls=%async_computation.2 | async-start | bytes 1179648 | tf_op jit(solution)/shard_map/all_to_all | solution.py:592
  101.1 3.0 %collective-permute-start.14 = (bf16[8,16,128]{2,1,0:T(8,128)(2,1)S(1)}, bf16[8,16,128]{2,1,0:T(8,128)(2,1)S(1)}, u32[]{:S(2)}, u32[]{:S(2)}) collective-permute-start(bf16[8,16,128]{2,1,0:T(8,128)(2,1)S(1)} %collective-permute-done.12.refs_1_), channel_id=1, source_target_pairs={{0,224},{32,0},{64,32},{96,64},{128,96},{160,128},{192,160},{224,1... | collective-permute-start | bytes 98312 | tf_op jit(solution)/shard_map/ppermute | solution.py:546
  105.5 2.7 %collective-permute-start.15 = (bf16[8,16,128]{2,1,0:T(8,128)(2,1)S(1)}, bf16[8,16,128]{2,1,0:T(8,128)(2,1)S(1)}, u32[]{:S(2)}, u32[]{:S(2)}) collective-permute-start(bf16[8,16,128]{2,1,0:T(8,128)(2,1)S(1)} %collective-permute-done.14.refs_2_), channel_id=1, source_target_pairs={{0,224},{32,0},{64,32},{96,64},{128,96},{160,128},{192,160},{224,1... | collective-permute-start | bytes 98312 | tf_op jit(solution)/shard_map/ppermute | solution.py:546
  109.7 4.0 %collective-permute-done.18.refs_4_ = bf16[8,16,128]{2,1,0:T(8,128)(2,1)S(1)} collective-permute-done((bf16[8,16,128]{2,1,0:T(8,128)(2,1)S(1)}, bf16[8,16,128]{2,1,0:T(8,128)(2,1)S(1)}, u32[]{:S(2)}, u32[]{:S(2)}) %collective-permute-start.18) | collective-permute-done | bytes 32800 | tf_op jit(solution)/shard_map/ppermute | solution.py:543
  118.8 2.2 %collective-permute-done.21.refs_5_ = bf16[1,21,16,128]{3,2,1,0:T(8,128)(2,1)S(1)} collective-permute-done((bf16[1,21,16,128]{3,2,1,0:T(8,128)(2,1)S(1)}, bf16[1,21,16,128]{3,2,1,0:T(8,128)(2,1)S(1)}, u32[]{:S(2)}, u32[]{:S(2)}) %collective-permute-start.21) | collective-permute-done | bytes 86048 | tf_op jit(solution)/shard_map/ppermute | solution.py:516
  121.0 1.9 %collective-permute-start.22 = (bf16[2,22,16,128]{3,2,1,0:T(8,128)(2,1)S(1)}, bf16[2,22,16,128]{3,2,1,0:T(8,128)(2,1)S(1)}, u32[]{:S(2)}, u32[]{:S(2)}) collective-permute-start(bf16[2,22,16,128]{3,2,1,0:T(8,128)(2,1)S(1)} %get-tuple-element.91.refs_0_), channel_id=1, source_target_pairs={{0,12},{4,8},{8,4},{12,0},{16,28},{20,24},{24,20},{28,16},{1,13},{... | collective-permute-start | bytes 540680 | tf_op jit(solution)/shard_map/ppermute | solution.py:516
  123.1 4.0 %collective-permute-done.23.refs_3_ = bf16[2,21,16,128]{3,2,1,0:T(8,128)(2,1)S(1)} collective-permute-done((bf16[2,21,16,128]{3,2,1,0:T(8,128)(2,1)S(1)}, bf16[2,21,16,128]{3,2,1,0:T(8,128)(2,1)S(1)}, u32[]{:S(2)}, u32[]{:S(2)}) %collective-permute-start.23) | collective-permute-done | bytes 172064 | tf_op jit(solution)/shard_map/ppermute | solution.py:516
  127.5 9.2 %collective-permute-start.29 = (bf16[4,21,16,128]{3,2,1,0:T(8,128)(2,1)S(1)}, bf16[4,21,16,128]{3,2,1,0:T(8,128)(2,1)S(1)}, u32[]{:S(2)}, u32[]{:S(2)}) collective-permute-start(bf16[4,21,16,128]{3,2,1,0:T(8,128)(2,1)S(1)} %get-tuple-element.95.refs_1_), channel_id=1, source_target_pairs={{0,2},{2,0},{1,3},{3,1},{4,6},{6,4},{5,7},{7,5},{8,10},{10,8},{9,1... | collective-permute-start | bytes 1032200 | tf_op jit(solution)/shard_map/ppermute | solution.py:516
  139.4 4.5 %collective-permute-start.31 = (bf16[4,22,16,128]{3,2,1,0:T(8,128)(2,1)S(1)}, bf16[4,22,16,128]{3,2,1,0:T(8,128)(2,1)S(1)}, u32[]{:S(2)}, u32[]{:S(2)}) collective-permute-start(bf16[4,22,16,128]{3,2,1,0:T(8,128)(2,1)S(1)} %collective-permute-done.25.refs_3_), channel_id=1, source_target_pairs={{0,2},{2,0},{1,3},{3,1},{4,6},{6,4},{5,7},{7,5},{8,10},{10,8},{9,1... | collective-permute-start | bytes 1081352 | tf_op jit(solution)/shard_map/ppermute | solution.py:516
  143.9 3.7 %collective-permute-done.26.refs_4_ = bf16[4,21,16,128]{3,2,1,0:T(8,128)(2,1)S(1)} collective-permute-done((bf16[4,21,16,128]{3,2,1,0:T(8,128)(2,1)S(1)}, bf16[4,21,16,128]{3,2,1,0:T(8,128)(2,1)S(1)}, u32[]{:S(2)}, u32[]{:S(2)}) %collective-permute-start.26) | collective-permute-done | bytes 344096 | tf_op jit(solution)/shard_map/ppermute | solution.py:516
  150.2 2.9 %untile.1 = bf16[1728,1152]{1,0:T(8,128)(2,1)} custom-call(s32[1]{0:T(128)} %bitcast.where_ref, s32[1]{0:T(128)} %bitcast.1.core_ref.half_ref, bf16[4,22,16,128]{3,2,1,0:T(8,128)(2,1)S(1)} %get-tuple-element.94.refs_0_, bf16[4,21,16,128]{3,2,1,0:T(8,128)(2,1)S(1)} %get-tuple-element.95.refs_1_, bf16[4,21,16,128]{3,2,1,0:T(8,128)(2,1)S(1)} %get-tuple-element.96.refs_2_, ...), custom_call_target="tpu_custom_call" | custom-call | tf_op jit(solution)/shard_map/untile/pallas_call | solution.py:504
  (81 shorter events, 34.6 us)
Async XLA Ops:
  2.9 21.3 %all-to-all-start = ((bf16[16,16,1728]{2,1,0:T(8,128)(2,1)}), bf16[16,16,1728]{2,1,0:T(8,128)(2,1)S(1)}, u32[]{:S(2)}, u32[]{:S(2)}) async-start(bf16[16,16,1728]{2,1,0:T(8,128)(2,1)} %bitcast.34), calls=%async_computation | async-start | bytes 1835008 | tf_op jit(solution)/shard_map/all_to_all | solution.py:571
  38.2 10.7 %collective-permute-start.2 = (bf16[4,22,16,128]{3,2,1,0:T(8,128)(2,1)}, bf16[4,22,16,128]{3,2,1,0:T(8,128)(2,1)S(1)}, u32[]{:S(2)}, u32[]{:S(2)}) collective-permute-start(bf16[4,22,16,128]{3,2,1,0:T(8,128)(2,1)} %get-tuple-element.54), channel_id=1, source_target_pairs={{0,4},{4,0},{8,12},{12,8},{16,20},{20,16},{24,28},{28,24},{1,5},{5... | collective-permute-start | bytes 1081352 | tf_op jit(solution)/shard_map/ppermute | solution.py:516
  38.2 10.7 %collective-permute-start.3 = (bf16[4,21,16,128]{3,2,1,0:T(8,128)(2,1)}, bf16[4,21,16,128]{3,2,1,0:T(8,128)(2,1)S(1)}, u32[]{:S(2)}, u32[]{:S(2)}) collective-permute-start(bf16[4,21,16,128]{3,2,1,0:T(8,128)(2,1)} %get-tuple-element.55), channel_id=1, source_target_pairs={{0,12},{4,8},{8,4},{12,0},{16,28},{20,24},{24,20},{28,16},{1,13},{... | collective-permute-start | bytes 1032200 | tf_op jit(solution)/shard_map/ppermute | solution.py:516
  39.4 9.6 %collective-permute-start.4 = (bf16[4,21,16,128]{3,2,1,0:T(8,128)(2,1)}, bf16[4,21,16,128]{3,2,1,0:T(8,128)(2,1)S(1)}, u32[]{:S(2)}, u32[]{:S(2)}) collective-permute-start(bf16[4,21,16,128]{3,2,1,0:T(8,128)(2,1)} %get-tuple-element.56), channel_id=1, source_target_pairs={{0,16},{4,20},{8,24},{12,28},{16,0},{20,4},{24,8},{28,12},{1,17},{... | collective-permute-start | bytes 1032200 | tf_op jit(solution)/shard_map/ppermute | solution.py:516
  48.9 19.0 %collective-permute-start.11 = (bf16[256,640]{1,0:T(8,128)(2,1)S(1)}, bf16[256,640]{1,0:T(8,128)(2,1)S(1)}, u32[]{:S(2)}, u32[]{:S(2)}) collective-permute-start(bf16[256,640]{1,0:T(8,128)(2,1)S(1)} %get-tuple-element.70), channel_id=1, source_target_pairs={{0,1},{1,0},{2,3},{3,2},{4,5},{5,4},{6,7},{7,6},{8,9},{9,8},{10,11... | collective-permute-start | bytes 983048 | tf_op jit(solution)/shard_map/ppermute | solution.py:586
  51.6 9.5 %collective-permute-start.5 = (bf16[2,22,16,128]{3,2,1,0:T(8,128)(2,1)S(1)}, bf16[2,22,16,128]{3,2,1,0:T(8,128)(2,1)S(1)}, u32[]{:S(2)}, u32[]{:S(2)}) collective-permute-start(bf16[2,22,16,128]{3,2,1,0:T(8,128)(2,1)S(1)} %get-tuple-element.63), channel_id=1, source_target_pairs={{0,12},{4,8},{8,4},{12,0},{16,28},{20,24},{24,20},{28,16},{1,13},{... | collective-permute-start | bytes 540680 | tf_op jit(solution)/shard_map/ppermute | solution.py:516
  53.0 8.1 %collective-permute-start.6 = (bf16[2,21,16,128]{3,2,1,0:T(8,128)(2,1)S(1)}, bf16[2,21,16,128]{3,2,1,0:T(8,128)(2,1)S(1)}, u32[]{:S(2)}, u32[]{:S(2)}) collective-permute-start(bf16[2,21,16,128]{3,2,1,0:T(8,128)(2,1)S(1)} %get-tuple-element.64), channel_id=1, source_target_pairs={{0,16},{4,20},{8,24},{12,28},{16,0},{20,4},{24,8},{28,12},{1,17},{... | collective-permute-start | bytes 516104 | tf_op jit(solution)/shard_map/ppermute | solution.py:516
  53.0 8.1 %collective-permute-start.7 = (bf16[2,21,16,128]{3,2,1,0:T(8,128)(2,1)S(1)}, bf16[2,21,16,128]{3,2,1,0:T(8,128)(2,1)S(1)}, u32[]{:S(2)}, u32[]{:S(2)}) collective-permute-start(bf16[2,21,16,128]{3,2,1,0:T(8,128)(2,1)S(1)} %get-tuple-element.65), channel_id=1, source_target_pairs={{0,4},{4,0},{8,12},{12,8},{16,20},{20,16},{24,28},{28,24},{1,5},{5... | collective-permute-start | bytes 516104 | tf_op jit(solution)/shard_map/ppermute | solution.py:516
  61.2 6.6 %collective-permute-start.8 = (bf16[1,22,16,128]{3,2,1,0:T(8,128)(2,1)S(1)}, bf16[1,22,16,128]{3,2,1,0:T(8,128)(2,1)S(1)}, u32[]{:S(2)}, u32[]{:S(2)}) collective-permute-start(bf16[1,22,16,128]{3,2,1,0:T(8,128)(2,1)S(1)} %get-tuple-element.67), channel_id=1, source_target_pairs={{0,16},{4,20},{8,24},{12,28},{16,0},{20,4},{24,8},{28,12},{1,17},{... | collective-permute-start | bytes 270344 | tf_op jit(solution)/shard_map/ppermute | solution.py:516
  63.3 4.5 %collective-permute-start.10 = (bf16[1,21,16,128]{3,2,1,0:T(8,128)(2,1)S(1)}, bf16[1,21,16,128]{3,2,1,0:T(8,128)(2,1)S(1)}, u32[]{:S(2)}, u32[]{:S(2)}) collective-permute-start(bf16[1,21,16,128]{3,2,1,0:T(8,128)(2,1)S(1)} %get-tuple-element.69), channel_id=1, source_target_pairs={{0,12},{4,8},{8,4},{12,0},{16,28},{20,24},{24,20},{28,16},{1,13},{... | collective-permute-start | bytes 258056 | tf_op jit(solution)/shard_map/ppermute | solution.py:516
  86.9 4.4 %collective-permute-start.13 = (bf16[8,16,128]{2,1,0:T(8,128)(2,1)S(1)}, bf16[8,16,128]{2,1,0:T(8,128)(2,1)S(1)}, u32[]{:S(2)}, u32[]{:S(2)}) collective-permute-start(bf16[8,16,128]{2,1,0:T(8,128)(2,1)S(1)} %reduce.1.refs_0_), channel_id=1, source_target_pairs={{0,32},{32,64},{64,96},{96,128},{128,160},{160,192},{192,224},{224... | collective-permute-start | bytes 98312 | tf_op jit(solution)/shard_map/ppermute | solution.py:543
  91.3 22.4 %all-to-all-start.2 = ((bf16[16,16,1152]{2,1,0:T(8,128)(2,1)}), bf16[16,16,1152]{2,1,0:T(8,128)(2,1)S(1)}, u32[]{:S(2)}, u32[]{:S(2)}) async-start(bf16[16,16,1152]{2,1,0:T(8,128)(2,1)} %bitcast.13), calls=%async_computation.2 | async-start | bytes 1179648 | tf_op jit(solution)/shard_map/all_to_all | solution.py:592
  101.1 4.4 %collective-permute-start.16 = (bf16[8,16,128]{2,1,0:T(8,128)(2,1)S(1)}, bf16[8,16,128]{2,1,0:T(8,128)(2,1)S(1)}, u32[]{:S(2)}, u32[]{:S(2)}) collective-permute-start(bf16[8,16,128]{2,1,0:T(8,128)(2,1)S(1)} %collective-permute-done.13.refs_7_), channel_id=1, source_target_pairs={{0,32},{32,64},{64,96},{96,128},{128,160},{160,192},{192,224},{224... | collective-permute-start | bytes 98312 | tf_op jit(solution)/shard_map/ppermute | solution.py:543
  101.1 4.4 %collective-permute-start.14 = (bf16[8,16,128]{2,1,0:T(8,128)(2,1)S(1)}, bf16[8,16,128]{2,1,0:T(8,128)(2,1)S(1)}, u32[]{:S(2)}, u32[]{:S(2)}) collective-permute-start(bf16[8,16,128]{2,1,0:T(8,128)(2,1)S(1)} %collective-permute-done.12.refs_1_), channel_id=1, source_target_pairs={{0,224},{32,0},{64,32},{96,64},{128,96},{160,128},{192,160},{224,1... | collective-permute-start | bytes 98312 | tf_op jit(solution)/shard_map/ppermute | solution.py:546
  113.7 7.2 %collective-permute-start.19 = (bf16[1,22,16,128]{3,2,1,0:T(8,128)(2,1)S(1)}, bf16[1,22,16,128]{3,2,1,0:T(8,128)(2,1)S(1)}, u32[]{:S(2)}, u32[]{:S(2)}) collective-permute-start(bf16[1,22,16,128]{3,2,1,0:T(8,128)(2,1)S(1)} %get-tuple-element.88.refs_0_), channel_id=1, source_target_pairs={{0,16},{4,20},{8,24},{12,28},{16,0},{20,4},{24,8},{28,12},{1,17},{... | collective-permute-start | bytes 270344 | tf_op jit(solution)/shard_map/ppermute | solution.py:516
  116.4 4.5 %collective-permute-start.21 = (bf16[1,21,16,128]{3,2,1,0:T(8,128)(2,1)S(1)}, bf16[1,21,16,128]{3,2,1,0:T(8,128)(2,1)S(1)}, u32[]{:S(2)}, u32[]{:S(2)}) collective-permute-start(bf16[1,21,16,128]{3,2,1,0:T(8,128)(2,1)S(1)} %get-tuple-element.90.refs_4_), channel_id=1, source_target_pairs={{0,12},{4,8},{8,4},{12,0},{16,28},{20,24},{24,20},{28,16},{1,13},{... | collective-permute-start | bytes 258056 | tf_op jit(solution)/shard_map/ppermute | solution.py:516
  121.0 6.4 %collective-permute-start.22 = (bf16[2,22,16,128]{3,2,1,0:T(8,128)(2,1)S(1)}, bf16[2,22,16,128]{3,2,1,0:T(8,128)(2,1)S(1)}, u32[]{:S(2)}, u32[]{:S(2)}) collective-permute-start(bf16[2,22,16,128]{3,2,1,0:T(8,128)(2,1)S(1)} %get-tuple-element.91.refs_0_), channel_id=1, source_target_pairs={{0,12},{4,8},{8,4},{12,0},{16,28},{20,24},{24,20},{28,16},{1,13},{... | collective-permute-start | bytes 540680 | tf_op jit(solution)/shard_map/ppermute | solution.py:516
  127.4 11.9 %collective-permute-start.25 = (bf16[4,22,16,128]{3,2,1,0:T(8,128)(2,1)S(1)}, bf16[4,22,16,128]{3,2,1,0:T(8,128)(2,1)S(1)}, u32[]{:S(2)}, u32[]{:S(2)}) collective-permute-start(bf16[4,22,16,128]{3,2,1,0:T(8,128)(2,1)S(1)} %get-tuple-element.94.refs_0_), channel_id=1, source_target_pairs={{0,4},{4,0},{8,12},{12,8},{16,20},{20,16},{24,28},{28,24},{1,5},{5... | collective-permute-start | bytes 1081352 | tf_op jit(solution)/shard_map/ppermute | solution.py:516
  127.5 16.4 %collective-permute-start.29 = (bf16[4,21,16,128]{3,2,1,0:T(8,128)(2,1)S(1)}, bf16[4,21,16,128]{3,2,1,0:T(8,128)(2,1)S(1)}, u32[]{:S(2)}, u32[]{:S(2)}) collective-permute-start(bf16[4,21,16,128]{3,2,1,0:T(8,128)(2,1)S(1)} %get-tuple-element.95.refs_1_), channel_id=1, source_target_pairs={{0,2},{2,0},{1,3},{3,1},{4,6},{6,4},{5,7},{7,5},{8,10},{10,8},{9,1... | collective-permute-start | bytes 1032200 | tf_op jit(solution)/shard_map/ppermute | solution.py:516
  136.8 10.9 %collective-permute-start.26 = (bf16[4,21,16,128]{3,2,1,0:T(8,128)(2,1)S(1)}, bf16[4,21,16,128]{3,2,1,0:T(8,128)(2,1)S(1)}, u32[]{:S(2)}, u32[]{:S(2)}) collective-permute-start(bf16[4,21,16,128]{3,2,1,0:T(8,128)(2,1)S(1)} %get-tuple-element.95.refs_1_), channel_id=1, source_target_pairs={{0,12},{4,8},{8,4},{12,0},{16,28},{20,24},{24,20},{28,16},{1,13},{... | collective-permute-start | bytes 1032200 | tf_op jit(solution)/shard_map/ppermute | solution.py:516
  137.6 10.8 %collective-permute-start.27 = (bf16[4,21,16,128]{3,2,1,0:T(8,128)(2,1)S(1)}, bf16[4,21,16,128]{3,2,1,0:T(8,128)(2,1)S(1)}, u32[]{:S(2)}, u32[]{:S(2)}) collective-permute-start(bf16[4,21,16,128]{3,2,1,0:T(8,128)(2,1)S(1)} %get-tuple-element.96.refs_2_), channel_id=1, source_target_pairs={{0,16},{4,20},{8,24},{12,28},{16,0},{20,4},{24,8},{28,12},{1,17},{... | collective-permute-start | bytes 1032200 | tf_op jit(solution)/shard_map/ppermute | solution.py:516
  138.7 10.8 %collective-permute-start.28 = (bf16[4,22,16,128]{3,2,1,0:T(8,128)(2,1)S(1)}, bf16[4,22,16,128]{3,2,1,0:T(8,128)(2,1)S(1)}, u32[]{:S(2)}, u32[]{:S(2)}) collective-permute-start(bf16[4,22,16,128]{3,2,1,0:T(8,128)(2,1)S(1)} %get-tuple-element.94.refs_0_), channel_id=1, source_target_pairs={{0,2},{2,0},{1,3},{3,1},{4,6},{6,4},{5,7},{7,5},{8,10},{10,8},{9,1... | collective-permute-start | bytes 1081352 | tf_op jit(solution)/shard_map/ppermute | solution.py:516
  139.4 10.8 %collective-permute-start.31 = (bf16[4,22,16,128]{3,2,1,0:T(8,128)(2,1)S(1)}, bf16[4,22,16,128]{3,2,1,0:T(8,128)(2,1)S(1)}, u32[]{:S(2)}, u32[]{:S(2)}) collective-permute-start(bf16[4,22,16,128]{3,2,1,0:T(8,128)(2,1)S(1)} %collective-permute-done.25.refs_3_), channel_id=1, source_target_pairs={{0,2},{2,0},{1,3},{3,1},{4,6},{6,4},{5,7},{7,5},{8,10},{10,8},{9,1... | collective-permute-start | bytes 1081352 | tf_op jit(solution)/shard_map/ppermute | solution.py:516
  143.9 5.6 %collective-permute-start.30 = (bf16[4,21,16,128]{3,2,1,0:T(8,128)(2,1)S(1)}, bf16[4,21,16,128]{3,2,1,0:T(8,128)(2,1)S(1)}, u32[]{:S(2)}, u32[]{:S(2)}) collective-permute-start(bf16[4,21,16,128]{3,2,1,0:T(8,128)(2,1)S(1)} %get-tuple-element.96.refs_2_), channel_id=1, source_target_pairs={{0,2},{2,0},{1,3},{3,1},{4,6},{6,4},{5,7},{7,5},{8,10},{10,8},{9,1... | collective-permute-start | bytes 1032200 | tf_op jit(solution)/shard_map/ppermute | solution.py:516
  (19 other events, 48.9 us)

commit v7 on v6

--- a/solution.py
+++ b/solution.py
@@ -221,7 +221,7 @@
             pltpu.VMEM((hw, tokens), F32),
             pltpu.SemaphoreType.DMA((3,)),
         ],
-        compiler_params=pltpu.CompilerParams(vmem_limit_bytes=50 * 2**20),
+        compiler_params=pltpu.CompilerParams(vmem_limit_bytes=52 * 2**20),
         name="attend",
     )(core, x, affine, wt, qg, kg)
 
@@ -286,7 +286,7 @@
             pltpu.VMEM((wt.shape[0], tokens), BF),
             pltpu.SemaphoreType.DMA((3,)),
         ],
-        compiler_params=pltpu.CompilerParams(vmem_limit_bytes=18 * 2**20),
+        compiler_params=pltpu.CompilerParams(vmem_limit_bytes=30 * 2**20),
         name="split",
     )(core, which, x, affine, wt, gp_keep, gp_send, att)
 
@@ -451,28 +451,47 @@
     )(parts)
 
 
-def place_kernel(clip_ref, *refs):
-    clips = len(refs) - 4
-    pieces, out_refs, all_s = refs[:clips], refs[clips:-1], refs[-1]
-    size = pieces[0].shape[0]
-    for shift, piece in enumerate(pieces):
-        all_s[pl.ds(lax.rem(clip_ref[0] + shift, clips) * size, size)] = piece[...]
+def trio_kernel(own_ref, below_ref, above_ref, all_ref, two_ref):
+    size = own_ref.shape[0]
+    for i, ref in enumerate((below_ref, own_ref, above_ref)):
+        all_ref[i * size : (i + 1) * size] = ref[...]
+        if i < 2:
+            two_ref[i * size : (i + 1) * size] = ref[...]
+
+
+def trio(own, below, above):
+    size = own.shape[0]
+    return pl.pallas_call(
+        trio_kernel,
+        out_shape=tuple(jax.ShapeDtypeStruct((n * size,) + own.shape[1:], BF) for n in (3, 2)),
+        compiler_params=pltpu.CompilerParams(vmem_limit_bytes=4 * 2**20),
+        name="trio",
+    )(own, below, above)
+
+
+def place_kernel(clip_ref, near_ref, below_ref, above_ref, *refs, clips):
+    out_refs, all_s = refs[:-1], refs[-1]
+    size = all_s.shape[0] // clips
+    for ref, first in ((near_ref, -1), (below_ref, -4), (above_ref, 2)):
+        for i in range(ref.shape[0] // size):
+            at = lax.rem(clip_ref[0] + (first + i + clips), clips) * size
+            all_s[pl.ds(at, size)] = ref[i * size : (i + 1) * size]
     for (lo, hi), out_ref in zip(bounds(clips * size), out_refs):
         out_ref[0] = all_s[lo:hi]
 
 
-def place(clip, pieces):
-    total = len(pieces) * pieces[0].shape[0]
+def place(clip, near, below, above, clips):
+    total = near.shape[0] // 3 * clips
     smem = pl.BlockSpec(memory_space=pltpu.SMEM)
     vmem = pl.BlockSpec(memory_space=pltpu.VMEM)
     return pl.pallas_call(
-        place_kernel,
-        in_specs=[smem] + [vmem] * len(pieces),
+        functools.partial(place_kernel, clips=clips),
+        in_specs=[smem, vmem, vmem, vmem],
         out_shape=tuple(jax.ShapeDtypeStruct((1, hi - lo, ROWS, LANES), BF) for lo, hi in bounds(total)),
         scratch_shapes=[pltpu.VMEM((total, ROWS, LANES), BF)],
         compiler_params=pltpu.CompilerParams(vmem_limit_bytes=4 * 2**20),
         name="place",
-    )(clip, *pieces)
+    )(clip, near, below, above)
 
 
 def untile_kernel(where_ref, half_ref, *refs):
@@ -533,19 +552,15 @@
     return close(keep, meet(send, 2)), beside
 
 
-def ring(own, axis, home):
+def shift(x, axis, step):
     count = lax.axis_size(axis)
-    pieces = [own] * count
-    up = down = own
-    for step in range(1, count // 2 + 1):
-        if step == 2:
-            up, down, home = lax.optimization_barrier((up, down, home))
-        up = lax.ppermute(up, axis, [(i, (i + 1) % count) for i in range(count)])
-        pieces[count - step] = up
-        if step < count - step:
-            down = lax.ppermute(down, axis, [(i, (i - 1) % count) for i in range(count)])
-            pieces[step] = down
-    return pieces, home
+    return lax.ppermute(x, axis, [(i, (i + step) % count) for i in range(count)])
+
+
+def gather_clips(own, home):
+    near, two = trio(own, shift(own, "dp", 1), shift(own, "dp", -1))
+    near, two, home = lax.optimization_barrier((near, two, home))
+    return near, shift(near, "dp", 3), shift(two, "dp", -3), home
 
 
 def gather_plane(have, where, half, rows, width):
@@ -583,16 +598,18 @@
     found = outer(where, gp_keep, gp_other, mod, mod_other, padded)
     send, keep = split(core, which, x, affine, wt, gp_keep, gp_send, att_t)
     own, send = sum_plane(found, send)
+    own, send = lax.optimization_barrier((own, send))
     recv = lax.ppermute(send, "tensor", [(0, 1), (1, 0)])
+    own = exchange(own.reshape((clips, own.shape[0] // clips) + own.shape[1:]), "dp")
+    own, recv = lax.optimization_barrier((own, recv))
+    own = reduce(own, 1.0 / math.sqrt(clips * frames * patches))
     home = finish(which, recv, keep, width).reshape(frames, own_patches, width)
-    own, home = lax.optimization_barrier((own, home))
-    own = exchange(own.reshape((clips, own.shape[0] // clips) + own.shape[1:]), "dp")
-    own = reduce(own, 1.0 / math.sqrt(clips * frames * patches))
-    pieces, home = ring(own, "dp", home)
+    near, below, above, home = gather_clips(own, home)
     home = lax.all_to_all(home, SEQ, split_axis=0, concat_axis=0, tiled=True)
-    pieces, home = lax.optimization_barrier((pieces, home))
+    below, home = lax.optimization_barrier((below, home))
     grad_t, att_t = unpack(home.reshape(patches, width))
-    have = place(lax.axis_index("dp").astype(jnp.int32).reshape(1), pieces)
+    clip = lax.axis_index("dp").astype(jnp.int32).reshape(1)
+    have = place(clip, near, below, above, clips)
     grad_qkv = gather_plane(have, where, core, 3 * hw, width)
     grad_qkv = grad_qkv.reshape(3, hw, width).transpose(2, 0, 1)
     return (att_t.T[None, None], grad_t.T[None, None], grad_qkv)

time: 154 us -> 144 us (0.935)
  blocking collectives: 17.4 us -> 0 us
  Pallas kernels: 20.4 us -> 23.5 us
  starting transfers between devices: 58.2 us -> 60.3 us
    all_to_all x1 -> x0, blocking collectives: 17.4 us -> none  [exchange(): return lax.all_to_all(parts, axis, split_axis=0, concat_axis=0, tiled=True)]
    all_to_all x0 -> x1, starting transfers between devices: none -> 8.18 us  [exchange(): return lax.all_to_all(parts, axis, split_axis=0, concat_axis=0, tiled=True)]
    ppermute x26, waiting for transfers between devices: 25.9 us -> 20.1 us  [swap(): return lax.ppermute(x, axes, [(i, i ^ k) for i in range(count)])]
    ppermute x1, waiting for transfers between devices: 0.01 us -> 5.19 us  [body(): recv = lax.ppermute(send, 'tensor', [(0, 1), (1, 0)])]
    ppermute x26, starting transfers between devices: 30.6 us -> 26.1 us  [swap(): return lax.ppermute(x, axes, [(i, i ^ k) for i in range(count)])]
    ppermute x7 -> x4, starting transfers between devices: 8.47 us -> 6.02 us  [shift(): lax.ppermute(x, axis, [(i, (i + step) % count) for i in range(count)])]
    all_to_all x0 -> x1, waiting for transfers between devices: none -> 1.79 us  [exchange(): return lax.all_to_all(parts, axis, split_axis=0, concat_axis=0, tiled=True)]
    ppermute x7 -> x4, waiting for transfers between devices: 8.57 us -> 7.26 us  [shift(): lax.ppermute(x, axis, [(i, (i + step) % count) for i in range(count)])]
  transfers between devices with their start and end apart: 36 -> 34, of which waited for: 17 -> 20; matrix products, arithmetic and copies ran while one was open for 2% -> 2% of each run, Pallas kernels for 3% -> 4%
where the time goes in v7:
time: 144 us; the launch traced here: 142 us
  starting transfers between devices  60.3 us (42%)
  waiting for transfers between devices  47 us (33%)
  Pallas kernels  23.5 us (16%)
  local copies, waits for them, and re-layouts  9.19 us (6%)
    ppermute x26, starting transfers between devices, swap(): return lax.ppermute(x, axes, [(i, i ^ k) for i in range(count)])  26.1 us
    ppermute x26, waiting for transfers between devices, swap(): return lax.ppermute(x, axes, [(i, i ^ k) for i in range(count)])  20.1 us
    all_to_all x1, waiting for transfers between devices, body(): lax.all_to_all(x, SEQ, split_axis=0, concat_axis=0, tiled=True)  11.5 us
    all_to_all x1, starting transfers between devices, body(): home = lax.all_to_all(home, SEQ, split_axis=0, concat_axis=0, tiled=True)  10.6 us
    all_to_all x1, starting transfers between devices, exchange(): return lax.all_to_all(parts, axis, split_axis=0, concat_axis=0, tiled=True)  8.18 us
    unnamed x16, local copies, waits for them, and re-layouts  7.7 us
    ppermute x4, waiting for transfers between devices, shift(): lax.ppermute(x, axis, [(i, (i + step) % count) for i in range(count)])  7.26 us
    pallas_call x1, Pallas kernels, attend(): pl.pallas_call(functools.partial(attend_kernel, patches=patches, heads=he...  7.12 us
  transfers between devices with their start and end apart: 34, of which 20 were waited for; matrix products, arithmetic and copies ran while one was open for 2% of the time, Pallas kernels for 4%

profile of v7, /device:TPU:1, one launch (start us, length us, event | category | flops | bytes accessed | tf_op | source)
XLA Modules:
  0.0 142.2 jit_solution(2371780727261870246)
XLA Ops:
  0.6 2.2 %pack.1 = bf16[256,1728]{1,0:T(8,128)(2,1)} custom-call(bf16[256,1152]{1,0:T(8,128)(2,1)} %bitcast.34, bf16[576,256]{1,0:T(8,128)(2,1)} %bitcast.35), custom_call_target="tpu_custom_call" | custom-call | tf_op jit(solution)/shard_map/pack/pallas_call | solution.py:52
  2.9 6.9 %all-to-all-start = ((bf16[16,16,1728]{2,1,0:T(8,128)(2,1)}), bf16[16,16,1728]{2,1,0:T(8,128)(2,1)S(1)}, u32[]{:S(2)}, u32[]{:S(2)}) async-start(bf16[16,16,1728]{2,1,0:T(8,128)(2,1)} %bitcast.33), calls=%async_computation | async-start | bytes 1835008 | tf_op jit(solution)/shard_map/all_to_all | solution.py:586
  12.7 11.5 %all-to-all-done = bf16[16,16,1728]{2,1,0:T(8,128)(2,1)S(1)} async-done(((bf16[16,16,1728]{2,1,0:T(8,128)(2,1)}), bf16[16,16,1728]{2,1,0:T(8,128)(2,1)S(1)}, u32[]{:S(2)}, u32[]{:S(2)}) %all-to-all-start) | async-done | bytes 884768 | tf_op jit(solution)/shard_map/all_to_all | solution.py:586
  25.1 7.1 %attend.1 = (bf16[256,1152]{1,0:T(8,128)(2,1)S(1)}, bf16[864,256]{1,0:T(8,128)(2,1)S(1)}, bf16[864,256]{1,0:T(8,128)(2,1)S(1)}, bf16[576,256]{1,0:T(8,128)(2,1)S(1)}) custom-call(s32[1]{0:T(128)} %bitcast.1.core_ref.half_ref, bf16[256,1728]{1,0:T(8,128)(2,1)} %bitcast.29, f32[2,1152]{1,0:T(2,128)S(1)} %pad_maximum_fusion.affine_ref, ...), custom_call_target="tpu_custom_call" | custom-call | tf_op jit(solution)/shard_map/attend/pallas_call | solution.py:203
  36.1 2.3 %outer.1 = (bf16[4,22,16,128]{3,2,1,0:T(8,128)(2,1)}, bf16[4,21,16,128]{3,2,1,0:T(8,128)(2,1)}, bf16[4,21,16,128]{3,2,1,0:T(8,128)(2,1)}, bf16[4,64,16,128]{3,2,1,0:T(8,128)(2,1)S(1)}) custom-call(s32[1]{0:T(128)} %bitcast.where_ref, bf16[864,256]{1,0:T(8,128)(2,1)S(1)} %get-tuple-element.47.gp_a.gp_keep_ref, ...), custom_call_target="tpu_custom_call" | custom-call | tf_op jit(solution)/shard_map/outer/pallas_call | solution.py:324
  40.1 2.1 %copy-done = bf16[1152,3,576]{0,2,1:T(8,128)(2,1)S(1)} copy-done((bf16[1152,3,576]{0,2,1:T(8,128)(2,1)S(1)}, bf16[1152,3,576]{0,2,1:T(8,128)(2,1)}, u32[]{:S(2)}) %copy-start) | copy-done | bytes 3981336
  45.4 3.7 %split.1 = (bf16[256,640]{1,0:T(8,128)(2,1)S(1)}, f32[256,1920]{1,0:T(8,128)S(1)}) custom-call(s32[1]{0:T(128)} %bitcast.1.core_ref.half_ref, s32[1]{0:T(128)} %bitcast.11.which_ref, bf16[256,1728]{1,0:T(8,128)(2,1)S(1)} %bitcast.30, f32[2,1152]{1,0:T(2,128)S(1)} %pad_maximum_fusion.affine_ref, bf16[1728,1152]{1,0:T(8,128)(2,1)S(1)} %bitcast.28, ...), custom_call_target="tpu_custom_call" | custom-call | tf_op jit(solution)/shard_map/split/pallas_call | solution.py:277
  53.8 3.1 %collective-permute-done.6.refs_1_ = bf16[2,21,16,128]{3,2,1,0:T(8,128)(2,1)S(1)} collective-permute-done((bf16[2,21,16,128]{3,2,1,0:T(8,128)(2,1)S(1)}, bf16[2,21,16,128]{3,2,1,0:T(8,128)(2,1)S(1)}, u32[]{:S(2)}, u32[]{:S(2)}) %collective-permute-start.6) | collective-permute-done | bytes 172064 | tf_op jit(solution)/shard_map/ppermute | solution.py:535
  60.1 2.0 %collective-permute-done.9.refs_1_ = bf16[1,21,16,128]{3,2,1,0:T(8,128)(2,1)S(1)} collective-permute-done((bf16[1,21,16,128]{3,2,1,0:T(8,128)(2,1)S(1)}, bf16[1,21,16,128]{3,2,1,0:T(8,128)(2,1)S(1)}, u32[]{:S(2)}, u32[]{:S(2)}) %collective-permute-start.9) | collective-permute-done | bytes 86048 | tf_op jit(solution)/shard_map/ppermute | solution.py:535
  64.1 8.2 %all-to-all-start.1 = ((bf16[8,8,16,128]{3,2,1,0:T(8,128)(2,1)}), bf16[8,8,16,128]{3,2,1,0:T(8,128)(2,1)S(1)}, u32[]{:S(2)}, u32[]{:S(2)}) async-start(bf16[8,8,16,128]{3,2,1,0:T(8,128)(2,1)} %bitcast.13), calls=%async_computation.1 | async-start | bytes 524288 | tf_op jit(solution)/shard_map/all_to_all | solution.py:540
  72.3 2.5 %collective-permute-start.11 = (bf16[256,640]{1,0:T(8,128)(2,1)}, bf16[256,640]{1,0:T(8,128)(2,1)S(1)}, u32[]{:S(2)}, u32[]{:S(2)}) collective-permute-start(bf16[256,640]{1,0:T(8,128)(2,1)} %copy-done.7), channel_id=1, source_target_pairs={{0,1},{1,0},{2,3},{3,2},{4,5},{5,4},{6,7},{7,6},{8,9},{9,8},{10,11... | collective-permute-start | bytes 983048 | tf_op jit(solution)/shard_map/ppermute | solution.py:602
  74.8 5.2 %collective-permute-done.11.recv_ref = bf16[256,640]{1,0:T(8,128)(2,1)S(1)} collective-permute-done((bf16[256,640]{1,0:T(8,128)(2,1)}, bf16[256,640]{1,0:T(8,128)(2,1)S(1)}, u32[]{:S(2)}, u32[]{:S(2)}) %collective-permute-start.11) | collective-permute-done | bytes 327712 | tf_op jit(solution)/shard_map/ppermute | solution.py:602
  80.0 1.8 %all-to-all-done.1.parts_ref = bf16[8,8,16,128]{3,2,1,0:T(8,128)(2,1)S(1)} async-done(((bf16[8,8,16,128]{3,2,1,0:T(8,128)(2,1)}), bf16[8,8,16,128]{3,2,1,0:T(8,128)(2,1)S(1)}, u32[]{:S(2)}, u32[]{:S(2)}) %all-to-all-start.1) | async-done | bytes 262176 | tf_op jit(solution)/shard_map/all_to_all | solution.py:540
  84.9 2.2 %collective-permute-done.12.below_ref = bf16[8,16,128]{2,1,0:T(8,128)(2,1)S(1)} collective-permute-done((bf16[8,16,128]{2,1,0:T(8,128)(2,1)S(1)}, bf16[8,16,128]{2,1,0:T(8,128)(2,1)S(1)}, u32[]{:S(2)}, u32[]{:S(2)}) %collective-permute-start.12) | collective-permute-done | bytes 32800 | tf_op jit(solution)/shard_map/ppermute | solution.py:557
  87.2 10.6 %all-to-all-start.2 = ((bf16[16,16,1152]{2,1,0:T(8,128)(2,1)}), bf16[16,16,1152]{2,1,0:T(8,128)(2,1)S(1)}, u32[]{:S(2)}, u32[]{:S(2)}) async-start(bf16[16,16,1152]{2,1,0:T(8,128)(2,1)} %bitcast.14), calls=%async_computation.2 | async-start | bytes 1179648 | tf_op jit(solution)/shard_map/all_to_all | solution.py:608
  98.1 4.2 %collective-permute-start.15 = (bf16[16,16,128]{2,1,0:T(8,128)(2,1)S(1)}, bf16[16,16,128]{2,1,0:T(8,128)(2,1)S(1)}, u32[]{:S(2)}, u32[]{:S(2)}) collective-permute-start(bf16[16,16,128]{2,1,0:T(8,128)(2,1)S(1)} %get-tuple-element.81), channel_id=1, source_target_pairs={{0,160},{32,192},{64,224},{96,0},{128,32},{160,64},{192,96},{224,1... | collective-permute-start | bytes 196616 | tf_op jit(solution)/shard_map/ppermute | solution.py:557
  102.2 5.0 %collective-permute-done.14.below_ref = bf16[24,16,128]{2,1,0:T(8,128)(2,1)S(1)} collective-permute-done((bf16[24,16,128]{2,1,0:T(8,128)(2,1)S(1)}, bf16[24,16,128]{2,1,0:T(8,128)(2,1)S(1)}, u32[]{:S(2)}, u32[]{:S(2)}) %collective-permute-start.14) | collective-permute-done | bytes 98336 | tf_op jit(solution)/shard_map/ppermute | solution.py:557
  110.0 1.8 %collective-permute-start.18 = (bf16[1,21,16,128]{3,2,1,0:T(8,128)(2,1)S(1)}, bf16[1,21,16,128]{3,2,1,0:T(8,128)(2,1)S(1)}, u32[]{:S(2)}, u32[]{:S(2)}) collective-permute-start(bf16[1,21,16,128]{3,2,1,0:T(8,128)(2,1)S(1)} %get-tuple-element.84.refs_4_), channel_id=1, source_target_pairs={{0,12},{4,8},{8,4},{12,0},{16,28},{20,24},{24,20},{28,16},{1,13},{... | collective-permute-start | bytes 258056 | tf_op jit(solution)/shard_map/ppermute | solution.py:535
  114.6 1.9 %collective-permute-start.19 = (bf16[2,22,16,128]{3,2,1,0:T(8,128)(2,1)S(1)}, bf16[2,22,16,128]{3,2,1,0:T(8,128)(2,1)S(1)}, u32[]{:S(2)}, u32[]{:S(2)}) collective-permute-start(bf16[2,22,16,128]{3,2,1,0:T(8,128)(2,1)S(1)} %get-tuple-element.85.refs_0_), channel_id=1, source_target_pairs={{0,12},{4,8},{8,4},{12,0},{16,28},{20,24},{24,20},{28,16},{1,13},{... | collective-permute-start | bytes 540680 | tf_op jit(solution)/shard_map/ppermute | solution.py:535
  116.7 4.0 %collective-permute-done.20.refs_3_ = bf16[2,21,16,128]{3,2,1,0:T(8,128)(2,1)S(1)} collective-permute-done((bf16[2,21,16,128]{3,2,1,0:T(8,128)(2,1)S(1)}, bf16[2,21,16,128]{3,2,1,0:T(8,128)(2,1)S(1)}, u32[]{:S(2)}, u32[]{:S(2)}) %collective-permute-start.20) | collective-permute-done | bytes 172064 | tf_op jit(solution)/shard_map/ppermute | solution.py:535
  121.4 4.4 %collective-permute-start.26 = (bf16[4,21,16,128]{3,2,1,0:T(8,128)(2,1)S(1)}, bf16[4,21,16,128]{3,2,1,0:T(8,128)(2,1)S(1)}, u32[]{:S(2)}, u32[]{:S(2)}) collective-permute-start(bf16[4,21,16,128]{3,2,1,0:T(8,128)(2,1)S(1)} %get-tuple-element.89.refs_1_), channel_id=1, source_target_pairs={{0,2},{2,0},{1,3},{3,1},{4,6},{6,4},{5,7},{7,5},{8,10},{10,8},{9,1... | collective-permute-start | bytes 1032200 | tf_op jit(solution)/shard_map/ppermute | solution.py:535
  128.5 4.7 %collective-permute-start.28 = (bf16[4,22,16,128]{3,2,1,0:T(8,128)(2,1)S(1)}, bf16[4,22,16,128]{3,2,1,0:T(8,128)(2,1)S(1)}, u32[]{:S(2)}, u32[]{:S(2)}) collective-permute-start(bf16[4,22,16,128]{3,2,1,0:T(8,128)(2,1)S(1)} %collective-permute-done.22.refs_3_), channel_id=1, source_target_pairs={{0,2},{2,0},{1,3},{3,1},{4,6},{6,4},{5,7},{7,5},{8,10},{10,8},{9,1... | collective-permute-start | bytes 1081352 | tf_op jit(solution)/shard_map/ppermute | solution.py:535
  133.1 3.2 %collective-permute-done.23.refs_4_ = bf16[4,21,16,128]{3,2,1,0:T(8,128)(2,1)S(1)} collective-permute-done((bf16[4,21,16,128]{3,2,1,0:T(8,128)(2,1)S(1)}, bf16[4,21,16,128]{3,2,1,0:T(8,128)(2,1)S(1)}, u32[]{:S(2)}, u32[]{:S(2)}) %collective-permute-start.23) | collective-permute-done | bytes 344096 | tf_op jit(solution)/shard_map/ppermute | solution.py:535
  139.3 2.9 %untile.1 = bf16[1728,1152]{1,0:T(8,128)(2,1)} custom-call(s32[1]{0:T(128)} %bitcast.where_ref, s32[1]{0:T(128)} %bitcast.1.core_ref.half_ref, bf16[4,22,16,128]{3,2,1,0:T(8,128)(2,1)S(1)} %get-tuple-element.88.refs_0_, bf16[4,21,16,128]{3,2,1,0:T(8,128)(2,1)S(1)} %get-tuple-element.89.refs_1_, bf16[4,21,16,128]{3,2,1,0:T(8,128)(2,1)S(1)} %get-tuple-element.90.refs_2_, ...), custom_call_target="tpu_custom_call" | custom-call | tf_op jit(solution)/shard_map/untile/pallas_call | solution.py:523
  (79 shorter events, 37.9 us)
Async XLA Ops:
  2.9 21.3 %all-to-all-start = ((bf16[16,16,1728]{2,1,0:T(8,128)(2,1)}), bf16[16,16,1728]{2,1,0:T(8,128)(2,1)S(1)}, u32[]{:S(2)}, u32[]{:S(2)}) async-start(bf16[16,16,1728]{2,1,0:T(8,128)(2,1)} %bitcast.33), calls=%async_computation | async-start | bytes 1835008 | tf_op jit(solution)/shard_map/all_to_all | solution.py:586
  38.5 10.8 %collective-permute-start.2 = (bf16[4,22,16,128]{3,2,1,0:T(8,128)(2,1)}, bf16[4,22,16,128]{3,2,1,0:T(8,128)(2,1)}, u32[]{:S(2)}, u32[]{:S(2)}) collective-permute-start(bf16[4,22,16,128]{3,2,1,0:T(8,128)(2,1)} %get-tuple-element.51), channel_id=1, source_target_pairs={{0,4},{4,0},{8,12},{12,8},{16,20},{20,16},{24,28},{28,24},{1,5},{5... | collective-permute-start | bytes 1081352 | tf_op jit(solution)/shard_map/ppermute | solution.py:535
  38.5 10.8 %collective-permute-start.3 = (bf16[4,21,16,128]{3,2,1,0:T(8,128)(2,1)}, bf16[4,21,16,128]{3,2,1,0:T(8,128)(2,1)}, u32[]{:S(2)}, u32[]{:S(2)}) collective-permute-start(bf16[4,21,16,128]{3,2,1,0:T(8,128)(2,1)} %get-tuple-element.52), channel_id=1, source_target_pairs={{0,12},{4,8},{8,4},{12,0},{16,28},{20,24},{24,20},{28,16},{1,13},{... | collective-permute-start | bytes 1032200 | tf_op jit(solution)/shard_map/ppermute | solution.py:535
  39.6 9.7 %collective-permute-start.4 = (bf16[4,21,16,128]{3,2,1,0:T(8,128)(2,1)}, bf16[4,21,16,128]{3,2,1,0:T(8,128)(2,1)}, u32[]{:S(2)}, u32[]{:S(2)}) collective-permute-start(bf16[4,21,16,128]{3,2,1,0:T(8,128)(2,1)} %get-tuple-element.53), channel_id=1, source_target_pairs={{0,16},{4,20},{8,24},{12,28},{16,0},{20,4},{24,8},{28,12},{1,17},{... | collective-permute-start | bytes 1032200 | tf_op jit(solution)/shard_map/ppermute | solution.py:535
  50.7 7.3 %collective-permute-start.5 = (bf16[2,22,16,128]{3,2,1,0:T(8,128)(2,1)S(1)}, bf16[2,22,16,128]{3,2,1,0:T(8,128)(2,1)S(1)}, u32[]{:S(2)}, u32[]{:S(2)}) collective-permute-start(bf16[2,22,16,128]{3,2,1,0:T(8,128)(2,1)S(1)} %get-tuple-element.60), channel_id=1, source_target_pairs={{0,12},{4,8},{8,4},{12,0},{16,28},{20,24},{24,20},{28,16},{1,13},{... | collective-permute-start | bytes 540680 | tf_op jit(solution)/shard_map/ppermute | solution.py:535
  52.3 4.6 %collective-permute-start.6 = (bf16[2,21,16,128]{3,2,1,0:T(8,128)(2,1)S(1)}, bf16[2,21,16,128]{3,2,1,0:T(8,128)(2,1)S(1)}, u32[]{:S(2)}, u32[]{:S(2)}) collective-permute-start(bf16[2,21,16,128]{3,2,1,0:T(8,128)(2,1)S(1)} %get-tuple-element.61), channel_id=1, source_target_pairs={{0,16},{4,20},{8,24},{12,28},{16,0},{20,4},{24,8},{28,12},{1,17},{... | collective-permute-start | bytes 516104 | tf_op jit(solution)/shard_map/ppermute | solution.py:535
  53.5 4.6 %collective-permute-start.7 = (bf16[2,21,16,128]{3,2,1,0:T(8,128)(2,1)S(1)}, bf16[2,21,16,128]{3,2,1,0:T(8,128)(2,1)S(1)}, u32[]{:S(2)}, u32[]{:S(2)}) collective-permute-start(bf16[2,21,16,128]{3,2,1,0:T(8,128)(2,1)S(1)} %get-tuple-element.62), channel_id=1, source_target_pairs={{0,4},{4,0},{8,12},{12,8},{16,20},{20,16},{24,28},{28,24},{1,5},{5... | collective-permute-start | bytes 516104 | tf_op jit(solution)/shard_map/ppermute | solution.py:535
  58.2 5.2 %collective-permute-start.8 = (bf16[1,22,16,128]{3,2,1,0:T(8,128)(2,1)S(1)}, bf16[1,22,16,128]{3,2,1,0:T(8,128)(2,1)S(1)}, u32[]{:S(2)}, u32[]{:S(2)}) collective-permute-start(bf16[1,22,16,128]{3,2,1,0:T(8,128)(2,1)S(1)} %get-tuple-element.64), channel_id=1, source_target_pairs={{0,16},{4,20},{8,24},{12,28},{16,0},{20,4},{24,8},{28,12},{1,17},{... | collective-permute-start | bytes 270344 | tf_op jit(solution)/shard_map/ppermute | solution.py:535
  58.8 4.5 %collective-permute-start.10 = (bf16[1,21,16,128]{3,2,1,0:T(8,128)(2,1)S(1)}, bf16[1,21,16,128]{3,2,1,0:T(8,128)(2,1)S(1)}, u32[]{:S(2)}, u32[]{:S(2)}) collective-permute-start(bf16[1,21,16,128]{3,2,1,0:T(8,128)(2,1)S(1)} %get-tuple-element.66), channel_id=1, source_target_pairs={{0,12},{4,8},{8,4},{12,0},{16,28},{20,24},{24,20},{28,16},{1,13},{... | collective-permute-start | bytes 258056 | tf_op jit(solution)/shard_map/ppermute | solution.py:535
  64.1 17.6 %all-to-all-start.1 = ((bf16[8,8,16,128]{3,2,1,0:T(8,128)(2,1)}), bf16[8,8,16,128]{3,2,1,0:T(8,128)(2,1)S(1)}, u32[]{:S(2)}, u32[]{:S(2)}) async-start(bf16[8,8,16,128]{3,2,1,0:T(8,128)(2,1)} %bitcast.13), calls=%async_computation.1 | async-start | bytes 524288 | tf_op jit(solution)/shard_map/all_to_all | solution.py:540
  72.3 7.6 %collective-permute-start.11 = (bf16[256,640]{1,0:T(8,128)(2,1)}, bf16[256,640]{1,0:T(8,128)(2,1)S(1)}, u32[]{:S(2)}, u32[]{:S(2)}) collective-permute-start(bf16[256,640]{1,0:T(8,128)(2,1)} %copy-done.7), channel_id=1, source_target_pairs={{0,1},{1,0},{2,3},{3,2},{4,5},{5,4},{6,7},{7,6},{8,9},{9,8},{10,11... | collective-permute-start | bytes 983048 | tf_op jit(solution)/shard_map/ppermute | solution.py:602
  87.2 21.2 %all-to-all-start.2 = ((bf16[16,16,1152]{2,1,0:T(8,128)(2,1)}), bf16[16,16,1152]{2,1,0:T(8,128)(2,1)S(1)}, u32[]{:S(2)}, u32[]{:S(2)}) async-start(bf16[16,16,1152]{2,1,0:T(8,128)(2,1)} %bitcast.14), calls=%async_computation.2 | async-start | bytes 1179648 | tf_op jit(solution)/shard_map/all_to_all | solution.py:608
  97.7 9.5 %collective-permute-start.14 = (bf16[24,16,128]{2,1,0:T(8,128)(2,1)S(1)}, bf16[24,16,128]{2,1,0:T(8,128)(2,1)S(1)}, u32[]{:S(2)}, u32[]{:S(2)}) collective-permute-start(bf16[24,16,128]{2,1,0:T(8,128)(2,1)S(1)} %get-tuple-element.75.near_ref), channel_id=1, source_target_pairs={{0,96},{32,128},{64,160},{96,192},{128,224},{160,0},{192,32},{224,... | collective-permute-start | bytes 294920 | tf_op jit(solution)/shard_map/ppermute | solution.py:557
  98.1 10.3 %collective-permute-start.15 = (bf16[16,16,128]{2,1,0:T(8,128)(2,1)S(1)}, bf16[16,16,128]{2,1,0:T(8,128)(2,1)S(1)}, u32[]{:S(2)}, u32[]{:S(2)}) collective-permute-start(bf16[16,16,128]{2,1,0:T(8,128)(2,1)S(1)} %get-tuple-element.81), channel_id=1, source_target_pairs={{0,160},{32,192},{64,224},{96,0},{128,32},{160,64},{192,96},{224,1... | collective-permute-start | bytes 196616 | tf_op jit(solution)/shard_map/ppermute | solution.py:557
  108.4 6.1 %collective-permute-start.16 = (bf16[1,22,16,128]{3,2,1,0:T(8,128)(2,1)S(1)}, bf16[1,22,16,128]{3,2,1,0:T(8,128)(2,1)S(1)}, u32[]{:S(2)}, u32[]{:S(2)}) collective-permute-start(bf16[1,22,16,128]{3,2,1,0:T(8,128)(2,1)S(1)} %get-tuple-element.82.refs_0_), channel_id=1, source_target_pairs={{0,16},{4,20},{8,24},{12,28},{16,0},{20,4},{24,8},{28,12},{1,17},{... | collective-permute-start | bytes 270344 | tf_op jit(solution)/shard_map/ppermute | solution.py:535
  110.0 4.5 %collective-permute-start.18 = (bf16[1,21,16,128]{3,2,1,0:T(8,128)(2,1)S(1)}, bf16[1,21,16,128]{3,2,1,0:T(8,128)(2,1)S(1)}, u32[]{:S(2)}, u32[]{:S(2)}) collective-permute-start(bf16[1,21,16,128]{3,2,1,0:T(8,128)(2,1)S(1)} %get-tuple-element.84.refs_4_), channel_id=1, source_target_pairs={{0,12},{4,8},{8,4},{12,0},{16,28},{20,24},{24,20},{28,16},{1,13},{... | collective-permute-start | bytes 258056 | tf_op jit(solution)/shard_map/ppermute | solution.py:535
  114.6 6.4 %collective-permute-start.19 = (bf16[2,22,16,128]{3,2,1,0:T(8,128)(2,1)S(1)}, bf16[2,22,16,128]{3,2,1,0:T(8,128)(2,1)S(1)}, u32[]{:S(2)}, u32[]{:S(2)}) collective-permute-start(bf16[2,22,16,128]{3,2,1,0:T(8,128)(2,1)S(1)} %get-tuple-element.85.refs_0_), channel_id=1, source_target_pairs={{0,12},{4,8},{8,4},{12,0},{16,28},{20,24},{24,20},{28,16},{1,13},{... | collective-permute-start | bytes 540680 | tf_op jit(solution)/shard_map/ppermute | solution.py:535
  121.0 7.4 %collective-permute-start.22 = (bf16[4,22,16,128]{3,2,1,0:T(8,128)(2,1)S(1)}, bf16[4,22,16,128]{3,2,1,0:T(8,128)(2,1)S(1)}, u32[]{:S(2)}, u32[]{:S(2)}) collective-permute-start(bf16[4,22,16,128]{3,2,1,0:T(8,128)(2,1)S(1)} %get-tuple-element.88.refs_0_), channel_id=1, source_target_pairs={{0,4},{4,0},{8,12},{12,8},{16,20},{20,16},{24,28},{28,24},{1,5},{5... | collective-permute-start | bytes 1081352 | tf_op jit(solution)/shard_map/ppermute | solution.py:535
  121.4 11.7 %collective-permute-start.26 = (bf16[4,21,16,128]{3,2,1,0:T(8,128)(2,1)S(1)}, bf16[4,21,16,128]{3,2,1,0:T(8,128)(2,1)S(1)}, u32[]{:S(2)}, u32[]{:S(2)}) collective-permute-start(bf16[4,21,16,128]{3,2,1,0:T(8,128)(2,1)S(1)} %get-tuple-element.89.refs_1_), channel_id=1, source_target_pairs={{0,2},{2,0},{1,3},{3,1},{4,6},{6,4},{5,7},{7,5},{8,10},{10,8},{9,1... | collective-permute-start | bytes 1032200 | tf_op jit(solution)/shard_map/ppermute | solution.py:535
  125.8 10.5 %collective-permute-start.23 = (bf16[4,21,16,128]{3,2,1,0:T(8,128)(2,1)S(1)}, bf16[4,21,16,128]{3,2,1,0:T(8,128)(2,1)S(1)}, u32[]{:S(2)}, u32[]{:S(2)}) collective-permute-start(bf16[4,21,16,128]{3,2,1,0:T(8,128)(2,1)S(1)} %get-tuple-element.89.refs_1_), channel_id=1, source_target_pairs={{0,12},{4,8},{8,4},{12,0},{16,28},{20,24},{24,20},{28,16},{1,13},{... | collective-permute-start | bytes 1032200 | tf_op jit(solution)/shard_map/ppermute | solution.py:535
  126.8 10.7 %collective-permute-start.24 = (bf16[4,21,16,128]{3,2,1,0:T(8,128)(2,1)S(1)}, bf16[4,21,16,128]{3,2,1,0:T(8,128)(2,1)S(1)}, u32[]{:S(2)}, u32[]{:S(2)}) collective-permute-start(bf16[4,21,16,128]{3,2,1,0:T(8,128)(2,1)S(1)} %get-tuple-element.90.refs_2_), channel_id=1, source_target_pairs={{0,16},{4,20},{8,24},{12,28},{16,0},{20,4},{24,8},{28,12},{1,17},{... | collective-permute-start | bytes 1032200 | tf_op jit(solution)/shard_map/ppermute | solution.py:535
  127.6 11.0 %collective-permute-start.25 = (bf16[4,22,16,128]{3,2,1,0:T(8,128)(2,1)S(1)}, bf16[4,22,16,128]{3,2,1,0:T(8,128)(2,1)S(1)}, u32[]{:S(2)}, u32[]{:S(2)}) collective-permute-start(bf16[4,22,16,128]{3,2,1,0:T(8,128)(2,1)S(1)} %get-tuple-element.88.refs_0_), channel_id=1, source_target_pairs={{0,2},{2,0},{1,3},{3,1},{4,6},{6,4},{5,7},{7,5},{8,10},{10,8},{9,1... | collective-permute-start | bytes 1081352 | tf_op jit(solution)/shard_map/ppermute | solution.py:535
  128.5 10.8 %collective-permute-start.28 = (bf16[4,22,16,128]{3,2,1,0:T(8,128)(2,1)S(1)}, bf16[4,22,16,128]{3,2,1,0:T(8,128)(2,1)S(1)}, u32[]{:S(2)}, u32[]{:S(2)}) collective-permute-start(bf16[4,22,16,128]{3,2,1,0:T(8,128)(2,1)S(1)} %collective-permute-done.22.refs_3_), channel_id=1, source_target_pairs={{0,2},{2,0},{1,3},{3,1},{4,6},{6,4},{5,7},{7,5},{8,10},{10,8},{9,1... | collective-permute-start | bytes 1081352 | tf_op jit(solution)/shard_map/ppermute | solution.py:535
  133.1 5.4 %collective-permute-start.27 = (bf16[4,21,16,128]{3,2,1,0:T(8,128)(2,1)S(1)}, bf16[4,21,16,128]{3,2,1,0:T(8,128)(2,1)S(1)}, u32[]{:S(2)}, u32[]{:S(2)}) collective-permute-start(bf16[4,21,16,128]{3,2,1,0:T(8,128)(2,1)S(1)} %get-tuple-element.90.refs_2_), channel_id=1, source_target_pairs={{0,2},{2,0},{1,3},{3,1},{4,6},{6,4},{5,7},{7,5},{8,10},{10,8},{9,1... | collective-permute-start | bytes 1032200 | tf_op jit(solution)/shard_map/ppermute | solution.py:535
  (18 other events, 55.3 us)

commit v8 on v7

--- a/solution.py
+++ b/solution.py
@@ -226,13 +226,20 @@
     )(core, x, affine, wt, qg, kg)
 
 
-def split_kernel(core_ref, which_ref, x_ref, affine_ref, wt_hbm, gp_keep_ref, gp_send_ref, att_ref,
-                 send_ref, keep_ref, wt_s, gp_s, sems):
+def split_kernel(core_ref, which_ref, x_hbm, affine_hbm, wt_hbm, gp_keep_hbm, gp_send_hbm, att_hbm,
+                 send_ref, keep_ref, x_ref, affine_ref, wt_s, gp_keep_ref, gp_send_ref, att_ref, gp_s, sems):
     tokens, _ = x_ref.shape
     width = affine_ref.shape[1]
     hw = att_ref.shape[0]
     parts = [pl.ds(part * hw, hw) for part in range(3)]
-    copies = fetch([(wt_hbm.at[rows], wt_s.at[rows]) for rows in parts], sems)
+    copies = fetch(
+        [(x_hbm, x_ref), (gp_keep_hbm, gp_keep_ref), (gp_send_hbm, gp_send_ref)]
+        + [(wt_hbm.at[rows], wt_s.at[rows]) for rows in parts]
+        + [(affine_hbm, affine_ref), (att_hbm, att_ref)],
+        sems,
+    )
+    for copy in copies[:3]:
+        copy.wait()
     unit, inverse = unit_of(x_ref[:, :width].astype(F32))
     ident = eye(tokens)
     size = gp_keep_ref.shape[0]
@@ -242,11 +249,13 @@
     for part in range(3):
         at = slice(part * hw, (part + 1) * hw)
         rows = mm(ident, gp_s[at, :], NT).astype(BF)
-        copies[part].wait()
+        copies[3 + part].wait()
         grad = grad + mm(rows, wt_s[at, :], NN)
     half = width // 2
     win = send_ref.shape[1]
     mine_low = which_ref[0] == 0
+    for copy in copies[6:]:
+        copy.wait()
     scaled = grad * affine_ref[1:2]
     first = jnp.sum(scaled, axis=1, keepdims=True)
     second = jnp.sum(scaled * unit, axis=1, keepdims=True)
@@ -276,17 +285,14 @@
     vmem = pl.BlockSpec(memory_space=pltpu.VMEM)
     return pl.pallas_call(
         split_kernel,
-        in_specs=[smem, smem, vmem, vmem, pl.BlockSpec(memory_space=pltpu.HBM), vmem, vmem, vmem],
+        in_specs=[smem, smem] + [pl.BlockSpec(memory_space=pltpu.HBM)] * 6,
         out_shape=(
             jax.ShapeDtypeStruct((tokens, win), BF),
             jax.ShapeDtypeStruct((tokens, 2 * win + window_of(hw)), F32),
         ),
-        scratch_shapes=[
-            pltpu.VMEM(wt.shape, BF),
-            pltpu.VMEM((wt.shape[0], tokens), BF),
-            pltpu.SemaphoreType.DMA((3,)),
-        ],
-        compiler_params=pltpu.CompilerParams(vmem_limit_bytes=30 * 2**20),
+        scratch_shapes=[pltpu.VMEM(a.shape, a.dtype) for a in (x, affine, wt, gp_keep, gp_send, att)]
+        + [pltpu.VMEM((wt.shape[0], tokens), BF), pltpu.SemaphoreType.DMA((8,))],
+        compiler_params=pltpu.CompilerParams(vmem_limit_bytes=58 * 2**20),
         name="split",
     )(core, which, x, affine, wt, gp_keep, gp_send, att)
 
@@ -558,17 +564,18 @@
 
 
 def gather_clips(own, home):
-    near, two = trio(own, shift(own, "dp", 1), shift(own, "dp", -1))
-    near, two, home = lax.optimization_barrier((near, two, home))
+    below, above = shift(own, "dp", 1), shift(own, "dp", -1)
+    near, two = trio(own, below, above)
     return near, shift(near, "dp", 3), shift(two, "dp", -3), home
 
 
-def gather_plane(have, where, half, rows, width):
-    have = join(list(zip(have, meet(have, 2))))
+def gather_plane(have, where, half, rows, width, beside):
+    got, beside = lax.optimization_barrier((meet(have, 2), beside))
+    have = join(list(zip(have, got)))
     have = join(list(zip(have, meet(have, 1))))
     pieces = list(have) + meet(have, 0)
     pieces = pieces + [swap(piece, ("core",), 1) for piece in pieces]
-    return untile(where, half, pieces, rows, width)
+    return untile(where, half, pieces, rows, width), beside
 
 
 def body(latent, mod_shift, mod_scale, w_qkv, q_gain, k_gain, cotangent):
@@ -601,16 +608,15 @@
     own, send = lax.optimization_barrier((own, send))
     recv = lax.ppermute(send, "tensor", [(0, 1), (1, 0)])
     own = exchange(own.reshape((clips, own.shape[0] // clips) + own.shape[1:]), "dp")
+    own = reduce(own, 1.0 / math.sqrt(clips * frames * patches))
     own, recv = lax.optimization_barrier((own, recv))
-    own = reduce(own, 1.0 / math.sqrt(clips * frames * patches))
     home = finish(which, recv, keep, width).reshape(frames, own_patches, width)
     near, below, above, home = gather_clips(own, home)
     home = lax.all_to_all(home, SEQ, split_axis=0, concat_axis=0, tiled=True)
-    below, home = lax.optimization_barrier((below, home))
-    grad_t, att_t = unpack(home.reshape(patches, width))
     clip = lax.axis_index("dp").astype(jnp.int32).reshape(1)
     have = place(clip, near, below, above, clips)
-    grad_qkv = gather_plane(have, where, core, 3 * hw, width)
+    grad_qkv, home = gather_plane(have, where, core, 3 * hw, width, home)
+    grad_t, att_t = unpack(home.reshape(patches, width))
     grad_qkv = grad_qkv.reshape(3, hw, width).transpose(2, 0, 1)
     return (att_t.T[None, None], grad_t.T[None, None], grad_qkv)
 

time: 144 us -> 145 us (level)
  local copies, waits for them, and re-layouts: 9.19 us -> 3.17 us
  waiting for transfers between devices: 47 us -> 50.8 us
  Pallas kernels: 23.5 us -> 25.9 us
    unnamed x16 -> x12, local copies, waits for them, and re-layouts: 7.7 us -> 1.67 us
    ppermute x1, waiting for transfers between devices: 5.19 us -> 0.01 us  [body(): recv = lax.ppermute(send, 'tensor', [(0, 1), (1, 0)])]
    all_to_all x1, waiting for transfers between devices: 1.79 us -> 6.87 us  [exchange(): return lax.all_to_all(parts, axis, split_axis=0, concat_axis=0, tiled=True)]
    ppermute x26, waiting for transfers between devices: 20.1 us -> 23.4 us  [swap(): return lax.ppermute(x, axes, [(i, i ^ k) for i in range(count)])]
    pallas_call x1, Pallas kernels: 3.74 us -> 6.28 us  [split(): pl.pallas_call(split_kernel, in_specs=[smem, smem] + [pl.BlockSpec(memory...]
    ppermute x26, starting transfers between devices: 26.1 us -> 28.3 us  [swap(): return lax.ppermute(x, axes, [(i, i ^ k) for i in range(count)])]
    ppermute x4, waiting for transfers between devices: 7.26 us -> 9.01 us  [shift(): lax.ppermute(x, axis, [(i, (i + step) % count) for i in range(count)])]
  transfers between devices with their start and end apart: 34 -> 34, of which waited for: 20 -> 20; matrix products, arithmetic and copies ran while one was open for 2% -> 2% of each run, Pallas kernels for 4% -> 5%
where the time goes in v8:
time: 145 us; the launch traced here: 143 us
  starting transfers between devices  61.4 us (42%)
  waiting for transfers between devices  50.8 us (35%)
  Pallas kernels  25.9 us (18%)
  local copies, waits for them, and re-layouts  3.17 us (2%)
    ppermute x26, starting transfers between devices, swap(): return lax.ppermute(x, axes, [(i, i ^ k) for i in range(count)])  28.3 us
    ppermute x26, waiting for transfers between devices, swap(): return lax.ppermute(x, axes, [(i, i ^ k) for i in range(count)])  23.4 us
    all_to_all x1, waiting for transfers between devices, body(): lax.all_to_all(x, SEQ, split_axis=0, concat_axis=0, tiled=True)  11.5 us
    all_to_all x1, starting transfers between devices, body(): home = lax.all_to_all(home, SEQ, split_axis=0, concat_axis=0, tiled=True)  9.51 us
    ppermute x4, waiting for transfers between devices, shift(): lax.ppermute(x, axis, [(i, (i + step) % count) for i in range(count)])  9.01 us
    all_to_all x1, starting transfers between devices, exchange(): return lax.all_to_all(parts, axis, split_axis=0, concat_axis=0, tiled=True)  8.17 us
    pallas_call x1, Pallas kernels, attend(): pl.pallas_call(functools.partial(attend_kernel, patches=patches, heads=he...  7.12 us
    all_to_all x1, starting transfers between devices, body(): lax.all_to_all(x, SEQ, split_axis=0, concat_axis=0, tiled=True)  6.93 us
  transfers between devices with their start and end apart: 34, of which 20 were waited for; matrix products, arithmetic and copies ran while one was open for 2% of the time, Pallas kernels for 5%

profile of v8, /device:TPU:1, one launch (start us, length us, event | category | flops | bytes accessed | tf_op | source)
XLA Modules:
  0.0 143.4 jit_solution(3734394724330484438)
XLA Ops:
  0.6 2.2 %pack.1 = bf16[256,1728]{1,0:T(8,128)(2,1)} custom-call(bf16[256,1152]{1,0:T(8,128)(2,1)} %bitcast.34, bf16[576,256]{1,0:T(8,128)(2,1)} %bitcast.35), custom_call_target="tpu_custom_call" | custom-call | tf_op jit(solution)/shard_map/pack/pallas_call | solution.py:52
  2.9 6.9 %all-to-all-start = ((bf16[16,16,1728]{2,1,0:T(8,128)(2,1)}), bf16[16,16,1728]{2,1,0:T(8,128)(2,1)S(1)}, u32[]{:S(2)}, u32[]{:S(2)}) async-start(bf16[16,16,1728]{2,1,0:T(8,128)(2,1)} %bitcast.33), calls=%async_computation | async-start | bytes 1835008 | tf_op jit(solution)/shard_map/all_to_all | solution.py:593
  12.7 11.5 %all-to-all-done = bf16[16,16,1728]{2,1,0:T(8,128)(2,1)S(1)} async-done(((bf16[16,16,1728]{2,1,0:T(8,128)(2,1)}), bf16[16,16,1728]{2,1,0:T(8,128)(2,1)S(1)}, u32[]{:S(2)}, u32[]{:S(2)}) %all-to-all-start) | async-done | bytes 884768 | tf_op jit(solution)/shard_map/all_to_all | solution.py:593
  25.1 7.1 %attend.1 = (bf16[256,1152]{1,0:T(8,128)(2,1)S(1)}, bf16[864,256]{1,0:T(8,128)(2,1)S(1)}, bf16[864,256]{1,0:T(8,128)(2,1)S(1)}, bf16[576,256]{1,0:T(8,128)(2,1)S(1)}) custom-call(s32[1]{0:T(128)} %bitcast.2.core_ref.half_ref, bf16[256,1728]{1,0:T(8,128)(2,1)} %bitcast.30, f32[2,1152]{1,0:T(2,128)S(1)} %pad_maximum_fusion.affine_ref.affine_hbm, ...), custom_call_target="tpu_custom_call" | custom-call | tf_op jit(solution)/shard_map/attend/pallas_call | solution.py:203
  33.9 2.3 %collective-permute-done.gp_b = bf16[864,256]{1,0:T(8,128)(2,1)S(1)} collective-permute-done((bf16[864,256]{1,0:T(8,128)(2,1)S(1)}, bf16[864,256]{1,0:T(8,128)(2,1)S(1)}, u32[]{:S(2)}, u32[]{:S(2)}) %collective-permute-start) | collective-permute-done | bytes 442400 | tf_op jit(solution)/shard_map/ppermute | solution.py:541
  36.1 2.3 %outer.1 = (bf16[4,22,16,128]{3,2,1,0:T(8,128)(2,1)}, bf16[4,21,16,128]{3,2,1,0:T(8,128)(2,1)}, bf16[4,21,16,128]{3,2,1,0:T(8,128)(2,1)}, bf16[4,64,16,128]{3,2,1,0:T(8,128)(2,1)S(1)}) custom-call(s32[1]{0:T(128)} %bitcast.1.where_ref, bf16[864,256]{1,0:T(8,128)(2,1)S(1)} %get-tuple-element.46.gp_a.gp_keep_hbm, ...), custom_call_target="tpu_custom_call" | custom-call | tf_op jit(solution)/shard_map/outer/pallas_call | solution.py:330
  40.1 6.3 %split.1 = (bf16[256,640]{1,0:T(8,128)(2,1)}, f32[256,1920]{1,0:T(8,128)}) custom-call(s32[1]{0:T(128)} %bitcast.2.core_ref.half_ref, s32[1]{0:T(128)} %bitcast.12.which_ref, bf16[256,1728]{1,0:T(8,128)(2,1)} %bitcast.31, f32[2,1152]{1,0:T(2,128)} %copy-done.4, bf16[1728,1152]{1,0:T(8,128)(2,1)} %bitcast.29, bf16[864,256]{1,0:T(8,128)(2,1)} %copy-done.1, ...), custom_call_target="tpu_custom_call" | custom-call | tf_op jit(solution)/shard_map/split/pallas_call | solution.py:286
  46.4 2.8 %collective-permute-done.3.refs_1_ = bf16[4,21,16,128]{3,2,1,0:T(8,128)(2,1)} collective-permute-done((bf16[4,21,16,128]{3,2,1,0:T(8,128)(2,1)}, bf16[4,21,16,128]{3,2,1,0:T(8,128)(2,1)}, u32[]{:S(2)}, u32[]{:S(2)}) %collective-permute-start.3) | collective-permute-done | bytes 344096 | tf_op jit(solution)/shard_map/ppermute | solution.py:541
  52.3 4.5 %collective-permute-done.6.refs_1_ = bf16[2,21,16,128]{3,2,1,0:T(8,128)(2,1)S(1)} collective-permute-done((bf16[2,21,16,128]{3,2,1,0:T(8,128)(2,1)S(1)}, bf16[2,21,16,128]{3,2,1,0:T(8,128)(2,1)S(1)}, u32[]{:S(2)}, u32[]{:S(2)}) %collective-permute-start.6) | collective-permute-done | bytes 172064 | tf_op jit(solution)/shard_map/ppermute | solution.py:541
  63.8 8.2 %all-to-all-start.1 = ((bf16[8,8,16,128]{3,2,1,0:T(8,128)(2,1)}), bf16[8,8,16,128]{3,2,1,0:T(8,128)(2,1)S(1)}, u32[]{:S(2)}, u32[]{:S(2)}) async-start(bf16[8,8,16,128]{3,2,1,0:T(8,128)(2,1)} %bitcast.14), calls=%async_computation.1 | async-start | bytes 524288 | tf_op jit(solution)/shard_map/all_to_all | solution.py:546
  72.0 2.5 %collective-permute-start.11 = (bf16[256,640]{1,0:T(8,128)(2,1)}, bf16[256,640]{1,0:T(8,128)(2,1)S(1)}, u32[]{:S(2)}, u32[]{:S(2)}) collective-permute-start(bf16[256,640]{1,0:T(8,128)(2,1)} %get-tuple-element.68), channel_id=1, source_target_pairs={{0,1},{1,0},{2,3},{3,2},{4,5},{5,4},{6,7},{7,6},{8,9},{9,8},{10,11... | collective-permute-start | bytes 983048 | tf_op jit(solution)/shard_map/ppermute | solution.py:609
  74.4 6.9 %all-to-all-done.1.parts_ref = bf16[8,8,16,128]{3,2,1,0:T(8,128)(2,1)S(1)} async-done(((bf16[8,8,16,128]{3,2,1,0:T(8,128)(2,1)}), bf16[8,8,16,128]{3,2,1,0:T(8,128)(2,1)S(1)}, u32[]{:S(2)}, u32[]{:S(2)}) %all-to-all-start.1) | async-done | bytes 262176 | tf_op jit(solution)/shard_map/all_to_all | solution.py:546
  82.9 9.5 %all-to-all-start.2 = ((bf16[16,16,1152]{2,1,0:T(8,128)(2,1)}), bf16[16,16,1152]{2,1,0:T(8,128)(2,1)S(1)}, u32[]{:S(2)}, u32[]{:S(2)}) async-start(bf16[16,16,1152]{2,1,0:T(8,128)(2,1)} %bitcast.15), calls=%async_computation.2 | async-start | bytes 1179648 | tf_op jit(solution)/shard_map/all_to_all | solution.py:615
  95.2 2.7 %collective-permute-done.12.below_ref = bf16[8,16,128]{2,1,0:T(8,128)(2,1)S(1)} collective-permute-done((bf16[8,16,128]{2,1,0:T(8,128)(2,1)S(1)}, bf16[8,16,128]{2,1,0:T(8,128)(2,1)S(1)}, u32[]{:S(2)}, u32[]{:S(2)}) %collective-permute-start.12) | collective-permute-done | bytes 32800 | tf_op jit(solution)/shard_map/ppermute | solution.py:563
  98.3 4.2 %collective-permute-start.15 = (bf16[16,16,128]{2,1,0:T(8,128)(2,1)S(1)}, bf16[16,16,128]{2,1,0:T(8,128)(2,1)S(1)}, u32[]{:S(2)}, u32[]{:S(2)}) collective-permute-start(bf16[16,16,128]{2,1,0:T(8,128)(2,1)S(1)} %get-tuple-element.71), channel_id=1, source_target_pairs={{0,160},{32,192},{64,224},{96,0},{128,32},{160,64},{192,96},{224,1... | collective-permute-start | bytes 196616 | tf_op jit(solution)/shard_map/ppermute | solution.py:563
  102.5 2.2 %collective-permute-done.15.above_ref = bf16[16,16,128]{2,1,0:T(8,128)(2,1)S(1)} collective-permute-done((bf16[16,16,128]{2,1,0:T(8,128)(2,1)S(1)}, bf16[16,16,128]{2,1,0:T(8,128)(2,1)S(1)}, u32[]{:S(2)}, u32[]{:S(2)}) %collective-permute-start.15) | collective-permute-done | bytes 65568 | tf_op jit(solution)/shard_map/ppermute | solution.py:563
  104.6 2.8 %collective-permute-done.14.below_ref = bf16[24,16,128]{2,1,0:T(8,128)(2,1)S(1)} collective-permute-done((bf16[24,16,128]{2,1,0:T(8,128)(2,1)S(1)}, bf16[24,16,128]{2,1,0:T(8,128)(2,1)S(1)}, u32[]{:S(2)}, u32[]{:S(2)}) %collective-permute-start.14) | collective-permute-done | bytes 98336 | tf_op jit(solution)/shard_map/ppermute | solution.py:563
  109.1 2.3 %collective-permute-start.18 = (bf16[1,21,16,128]{3,2,1,0:T(8,128)(2,1)S(1)}, bf16[1,21,16,128]{3,2,1,0:T(8,128)(2,1)S(1)}, u32[]{:S(2)}, u32[]{:S(2)}) collective-permute-start(bf16[1,21,16,128]{3,2,1,0:T(8,128)(2,1)S(1)} %get-tuple-element.74.refs_4_), channel_id=1, source_target_pairs={{0,12},{4,8},{8,4},{12,0},{16,28},{20,24},{24,20},{28,16},{1,13},{... | collective-permute-start | bytes 258056 | tf_op jit(solution)/shard_map/ppermute | solution.py:541
  113.7 2.4 %collective-permute-start.19 = (bf16[2,22,16,128]{3,2,1,0:T(8,128)(2,1)S(1)}, bf16[2,22,16,128]{3,2,1,0:T(8,128)(2,1)S(1)}, u32[]{:S(2)}, u32[]{:S(2)}) collective-permute-start(bf16[2,22,16,128]{3,2,1,0:T(8,128)(2,1)S(1)} %get-tuple-element.83.refs_0_), channel_id=1, source_target_pairs={{0,12},{4,8},{8,4},{12,0},{16,28},{20,24},{24,20},{28,16},{1,13},{... | collective-permute-start | bytes 540680 | tf_op jit(solution)/shard_map/ppermute | solution.py:541
  116.9 3.5 %collective-permute-done.20.refs_3_ = bf16[2,21,16,128]{3,2,1,0:T(8,128)(2,1)S(1)} collective-permute-done((bf16[2,21,16,128]{3,2,1,0:T(8,128)(2,1)S(1)}, bf16[2,21,16,128]{3,2,1,0:T(8,128)(2,1)S(1)}, u32[]{:S(2)}, u32[]{:S(2)}) %collective-permute-start.20) | collective-permute-done | bytes 172064 | tf_op jit(solution)/shard_map/ppermute | solution.py:541
  121.6 5.4 %collective-permute-start.26 = (bf16[4,21,16,128]{3,2,1,0:T(8,128)(2,1)S(1)}, bf16[4,21,16,128]{3,2,1,0:T(8,128)(2,1)S(1)}, u32[]{:S(2)}, u32[]{:S(2)}) collective-permute-start(bf16[4,21,16,128]{3,2,1,0:T(8,128)(2,1)S(1)} %get-tuple-element.87.refs_1_), channel_id=1, source_target_pairs={{0,2},{2,0},{1,3},{3,1},{4,6},{6,4},{5,7},{7,5},{8,10},{10,8},{9,1... | collective-permute-start | bytes 1032200 | tf_op jit(solution)/shard_map/ppermute | solution.py:541
  130.5 3.8 %collective-permute-start.28 = (bf16[4,22,16,128]{3,2,1,0:T(8,128)(2,1)S(1)}, bf16[4,22,16,128]{3,2,1,0:T(8,128)(2,1)S(1)}, u32[]{:S(2)}, u32[]{:S(2)}) collective-permute-start(bf16[4,22,16,128]{3,2,1,0:T(8,128)(2,1)S(1)} %collective-permute-done.22.refs_3_), channel_id=1, source_target_pairs={{0,2},{2,0},{1,3},{3,1},{4,6},{6,4},{5,7},{7,5},{8,10},{10,8},{9,1... | collective-permute-start | bytes 1081352 | tf_op jit(solution)/shard_map/ppermute | solution.py:541
  134.3 3.2 %collective-permute-done.23.refs_4_ = bf16[4,21,16,128]{3,2,1,0:T(8,128)(2,1)S(1)} collective-permute-done((bf16[4,21,16,128]{3,2,1,0:T(8,128)(2,1)S(1)}, bf16[4,21,16,128]{3,2,1,0:T(8,128)(2,1)S(1)}, u32[]{:S(2)}, u32[]{:S(2)}) %collective-permute-start.23) | collective-permute-done | bytes 344096 | tf_op jit(solution)/shard_map/ppermute | solution.py:541
  140.5 2.9 %untile.1 = bf16[1728,1152]{1,0:T(8,128)(2,1)} custom-call(s32[1]{0:T(128)} %bitcast.1.where_ref, s32[1]{0:T(128)} %bitcast.2.core_ref.half_ref, bf16[4,22,16,128]{3,2,1,0:T(8,128)(2,1)S(1)} %get-tuple-element.86.refs_0_, bf16[4,21,16,128]{3,2,1,0:T(8,128)(2,1)S(1)} %get-tuple-element.87.refs_1_, bf16[4,21,16,128]{3,2,1,0:T(8,128)(2,1)S(1)} %get-tuple-element.88.refs_2_, ...), custom_call_target="tpu_custom_call" | custom-call | tf_op jit(solution)/shard_map/untile/pallas_call | solution.py:529
  (75 shorter events, 34.3 us)
Async XLA Ops:
  2.9 21.3 %all-to-all-start = ((bf16[16,16,1728]{2,1,0:T(8,128)(2,1)}), bf16[16,16,1728]{2,1,0:T(8,128)(2,1)S(1)}, u32[]{:S(2)}, u32[]{:S(2)}) async-start(bf16[16,16,1728]{2,1,0:T(8,128)(2,1)} %bitcast.33), calls=%async_computation | async-start | bytes 1835008 | tf_op jit(solution)/shard_map/all_to_all | solution.py:593
  38.5 10.8 %collective-permute-start.2 = (bf16[4,22,16,128]{3,2,1,0:T(8,128)(2,1)}, bf16[4,22,16,128]{3,2,1,0:T(8,128)(2,1)S(1)}, u32[]{:S(2)}, u32[]{:S(2)}) collective-permute-start(bf16[4,22,16,128]{3,2,1,0:T(8,128)(2,1)} %get-tuple-element.50), channel_id=1, source_target_pairs={{0,4},{4,0},{8,12},{12,8},{16,20},{20,16},{24,28},{28,24},{1,5},{5... | collective-permute-start | bytes 1081352 | tf_op jit(solution)/shard_map/ppermute | solution.py:541
  38.5 10.8 %collective-permute-start.3 = (bf16[4,21,16,128]{3,2,1,0:T(8,128)(2,1)}, bf16[4,21,16,128]{3,2,1,0:T(8,128)(2,1)}, u32[]{:S(2)}, u32[]{:S(2)}) collective-permute-start(bf16[4,21,16,128]{3,2,1,0:T(8,128)(2,1)} %get-tuple-element.51), channel_id=1, source_target_pairs={{0,12},{4,8},{8,4},{12,0},{16,28},{20,24},{24,20},{28,16},{1,13},{... | collective-permute-start | bytes 1032200 | tf_op jit(solution)/shard_map/ppermute | solution.py:541
  39.6 9.7 %collective-permute-start.4 = (bf16[4,21,16,128]{3,2,1,0:T(8,128)(2,1)}, bf16[4,21,16,128]{3,2,1,0:T(8,128)(2,1)}, u32[]{:S(2)}, u32[]{:S(2)}) collective-permute-start(bf16[4,21,16,128]{3,2,1,0:T(8,128)(2,1)} %get-tuple-element.52), channel_id=1, source_target_pairs={{0,16},{4,20},{8,24},{12,28},{16,0},{20,4},{24,8},{28,12},{1,17},{... | collective-permute-start | bytes 1032200 | tf_op jit(solution)/shard_map/ppermute | solution.py:541
  50.6 6.3 %collective-permute-start.5 = (bf16[2,22,16,128]{3,2,1,0:T(8,128)(2,1)S(1)}, bf16[2,22,16,128]{3,2,1,0:T(8,128)(2,1)S(1)}, u32[]{:S(2)}, u32[]{:S(2)}) collective-permute-start(bf16[2,22,16,128]{3,2,1,0:T(8,128)(2,1)S(1)} %get-tuple-element.59), channel_id=1, source_target_pairs={{0,12},{4,8},{8,4},{12,0},{16,28},{20,24},{24,20},{28,16},{1,13},{... | collective-permute-start | bytes 540680 | tf_op jit(solution)/shard_map/ppermute | solution.py:541
  52.2 4.6 %collective-permute-start.6 = (bf16[2,21,16,128]{3,2,1,0:T(8,128)(2,1)S(1)}, bf16[2,21,16,128]{3,2,1,0:T(8,128)(2,1)S(1)}, u32[]{:S(2)}, u32[]{:S(2)}) collective-permute-start(bf16[2,21,16,128]{3,2,1,0:T(8,128)(2,1)S(1)} %get-tuple-element.60), channel_id=1, source_target_pairs={{0,16},{4,20},{8,24},{12,28},{16,0},{20,4},{24,8},{28,12},{1,17},{... | collective-permute-start | bytes 516104 | tf_op jit(solution)/shard_map/ppermute | solution.py:541
  52.3 4.6 %collective-permute-start.7 = (bf16[2,21,16,128]{3,2,1,0:T(8,128)(2,1)S(1)}, bf16[2,21,16,128]{3,2,1,0:T(8,128)(2,1)S(1)}, u32[]{:S(2)}, u32[]{:S(2)}) collective-permute-start(bf16[2,21,16,128]{3,2,1,0:T(8,128)(2,1)S(1)} %get-tuple-element.61), channel_id=1, source_target_pairs={{0,4},{4,0},{8,12},{12,8},{16,20},{20,16},{24,28},{28,24},{1,5},{5... | collective-permute-start | bytes 516104 | tf_op jit(solution)/shard_map/ppermute | solution.py:541
  57.1 6.0 %collective-permute-start.8 = (bf16[1,22,16,128]{3,2,1,0:T(8,128)(2,1)S(1)}, bf16[1,22,16,128]{3,2,1,0:T(8,128)(2,1)S(1)}, u32[]{:S(2)}, u32[]{:S(2)}) collective-permute-start(bf16[1,22,16,128]{3,2,1,0:T(8,128)(2,1)S(1)} %get-tuple-element.63), channel_id=1, source_target_pairs={{0,16},{4,20},{8,24},{12,28},{16,0},{20,4},{24,8},{28,12},{1,17},{... | collective-permute-start | bytes 270344 | tf_op jit(solution)/shard_map/ppermute | solution.py:541
  58.5 4.5 %collective-permute-start.10 = (bf16[1,21,16,128]{3,2,1,0:T(8,128)(2,1)S(1)}, bf16[1,21,16,128]{3,2,1,0:T(8,128)(2,1)S(1)}, u32[]{:S(2)}, u32[]{:S(2)}) collective-permute-start(bf16[1,21,16,128]{3,2,1,0:T(8,128)(2,1)S(1)} %get-tuple-element.65), channel_id=1, source_target_pairs={{0,12},{4,8},{8,4},{12,0},{16,28},{20,24},{24,20},{28,16},{1,13},{... | collective-permute-start | bytes 258056 | tf_op jit(solution)/shard_map/ppermute | solution.py:541
  63.8 17.5 %all-to-all-start.1 = ((bf16[8,8,16,128]{3,2,1,0:T(8,128)(2,1)}), bf16[8,8,16,128]{3,2,1,0:T(8,128)(2,1)S(1)}, u32[]{:S(2)}, u32[]{:S(2)}) async-start(bf16[8,8,16,128]{3,2,1,0:T(8,128)(2,1)} %bitcast.14), calls=%async_computation.1 | async-start | bytes 524288 | tf_op jit(solution)/shard_map/all_to_all | solution.py:546
  72.0 9.4 %collective-permute-start.11 = (bf16[256,640]{1,0:T(8,128)(2,1)}, bf16[256,640]{1,0:T(8,128)(2,1)S(1)}, u32[]{:S(2)}, u32[]{:S(2)}) collective-permute-start(bf16[256,640]{1,0:T(8,128)(2,1)} %get-tuple-element.68), channel_id=1, source_target_pairs={{0,1},{1,0},{2,3},{3,2},{4,5},{5,4},{6,7},{7,6},{8,9},{9,8},{10,11... | collective-permute-start | bytes 983048 | tf_op jit(solution)/shard_map/ppermute | solution.py:609
  82.9 30.8 %all-to-all-start.2 = ((bf16[16,16,1152]{2,1,0:T(8,128)(2,1)}), bf16[16,16,1152]{2,1,0:T(8,128)(2,1)S(1)}, u32[]{:S(2)}, u32[]{:S(2)}) async-start(bf16[16,16,1152]{2,1,0:T(8,128)(2,1)} %bitcast.15), calls=%async_computation.2 | async-start | bytes 1179648 | tf_op jit(solution)/shard_map/all_to_all | solution.py:615
  97.9 9.6 %collective-permute-start.14 = (bf16[24,16,128]{2,1,0:T(8,128)(2,1)S(1)}, bf16[24,16,128]{2,1,0:T(8,128)(2,1)S(1)}, u32[]{:S(2)}, u32[]{:S(2)}) collective-permute-start(bf16[24,16,128]{2,1,0:T(8,128)(2,1)S(1)} %get-tuple-element.70.near_ref), channel_id=1, source_target_pairs={{0,96},{32,128},{64,160},{96,192},{128,224},{160,0},{192,32},{224,... | collective-permute-start | bytes 294920 | tf_op jit(solution)/shard_map/ppermute | solution.py:563
  98.3 6.4 %collective-permute-start.15 = (bf16[16,16,128]{2,1,0:T(8,128)(2,1)S(1)}, bf16[16,16,128]{2,1,0:T(8,128)(2,1)S(1)}, u32[]{:S(2)}, u32[]{:S(2)}) collective-permute-start(bf16[16,16,128]{2,1,0:T(8,128)(2,1)S(1)} %get-tuple-element.71), channel_id=1, source_target_pairs={{0,160},{32,192},{64,224},{96,0},{128,32},{160,64},{192,96},{224,1... | collective-permute-start | bytes 196616 | tf_op jit(solution)/shard_map/ppermute | solution.py:563
  107.5 6.2 %collective-permute-start.16 = (bf16[1,22,16,128]{3,2,1,0:T(8,128)(2,1)S(1)}, bf16[1,22,16,128]{3,2,1,0:T(8,128)(2,1)S(1)}, u32[]{:S(2)}, u32[]{:S(2)}) collective-permute-start(bf16[1,22,16,128]{3,2,1,0:T(8,128)(2,1)S(1)} %get-tuple-element.72.refs_0_), channel_id=1, source_target_pairs={{0,16},{4,20},{8,24},{12,28},{16,0},{20,4},{24,8},{28,12},{1,17},{... | collective-permute-start | bytes 270344 | tf_op jit(solution)/shard_map/ppermute | solution.py:541
  109.1 4.5 %collective-permute-start.18 = (bf16[1,21,16,128]{3,2,1,0:T(8,128)(2,1)S(1)}, bf16[1,21,16,128]{3,2,1,0:T(8,128)(2,1)S(1)}, u32[]{:S(2)}, u32[]{:S(2)}) collective-permute-start(bf16[1,21,16,128]{3,2,1,0:T(8,128)(2,1)S(1)} %get-tuple-element.74.refs_4_), channel_id=1, source_target_pairs={{0,12},{4,8},{8,4},{12,0},{16,28},{20,24},{24,20},{28,16},{1,13},{... | collective-permute-start | bytes 258056 | tf_op jit(solution)/shard_map/ppermute | solution.py:541
  113.7 7.4 %collective-permute-start.19 = (bf16[2,22,16,128]{3,2,1,0:T(8,128)(2,1)S(1)}, bf16[2,22,16,128]{3,2,1,0:T(8,128)(2,1)S(1)}, u32[]{:S(2)}, u32[]{:S(2)}) collective-permute-start(bf16[2,22,16,128]{3,2,1,0:T(8,128)(2,1)S(1)} %get-tuple-element.83.refs_0_), channel_id=1, source_target_pairs={{0,12},{4,8},{8,4},{12,0},{16,28},{20,24},{24,20},{28,16},{1,13},{... | collective-permute-start | bytes 540680 | tf_op jit(solution)/shard_map/ppermute | solution.py:541
  121.2 9.3 %collective-permute-start.22 = (bf16[4,22,16,128]{3,2,1,0:T(8,128)(2,1)S(1)}, bf16[4,22,16,128]{3,2,1,0:T(8,128)(2,1)S(1)}, u32[]{:S(2)}, u32[]{:S(2)}) collective-permute-start(bf16[4,22,16,128]{3,2,1,0:T(8,128)(2,1)S(1)} %get-tuple-element.86.refs_0_), channel_id=1, source_target_pairs={{0,4},{4,0},{8,12},{12,8},{16,20},{20,16},{24,28},{28,24},{1,5},{5... | collective-permute-start | bytes 1081352 | tf_op jit(solution)/shard_map/ppermute | solution.py:541
  121.6 12.7 %collective-permute-start.26 = (bf16[4,21,16,128]{3,2,1,0:T(8,128)(2,1)S(1)}, bf16[4,21,16,128]{3,2,1,0:T(8,128)(2,1)S(1)}, u32[]{:S(2)}, u32[]{:S(2)}) collective-permute-start(bf16[4,21,16,128]{3,2,1,0:T(8,128)(2,1)S(1)} %get-tuple-element.87.refs_1_), channel_id=1, source_target_pairs={{0,2},{2,0},{1,3},{3,1},{4,6},{6,4},{5,7},{7,5},{8,10},{10,8},{9,1... | collective-permute-start | bytes 1032200 | tf_op jit(solution)/shard_map/ppermute | solution.py:541
  127.0 10.5 %collective-permute-start.23 = (bf16[4,21,16,128]{3,2,1,0:T(8,128)(2,1)S(1)}, bf16[4,21,16,128]{3,2,1,0:T(8,128)(2,1)S(1)}, u32[]{:S(2)}, u32[]{:S(2)}) collective-permute-start(bf16[4,21,16,128]{3,2,1,0:T(8,128)(2,1)S(1)} %get-tuple-element.87.refs_1_), channel_id=1, source_target_pairs={{0,12},{4,8},{8,4},{12,0},{16,28},{20,24},{24,20},{28,16},{1,13},{... | collective-permute-start | bytes 1032200 | tf_op jit(solution)/shard_map/ppermute | solution.py:541
  127.9 10.8 %collective-permute-start.24 = (bf16[4,21,16,128]{3,2,1,0:T(8,128)(2,1)S(1)}, bf16[4,21,16,128]{3,2,1,0:T(8,128)(2,1)S(1)}, u32[]{:S(2)}, u32[]{:S(2)}) collective-permute-start(bf16[4,21,16,128]{3,2,1,0:T(8,128)(2,1)S(1)} %get-tuple-element.88.refs_2_), channel_id=1, source_target_pairs={{0,16},{4,20},{8,24},{12,28},{16,0},{20,4},{24,8},{28,12},{1,17},{... | collective-permute-start | bytes 1032200 | tf_op jit(solution)/shard_map/ppermute | solution.py:541
  129.6 10.1 %collective-permute-start.25 = (bf16[4,22,16,128]{3,2,1,0:T(8,128)(2,1)S(1)}, bf16[4,22,16,128]{3,2,1,0:T(8,128)(2,1)S(1)}, u32[]{:S(2)}, u32[]{:S(2)}) collective-permute-start(bf16[4,22,16,128]{3,2,1,0:T(8,128)(2,1)S(1)} %get-tuple-element.86.refs_0_), channel_id=1, source_target_pairs={{0,2},{2,0},{1,3},{3,1},{4,6},{6,4},{5,7},{7,5},{8,10},{10,8},{9,1... | collective-permute-start | bytes 1081352 | tf_op jit(solution)/shard_map/ppermute | solution.py:541
  130.5 10.0 %collective-permute-start.28 = (bf16[4,22,16,128]{3,2,1,0:T(8,128)(2,1)S(1)}, bf16[4,22,16,128]{3,2,1,0:T(8,128)(2,1)S(1)}, u32[]{:S(2)}, u32[]{:S(2)}) collective-permute-start(bf16[4,22,16,128]{3,2,1,0:T(8,128)(2,1)S(1)} %collective-permute-done.22.refs_3_), channel_id=1, source_target_pairs={{0,2},{2,0},{1,3},{3,1},{4,6},{6,4},{5,7},{7,5},{8,10},{10,8},{9,1... | collective-permute-start | bytes 1081352 | tf_op jit(solution)/shard_map/ppermute | solution.py:541
  134.3 5.4 %collective-permute-start.27 = (bf16[4,21,16,128]{3,2,1,0:T(8,128)(2,1)S(1)}, bf16[4,21,16,128]{3,2,1,0:T(8,128)(2,1)S(1)}, u32[]{:S(2)}, u32[]{:S(2)}) collective-permute-start(bf16[4,21,16,128]{3,2,1,0:T(8,128)(2,1)S(1)} %get-tuple-element.88.refs_2_), channel_id=1, source_target_pairs={{0,2},{2,0},{1,3},{3,1},{4,6},{6,4},{5,7},{7,5},{8,10},{10,8},{9,1... | collective-permute-start | bytes 1032200 | tf_op jit(solution)/shard_map/ppermute | solution.py:541
  (16 other events, 106.4 us)

commit v9 on v6

--- a/solution.py
+++ b/solution.py
@@ -286,7 +286,7 @@
             pltpu.VMEM((wt.shape[0], tokens), BF),
             pltpu.SemaphoreType.DMA((3,)),
         ],
-        compiler_params=pltpu.CompilerParams(vmem_limit_bytes=18 * 2**20),
+        compiler_params=pltpu.CompilerParams(vmem_limit_bytes=40 * 2**20),
         name="split",
     )(core, which, x, affine, wt, gp_keep, gp_send, att)
 
@@ -306,12 +306,11 @@
             j = (start + at) // LANES
             tiles_s[j * tiles : (j + 1) * tiles] = found[:, at : at + LANES].reshape(tiles, ROWS, LANES)
     size = tiles_s.shape[0] // 8
-    keep_ref = out_refs[-1]
-    for (lo, hi), order, send_ref in zip(bounds(size), ORDERS, out_refs):
+    for (lo, hi), order, send_ref, keep_ref in zip(bounds(size), ORDERS, out_refs[::2], out_refs[1::2]):
         for q in range(4):
             k = picked(q, order[1:])
             at = (where_ref[0] ^ k) * size + lo
-            keep_ref[q, lo:hi] = tiles_s[pl.ds(at, hi - lo)]
+            keep_ref[q] = tiles_s[pl.ds(at, hi - lo)]
             at = (where_ref[0] ^ (k ^ order[0])) * size + lo
             send_ref[q] = tiles_s[pl.ds(at, hi - lo)]
 
@@ -319,12 +318,11 @@
 def outer(where, gp_a, gp_b, mod_a, mod_b, padded):
     smem = pl.BlockSpec(memory_space=pltpu.SMEM)
     vmem = pl.BlockSpec(memory_space=pltpu.VMEM)
-    size = padded // 8
-    shapes = [jax.ShapeDtypeStruct((4, n, ROWS, LANES), BF) for n in [hi - lo for lo, hi in bounds(size)] + [size]]
+    shapes = [jax.ShapeDtypeStruct((4, hi - lo, ROWS, LANES), BF) for lo, hi in bounds(padded // 8)]
     return pl.pallas_call(
         outer_kernel,
         in_specs=[smem] + [vmem] * 4,
-        out_shape=tuple(shapes),
+        out_shape=tuple(shape for shape in shapes for _ in range(2)),
         scratch_shapes=[pltpu.VMEM((padded, ROWS, LANES), BF)],
         compiler_params=pltpu.CompilerParams(vmem_limit_bytes=16 * 2**20),
         name="outer",
@@ -381,42 +379,48 @@
     )(which, recv, keep)
 
 
-def fold_kernel(keep_ref, *refs):
-    count = (len(refs) - 1) // 2
-    got_refs, send_refs, left_ref = refs[:count], refs[count:-1], refs[-1]
-    for (lo, hi), got_ref, send_ref in zip(bounds(keep_ref.shape[1]), got_refs, send_refs):
+def fold_kernel(*refs):
+    count = len(refs) // 4
+    for i in range(count):
+        keep_ref, got_ref = refs[2 * i : 2 * i + 2]
+        send_ref, left_ref = refs[2 * count + 2 * i : 2 * count + 2 * i + 2]
         for q in range(keep_ref.shape[0]):
-            total = (keep_ref[q, lo:hi].astype(F32) + got_ref[q].astype(F32)).astype(BF)
+            total = (keep_ref[q].astype(F32) + got_ref[q].astype(F32)).astype(BF)
             if q % 2:
                 send_ref[q // 2] = total
             else:
-                left_ref[q // 2, lo:hi] = total
-
-
-def fold(keep, got):
-    shapes = [jax.ShapeDtypeStruct((x.shape[0] // 2,) + x.shape[1:], BF) for x in (*got, keep)]
+                left_ref[q // 2] = total
+
+
+def fold(pairs):
+    shapes = []
+    for keep, _ in pairs:
+        shapes += [jax.ShapeDtypeStruct((keep.shape[0] // 2,) + keep.shape[1:], BF)] * 2
     found = pl.pallas_call(
         fold_kernel,
         out_shape=tuple(shapes),
         compiler_params=pltpu.CompilerParams(vmem_limit_bytes=8 * 2**20),
         name="fold",
-    )(keep, *got)
-    return found[:-1], found[-1]
-
-
-def close_kernel(keep_ref, *refs):
-    out_ref = refs[-1]
-    for (lo, hi), got_ref in zip(bounds(keep_ref.shape[1]), refs):
-        out_ref[lo:hi] = (keep_ref[0, lo:hi].astype(F32) + got_ref[0].astype(F32)).astype(BF)
-
-
-def close(keep, got):
+    )(*[x for pair in pairs for x in pair])
+    return found[::2], found[1::2]
+
+
+def close_kernel(*refs):
+    out_ref, at = refs[-1], 0
+    for keep_ref, got_ref in zip(refs[:-1:2], refs[1:-1:2]):
+        count = keep_ref.shape[1]
+        out_ref[at : at + count] = (keep_ref[0].astype(F32) + got_ref[0].astype(F32)).astype(BF)
+        at += count
+
+
+def close(pairs):
+    count = sum(keep.shape[1] for keep, _ in pairs)
     return pl.pallas_call(
         close_kernel,
-        out_shape=jax.ShapeDtypeStruct(keep.shape[1:], BF),
+        out_shape=jax.ShapeDtypeStruct((count, ROWS, LANES), BF),
         compiler_params=pltpu.CompilerParams(vmem_limit_bytes=8 * 2**20),
         name="close",
-    )(keep, *got)
+    )(*[x for pair in pairs for x in pair])
 
 
 def join_kernel(*refs):
@@ -526,11 +530,11 @@
 
 
 def sum_plane(found, beside):
-    send, keep = found[:-1], found[-1]
+    send, keep = found[::2], found[1::2]
     got, beside = lax.optimization_barrier((meet(send, 0), beside))
-    send, keep = fold(keep, got)
-    send, keep = fold(keep, meet(send, 1))
-    return close(keep, meet(send, 2)), beside
+    send, keep = fold(list(zip(keep, got)))
+    send, keep = fold(list(zip(keep, meet(send, 1))))
+    return close(list(zip(keep, meet(send, 2)))), beside
 
 
 def ring(own, axis, home):

time: 154 us -> 154 us (level)
  waiting for transfers between devices: 46 us -> 47.9 us
    ppermute x26, waiting for transfers between devices: 25.9 us -> 27.8 us  [swap(): return lax.ppermute(x, axes, [(i, i ^ k) for i in range(count)])]
    unnamed x14 -> x18, local copies, waits for them, and re-layouts: 7.46 us -> 6.04 us
where the time goes in v9:
time: 154 us; the launch traced here: 153 us
  starting transfers between devices  58.1 us (38%)
  waiting for transfers between devices  47.9 us (31%)
  Pallas kernels  20.3 us (13%)
  blocking collectives  17.4 us (11%)
  local copies, waits for them, and re-layouts  7.53 us (5%)
    ppermute x26, starting transfers between devices, swap(): return lax.ppermute(x, axes, [(i, i ^ k) for i in range(count)])  30.5 us
    ppermute x26, waiting for transfers between devices, swap(): return lax.ppermute(x, axes, [(i, i ^ k) for i in range(count)])  27.8 us
    all_to_all x1, blocking collectives, exchange(): return lax.all_to_all(parts, axis, split_axis=0, concat_axis=0, tiled=True)  17.4 us
    all_to_all x1, waiting for transfers between devices, body(): lax.all_to_all(x, SEQ, split_axis=0, concat_axis=0, tiled=True)  11.5 us
    all_to_all x1, starting transfers between devices, body(): home = lax.all_to_all(home, SEQ, split_axis=0, concat_axis=0, tiled=True)  9.76 us
    ppermute x4, waiting for transfers between devices, ring(): up = lax.ppermute(up, axis, [(i, (i + 1) % count) for i in range(count)])  8.56 us
    ppermute x3, starting transfers between devices, ring(): lax.ppermute(down, axis, [(i, (i - 1) % count) for i in range(count)])  8.19 us
    all_to_all x1, starting transfers between devices, body(): lax.all_to_all(x, SEQ, split_axis=0, concat_axis=0, tiled=True)  6.93 us
  transfers between devices with their start and end apart: 36, of which 17 were waited for; matrix products, arithmetic and copies ran while one was open for 2% of the time, Pallas kernels for 3%

profile of v9, /device:TPU:1, one launch (start us, length us, event | category | flops | bytes accessed | tf_op | source)
XLA Modules:
  0.0 153.4 jit_solution(4510136615606241010)
XLA Ops:
  0.6 2.2 %pack.1 = bf16[256,1728]{1,0:T(8,128)(2,1)} custom-call(bf16[256,1152]{1,0:T(8,128)(2,1)} %bitcast.35, bf16[576,256]{1,0:T(8,128)(2,1)} %bitcast.36), custom_call_target="tpu_custom_call" | custom-call | tf_op jit(solution)/shard_map/pack/pallas_call | solution.py:52
  2.9 6.9 %all-to-all-start = ((bf16[16,16,1728]{2,1,0:T(8,128)(2,1)}), bf16[16,16,1728]{2,1,0:T(8,128)(2,1)S(1)}, u32[]{:S(2)}, u32[]{:S(2)}) async-start(bf16[16,16,1728]{2,1,0:T(8,128)(2,1)} %bitcast.34), calls=%async_computation | async-start | bytes 1835008 | tf_op jit(solution)/shard_map/all_to_all | solution.py:575
  12.7 11.5 %all-to-all-done = bf16[16,16,1728]{2,1,0:T(8,128)(2,1)S(1)} async-done(((bf16[16,16,1728]{2,1,0:T(8,128)(2,1)}), bf16[16,16,1728]{2,1,0:T(8,128)(2,1)S(1)}, u32[]{:S(2)}, u32[]{:S(2)}) %all-to-all-start) | async-done | bytes 884768 | tf_op jit(solution)/shard_map/all_to_all | solution.py:575
  24.2 6.0 %attend.1 = (bf16[256,1152]{1,0:T(8,128)(2,1)S(1)}, bf16[864,256]{1,0:T(8,128)(2,1)S(1)}, bf16[864,256]{1,0:T(8,128)(2,1)S(1)}, bf16[576,256]{1,0:T(8,128)(2,1)S(1)}) custom-call(s32[1]{0:T(128)} %bitcast.1.core_ref.half_ref, bf16[256,1728]{1,0:T(8,128)(2,1)S(1)} %bitcast.29, f32[2,1152]{1,0:T(2,128)S(1)} %pad_maximum_fusion.affine_ref, ...), custom_call_target="tpu_custom_call" | custom-call | tf_op jit(solution)/shard_map/attend/pallas_call | solution.py:203
  31.8 2.3 %collective-permute-done.gp_b = bf16[864,256]{1,0:T(8,128)(2,1)S(1)} collective-permute-done((bf16[864,256]{1,0:T(8,128)(2,1)S(1)}, bf16[864,256]{1,0:T(8,128)(2,1)S(1)}, u32[]{:S(2)}, u32[]{:S(2)}) %collective-permute-start) | collective-permute-done | bytes 442400 | tf_op jit(solution)/shard_map/ppermute | solution.py:520
  34.0 2.3 %outer.1 = (bf16[4,22,16,128]{3,2,1,0:T(8,128)(2,1)}, bf16[4,22,16,128]{3,2,1,0:T(8,128)(2,1)S(1)}, bf16[4,21,16,128]{3,2,1,0:T(8,128)(2,1)}, bf16[4,21,16,128]{...) custom-call(s32[1]{0:T(128)} %bitcast.where_ref, ...), custom_call_target="tpu_custom_call" | custom-call | tf_op jit(solution)/shard_map/outer/pallas_call | solution.py:322
  40.2 2.1 %copy-done = bf16[1152,3,576]{0,2,1:T(8,128)(2,1)S(1)} copy-done((bf16[1152,3,576]{0,2,1:T(8,128)(2,1)S(1)}, bf16[1152,3,576]{0,2,1:T(8,128)(2,1)}, u32[]{:S(2)}) %copy-start) | copy-done | bytes 3981336
  43.3 3.7 %split.1 = (bf16[256,640]{1,0:T(8,128)(2,1)S(1)}, f32[256,1920]{1,0:T(8,128)S(1)}) custom-call(s32[1]{0:T(128)} %bitcast.1.core_ref.half_ref, s32[1]{0:T(128)} %bitcast.11.which_ref, bf16[256,1728]{1,0:T(8,128)(2,1)S(1)} %bitcast.30, f32[2,1152]{1,0:T(2,128)S(1)} %pad_maximum_fusion.affine_ref, bf16[1728,1152]{1,0:T(8,128)(2,1)S(1)} %bitcast.28, ...), custom_call_target="tpu_custom_call" | custom-call | tf_op jit(solution)/shard_map/split/pallas_call | solution.py:277
  47.0 2.2 %collective-permute-done.3.refs_3_ = bf16[4,21,16,128]{3,2,1,0:T(8,128)(2,1)S(1)} collective-permute-done((bf16[4,21,16,128]{3,2,1,0:T(8,128)(2,1)}, bf16[4,21,16,128]{3,2,1,0:T(8,128)(2,1)S(1)}, u32[]{:S(2)}, u32[]{:S(2)}) %collective-permute-start.3) | collective-permute-done | bytes 344096 | tf_op jit(solution)/shard_map/ppermute | solution.py:520
  49.2 2.4 %collective-permute-start.11 = (bf16[256,640]{1,0:T(8,128)(2,1)S(1)}, bf16[256,640]{1,0:T(8,128)(2,1)S(1)}, u32[]{:S(2)}, u32[]{:S(2)}) collective-permute-start(bf16[256,640]{1,0:T(8,128)(2,1)S(1)} %get-tuple-element.82), channel_id=1, source_target_pairs={{0,1},{1,0},{2,3},{3,2},{4,5},{5,4},{6,7},{7,6},{8,9},{9,8},{10,11... | collective-permute-start | bytes 983048 | tf_op jit(solution)/shard_map/ppermute | solution.py:590
  53.4 8.1 %collective-permute-done.6.refs_3_ = bf16[2,21,16,128]{3,2,1,0:T(8,128)(2,1)S(1)} collective-permute-done((bf16[2,21,16,128]{3,2,1,0:T(8,128)(2,1)S(1)}, bf16[2,21,16,128]{3,2,1,0:T(8,128)(2,1)S(1)}, u32[]{:S(2)}, u32[]{:S(2)}) %collective-permute-start.6) | collective-permute-done | bytes 172064 | tf_op jit(solution)/shard_map/ppermute | solution.py:520
  64.5 2.7 %collective-permute-done.9.refs_3_ = bf16[1,21,16,128]{3,2,1,0:T(8,128)(2,1)S(1)} collective-permute-done((bf16[1,21,16,128]{3,2,1,0:T(8,128)(2,1)S(1)}, bf16[1,21,16,128]{3,2,1,0:T(8,128)(2,1)S(1)}, u32[]{:S(2)}, u32[]{:S(2)}) %collective-permute-start.9) | collective-permute-done | bytes 86048 | tf_op jit(solution)/shard_map/ppermute | solution.py:520
  69.8 17.4 %all_to_all.15.parts_ref = bf16[8,8,16,128]{3,2,1,0:T(8,128)(2,1)S(1)} all-to-all(bf16[8,8,16,128]{3,2,1,0:T(8,128)(2,1)S(1)} %bitcast.32), channel_id=1, replica_groups=mesh['dp'=8,'xlo'=2,'y'=4,'core'=2,'tensor'=2] {'dp'}, dimensions={0} | all-to-all | bytes 524288 | tf_op jit(solution)/shard_map/all_to_all | solution.py:525
  87.5 2.5 %collective-permute-start.12 = (bf16[8,16,128]{2,1,0:T(8,128)(2,1)S(1)}, bf16[8,16,128]{2,1,0:T(8,128)(2,1)S(1)}, u32[]{:S(2)}, u32[]{:S(2)}) collective-permute-start(bf16[8,16,128]{2,1,0:T(8,128)(2,1)S(1)} %reduce.1.refs_0_), channel_id=1, source_target_pairs={{0,224},{32,0},{64,32},{96,64},{128,96},{160,128},{192,160},{224,1... | collective-permute-start | bytes 98312 | tf_op jit(solution)/shard_map/ppermute | solution.py:550
  91.6 9.8 %all-to-all-start.2 = ((bf16[16,16,1152]{2,1,0:T(8,128)(2,1)}), bf16[16,16,1152]{2,1,0:T(8,128)(2,1)S(1)}, u32[]{:S(2)}, u32[]{:S(2)}) async-start(bf16[16,16,1152]{2,1,0:T(8,128)(2,1)} %bitcast.13), calls=%async_computation.2 | async-start | bytes 1179648 | tf_op jit(solution)/shard_map/all_to_all | solution.py:596
  101.4 3.0 %collective-permute-start.14 = (bf16[8,16,128]{2,1,0:T(8,128)(2,1)S(1)}, bf16[8,16,128]{2,1,0:T(8,128)(2,1)S(1)}, u32[]{:S(2)}, u32[]{:S(2)}) collective-permute-start(bf16[8,16,128]{2,1,0:T(8,128)(2,1)S(1)} %collective-permute-done.12.refs_1_), channel_id=1, source_target_pairs={{0,224},{32,0},{64,32},{96,64},{128,96},{160,128},{192,160},{224,1... | collective-permute-start | bytes 98312 | tf_op jit(solution)/shard_map/ppermute | solution.py:550
  105.8 2.7 %collective-permute-start.15 = (bf16[8,16,128]{2,1,0:T(8,128)(2,1)S(1)}, bf16[8,16,128]{2,1,0:T(8,128)(2,1)S(1)}, u32[]{:S(2)}, u32[]{:S(2)}) collective-permute-start(bf16[8,16,128]{2,1,0:T(8,128)(2,1)S(1)} %collective-permute-done.14.refs_2_), channel_id=1, source_target_pairs={{0,224},{32,0},{64,32},{96,64},{128,96},{160,128},{192,160},{224,1... | collective-permute-start | bytes 98312 | tf_op jit(solution)/shard_map/ppermute | solution.py:550
  110.1 4.0 %collective-permute-done.18.refs_4_ = bf16[8,16,128]{2,1,0:T(8,128)(2,1)S(1)} collective-permute-done((bf16[8,16,128]{2,1,0:T(8,128)(2,1)S(1)}, bf16[8,16,128]{2,1,0:T(8,128)(2,1)S(1)}, u32[]{:S(2)}, u32[]{:S(2)}) %collective-permute-start.18) | collective-permute-done | bytes 32800 | tf_op jit(solution)/shard_map/ppermute | solution.py:547
  119.1 2.2 %collective-permute-done.21.refs_5_ = bf16[1,21,16,128]{3,2,1,0:T(8,128)(2,1)S(1)} collective-permute-done((bf16[1,21,16,128]{3,2,1,0:T(8,128)(2,1)S(1)}, bf16[1,21,16,128]{3,2,1,0:T(8,128)(2,1)S(1)}, u32[]{:S(2)}, u32[]{:S(2)}) %collective-permute-start.21) | collective-permute-done | bytes 86048 | tf_op jit(solution)/shard_map/ppermute | solution.py:520
  123.4 4.0 %collective-permute-done.23.refs_3_ = bf16[2,21,16,128]{3,2,1,0:T(8,128)(2,1)S(1)} collective-permute-done((bf16[2,21,16,128]{3,2,1,0:T(8,128)(2,1)S(1)}, bf16[2,21,16,128]{3,2,1,0:T(8,128)(2,1)S(1)}, u32[]{:S(2)}, u32[]{:S(2)}) %collective-permute-start.23) | collective-permute-done | bytes 172064 | tf_op jit(solution)/shard_map/ppermute | solution.py:520
  127.9 9.2 %collective-permute-start.29 = (bf16[4,21,16,128]{3,2,1,0:T(8,128)(2,1)S(1)}, bf16[4,21,16,128]{3,2,1,0:T(8,128)(2,1)S(1)}, u32[]{:S(2)}, u32[]{:S(2)}) collective-permute-start(bf16[4,21,16,128]{3,2,1,0:T(8,128)(2,1)S(1)} %get-tuple-element.107.refs_1_), channel_id=1, source_target_pairs={{0,2},{2,0},{1,3},{3,1},{4,6},{6,4},{5,7},{7,5},{8,10},{10,8},{9,1... | collective-permute-start | bytes 1032200 | tf_op jit(solution)/shard_map/ppermute | solution.py:520
  139.7 4.5 %collective-permute-start.31 = (bf16[4,22,16,128]{3,2,1,0:T(8,128)(2,1)S(1)}, bf16[4,22,16,128]{3,2,1,0:T(8,128)(2,1)S(1)}, u32[]{:S(2)}, u32[]{:S(2)}) collective-permute-start(bf16[4,22,16,128]{3,2,1,0:T(8,128)(2,1)S(1)} %collective-permute-done.25.refs_3_), channel_id=1, source_target_pairs={{0,2},{2,0},{1,3},{3,1},{4,6},{6,4},{5,7},{7,5},{8,10},{10,8},{9,1... | collective-permute-start | bytes 1081352 | tf_op jit(solution)/shard_map/ppermute | solution.py:520
  144.3 3.7 %collective-permute-done.26.refs_4_ = bf16[4,21,16,128]{3,2,1,0:T(8,128)(2,1)S(1)} collective-permute-done((bf16[4,21,16,128]{3,2,1,0:T(8,128)(2,1)S(1)}, bf16[4,21,16,128]{3,2,1,0:T(8,128)(2,1)S(1)}, u32[]{:S(2)}, u32[]{:S(2)}) %collective-permute-start.26) | collective-permute-done | bytes 344096 | tf_op jit(solution)/shard_map/ppermute | solution.py:520
  150.5 2.9 %untile.1 = bf16[1728,1152]{1,0:T(8,128)(2,1)} custom-call(s32[1]{0:T(128)} %bitcast.where_ref, s32[1]{0:T(128)} %bitcast.1.core_ref.half_ref, bf16[4,22,16,128]{3,2,1,0:T(8,128)(2,1)S(1)} %get-tuple-element.106.refs_0_, bf16[4,21,16,128]{3,2,1,0:T(8,128)(2,1)S(1)} %get-tuple-element.107.refs_1_, bf16[4,21,16,128]{3,2,1,0:T(8,128)(2,1)S(1)} %get-tuple-element.108.refs_2_, ...), custom_call_target="tpu_custom_call" | custom-call | tf_op jit(solution)/shard_map/untile/pallas_call | solution.py:508
  (85 shorter events, 34.3 us)
Async XLA Ops:
  2.9 21.3 %all-to-all-start = ((bf16[16,16,1728]{2,1,0:T(8,128)(2,1)}), bf16[16,16,1728]{2,1,0:T(8,128)(2,1)S(1)}, u32[]{:S(2)}, u32[]{:S(2)}) async-start(bf16[16,16,1728]{2,1,0:T(8,128)(2,1)} %bitcast.34), calls=%async_computation | async-start | bytes 1835008 | tf_op jit(solution)/shard_map/all_to_all | solution.py:575
  38.5 10.7 %collective-permute-start.2 = (bf16[4,22,16,128]{3,2,1,0:T(8,128)(2,1)}, bf16[4,22,16,128]{3,2,1,0:T(8,128)(2,1)S(1)}, u32[]{:S(2)}, u32[]{:S(2)}) collective-permute-start(bf16[4,22,16,128]{3,2,1,0:T(8,128)(2,1)} %get-tuple-element.60), channel_id=1, source_target_pairs={{0,4},{4,0},{8,12},{12,8},{16,20},{20,16},{24,28},{28,24},{1,5},{5... | collective-permute-start | bytes 1081352 | tf_op jit(solution)/shard_map/ppermute | solution.py:520
  38.5 10.7 %collective-permute-start.3 = (bf16[4,21,16,128]{3,2,1,0:T(8,128)(2,1)}, bf16[4,21,16,128]{3,2,1,0:T(8,128)(2,1)S(1)}, u32[]{:S(2)}, u32[]{:S(2)}) collective-permute-start(bf16[4,21,16,128]{3,2,1,0:T(8,128)(2,1)} %get-tuple-element.61), channel_id=1, source_target_pairs={{0,12},{4,8},{8,4},{12,0},{16,28},{20,24},{24,20},{28,16},{1,13},{... | collective-permute-start | bytes 1032200 | tf_op jit(solution)/shard_map/ppermute | solution.py:520
  39.7 9.6 %collective-permute-start.4 = (bf16[4,21,16,128]{3,2,1,0:T(8,128)(2,1)}, bf16[4,21,16,128]{3,2,1,0:T(8,128)(2,1)S(1)}, u32[]{:S(2)}, u32[]{:S(2)}) collective-permute-start(bf16[4,21,16,128]{3,2,1,0:T(8,128)(2,1)} %get-tuple-element.62), channel_id=1, source_target_pairs={{0,16},{4,20},{8,24},{12,28},{16,0},{20,4},{24,8},{28,12},{1,17},{... | collective-permute-start | bytes 1032200 | tf_op jit(solution)/shard_map/ppermute | solution.py:520
  49.2 19.0 %collective-permute-start.11 = (bf16[256,640]{1,0:T(8,128)(2,1)S(1)}, bf16[256,640]{1,0:T(8,128)(2,1)S(1)}, u32[]{:S(2)}, u32[]{:S(2)}) collective-permute-start(bf16[256,640]{1,0:T(8,128)(2,1)S(1)} %get-tuple-element.82), channel_id=1, source_target_pairs={{0,1},{1,0},{2,3},{3,2},{4,5},{5,4},{6,7},{7,6},{8,9},{9,8},{10,11... | collective-permute-start | bytes 983048 | tf_op jit(solution)/shard_map/ppermute | solution.py:590
  51.9 9.5 %collective-permute-start.5 = (bf16[2,22,16,128]{3,2,1,0:T(8,128)(2,1)S(1)}, bf16[2,22,16,128]{3,2,1,0:T(8,128)(2,1)S(1)}, u32[]{:S(2)}, u32[]{:S(2)}) collective-permute-start(bf16[2,22,16,128]{3,2,1,0:T(8,128)(2,1)S(1)} %get-tuple-element.71), channel_id=1, source_target_pairs={{0,12},{4,8},{8,4},{12,0},{16,28},{20,24},{24,20},{28,16},{1,13},{... | collective-permute-start | bytes 540680 | tf_op jit(solution)/shard_map/ppermute | solution.py:520
  53.4 8.1 %collective-permute-start.6 = (bf16[2,21,16,128]{3,2,1,0:T(8,128)(2,1)S(1)}, bf16[2,21,16,128]{3,2,1,0:T(8,128)(2,1)S(1)}, u32[]{:S(2)}, u32[]{:S(2)}) collective-permute-start(bf16[2,21,16,128]{3,2,1,0:T(8,128)(2,1)S(1)} %get-tuple-element.73), channel_id=1, source_target_pairs={{0,16},{4,20},{8,24},{12,28},{16,0},{20,4},{24,8},{28,12},{1,17},{... | collective-permute-start | bytes 516104 | tf_op jit(solution)/shard_map/ppermute | solution.py:520
  53.4 8.1 %collective-permute-start.7 = (bf16[2,21,16,128]{3,2,1,0:T(8,128)(2,1)S(1)}, bf16[2,21,16,128]{3,2,1,0:T(8,128)(2,1)S(1)}, u32[]{:S(2)}, u32[]{:S(2)}) collective-permute-start(bf16[2,21,16,128]{3,2,1,0:T(8,128)(2,1)S(1)} %get-tuple-element.75), channel_id=1, source_target_pairs={{0,4},{4,0},{8,12},{12,8},{16,20},{20,16},{24,28},{28,24},{1,5},{5... | collective-permute-start | bytes 516104 | tf_op jit(solution)/shard_map/ppermute | solution.py:520
  61.6 6.6 %collective-permute-start.8 = (bf16[1,22,16,128]{3,2,1,0:T(8,128)(2,1)S(1)}, bf16[1,22,16,128]{3,2,1,0:T(8,128)(2,1)S(1)}, u32[]{:S(2)}, u32[]{:S(2)}) collective-permute-start(bf16[1,22,16,128]{3,2,1,0:T(8,128)(2,1)S(1)} %get-tuple-element.77), channel_id=1, source_target_pairs={{0,16},{4,20},{8,24},{12,28},{16,0},{20,4},{24,8},{28,12},{1,17},{... | collective-permute-start | bytes 270344 | tf_op jit(solution)/shard_map/ppermute | solution.py:520
  63.6 4.5 %collective-permute-start.10 = (bf16[1,21,16,128]{3,2,1,0:T(8,128)(2,1)S(1)}, bf16[1,21,16,128]{3,2,1,0:T(8,128)(2,1)S(1)}, u32[]{:S(2)}, u32[]{:S(2)}) collective-permute-start(bf16[1,21,16,128]{3,2,1,0:T(8,128)(2,1)S(1)} %get-tuple-element.81), channel_id=1, source_target_pairs={{0,12},{4,8},{8,4},{12,0},{16,28},{20,24},{24,20},{28,16},{1,13},{... | collective-permute-start | bytes 258056 | tf_op jit(solution)/shard_map/ppermute | solution.py:520
  87.2 4.4 %collective-permute-start.13 = (bf16[8,16,128]{2,1,0:T(8,128)(2,1)S(1)}, bf16[8,16,128]{2,1,0:T(8,128)(2,1)S(1)}, u32[]{:S(2)}, u32[]{:S(2)}) collective-permute-start(bf16[8,16,128]{2,1,0:T(8,128)(2,1)S(1)} %reduce.1.refs_0_), channel_id=1, source_target_pairs={{0,32},{32,64},{64,96},{96,128},{128,160},{160,192},{192,224},{224... | collective-permute-start | bytes 98312 | tf_op jit(solution)/shard_map/ppermute | solution.py:547
  91.6 22.4 %all-to-all-start.2 = ((bf16[16,16,1152]{2,1,0:T(8,128)(2,1)}), bf16[16,16,1152]{2,1,0:T(8,128)(2,1)S(1)}, u32[]{:S(2)}, u32[]{:S(2)}) async-start(bf16[16,16,1152]{2,1,0:T(8,128)(2,1)} %bitcast.13), calls=%async_computation.2 | async-start | bytes 1179648 | tf_op jit(solution)/shard_map/all_to_all | solution.py:596
  101.4 4.4 %collective-permute-start.16 = (bf16[8,16,128]{2,1,0:T(8,128)(2,1)S(1)}, bf16[8,16,128]{2,1,0:T(8,128)(2,1)S(1)}, u32[]{:S(2)}, u32[]{:S(2)}) collective-permute-start(bf16[8,16,128]{2,1,0:T(8,128)(2,1)S(1)} %collective-permute-done.13.refs_7_), channel_id=1, source_target_pairs={{0,32},{32,64},{64,96},{96,128},{128,160},{160,192},{192,224},{224... | collective-permute-start | bytes 98312 | tf_op jit(solution)/shard_map/ppermute | solution.py:547
  101.4 4.4 %collective-permute-start.14 = (bf16[8,16,128]{2,1,0:T(8,128)(2,1)S(1)}, bf16[8,16,128]{2,1,0:T(8,128)(2,1)S(1)}, u32[]{:S(2)}, u32[]{:S(2)}) collective-permute-start(bf16[8,16,128]{2,1,0:T(8,128)(2,1)S(1)} %collective-permute-done.12.refs_1_), channel_id=1, source_target_pairs={{0,224},{32,0},{64,32},{96,64},{128,96},{160,128},{192,160},{224,1... | collective-permute-start | bytes 98312 | tf_op jit(solution)/shard_map/ppermute | solution.py:550
  114.1 7.2 %collective-permute-start.19 = (bf16[1,22,16,128]{3,2,1,0:T(8,128)(2,1)S(1)}, bf16[1,22,16,128]{3,2,1,0:T(8,128)(2,1)S(1)}, u32[]{:S(2)}, u32[]{:S(2)}) collective-permute-start(bf16[1,22,16,128]{3,2,1,0:T(8,128)(2,1)S(1)} %get-tuple-element.100.refs_0_), channel_id=1, source_target_pairs={{0,16},{4,20},{8,24},{12,28},{16,0},{20,4},{24,8},{28,12},{1,17},{... | collective-permute-start | bytes 270344 | tf_op jit(solution)/shard_map/ppermute | solution.py:520
  116.7 4.5 %collective-permute-start.21 = (bf16[1,21,16,128]{3,2,1,0:T(8,128)(2,1)S(1)}, bf16[1,21,16,128]{3,2,1,0:T(8,128)(2,1)S(1)}, u32[]{:S(2)}, u32[]{:S(2)}) collective-permute-start(bf16[1,21,16,128]{3,2,1,0:T(8,128)(2,1)S(1)} %get-tuple-element.102.refs_4_), channel_id=1, source_target_pairs={{0,12},{4,8},{8,4},{12,0},{16,28},{20,24},{24,20},{28,16},{1,13},{... | collective-permute-start | bytes 258056 | tf_op jit(solution)/shard_map/ppermute | solution.py:520
  121.3 6.4 %collective-permute-start.22 = (bf16[2,22,16,128]{3,2,1,0:T(8,128)(2,1)S(1)}, bf16[2,22,16,128]{3,2,1,0:T(8,128)(2,1)S(1)}, u32[]{:S(2)}, u32[]{:S(2)}) collective-permute-start(bf16[2,22,16,128]{3,2,1,0:T(8,128)(2,1)S(1)} %get-tuple-element.103.refs_0_), channel_id=1, source_target_pairs={{0,12},{4,8},{8,4},{12,0},{16,28},{20,24},{24,20},{28,16},{1,13},{... | collective-permute-start | bytes 540680 | tf_op jit(solution)/shard_map/ppermute | solution.py:520
  127.8 11.9 %collective-permute-start.25 = (bf16[4,22,16,128]{3,2,1,0:T(8,128)(2,1)S(1)}, bf16[4,22,16,128]{3,2,1,0:T(8,128)(2,1)S(1)}, u32[]{:S(2)}, u32[]{:S(2)}) collective-permute-start(bf16[4,22,16,128]{3,2,1,0:T(8,128)(2,1)S(1)} %get-tuple-element.106.refs_0_), channel_id=1, source_target_pairs={{0,4},{4,0},{8,12},{12,8},{16,20},{20,16},{24,28},{28,24},{1,5},{5... | collective-permute-start | bytes 1081352 | tf_op jit(solution)/shard_map/ppermute | solution.py:520
  127.9 16.4 %collective-permute-start.29 = (bf16[4,21,16,128]{3,2,1,0:T(8,128)(2,1)S(1)}, bf16[4,21,16,128]{3,2,1,0:T(8,128)(2,1)S(1)}, u32[]{:S(2)}, u32[]{:S(2)}) collective-permute-start(bf16[4,21,16,128]{3,2,1,0:T(8,128)(2,1)S(1)} %get-tuple-element.107.refs_1_), channel_id=1, source_target_pairs={{0,2},{2,0},{1,3},{3,1},{4,6},{6,4},{5,7},{7,5},{8,10},{10,8},{9,1... | collective-permute-start | bytes 1032200 | tf_op jit(solution)/shard_map/ppermute | solution.py:520
  137.1 10.9 %collective-permute-start.26 = (bf16[4,21,16,128]{3,2,1,0:T(8,128)(2,1)S(1)}, bf16[4,21,16,128]{3,2,1,0:T(8,128)(2,1)S(1)}, u32[]{:S(2)}, u32[]{:S(2)}) collective-permute-start(bf16[4,21,16,128]{3,2,1,0:T(8,128)(2,1)S(1)} %get-tuple-element.107.refs_1_), channel_id=1, source_target_pairs={{0,12},{4,8},{8,4},{12,0},{16,28},{20,24},{24,20},{28,16},{1,13},{... | collective-permute-start | bytes 1032200 | tf_op jit(solution)/shard_map/ppermute | solution.py:520
  138.0 10.8 %collective-permute-start.27 = (bf16[4,21,16,128]{3,2,1,0:T(8,128)(2,1)S(1)}, bf16[4,21,16,128]{3,2,1,0:T(8,128)(2,1)S(1)}, u32[]{:S(2)}, u32[]{:S(2)}) collective-permute-start(bf16[4,21,16,128]{3,2,1,0:T(8,128)(2,1)S(1)} %get-tuple-element.108.refs_2_), channel_id=1, source_target_pairs={{0,16},{4,20},{8,24},{12,28},{16,0},{20,4},{24,8},{28,12},{1,17},{... | collective-permute-start | bytes 1032200 | tf_op jit(solution)/shard_map/ppermute | solution.py:520
  139.1 10.8 %collective-permute-start.28 = (bf16[4,22,16,128]{3,2,1,0:T(8,128)(2,1)S(1)}, bf16[4,22,16,128]{3,2,1,0:T(8,128)(2,1)S(1)}, u32[]{:S(2)}, u32[]{:S(2)}) collective-permute-start(bf16[4,22,16,128]{3,2,1,0:T(8,128)(2,1)S(1)} %get-tuple-element.106.refs_0_), channel_id=1, source_target_pairs={{0,2},{2,0},{1,3},{3,1},{4,6},{6,4},{5,7},{7,5},{8,10},{10,8},{9,1... | collective-permute-start | bytes 1081352 | tf_op jit(solution)/shard_map/ppermute | solution.py:520
  139.7 10.8 %collective-permute-start.31 = (bf16[4,22,16,128]{3,2,1,0:T(8,128)(2,1)S(1)}, bf16[4,22,16,128]{3,2,1,0:T(8,128)(2,1)S(1)}, u32[]{:S(2)}, u32[]{:S(2)}) collective-permute-start(bf16[4,22,16,128]{3,2,1,0:T(8,128)(2,1)S(1)} %collective-permute-done.25.refs_3_), channel_id=1, source_target_pairs={{0,2},{2,0},{1,3},{3,1},{4,6},{6,4},{5,7},{7,5},{8,10},{10,8},{9,1... | collective-permute-start | bytes 1081352 | tf_op jit(solution)/shard_map/ppermute | solution.py:520
  144.2 5.6 %collective-permute-start.30 = (bf16[4,21,16,128]{3,2,1,0:T(8,128)(2,1)S(1)}, bf16[4,21,16,128]{3,2,1,0:T(8,128)(2,1)S(1)}, u32[]{:S(2)}, u32[]{:S(2)}) collective-permute-start(bf16[4,21,16,128]{3,2,1,0:T(8,128)(2,1)S(1)} %get-tuple-element.108.refs_2_), channel_id=1, source_target_pairs={{0,2},{2,0},{1,3},{3,1},{4,6},{6,4},{5,7},{7,5},{8,10},{10,8},{9,1... | collective-permute-start | bytes 1032200 | tf_op jit(solution)/shard_map/ppermute | solution.py:520
  (21 other events, 72.6 us)

commit v10 on v8

--- a/solution.py
+++ b/solution.py
@@ -297,7 +297,7 @@
     )(core, which, x, affine, wt, gp_keep, gp_send, att)
 
 
-def outer_kernel(where_ref, gp_a, gp_b, mod_a, mod_b, *refs):
+def outer_kernel(where_ref, core_ref, gp_a, gp_b, mod_a, mod_b, *refs):
     out_refs, tiles_s = refs[:-1], refs[-1]
     rows, width = gp_a.shape[0], mod_a.shape[1]
     tiles = rows // ROWS
@@ -313,40 +313,45 @@
             tiles_s[j * tiles : (j + 1) * tiles] = found[:, at : at + LANES].reshape(tiles, ROWS, LANES)
     size = tiles_s.shape[0] // 8
     keep_ref = out_refs[-1]
-    for (lo, hi), order, send_ref in zip(bounds(size), ORDERS, out_refs):
+    for (lo, hi), orders, send_ref in zip(bounds(size), ORDERS, out_refs):
+        order = masks_of(orders, core_ref[0])
         for q in range(4):
-            k = picked(q, order[1:])
+            k = picked(q, order[1], order[2])
             at = (where_ref[0] ^ k) * size + lo
             keep_ref[q, lo:hi] = tiles_s[pl.ds(at, hi - lo)]
             at = (where_ref[0] ^ (k ^ order[0])) * size + lo
             send_ref[q] = tiles_s[pl.ds(at, hi - lo)]
 
 
-def outer(where, gp_a, gp_b, mod_a, mod_b, padded):
+def outer(where, core, gp_a, gp_b, mod_a, mod_b, padded):
     smem = pl.BlockSpec(memory_space=pltpu.SMEM)
     vmem = pl.BlockSpec(memory_space=pltpu.VMEM)
     size = padded // 8
     shapes = [jax.ShapeDtypeStruct((4, n, ROWS, LANES), BF) for n in [hi - lo for lo, hi in bounds(size)] + [size]]
     return pl.pallas_call(
         outer_kernel,
-        in_specs=[smem] + [vmem] * 4,
+        in_specs=[smem, smem] + [vmem] * 4,
         out_shape=tuple(shapes),
         scratch_shapes=[pltpu.VMEM((padded, ROWS, LANES), BF)],
         compiler_params=pltpu.CompilerParams(vmem_limit_bytes=16 * 2**20),
         name="outer",
-    )(where, gp_a, gp_b, mod_a, mod_b)
-
-
-ORDERS = ((1, 3, 4), (3, 4, 1), (4, 1, 3))
+    )(where, core, gp_a, gp_b, mod_a, mod_b)
+
+
+ORDERS = (((1, 3, 4), (4, 1, 3)), ((3, 4, 1), (3, 4, 1)))
 
 
 def bounds(size):
-    cuts = [0, -(-size // 3), -(-2 * size // 3), size]
-    return list(zip(cuts[:-1], cuts[1:]))
-
-
-def picked(q, masks):
-    return (masks[0] if q % 2 else 0) ^ (masks[1] if q // 2 else 0)
+    cut = -(-2 * size // 3)
+    return [(0, cut), (cut, size)]
+
+
+def masks_of(orders, core):
+    return [jnp.where(core == 0, a, b) for a, b in zip(*orders)]
+
+
+def picked(q, first, second):
+    return (first if q % 2 else 0) ^ (second if q // 2 else 0)
 
 
 def window_of(half):
@@ -414,12 +419,15 @@
     out_ref = refs[-1]
     for (lo, hi), got_ref in zip(bounds(keep_ref.shape[1]), refs):
         out_ref[lo:hi] = (keep_ref[0, lo:hi].astype(F32) + got_ref[0].astype(F32)).astype(BF)
-
-
-def close(keep, got):
+    spare = out_ref.shape[0] - keep_ref.shape[1]
+    if spare:
+        out_ref[keep_ref.shape[1] :] = jnp.zeros((spare, ROWS, LANES), BF)
+
+
+def close(keep, got, size):
     return pl.pallas_call(
         close_kernel,
-        out_shape=jax.ShapeDtypeStruct(keep.shape[1:], BF),
+        out_shape=jax.ShapeDtypeStruct((size, ROWS, LANES), BF),
         compiler_params=pltpu.CompilerParams(vmem_limit_bytes=8 * 2**20),
         name="close",
     )(keep, *got)
@@ -482,18 +490,18 @@
         for i in range(ref.shape[0] // size):
             at = lax.rem(clip_ref[0] + (first + i + clips), clips) * size
             all_s[pl.ds(at, size)] = ref[i * size : (i + 1) * size]
-    for (lo, hi), out_ref in zip(bounds(clips * size), out_refs):
+    for (lo, hi), out_ref in zip(bounds(sum(ref.shape[1] for ref in out_refs)), out_refs):
         out_ref[0] = all_s[lo:hi]
 
 
-def place(clip, near, below, above, clips):
+def place(clip, near, below, above, clips, size):
     total = near.shape[0] // 3 * clips
     smem = pl.BlockSpec(memory_space=pltpu.SMEM)
     vmem = pl.BlockSpec(memory_space=pltpu.VMEM)
     return pl.pallas_call(
         functools.partial(place_kernel, clips=clips),
         in_specs=[smem, vmem, vmem, vmem],
-        out_shape=tuple(jax.ShapeDtypeStruct((1, hi - lo, ROWS, LANES), BF) for lo, hi in bounds(total)),
+        out_shape=tuple(jax.ShapeDtypeStruct((1, hi - lo, ROWS, LANES), BF) for lo, hi in bounds(size)),
         scratch_shapes=[pltpu.VMEM((total, ROWS, LANES), BF)],
         compiler_params=pltpu.CompilerParams(vmem_limit_bytes=4 * 2**20),
         name="place",
@@ -507,10 +515,11 @@
     for side in range(2):
         half = half_ref[0] ^ side
         for far in range(2):
-            for (lo, hi), order in zip(bounds(size), ORDERS):
+            for (lo, hi), orders in zip(bounds(size), ORDERS):
                 piece = next(pieces)
+                order = masks_of(orders, half)
                 for q in range(4):
-                    k = picked(q, (order[2], order[1])) ^ (order[0] * far)
+                    k = picked(q, order[2], order[1]) ^ (order[0] * far)
                     at = (half * 8 + (where_ref[0] ^ k)) * size + lo
                     tiles_s[pl.ds(at, hi - lo)] = piece[q]
     rows = out_ref.shape[0] // 2
@@ -546,16 +555,24 @@
     return lax.all_to_all(parts, axis, split_axis=0, concat_axis=0, tiled=True)
 
 
+def plane_size():
+    return lax.axis_size("xlo") * lax.axis_size("y")
+
+
 def meet(blocks, level):
-    return [swap(block, PLANE, order[level]) for block, order in zip(blocks, ORDERS)]
-
-
-def sum_plane(found, beside):
+    found = []
+    for block, orders in zip(blocks, ORDERS):
+        pairs = [(p * 2 + c, (p ^ orders[c][level]) * 2 + c) for p in range(plane_size()) for c in range(2)]
+        found.append(lax.ppermute(block, SEQ, pairs))
+    return found
+
+
+def sum_plane(found, beside, size):
     send, keep = found[:-1], found[-1]
     got, beside = lax.optimization_barrier((meet(send, 0), beside))
     send, keep = fold(keep, got)
     send, keep = fold(keep, meet(send, 1))
-    return close(keep, meet(send, 2)), beside
+    return close(keep, meet(send, 2), size), beside
 
 
 def shift(x, axis, step):
@@ -599,12 +616,11 @@
         core, x, affine, wt, q_gain[:, None], k_gain[:, None], own_patches, heads, hd
     )
     used = (3 * hw // 2 // ROWS) * (width // LANES)
-    group = 8 * clips
-    padded = -(-used // group) * group
+    size = -(-used // plane_size())
     gp_other, mod_other = swap(gp_send, ("core",), 1), swap(mod, ("core",), 1)
-    found = outer(where, gp_keep, gp_other, mod, mod_other, padded)
+    found = outer(where, core, gp_keep, gp_other, mod, mod_other, size * plane_size())
     send, keep = split(core, which, x, affine, wt, gp_keep, gp_send, att_t)
-    own, send = sum_plane(found, send)
+    own, send = sum_plane(found, send, -(-size // clips) * clips)
     own, send = lax.optimization_barrier((own, send))
     recv = lax.ppermute(send, "tensor", [(0, 1), (1, 0)])
     own = exchange(own.reshape((clips, own.shape[0] // clips) + own.shape[1:]), "dp")
@@ -614,7 +630,7 @@
     near, below, above, home = gather_clips(own, home)
     home = lax.all_to_all(home, SEQ, split_axis=0, concat_axis=0, tiled=True)
     clip = lax.axis_index("dp").astype(jnp.int32).reshape(1)
-    have = place(clip, near, below, above, clips)
+    have = place(clip, near, below, above, clips, size)
     grad_qkv, home = gather_plane(have, where, core, 3 * hw, width, home)
     grad_t, att_t = unpack(home.reshape(patches, width))
     grad_qkv = grad_qkv.reshape(3, hw, width).transpose(2, 0, 1)

time: 145 us -> 151 us (1.041); the launches traced: 143 us -> 148 us
  waiting for transfers between devices: 50.8 us -> 64.1 us
  starting transfers between devices: 61.4 us -> 52.5 us
    ppermute x0 -> x12, waiting for transfers between devices: none -> 34 us  [meet(): found.append(lax.ppermute(block, SEQ, pairs))]
    ppermute x26 -> x6, waiting for transfers between devices: 23.4 us -> 2.46 us  [swap(): return lax.ppermute(x, axes, [(i, i ^ k) for i in range(count)])]
    ppermute x26 -> x6, starting transfers between devices: 28.3 us -> 7.97 us  [swap(): return lax.ppermute(x, axes, [(i, i ^ k) for i in range(count)])]
    ppermute x0 -> x12, starting transfers between devices: none -> 13.1 us  [meet(): found.append(lax.ppermute(block, SEQ, pairs))]
    all_to_all x1, starting transfers between devices: 9.51 us -> 7.8 us  [body(): home = lax.all_to_all(home, SEQ, split_axis=0, concat_axis=0, tiled=True)]
  transfers between devices with their start and end apart: 34 -> 26, of which waited for: 20 -> 19; matrix products, arithmetic and copies ran while one was open for 2% -> 2% of each run, Pallas kernels for 5% -> 5%
where the time goes in v10:
time: 151 us; the launch traced here: 148 us
  waiting for transfers between devices  64.1 us (42%)
  starting transfers between devices  52.5 us (35%)
  Pallas kernels  26 us (17%)
  local copies, waits for them, and re-layouts  3.16 us (2%)
    ppermute x12, waiting for transfers between devices, meet(): found.append(lax.ppermute(block, SEQ, pairs))  34 us
    ppermute x12, starting transfers between devices, meet(): found.append(lax.ppermute(block, SEQ, pairs))  13.1 us
    all_to_all x1, waiting for transfers between devices, body(): lax.all_to_all(x, SEQ, split_axis=0, concat_axis=0, tiled=True)  11.5 us
    ppermute x4, waiting for transfers between devices, shift(): lax.ppermute(x, axis, [(i, (i + step) % count) for i in range(count)])  9.13 us
    all_to_all x1, starting transfers between devices, exchange(): return lax.all_to_all(parts, axis, split_axis=0, concat_axis=0, tiled=True)  8.18 us
    ppermute x6, starting transfers between devices, swap(): return lax.ppermute(x, axes, [(i, i ^ k) for i in range(count)])  7.97 us
    all_to_all x1, starting transfers between devices, body(): home = lax.all_to_all(home, SEQ, split_axis=0, concat_axis=0, tiled=True)  7.8 us
    pallas_call x1, Pallas kernels, attend(): pl.pallas_call(functools.partial(attend_kernel, patches=patches, heads=he...  7.12 us
  transfers between devices with their start and end apart: 26, of which 19 were waited for; matrix products, arithmetic and copies ran while one was open for 2% of the time, Pallas kernels for 5%

profile of v10, /device:TPU:1, one launch (start us, length us, event | category | flops | bytes accessed | tf_op | source)
XLA Modules:
  0.0 147.8 jit_solution(18327643661868486459)
XLA Ops:
  0.6 2.2 %pack.1 = bf16[256,1728]{1,0:T(8,128)(2,1)} custom-call(bf16[256,1152]{1,0:T(8,128)(2,1)} %bitcast.34, bf16[576,256]{1,0:T(8,128)(2,1)} %bitcast.35), custom_call_target="tpu_custom_call" | custom-call | tf_op jit(solution)/shard_map/pack/pallas_call | solution.py:52
  2.9 6.9 %all-to-all-start = ((bf16[16,16,1728]{2,1,0:T(8,128)(2,1)}), bf16[16,16,1728]{2,1,0:T(8,128)(2,1)S(1)}, u32[]{:S(2)}, u32[]{:S(2)}) async-start(bf16[16,16,1728]{2,1,0:T(8,128)(2,1)} %bitcast.33), calls=%async_computation | async-start | bytes 1835008 | tf_op jit(solution)/shard_map/all_to_all | solution.py:610
  12.7 11.5 %all-to-all-done = bf16[16,16,1728]{2,1,0:T(8,128)(2,1)S(1)} async-done(((bf16[16,16,1728]{2,1,0:T(8,128)(2,1)}), bf16[16,16,1728]{2,1,0:T(8,128)(2,1)S(1)}, u32[]{:S(2)}, u32[]{:S(2)}) %all-to-all-start) | async-done | bytes 884768 | tf_op jit(solution)/shard_map/all_to_all | solution.py:610
  25.1 7.1 %attend.1 = (bf16[256,1152]{1,0:T(8,128)(2,1)S(1)}, bf16[864,256]{1,0:T(8,128)(2,1)S(1)}, bf16[864,256]{1,0:T(8,128)(2,1)S(1)}, bf16[576,256]{1,0:T(8,128)(2,1)S(1)}) custom-call(s32[1]{0:T(128)} %bitcast.2.core_ref.half_ref, bf16[256,1728]{1,0:T(8,128)(2,1)} %bitcast.30, f32[2,1152]{1,0:T(2,128)S(1)} %pad_maximum_fusion.affine_ref.affine_hbm, ...), custom_call_target="tpu_custom_call" | custom-call | tf_op jit(solution)/shard_map/attend/pallas_call | solution.py:203
  33.9 2.3 %collective-permute-done.gp_b = bf16[864,256]{1,0:T(8,128)(2,1)S(1)} collective-permute-done((bf16[864,256]{1,0:T(8,128)(2,1)S(1)}, bf16[864,256]{1,0:T(8,128)(2,1)S(1)}, u32[]{:S(2)}, u32[]{:S(2)}) %collective-permute-start) | collective-permute-done | bytes 442400 | tf_op jit(solution)/shard_map/ppermute | solution.py:550
  36.1 2.4 %outer.1 = (bf16[4,41,16,128]{3,2,1,0:T(8,128)(2,1)}, bf16[4,20,16,128]{3,2,1,0:T(8,128)(2,1)}, bf16[4,61,16,128]{3,2,1,0:T(8,128)(2,1)S(1)}) custom-call(s32[1]{0:T(128)} %bitcast.1.where_ref, s32[1]{0:T(128)} %bitcast.2.core_ref.half_ref, bf16[864,256]{1,0:T(8,128)(2,1)S(1)} %get-tuple-element.38.gp_a.gp_keep_hbm, ...), custom_call_target="tpu_custom_call" | custom-call | tf_op jit(solution)/shard_map/outer/pallas_call | solution.py:331
  39.8 6.3 %split.1 = (bf16[256,640]{1,0:T(8,128)(2,1)}, f32[256,1920]{1,0:T(8,128)}) custom-call(s32[1]{0:T(128)} %bitcast.2.core_ref.half_ref, s32[1]{0:T(128)} %bitcast.12.which_ref, bf16[256,1728]{1,0:T(8,128)(2,1)} %bitcast.31, f32[2,1152]{1,0:T(2,128)} %copy-done.4, bf16[1728,1152]{1,0:T(8,128)(2,1)} %bitcast.29, bf16[864,256]{1,0:T(8,128)(2,1)} %copy-done.1, ...), custom_call_target="tpu_custom_call" | custom-call | tf_op jit(solution)/shard_map/split/pallas_call | solution.py:286
  46.1 3.4 %collective-permute-done.3.refs_1_ = bf16[4,20,16,128]{3,2,1,0:T(8,128)(2,1)S(1)} collective-permute-done((bf16[4,20,16,128]{3,2,1,0:T(8,128)(2,1)}, bf16[4,20,16,128]{3,2,1,0:T(8,128)(2,1)S(1)}, u32[]{:S(2)}, u32[]{:S(2)}) %collective-permute-start.3) | collective-permute-done | bytes 327712 | tf_op jit(solution)/shard_map/ppermute | solution.py:566
  52.2 3.2 %collective-permute-done.5.refs_1_ = bf16[2,20,16,128]{3,2,1,0:T(8,128)(2,1)S(1)} collective-permute-done((bf16[2,20,16,128]{3,2,1,0:T(8,128)(2,1)S(1)}, bf16[2,20,16,128]{3,2,1,0:T(8,128)(2,1)S(1)}, u32[]{:S(2)}, u32[]{:S(2)}) %collective-permute-start.5) | collective-permute-done | bytes 163872 | tf_op jit(solution)/shard_map/ppermute | solution.py:566
  59.1 2.6 %collective-permute-done.7.refs_1_ = bf16[1,20,16,128]{3,2,1,0:T(8,128)(2,1)S(1)} collective-permute-done((bf16[1,20,16,128]{3,2,1,0:T(8,128)(2,1)S(1)}, bf16[1,20,16,128]{3,2,1,0:T(8,128)(2,1)S(1)}, u32[]{:S(2)}, u32[]{:S(2)}) %collective-permute-start.7) | collective-permute-done | bytes 81952 | tf_op jit(solution)/shard_map/ppermute | solution.py:566
  63.6 8.2 %all-to-all-start.1 = ((bf16[8,8,16,128]{3,2,1,0:T(8,128)(2,1)}), bf16[8,8,16,128]{3,2,1,0:T(8,128)(2,1)S(1)}, u32[]{:S(2)}, u32[]{:S(2)}) async-start(bf16[8,8,16,128]{3,2,1,0:T(8,128)(2,1)} %bitcast.14), calls=%async_computation.1 | async-start | bytes 524288 | tf_op jit(solution)/shard_map/all_to_all | solution.py:555
  71.8 2.5 %collective-permute-start.8 = (bf16[256,640]{1,0:T(8,128)(2,1)}, bf16[256,640]{1,0:T(8,128)(2,1)S(1)}, u32[]{:S(2)}, u32[]{:S(2)}) collective-permute-start(bf16[256,640]{1,0:T(8,128)(2,1)} %get-tuple-element.56), channel_id=1, source_target_pairs={{0,1},{1,0},{2,3},{3,2},{4,5},{5,4},{6,7},{7,6},{8,9},{9,8},{10,11... | collective-permute-start | bytes 983048 | tf_op jit(solution)/shard_map/ppermute | solution.py:625
  74.3 7.0 %all-to-all-done.1.parts_ref = bf16[8,8,16,128]{3,2,1,0:T(8,128)(2,1)S(1)} async-done(((bf16[8,8,16,128]{3,2,1,0:T(8,128)(2,1)}), bf16[8,8,16,128]{3,2,1,0:T(8,128)(2,1)S(1)}, u32[]{:S(2)}, u32[]{:S(2)}) %all-to-all-start.1) | async-done | bytes 262176 | tf_op jit(solution)/shard_map/all_to_all | solution.py:555
  82.9 7.8 %all-to-all-start.2 = ((bf16[16,16,1152]{2,1,0:T(8,128)(2,1)}), bf16[16,16,1152]{2,1,0:T(8,128)(2,1)S(1)}, u32[]{:S(2)}, u32[]{:S(2)}) async-start(bf16[16,16,1152]{2,1,0:T(8,128)(2,1)} %bitcast.15), calls=%async_computation.2 | async-start | bytes 1179648 | tf_op jit(solution)/shard_map/all_to_all | solution.py:631
  93.4 2.7 %collective-permute-done.9.below_ref = bf16[8,16,128]{2,1,0:T(8,128)(2,1)S(1)} collective-permute-done((bf16[8,16,128]{2,1,0:T(8,128)(2,1)S(1)}, bf16[8,16,128]{2,1,0:T(8,128)(2,1)S(1)}, u32[]{:S(2)}, u32[]{:S(2)}) %collective-permute-start.9) | collective-permute-done | bytes 32800 | tf_op jit(solution)/shard_map/ppermute | solution.py:580
  96.5 4.2 %collective-permute-start.12 = (bf16[16,16,128]{2,1,0:T(8,128)(2,1)S(1)}, bf16[16,16,128]{2,1,0:T(8,128)(2,1)S(1)}, u32[]{:S(2)}, u32[]{:S(2)}) collective-permute-start(bf16[16,16,128]{2,1,0:T(8,128)(2,1)S(1)} %get-tuple-element.59), channel_id=1, source_target_pairs={{0,160},{32,192},{64,224},{96,0},{128,32},{160,64},{192,96},{224,1... | collective-permute-start | bytes 196616 | tf_op jit(solution)/shard_map/ppermute | solution.py:580
  102.9 3.0 %collective-permute-done.11.below_ref = bf16[24,16,128]{2,1,0:T(8,128)(2,1)S(1)} collective-permute-done((bf16[24,16,128]{2,1,0:T(8,128)(2,1)S(1)}, bf16[24,16,128]{2,1,0:T(8,128)(2,1)S(1)}, u32[]{:S(2)}, u32[]{:S(2)}) %collective-permute-start.11) | collective-permute-done | bytes 98336 | tf_op jit(solution)/shard_map/ppermute | solution.py:580
  108.4 2.6 %collective-permute-done.14.refs_3_ = bf16[1,20,16,128]{3,2,1,0:T(8,128)(2,1)S(1)} collective-permute-done((bf16[1,20,16,128]{3,2,1,0:T(8,128)(2,1)S(1)}, bf16[1,20,16,128]{3,2,1,0:T(8,128)(2,1)S(1)}, u32[]{:S(2)}, u32[]{:S(2)}) %collective-permute-start.14) | collective-permute-done | bytes 81952 | tf_op jit(solution)/shard_map/ppermute | solution.py:566
  113.4 2.8 %collective-permute-done.16.refs_3_ = bf16[2,20,16,128]{3,2,1,0:T(8,128)(2,1)S(1)} collective-permute-done((bf16[2,20,16,128]{3,2,1,0:T(8,128)(2,1)S(1)}, bf16[2,20,16,128]{3,2,1,0:T(8,128)(2,1)S(1)}, u32[]{:S(2)}, u32[]{:S(2)}) %collective-permute-start.16) | collective-permute-done | bytes 163872 | tf_op jit(solution)/shard_map/ppermute | solution.py:566
  121.7 6.5 %collective-permute-done.17.refs_2_ = bf16[4,41,16,128]{3,2,1,0:T(8,128)(2,1)S(1)} collective-permute-done((bf16[4,41,16,128]{3,2,1,0:T(8,128)(2,1)S(1)}, bf16[4,41,16,128]{3,2,1,0:T(8,128)(2,1)S(1)}, u32[]{:S(2)}, u32[]{:S(2)}) %collective-permute-start.17) | collective-permute-done | bytes 671776 | tf_op jit(solution)/shard_map/ppermute | solution.py:566
  128.2 4.1 %collective-permute-start.21 = (bf16[4,41,16,128]{3,2,1,0:T(8,128)(2,1)S(1)}, bf16[4,41,16,128]{3,2,1,0:T(8,128)(2,1)S(1)}, u32[]{:S(2)}, u32[]{:S(2)}) collective-permute-start(bf16[4,41,16,128]{3,2,1,0:T(8,128)(2,1)S(1)} %collective-permute-done.17.refs_2_), channel_id=1, source_target_pairs={{0,2},{2,0},{1,3},{3,1},{4,6},{6,4},{5,7},{7,5},{8,10},{10,8},{9,1... | collective-permute-start | bytes 2015240 | tf_op jit(solution)/shard_map/ppermute | solution.py:550
  132.3 2.4 %collective-permute-start.18 = (bf16[4,20,16,128]{3,2,1,0:T(8,128)(2,1)S(1)}, bf16[4,20,16,128]{3,2,1,0:T(8,128)(2,1)S(1)}, u32[]{:S(2)}, u32[]{:S(2)}) collective-permute-start(bf16[4,20,16,128]{3,2,1,0:T(8,128)(2,1)S(1)} %get-tuple-element.72.refs_1_), channel_id=1, source_target_pairs={{0,12},{2,14},{4,8},{6,10},{8,4},{10,6},{12,0},{14,2},{16,28},{18,... | collective-permute-start | bytes 983048 | tf_op jit(solution)/shard_map/ppermute | solution.py:566
  135.0 7.9 %collective-permute-done.18.refs_3_ = bf16[4,20,16,128]{3,2,1,0:T(8,128)(2,1)S(1)} collective-permute-done((bf16[4,20,16,128]{3,2,1,0:T(8,128)(2,1)S(1)}, bf16[4,20,16,128]{3,2,1,0:T(8,128)(2,1)S(1)}, u32[]{:S(2)}, u32[]{:S(2)}) %collective-permute-start.18) | collective-permute-done | bytes 327712 | tf_op jit(solution)/shard_map/ppermute | solution.py:566
  144.9 2.9 %untile.1 = bf16[1728,1152]{1,0:T(8,128)(2,1)} custom-call(s32[1]{0:T(128)} %bitcast.1.where_ref, s32[1]{0:T(128)} %bitcast.2.core_ref.half_ref, bf16[4,41,16,128]{3,2,1,0:T(8,128)(2,1)S(1)} %get-tuple-element.71.refs_0_, bf16[4,20,16,128]{3,2,1,0:T(8,128)(2,1)S(1)} %get-tuple-element.72.refs_1_, ...), custom_call_target="tpu_custom_call" | custom-call | tf_op jit(solution)/shard_map/untile/pallas_call | solution.py:538
  (59 shorter events, 34.7 us)
Async XLA Ops:
  2.9 21.3 %all-to-all-start = ((bf16[16,16,1728]{2,1,0:T(8,128)(2,1)}), bf16[16,16,1728]{2,1,0:T(8,128)(2,1)S(1)}, u32[]{:S(2)}, u32[]{:S(2)}) async-start(bf16[16,16,1728]{2,1,0:T(8,128)(2,1)} %bitcast.33), calls=%async_computation | async-start | bytes 1835008 | tf_op jit(solution)/shard_map/all_to_all | solution.py:610
  33.0 3.1 %collective-permute-start.1 = (bf16[256,1152]{1,0:T(8,128)(2,1)S(1)}, bf16[256,1152]{1,0:T(8,128)(2,1)S(1)}, u32[]{:S(2)}, u32[]{:S(2)}) collective-permute-start(bf16[256,1152]{1,0:T(8,128)(2,1)S(1)} %get-tuple-element.40.mod_a), channel_id=1, source_target_pairs={{0,2},{2,0},{1,3},{3,1},{4,6},{6,4},{5,7},{7,5},{8,10},{10,8},{9,1... | collective-permute-start | bytes 1769480 | tf_op jit(solution)/shard_map/ppermute | solution.py:550
  38.5 11.0 %collective-permute-start.2 = (bf16[4,41,16,128]{3,2,1,0:T(8,128)(2,1)}, bf16[4,41,16,128]{3,2,1,0:T(8,128)(2,1)}, u32[]{:S(2)}, u32[]{:S(2)}) collective-permute-start(bf16[4,41,16,128]{3,2,1,0:T(8,128)(2,1)} %get-tuple-element.42), channel_id=1, source_target_pairs={{0,4},{2,18},{4,0},{6,22},{8,12},{10,26},{12,8},{14,30},{16,20},{1... | collective-permute-start | bytes 2015240 | tf_op jit(solution)/shard_map/ppermute | solution.py:566
  38.8 10.7 %collective-permute-start.3 = (bf16[4,20,16,128]{3,2,1,0:T(8,128)(2,1)}, bf16[4,20,16,128]{3,2,1,0:T(8,128)(2,1)S(1)}, u32[]{:S(2)}, u32[]{:S(2)}) collective-permute-start(bf16[4,20,16,128]{3,2,1,0:T(8,128)(2,1)} %get-tuple-element.43), channel_id=1, source_target_pairs={{0,12},{2,14},{4,8},{6,10},{8,4},{10,6},{12,0},{14,2},{16,28},{18,... | collective-permute-start | bytes 983048 | tf_op jit(solution)/shard_map/ppermute | solution.py:566
  50.9 6.4 %collective-permute-start.4 = (bf16[2,41,16,128]{3,2,1,0:T(8,128)(2,1)S(1)}, bf16[2,41,16,128]{3,2,1,0:T(8,128)(2,1)S(1)}, u32[]{:S(2)}, u32[]{:S(2)}) collective-permute-start(bf16[2,41,16,128]{3,2,1,0:T(8,128)(2,1)S(1)} %get-tuple-element.49), channel_id=1, source_target_pairs={{0,12},{2,6},{4,8},{6,2},{8,4},{10,14},{12,0},{14,10},{16,28},{18,... | collective-permute-start | bytes 1007624 | tf_op jit(solution)/shard_map/ppermute | solution.py:566
  51.0 4.4 %collective-permute-start.5 = (bf16[2,20,16,128]{3,2,1,0:T(8,128)(2,1)S(1)}, bf16[2,20,16,128]{3,2,1,0:T(8,128)(2,1)S(1)}, u32[]{:S(2)}, u32[]{:S(2)}) collective-permute-start(bf16[2,20,16,128]{3,2,1,0:T(8,128)(2,1)S(1)} %get-tuple-element.50), channel_id=1, source_target_pairs={{0,16},{2,18},{4,20},{6,22},{8,24},{10,26},{12,28},{14,30},{16,0},... | collective-permute-start | bytes 491528 | tf_op jit(solution)/shard_map/ppermute | solution.py:566
  57.4 5.5 %collective-permute-start.6 = (bf16[1,41,16,128]{3,2,1,0:T(8,128)(2,1)S(1)}, bf16[1,41,16,128]{3,2,1,0:T(8,128)(2,1)S(1)}, u32[]{:S(2)}, u32[]{:S(2)}) collective-permute-start(bf16[1,41,16,128]{3,2,1,0:T(8,128)(2,1)S(1)} %get-tuple-element.52), channel_id=1, source_target_pairs={{0,16},{2,14},{4,20},{6,10},{8,24},{10,6},{12,28},{14,2},{16,0},{1... | collective-permute-start | bytes 503816 | tf_op jit(solution)/shard_map/ppermute | solution.py:566
  58.5 3.3 %collective-permute-start.7 = (bf16[1,20,16,128]{3,2,1,0:T(8,128)(2,1)S(1)}, bf16[1,20,16,128]{3,2,1,0:T(8,128)(2,1)S(1)}, u32[]{:S(2)}, u32[]{:S(2)}) collective-permute-start(bf16[1,20,16,128]{3,2,1,0:T(8,128)(2,1)S(1)} %get-tuple-element.53), channel_id=1, source_target_pairs={{0,4},{2,6},{4,0},{6,2},{8,12},{10,14},{12,8},{14,10},{16,20},{18,... | collective-permute-start | bytes 245768 | tf_op jit(solution)/shard_map/ppermute | solution.py:566
  63.6 17.6 %all-to-all-start.1 = ((bf16[8,8,16,128]{3,2,1,0:T(8,128)(2,1)}), bf16[8,8,16,128]{3,2,1,0:T(8,128)(2,1)S(1)}, u32[]{:S(2)}, u32[]{:S(2)}) async-start(bf16[8,8,16,128]{3,2,1,0:T(8,128)(2,1)} %bitcast.14), calls=%async_computation.1 | async-start | bytes 524288 | tf_op jit(solution)/shard_map/all_to_all | solution.py:555
  71.8 9.5 %collective-permute-start.8 = (bf16[256,640]{1,0:T(8,128)(2,1)}, bf16[256,640]{1,0:T(8,128)(2,1)S(1)}, u32[]{:S(2)}, u32[]{:S(2)}) collective-permute-start(bf16[256,640]{1,0:T(8,128)(2,1)} %get-tuple-element.56), channel_id=1, source_target_pairs={{0,1},{1,0},{2,3},{3,2},{4,5},{5,4},{6,7},{7,6},{8,9},{9,8},{10,11... | collective-permute-start | bytes 983048 | tf_op jit(solution)/shard_map/ppermute | solution.py:625
  82.9 28.5 %all-to-all-start.2 = ((bf16[16,16,1152]{2,1,0:T(8,128)(2,1)}), bf16[16,16,1152]{2,1,0:T(8,128)(2,1)S(1)}, u32[]{:S(2)}, u32[]{:S(2)}) async-start(bf16[16,16,1152]{2,1,0:T(8,128)(2,1)} %bitcast.15), calls=%async_computation.2 | async-start | bytes 1179648 | tf_op jit(solution)/shard_map/all_to_all | solution.py:631
  90.7 2.8 %collective-permute-start.10 = (bf16[8,16,128]{2,1,0:T(8,128)(2,1)S(1)}, bf16[8,16,128]{2,1,0:T(8,128)(2,1)S(1)}, u32[]{:S(2)}, u32[]{:S(2)}) collective-permute-start(bf16[8,16,128]{2,1,0:T(8,128)(2,1)S(1)} %reduce.1.own_ref), channel_id=1, source_target_pairs={{0,224},{32,0},{64,32},{96,64},{128,96},{160,128},{192,160},{224,1... | collective-permute-start | bytes 98312 | tf_op jit(solution)/shard_map/ppermute | solution.py:580
  91.9 4.3 %collective-permute-start.9 = (bf16[8,16,128]{2,1,0:T(8,128)(2,1)S(1)}, bf16[8,16,128]{2,1,0:T(8,128)(2,1)S(1)}, u32[]{:S(2)}, u32[]{:S(2)}) collective-permute-start(bf16[8,16,128]{2,1,0:T(8,128)(2,1)S(1)} %reduce.1.own_ref), channel_id=1, source_target_pairs={{0,32},{32,64},{64,96},{96,128},{128,160},{160,192},{192,224},{224... | collective-permute-start | bytes 98312 | tf_op jit(solution)/shard_map/ppermute | solution.py:580
  96.2 9.7 %collective-permute-start.11 = (bf16[24,16,128]{2,1,0:T(8,128)(2,1)S(1)}, bf16[24,16,128]{2,1,0:T(8,128)(2,1)S(1)}, u32[]{:S(2)}, u32[]{:S(2)}) collective-permute-start(bf16[24,16,128]{2,1,0:T(8,128)(2,1)S(1)} %get-tuple-element.58.near_ref), channel_id=1, source_target_pairs={{0,96},{32,128},{64,160},{96,192},{128,224},{160,0},{192,32},{224,... | collective-permute-start | bytes 294920 | tf_op jit(solution)/shard_map/ppermute | solution.py:580
  96.5 6.3 %collective-permute-start.12 = (bf16[16,16,128]{2,1,0:T(8,128)(2,1)S(1)}, bf16[16,16,128]{2,1,0:T(8,128)(2,1)S(1)}, u32[]{:S(2)}, u32[]{:S(2)}) collective-permute-start(bf16[16,16,128]{2,1,0:T(8,128)(2,1)S(1)} %get-tuple-element.59), channel_id=1, source_target_pairs={{0,160},{32,192},{64,224},{96,0},{128,32},{160,64},{192,96},{224,1... | collective-permute-start | bytes 196616 | tf_op jit(solution)/shard_map/ppermute | solution.py:580
  105.9 5.5 %collective-permute-start.13 = (bf16[1,41,16,128]{3,2,1,0:T(8,128)(2,1)S(1)}, bf16[1,41,16,128]{3,2,1,0:T(8,128)(2,1)S(1)}, u32[]{:S(2)}, u32[]{:S(2)}) collective-permute-start(bf16[1,41,16,128]{3,2,1,0:T(8,128)(2,1)S(1)} %get-tuple-element.60.refs_0_), channel_id=1, source_target_pairs={{0,16},{2,14},{4,20},{6,10},{8,24},{10,6},{12,28},{14,2},{16,0},{1... | collective-permute-start | bytes 503816 | tf_op jit(solution)/shard_map/ppermute | solution.py:566
  107.3 3.6 %collective-permute-start.14 = (bf16[1,20,16,128]{3,2,1,0:T(8,128)(2,1)S(1)}, bf16[1,20,16,128]{3,2,1,0:T(8,128)(2,1)S(1)}, u32[]{:S(2)}, u32[]{:S(2)}) collective-permute-start(bf16[1,20,16,128]{3,2,1,0:T(8,128)(2,1)S(1)} %get-tuple-element.61.refs_2_), channel_id=1, source_target_pairs={{0,4},{2,6},{4,0},{6,2},{8,12},{10,14},{12,8},{14,10},{16,20},{18,... | collective-permute-start | bytes 245768 | tf_op jit(solution)/shard_map/ppermute | solution.py:566
  111.4 6.4 %collective-permute-start.15 = (bf16[2,41,16,128]{3,2,1,0:T(8,128)(2,1)S(1)}, bf16[2,41,16,128]{3,2,1,0:T(8,128)(2,1)S(1)}, u32[]{:S(2)}, u32[]{:S(2)}) collective-permute-start(bf16[2,41,16,128]{3,2,1,0:T(8,128)(2,1)S(1)} %get-tuple-element.69.refs_0_), channel_id=1, source_target_pairs={{0,12},{2,6},{4,8},{6,2},{8,4},{10,14},{12,0},{14,10},{16,28},{18,... | collective-permute-start | bytes 1007624 | tf_op jit(solution)/shard_map/ppermute | solution.py:566
  112.1 4.2 %collective-permute-start.16 = (bf16[2,20,16,128]{3,2,1,0:T(8,128)(2,1)S(1)}, bf16[2,20,16,128]{3,2,1,0:T(8,128)(2,1)S(1)}, u32[]{:S(2)}, u32[]{:S(2)}) collective-permute-start(bf16[2,20,16,128]{3,2,1,0:T(8,128)(2,1)S(1)} %get-tuple-element.70.refs_2_), channel_id=1, source_target_pairs={{0,16},{2,18},{4,20},{6,22},{8,24},{10,26},{12,28},{14,30},{16,0},... | collective-permute-start | bytes 491528 | tf_op jit(solution)/shard_map/ppermute | solution.py:566
  117.9 10.3 %collective-permute-start.17 = (bf16[4,41,16,128]{3,2,1,0:T(8,128)(2,1)S(1)}, bf16[4,41,16,128]{3,2,1,0:T(8,128)(2,1)S(1)}, u32[]{:S(2)}, u32[]{:S(2)}) collective-permute-start(bf16[4,41,16,128]{3,2,1,0:T(8,128)(2,1)S(1)} %get-tuple-element.71.refs_0_), channel_id=1, source_target_pairs={{0,4},{2,18},{4,0},{6,22},{8,12},{10,26},{12,8},{14,30},{16,20},{1... | collective-permute-start | bytes 2015240 | tf_op jit(solution)/shard_map/ppermute | solution.py:566
  119.8 25.2 %collective-permute-start.19 = (bf16[4,41,16,128]{3,2,1,0:T(8,128)(2,1)S(1)}, bf16[4,41,16,128]{3,2,1,0:T(8,128)(2,1)S(1)}, u32[]{:S(2)}, u32[]{:S(2)}) collective-permute-start(bf16[4,41,16,128]{3,2,1,0:T(8,128)(2,1)S(1)} %get-tuple-element.71.refs_0_), channel_id=1, source_target_pairs={{0,2},{2,0},{1,3},{3,1},{4,6},{6,4},{5,7},{7,5},{8,10},{10,8},{9,1... | collective-permute-start | bytes 2015240 | tf_op jit(solution)/shard_map/ppermute | solution.py:550
  128.2 16.7 %collective-permute-start.21 = (bf16[4,41,16,128]{3,2,1,0:T(8,128)(2,1)S(1)}, bf16[4,41,16,128]{3,2,1,0:T(8,128)(2,1)S(1)}, u32[]{:S(2)}, u32[]{:S(2)}) collective-permute-start(bf16[4,41,16,128]{3,2,1,0:T(8,128)(2,1)S(1)} %collective-permute-done.17.refs_2_), channel_id=1, source_target_pairs={{0,2},{2,0},{1,3},{3,1},{4,6},{6,4},{5,7},{7,5},{8,10},{10,8},{9,1... | collective-permute-start | bytes 2015240 | tf_op jit(solution)/shard_map/ppermute | solution.py:550
  132.3 10.6 %collective-permute-start.18 = (bf16[4,20,16,128]{3,2,1,0:T(8,128)(2,1)S(1)}, bf16[4,20,16,128]{3,2,1,0:T(8,128)(2,1)S(1)}, u32[]{:S(2)}, u32[]{:S(2)}) collective-permute-start(bf16[4,20,16,128]{3,2,1,0:T(8,128)(2,1)S(1)} %get-tuple-element.72.refs_1_), channel_id=1, source_target_pairs={{0,12},{2,14},{4,8},{6,10},{8,4},{10,6},{12,0},{14,2},{16,28},{18,... | collective-permute-start | bytes 983048 | tf_op jit(solution)/shard_map/ppermute | solution.py:566
  134.7 10.0 %collective-permute-start.20 = (bf16[4,20,16,128]{3,2,1,0:T(8,128)(2,1)S(1)}, bf16[4,20,16,128]{3,2,1,0:T(8,128)(2,1)S(1)}, u32[]{:S(2)}, u32[]{:S(2)}) collective-permute-start(bf16[4,20,16,128]{3,2,1,0:T(8,128)(2,1)S(1)} %get-tuple-element.72.refs_1_), channel_id=1, source_target_pairs={{0,2},{2,0},{1,3},{3,1},{4,6},{6,4},{5,7},{7,5},{8,10},{10,8},{9,1... | collective-permute-start | bytes 983048 | tf_op jit(solution)/shard_map/ppermute | solution.py:550
  (8 other events, 78.3 us)

commit v11 on v10

--- a/solution.py
+++ b/solution.py
@@ -590,7 +590,9 @@
     got, beside = lax.optimization_barrier((meet(have, 2), beside))
     have = join(list(zip(have, got)))
     have = join(list(zip(have, meet(have, 1))))
-    pieces = list(have) + meet(have, 0)
+    got = meet(have, 0)
+    got[-1], have, beside = lax.optimization_barrier((got[-1], have, unpack(beside)))
+    pieces = list(have) + got
     pieces = pieces + [swap(piece, ("core",), 1) for piece in pieces]
     return untile(where, half, pieces, rows, width), beside
 
@@ -631,8 +633,8 @@
     home = lax.all_to_all(home, SEQ, split_axis=0, concat_axis=0, tiled=True)
     clip = lax.axis_index("dp").astype(jnp.int32).reshape(1)
     have = place(clip, near, below, above, clips, size)
-    grad_qkv, home = gather_plane(have, where, core, 3 * hw, width, home)
-    grad_t, att_t = unpack(home.reshape(patches, width))
+    home = home.reshape(patches, width)
+    grad_qkv, (grad_t, att_t) = gather_plane(have, where, core, 3 * hw, width, home)
     grad_qkv = grad_qkv.reshape(3, hw, width).transpose(2, 0, 1)
     return (att_t.T[None, None], grad_t.T[None, None], grad_qkv)
 

time: 151 us -> 141 us (0.934)
  waiting for transfers between devices: 64.1 us -> 57.3 us
  starting transfers between devices: 52.5 us -> 49.4 us
    ppermute x12, waiting for transfers between devices: 34 us -> 25.2 us  [meet(): found.append(lax.ppermute(block, SEQ, pairs))]
    ppermute x6, starting transfers between devices: 7.97 us -> 5.44 us  [swap(): return lax.ppermute(x, axes, [(i, i ^ k) for i in range(count)])]
    ppermute x6, waiting for transfers between devices: 2.46 us -> 4.44 us  [swap(): return lax.ppermute(x, axes, [(i, i ^ k) for i in range(count)])]
where the time goes in v11:
time: 141 us; the launch traced here: 138 us
  waiting for transfers between devices  57.3 us (41%)
  starting transfers between devices  49.4 us (35%)
  Pallas kernels  26 us (18%)
  local copies, waits for them, and re-layouts  3.16 us (2%)
    ppermute x12, waiting for transfers between devices, meet(): found.append(lax.ppermute(block, SEQ, pairs))  25.2 us
    ppermute x12, starting transfers between devices, meet(): found.append(lax.ppermute(block, SEQ, pairs))  12.5 us
    all_to_all x1, waiting for transfers between devices, body(): lax.all_to_all(x, SEQ, split_axis=0, concat_axis=0, tiled=True)  11.5 us
    ppermute x4, waiting for transfers between devices, shift(): lax.ppermute(x, axis, [(i, (i + step) % count) for i in range(count)])  9.13 us
    all_to_all x1, starting transfers between devices, exchange(): return lax.all_to_all(parts, axis, split_axis=0, concat_axis=0, tiled=True)  8.18 us
    all_to_all x1, starting transfers between devices, body(): home = lax.all_to_all(home, SEQ, split_axis=0, concat_axis=0, tiled=True)  7.8 us
    pallas_call x1, Pallas kernels, attend(): pl.pallas_call(functools.partial(attend_kernel, patches=patches, heads=he...  7.12 us
    all_to_all x1, waiting for transfers between devices, exchange(): return lax.all_to_all(parts, axis, split_axis=0, concat_axis=0, tiled=True)  6.99 us
  transfers between devices with their start and end apart: 26, of which 19 were waited for; matrix products, arithmetic and copies ran while one was open for 2% of the time, Pallas kernels for 5%

profile of v11, /device:TPU:1, one launch (start us, length us, event | category | flops | bytes accessed | tf_op | source)
XLA Modules:
  0.0 137.9 jit_solution(7741011351279729647)
XLA Ops:
  0.6 2.2 %pack.1 = bf16[256,1728]{1,0:T(8,128)(2,1)} custom-call(bf16[256,1152]{1,0:T(8,128)(2,1)} %bitcast.34, bf16[576,256]{1,0:T(8,128)(2,1)} %bitcast.35), custom_call_target="tpu_custom_call" | custom-call | tf_op jit(solution)/shard_map/pack/pallas_call | solution.py:52
  2.9 6.9 %all-to-all-start = ((bf16[16,16,1728]{2,1,0:T(8,128)(2,1)}), bf16[16,16,1728]{2,1,0:T(8,128)(2,1)S(1)}, u32[]{:S(2)}, u32[]{:S(2)}) async-start(bf16[16,16,1728]{2,1,0:T(8,128)(2,1)} %bitcast.33), calls=%async_computation | async-start | bytes 1835008 | tf_op jit(solution)/shard_map/all_to_all | solution.py:612
  12.7 11.5 %all-to-all-done = bf16[16,16,1728]{2,1,0:T(8,128)(2,1)S(1)} async-done(((bf16[16,16,1728]{2,1,0:T(8,128)(2,1)}), bf16[16,16,1728]{2,1,0:T(8,128)(2,1)S(1)}, u32[]{:S(2)}, u32[]{:S(2)}) %all-to-all-start) | async-done | bytes 884768 | tf_op jit(solution)/shard_map/all_to_all | solution.py:612
  25.1 7.1 %attend.1 = (bf16[256,1152]{1,0:T(8,128)(2,1)S(1)}, bf16[864,256]{1,0:T(8,128)(2,1)S(1)}, bf16[864,256]{1,0:T(8,128)(2,1)S(1)}, bf16[576,256]{1,0:T(8,128)(2,1)S(1)}) custom-call(s32[1]{0:T(128)} %bitcast.2.core_ref.half_ref, bf16[256,1728]{1,0:T(8,128)(2,1)} %bitcast.30, f32[2,1152]{1,0:T(2,128)S(1)} %pad_maximum_fusion.affine_ref.affine_hbm, ...), custom_call_target="tpu_custom_call" | custom-call | tf_op jit(solution)/shard_map/attend/pallas_call | solution.py:203
  33.9 2.3 %collective-permute-done.gp_b = bf16[864,256]{1,0:T(8,128)(2,1)S(1)} collective-permute-done((bf16[864,256]{1,0:T(8,128)(2,1)S(1)}, bf16[864,256]{1,0:T(8,128)(2,1)S(1)}, u32[]{:S(2)}, u32[]{:S(2)}) %collective-permute-start) | collective-permute-done | bytes 442400 | tf_op jit(solution)/shard_map/ppermute | solution.py:550
  36.1 2.4 %outer.1 = (bf16[4,41,16,128]{3,2,1,0:T(8,128)(2,1)}, bf16[4,20,16,128]{3,2,1,0:T(8,128)(2,1)}, bf16[4,61,16,128]{3,2,1,0:T(8,128)(2,1)S(1)}) custom-call(s32[1]{0:T(128)} %bitcast.1.where_ref, s32[1]{0:T(128)} %bitcast.2.core_ref.half_ref, bf16[864,256]{1,0:T(8,128)(2,1)S(1)} %get-tuple-element.43.gp_a.gp_keep_hbm, ...), custom_call_target="tpu_custom_call" | custom-call | tf_op jit(solution)/shard_map/outer/pallas_call | solution.py:331
  39.8 6.3 %split.1 = (bf16[256,640]{1,0:T(8,128)(2,1)}, f32[256,1920]{1,0:T(8,128)}) custom-call(s32[1]{0:T(128)} %bitcast.2.core_ref.half_ref, s32[1]{0:T(128)} %bitcast.12.which_ref, bf16[256,1728]{1,0:T(8,128)(2,1)} %bitcast.31, f32[2,1152]{1,0:T(2,128)} %copy-done.4, bf16[1728,1152]{1,0:T(8,128)(2,1)} %bitcast.29, bf16[864,256]{1,0:T(8,128)(2,1)} %copy-done.1, ...), custom_call_target="tpu_custom_call" | custom-call | tf_op jit(solution)/shard_map/split/pallas_call | solution.py:286
  46.1 3.4 %collective-permute-done.3.refs_1_ = bf16[4,20,16,128]{3,2,1,0:T(8,128)(2,1)S(1)} collective-permute-done((bf16[4,20,16,128]{3,2,1,0:T(8,128)(2,1)}, bf16[4,20,16,128]{3,2,1,0:T(8,128)(2,1)S(1)}, u32[]{:S(2)}, u32[]{:S(2)}) %collective-permute-start.3) | collective-permute-done | bytes 327712 | tf_op jit(solution)/shard_map/ppermute | solution.py:566
  52.2 3.2 %collective-permute-done.5.refs_1_ = bf16[2,20,16,128]{3,2,1,0:T(8,128)(2,1)S(1)} collective-permute-done((bf16[2,20,16,128]{3,2,1,0:T(8,128)(2,1)S(1)}, bf16[2,20,16,128]{3,2,1,0:T(8,128)(2,1)S(1)}, u32[]{:S(2)}, u32[]{:S(2)}) %collective-permute-start.5) | collective-permute-done | bytes 163872 | tf_op jit(solution)/shard_map/ppermute | solution.py:566
  55.4 1.9 %collective-permute-done.4.refs_0_ = bf16[2,41,16,128]{3,2,1,0:T(8,128)(2,1)S(1)} collective-permute-done((bf16[2,41,16,128]{3,2,1,0:T(8,128)(2,1)S(1)}, bf16[2,41,16,128]{3,2,1,0:T(8,128)(2,1)S(1)}, u32[]{:S(2)}, u32[]{:S(2)}) %collective-permute-start.4) | collective-permute-done | bytes 335904 | tf_op jit(solution)/shard_map/ppermute | solution.py:566
  59.1 2.6 %collective-permute-done.7.refs_1_ = bf16[1,20,16,128]{3,2,1,0:T(8,128)(2,1)S(1)} collective-permute-done((bf16[1,20,16,128]{3,2,1,0:T(8,128)(2,1)S(1)}, bf16[1,20,16,128]{3,2,1,0:T(8,128)(2,1)S(1)}, u32[]{:S(2)}, u32[]{:S(2)}) %collective-permute-start.7) | collective-permute-done | bytes 81952 | tf_op jit(solution)/shard_map/ppermute | solution.py:566
  63.6 8.2 %all-to-all-start.1 = ((bf16[8,8,16,128]{3,2,1,0:T(8,128)(2,1)}), bf16[8,8,16,128]{3,2,1,0:T(8,128)(2,1)S(1)}, u32[]{:S(2)}, u32[]{:S(2)}) async-start(bf16[8,8,16,128]{3,2,1,0:T(8,128)(2,1)} %bitcast.14), calls=%async_computation.1 | async-start | bytes 524288 | tf_op jit(solution)/shard_map/all_to_all | solution.py:555
  71.8 2.5 %collective-permute-start.8 = (bf16[256,640]{1,0:T(8,128)(2,1)}, bf16[256,640]{1,0:T(8,128)(2,1)S(1)}, u32[]{:S(2)}, u32[]{:S(2)}) collective-permute-start(bf16[256,640]{1,0:T(8,128)(2,1)} %get-tuple-element.61), channel_id=1, source_target_pairs={{0,1},{1,0},{2,3},{3,2},{4,5},{5,4},{6,7},{7,6},{8,9},{9,8},{10,11... | collective-permute-start | bytes 983048 | tf_op jit(solution)/shard_map/ppermute | solution.py:627
  74.3 7.0 %all-to-all-done.1.parts_ref = bf16[8,8,16,128]{3,2,1,0:T(8,128)(2,1)S(1)} async-done(((bf16[8,8,16,128]{3,2,1,0:T(8,128)(2,1)}), bf16[8,8,16,128]{3,2,1,0:T(8,128)(2,1)S(1)}, u32[]{:S(2)}, u32[]{:S(2)}) %all-to-all-start.1) | async-done | bytes 262176 | tf_op jit(solution)/shard_map/all_to_all | solution.py:555
  82.9 7.8 %all-to-all-start.2 = ((bf16[16,16,1152]{2,1,0:T(8,128)(2,1)}), bf16[16,16,1152]{2,1,0:T(8,128)(2,1)S(1)}, u32[]{:S(2)}, u32[]{:S(2)}) async-start(bf16[16,16,1152]{2,1,0:T(8,128)(2,1)} %bitcast.15), calls=%async_computation.2 | async-start | bytes 1179648 | tf_op jit(solution)/shard_map/all_to_all | solution.py:633
  93.4 2.7 %collective-permute-done.9.below_ref = bf16[8,16,128]{2,1,0:T(8,128)(2,1)S(1)} collective-permute-done((bf16[8,16,128]{2,1,0:T(8,128)(2,1)S(1)}, bf16[8,16,128]{2,1,0:T(8,128)(2,1)S(1)}, u32[]{:S(2)}, u32[]{:S(2)}) %collective-permute-start.9) | collective-permute-done | bytes 32800 | tf_op jit(solution)/shard_map/ppermute | solution.py:580
  96.5 4.2 %collective-permute-start.12 = (bf16[16,16,128]{2,1,0:T(8,128)(2,1)S(1)}, bf16[16,16,128]{2,1,0:T(8,128)(2,1)S(1)}, u32[]{:S(2)}, u32[]{:S(2)}) collective-permute-start(bf16[16,16,128]{2,1,0:T(8,128)(2,1)S(1)} %get-tuple-element.64), channel_id=1, source_target_pairs={{0,160},{32,192},{64,224},{96,0},{128,32},{160,64},{192,96},{224,1... | collective-permute-start | bytes 196616 | tf_op jit(solution)/shard_map/ppermute | solution.py:580
  100.7 2.1 %collective-permute-done.12.above_ref = bf16[16,16,128]{2,1,0:T(8,128)(2,1)S(1)} collective-permute-done((bf16[16,16,128]{2,1,0:T(8,128)(2,1)S(1)}, bf16[16,16,128]{2,1,0:T(8,128)(2,1)S(1)}, u32[]{:S(2)}, u32[]{:S(2)}) %collective-permute-start.12) | collective-permute-done | bytes 65568 | tf_op jit(solution)/shard_map/ppermute | solution.py:580
  102.9 3.0 %collective-permute-done.11.below_ref = bf16[24,16,128]{2,1,0:T(8,128)(2,1)S(1)} collective-permute-done((bf16[24,16,128]{2,1,0:T(8,128)(2,1)S(1)}, bf16[24,16,128]{2,1,0:T(8,128)(2,1)S(1)}, u32[]{:S(2)}, u32[]{:S(2)}) %collective-permute-start.11) | collective-permute-done | bytes 98336 | tf_op jit(solution)/shard_map/ppermute | solution.py:580
  108.4 2.6 %collective-permute-done.14.refs_3_ = bf16[1,20,16,128]{3,2,1,0:T(8,128)(2,1)S(1)} collective-permute-done((bf16[1,20,16,128]{3,2,1,0:T(8,128)(2,1)S(1)}, bf16[1,20,16,128]{3,2,1,0:T(8,128)(2,1)S(1)}, u32[]{:S(2)}, u32[]{:S(2)}) %collective-permute-start.14) | collective-permute-done | bytes 81952 | tf_op jit(solution)/shard_map/ppermute | solution.py:566
  113.4 2.8 %collective-permute-done.16.refs_3_ = bf16[2,20,16,128]{3,2,1,0:T(8,128)(2,1)S(1)} collective-permute-done((bf16[2,20,16,128]{3,2,1,0:T(8,128)(2,1)S(1)}, bf16[2,20,16,128]{3,2,1,0:T(8,128)(2,1)S(1)}, u32[]{:S(2)}, u32[]{:S(2)}) %collective-permute-start.16) | collective-permute-done | bytes 163872 | tf_op jit(solution)/shard_map/ppermute | solution.py:566
  122.7 5.6 %collective-permute-done.17.refs_3_ = bf16[4,20,16,128]{3,2,1,0:T(8,128)(2,1)S(1)} collective-permute-done((bf16[4,20,16,128]{3,2,1,0:T(8,128)(2,1)S(1)}, bf16[4,20,16,128]{3,2,1,0:T(8,128)(2,1)S(1)}, u32[]{:S(2)}, u32[]{:S(2)}) %collective-permute-start.17) | collective-permute-done | bytes 327712 | tf_op jit(solution)/shard_map/ppermute | solution.py:566
  128.3 2.8 %collective-permute-start.19 = (bf16[4,41,16,128]{3,2,1,0:T(8,128)(2,1)S(1)}, bf16[4,41,16,128]{3,2,1,0:T(8,128)(2,1)S(1)}, u32[]{:S(2)}, u32[]{:S(2)}) collective-permute-start(bf16[4,41,16,128]{3,2,1,0:T(8,128)(2,1)S(1)} %get-tuple-element.80.refs_0_), channel_id=1, source_target_pairs={{0,2},{2,0},{1,3},{3,1},{4,6},{6,4},{5,7},{7,5},{8,10},{10,8},{9,1... | collective-permute-start | bytes 2015240 | tf_op jit(solution)/shard_map/ppermute | solution.py:550
  135.0 2.9 %untile.1 = bf16[1728,1152]{1,0:T(8,128)(2,1)} custom-call(s32[1]{0:T(128)} %bitcast.1.where_ref, s32[1]{0:T(128)} %bitcast.2.core_ref.half_ref, bf16[4,41,16,128]{3,2,1,0:T(8,128)(2,1)S(1)} %get-tuple-element.80.refs_0_, bf16[4,20,16,128]{3,2,1,0:T(8,128)(2,1)S(1)} %get-tuple-element.81.refs_1_, ...), custom_call_target="tpu_custom_call" | custom-call | tf_op jit(solution)/shard_map/untile/pallas_call | solution.py:538
  (59 shorter events, 33.2 us)
Async XLA Ops:
  2.9 21.3 %all-to-all-start = ((bf16[16,16,1728]{2,1,0:T(8,128)(2,1)}), bf16[16,16,1728]{2,1,0:T(8,128)(2,1)S(1)}, u32[]{:S(2)}, u32[]{:S(2)}) async-start(bf16[16,16,1728]{2,1,0:T(8,128)(2,1)} %bitcast.33), calls=%async_computation | async-start | bytes 1835008 | tf_op jit(solution)/shard_map/all_to_all | solution.py:612
  33.0 3.1 %collective-permute-start.1 = (bf16[256,1152]{1,0:T(8,128)(2,1)S(1)}, bf16[256,1152]{1,0:T(8,128)(2,1)S(1)}, u32[]{:S(2)}, u32[]{:S(2)}) collective-permute-start(bf16[256,1152]{1,0:T(8,128)(2,1)S(1)} %get-tuple-element.45.mod_a), channel_id=1, source_target_pairs={{0,2},{2,0},{1,3},{3,1},{4,6},{6,4},{5,7},{7,5},{8,10},{10,8},{9,1... | collective-permute-start | bytes 1769480 | tf_op jit(solution)/shard_map/ppermute | solution.py:550
  38.5 11.0 %collective-permute-start.2 = (bf16[4,41,16,128]{3,2,1,0:T(8,128)(2,1)}, bf16[4,41,16,128]{3,2,1,0:T(8,128)(2,1)}, u32[]{:S(2)}, u32[]{:S(2)}) collective-permute-start(bf16[4,41,16,128]{3,2,1,0:T(8,128)(2,1)} %get-tuple-element.47), channel_id=1, source_target_pairs={{0,4},{2,18},{4,0},{6,22},{8,12},{10,26},{12,8},{14,30},{16,20},{1... | collective-permute-start | bytes 2015240 | tf_op jit(solution)/shard_map/ppermute | solution.py:566
  38.8 10.7 %collective-permute-start.3 = (bf16[4,20,16,128]{3,2,1,0:T(8,128)(2,1)}, bf16[4,20,16,128]{3,2,1,0:T(8,128)(2,1)S(1)}, u32[]{:S(2)}, u32[]{:S(2)}) collective-permute-start(bf16[4,20,16,128]{3,2,1,0:T(8,128)(2,1)} %get-tuple-element.48), channel_id=1, source_target_pairs={{0,12},{2,14},{4,8},{6,10},{8,4},{10,6},{12,0},{14,2},{16,28},{18,... | collective-permute-start | bytes 983048 | tf_op jit(solution)/shard_map/ppermute | solution.py:566
  50.9 6.4 %collective-permute-start.4 = (bf16[2,41,16,128]{3,2,1,0:T(8,128)(2,1)S(1)}, bf16[2,41,16,128]{3,2,1,0:T(8,128)(2,1)S(1)}, u32[]{:S(2)}, u32[]{:S(2)}) collective-permute-start(bf16[2,41,16,128]{3,2,1,0:T(8,128)(2,1)S(1)} %get-tuple-element.54), channel_id=1, source_target_pairs={{0,12},{2,6},{4,8},{6,2},{8,4},{10,14},{12,0},{14,10},{16,28},{18,... | collective-permute-start | bytes 1007624 | tf_op jit(solution)/shard_map/ppermute | solution.py:566
  51.0 4.4 %collective-permute-start.5 = (bf16[2,20,16,128]{3,2,1,0:T(8,128)(2,1)S(1)}, bf16[2,20,16,128]{3,2,1,0:T(8,128)(2,1)S(1)}, u32[]{:S(2)}, u32[]{:S(2)}) collective-permute-start(bf16[2,20,16,128]{3,2,1,0:T(8,128)(2,1)S(1)} %get-tuple-element.55), channel_id=1, source_target_pairs={{0,16},{2,18},{4,20},{6,22},{8,24},{10,26},{12,28},{14,30},{16,0},... | collective-permute-start | bytes 491528 | tf_op jit(solution)/shard_map/ppermute | solution.py:566
  57.4 5.5 %collective-permute-start.6 = (bf16[1,41,16,128]{3,2,1,0:T(8,128)(2,1)S(1)}, bf16[1,41,16,128]{3,2,1,0:T(8,128)(2,1)S(1)}, u32[]{:S(2)}, u32[]{:S(2)}) collective-permute-start(bf16[1,41,16,128]{3,2,1,0:T(8,128)(2,1)S(1)} %get-tuple-element.57), channel_id=1, source_target_pairs={{0,16},{2,14},{4,20},{6,10},{8,24},{10,6},{12,28},{14,2},{16,0},{1... | collective-permute-start | bytes 503816 | tf_op jit(solution)/shard_map/ppermute | solution.py:566
  58.5 3.3 %collective-permute-start.7 = (bf16[1,20,16,128]{3,2,1,0:T(8,128)(2,1)S(1)}, bf16[1,20,16,128]{3,2,1,0:T(8,128)(2,1)S(1)}, u32[]{:S(2)}, u32[]{:S(2)}) collective-permute-start(bf16[1,20,16,128]{3,2,1,0:T(8,128)(2,1)S(1)} %get-tuple-element.58), channel_id=1, source_target_pairs={{0,4},{2,6},{4,0},{6,2},{8,12},{10,14},{12,8},{14,10},{16,20},{18,... | collective-permute-start | bytes 245768 | tf_op jit(solution)/shard_map/ppermute | solution.py:566
  63.6 17.6 %all-to-all-start.1 = ((bf16[8,8,16,128]{3,2,1,0:T(8,128)(2,1)}), bf16[8,8,16,128]{3,2,1,0:T(8,128)(2,1)S(1)}, u32[]{:S(2)}, u32[]{:S(2)}) async-start(bf16[8,8,16,128]{3,2,1,0:T(8,128)(2,1)} %bitcast.14), calls=%async_computation.1 | async-start | bytes 524288 | tf_op jit(solution)/shard_map/all_to_all | solution.py:555
  71.8 9.5 %collective-permute-start.8 = (bf16[256,640]{1,0:T(8,128)(2,1)}, bf16[256,640]{1,0:T(8,128)(2,1)S(1)}, u32[]{:S(2)}, u32[]{:S(2)}) collective-permute-start(bf16[256,640]{1,0:T(8,128)(2,1)} %get-tuple-element.61), channel_id=1, source_target_pairs={{0,1},{1,0},{2,3},{3,2},{4,5},{5,4},{6,7},{7,6},{8,9},{9,8},{10,11... | collective-permute-start | bytes 983048 | tf_op jit(solution)/shard_map/ppermute | solution.py:627
  82.9 28.5 %all-to-all-start.2 = ((bf16[16,16,1152]{2,1,0:T(8,128)(2,1)}), bf16[16,16,1152]{2,1,0:T(8,128)(2,1)S(1)}, u32[]{:S(2)}, u32[]{:S(2)}) async-start(bf16[16,16,1152]{2,1,0:T(8,128)(2,1)} %bitcast.15), calls=%async_computation.2 | async-start | bytes 1179648 | tf_op jit(solution)/shard_map/all_to_all | solution.py:633
  90.7 2.8 %collective-permute-start.10 = (bf16[8,16,128]{2,1,0:T(8,128)(2,1)S(1)}, bf16[8,16,128]{2,1,0:T(8,128)(2,1)S(1)}, u32[]{:S(2)}, u32[]{:S(2)}) collective-permute-start(bf16[8,16,128]{2,1,0:T(8,128)(2,1)S(1)} %reduce.1.own_ref), channel_id=1, source_target_pairs={{0,224},{32,0},{64,32},{96,64},{128,96},{160,128},{192,160},{224,1... | collective-permute-start | bytes 98312 | tf_op jit(solution)/shard_map/ppermute | solution.py:580
  91.9 4.3 %collective-permute-start.9 = (bf16[8,16,128]{2,1,0:T(8,128)(2,1)S(1)}, bf16[8,16,128]{2,1,0:T(8,128)(2,1)S(1)}, u32[]{:S(2)}, u32[]{:S(2)}) collective-permute-start(bf16[8,16,128]{2,1,0:T(8,128)(2,1)S(1)} %reduce.1.own_ref), channel_id=1, source_target_pairs={{0,32},{32,64},{64,96},{96,128},{128,160},{160,192},{192,224},{224... | collective-permute-start | bytes 98312 | tf_op jit(solution)/shard_map/ppermute | solution.py:580
  96.2 9.7 %collective-permute-start.11 = (bf16[24,16,128]{2,1,0:T(8,128)(2,1)S(1)}, bf16[24,16,128]{2,1,0:T(8,128)(2,1)S(1)}, u32[]{:S(2)}, u32[]{:S(2)}) collective-permute-start(bf16[24,16,128]{2,1,0:T(8,128)(2,1)S(1)} %get-tuple-element.63.near_ref), channel_id=1, source_target_pairs={{0,96},{32,128},{64,160},{96,192},{128,224},{160,0},{192,32},{224,... | collective-permute-start | bytes 294920 | tf_op jit(solution)/shard_map/ppermute | solution.py:580
  96.5 6.3 %collective-permute-start.12 = (bf16[16,16,128]{2,1,0:T(8,128)(2,1)S(1)}, bf16[16,16,128]{2,1,0:T(8,128)(2,1)S(1)}, u32[]{:S(2)}, u32[]{:S(2)}) collective-permute-start(bf16[16,16,128]{2,1,0:T(8,128)(2,1)S(1)} %get-tuple-element.64), channel_id=1, source_target_pairs={{0,160},{32,192},{64,224},{96,0},{128,32},{160,64},{192,96},{224,1... | collective-permute-start | bytes 196616 | tf_op jit(solution)/shard_map/ppermute | solution.py:580
  105.9 5.5 %collective-permute-start.13 = (bf16[1,41,16,128]{3,2,1,0:T(8,128)(2,1)S(1)}, bf16[1,41,16,128]{3,2,1,0:T(8,128)(2,1)S(1)}, u32[]{:S(2)}, u32[]{:S(2)}) collective-permute-start(bf16[1,41,16,128]{3,2,1,0:T(8,128)(2,1)S(1)} %get-tuple-element.65.refs_0_), channel_id=1, source_target_pairs={{0,16},{2,14},{4,20},{6,10},{8,24},{10,6},{12,28},{14,2},{16,0},{1... | collective-permute-start | bytes 503816 | tf_op jit(solution)/shard_map/ppermute | solution.py:566
  107.3 3.6 %collective-permute-start.14 = (bf16[1,20,16,128]{3,2,1,0:T(8,128)(2,1)S(1)}, bf16[1,20,16,128]{3,2,1,0:T(8,128)(2,1)S(1)}, u32[]{:S(2)}, u32[]{:S(2)}) collective-permute-start(bf16[1,20,16,128]{3,2,1,0:T(8,128)(2,1)S(1)} %get-tuple-element.66.refs_2_), channel_id=1, source_target_pairs={{0,4},{2,6},{4,0},{6,2},{8,12},{10,14},{12,8},{14,10},{16,20},{18,... | collective-permute-start | bytes 245768 | tf_op jit(solution)/shard_map/ppermute | solution.py:566
  111.4 6.4 %collective-permute-start.15 = (bf16[2,41,16,128]{3,2,1,0:T(8,128)(2,1)S(1)}, bf16[2,41,16,128]{3,2,1,0:T(8,128)(2,1)S(1)}, u32[]{:S(2)}, u32[]{:S(2)}) collective-permute-start(bf16[2,41,16,128]{3,2,1,0:T(8,128)(2,1)S(1)} %get-tuple-element.71.refs_0_), channel_id=1, source_target_pairs={{0,12},{2,6},{4,8},{6,2},{8,4},{10,14},{12,0},{14,10},{16,28},{18,... | collective-permute-start | bytes 1007624 | tf_op jit(solution)/shard_map/ppermute | solution.py:566
  112.1 4.2 %collective-permute-start.16 = (bf16[2,20,16,128]{3,2,1,0:T(8,128)(2,1)S(1)}, bf16[2,20,16,128]{3,2,1,0:T(8,128)(2,1)S(1)}, u32[]{:S(2)}, u32[]{:S(2)}) collective-permute-start(bf16[2,20,16,128]{3,2,1,0:T(8,128)(2,1)S(1)} %get-tuple-element.72.refs_2_), channel_id=1, source_target_pairs={{0,16},{2,18},{4,20},{6,22},{8,24},{10,26},{12,28},{14,30},{16,0},... | collective-permute-start | bytes 491528 | tf_op jit(solution)/shard_map/ppermute | solution.py:566
  117.9 13.2 %collective-permute-start.18 = (bf16[4,41,16,128]{3,2,1,0:T(8,128)(2,1)S(1)}, bf16[4,41,16,128]{3,2,1,0:T(8,128)(2,1)S(1)}, u32[]{:S(2)}, u32[]{:S(2)}) collective-permute-start(bf16[4,41,16,128]{3,2,1,0:T(8,128)(2,1)S(1)} %get-tuple-element.80.refs_0_), channel_id=1, source_target_pairs={{0,4},{2,18},{4,0},{6,22},{8,12},{10,26},{12,8},{14,30},{16,20},{1... | collective-permute-start | bytes 2015240 | tf_op jit(solution)/shard_map/ppermute | solution.py:566
  119.8 8.5 %collective-permute-start.17 = (bf16[4,20,16,128]{3,2,1,0:T(8,128)(2,1)S(1)}, bf16[4,20,16,128]{3,2,1,0:T(8,128)(2,1)S(1)}, u32[]{:S(2)}, u32[]{:S(2)}) collective-permute-start(bf16[4,20,16,128]{3,2,1,0:T(8,128)(2,1)S(1)} %get-tuple-element.81.refs_1_), channel_id=1, source_target_pairs={{0,12},{2,14},{4,8},{6,10},{8,4},{10,6},{12,0},{14,2},{16,28},{18,... | collective-permute-start | bytes 983048 | tf_op jit(solution)/shard_map/ppermute | solution.py:566
  128.3 6.8 %collective-permute-start.19 = (bf16[4,41,16,128]{3,2,1,0:T(8,128)(2,1)S(1)}, bf16[4,41,16,128]{3,2,1,0:T(8,128)(2,1)S(1)}, u32[]{:S(2)}, u32[]{:S(2)}) collective-permute-start(bf16[4,41,16,128]{3,2,1,0:T(8,128)(2,1)S(1)} %get-tuple-element.80.refs_0_), channel_id=1, source_target_pairs={{0,2},{2,0},{1,3},{3,1},{4,6},{6,4},{5,7},{7,5},{8,10},{10,8},{9,1... | collective-permute-start | bytes 2015240 | tf_op jit(solution)/shard_map/ppermute | solution.py:550
  131.1 3.9 %collective-permute-start.21 = (bf16[4,41,16,128]{3,2,1,0:T(8,128)(2,1)S(1)}, bf16[4,41,16,128]{3,2,1,0:T(8,128)(2,1)S(1)}, u32[]{:S(2)}, u32[]{:S(2)}) collective-permute-start(bf16[4,41,16,128]{3,2,1,0:T(8,128)(2,1)S(1)} %collective-permute-done.18.refs_2_), channel_id=1, source_target_pairs={{0,2},{2,0},{1,3},{3,1},{4,6},{6,4},{5,7},{7,5},{8,10},{10,8},{9,1... | collective-permute-start | bytes 2015240 | tf_op jit(solution)/shard_map/ppermute | solution.py:550
  132.3 2.7 %collective-permute-start.22 = (bf16[4,20,16,128]{3,2,1,0:T(8,128)(2,1)S(1)}, bf16[4,20,16,128]{3,2,1,0:T(8,128)(2,1)S(1)}, u32[]{:S(2)}, u32[]{:S(2)}) collective-permute-start(bf16[4,20,16,128]{3,2,1,0:T(8,128)(2,1)S(1)} %collective-permute-done.17.refs_3_), channel_id=1, source_target_pairs={{0,2},{2,0},{1,3},{3,1},{4,6},{6,4},{5,7},{7,5},{8,10},{10,8},{9,1... | collective-permute-start | bytes 983048 | tf_op jit(solution)/shard_map/ppermute | solution.py:550
  (8 other events, 78.5 us)

commit v12 on v11

--- a/solution.py
+++ b/solution.py
@@ -581,8 +581,8 @@
 
 
 def gather_clips(own, home):
-    below, above = shift(own, "dp", 1), shift(own, "dp", -1)
-    near, two = trio(own, below, above)
+    near, two = trio(own, shift(own, "dp", 1), shift(own, "dp", -1))
+    near, two, home = lax.optimization_barrier((near, two, home))
     return near, shift(near, "dp", 3), shift(two, "dp", -3), home
 
 
@@ -626,8 +626,8 @@
     own, send = lax.optimization_barrier((own, send))
     recv = lax.ppermute(send, "tensor", [(0, 1), (1, 0)])
     own = exchange(own.reshape((clips, own.shape[0] // clips) + own.shape[1:]), "dp")
+    own, recv = lax.optimization_barrier((own, recv))
     own = reduce(own, 1.0 / math.sqrt(clips * frames * patches))
-    own, recv = lax.optimization_barrier((own, recv))
     home = finish(which, recv, keep, width).reshape(frames, own_patches, width)
     near, below, above, home = gather_clips(own, home)
     home = lax.all_to_all(home, SEQ, split_axis=0, concat_axis=0, tiled=True)

time: 141 us -> 139 us (0.986); the launches traced: 138 us -> 138 us
    all_to_all x1, waiting for transfers between devices: 6.99 us -> 1.8 us  [exchange(): return lax.all_to_all(parts, axis, split_axis=0, concat_axis=0, tiled=True)]
    ppermute x1, waiting for transfers between devices: 0.01 us -> 5.19 us  [body(): recv = lax.ppermute(send, 'tensor', [(0, 1), (1, 0)])]
    ppermute x12, starting transfers between devices: 12.5 us -> 10.3 us  [meet(): found.append(lax.ppermute(block, SEQ, pairs))]
    ppermute x4, waiting for transfers between devices: 9.13 us -> 7.46 us  [shift(): lax.ppermute(x, axis, [(i, (i + step) % count) for i in range(count)])]
    ppermute x12, waiting for transfers between devices: 25.2 us -> 26.9 us  [meet(): found.append(lax.ppermute(block, SEQ, pairs))]
    all_to_all x1, starting transfers between devices: 7.8 us -> 9.33 us  [body(): home = lax.all_to_all(home, SEQ, split_axis=0, concat_axis=0, tiled=True)]
  transfers between devices with their start and end apart: 26 -> 26, of which waited for: 19 -> 19; matrix products, arithmetic and copies ran while one was open for 2% -> 2% of each run, Pallas kernels for 5% -> 6%
where the time goes in v12:
time: 139 us; the launch traced here: 138 us
  waiting for transfers between devices  57.3 us (41%)
  starting transfers between devices  49.8 us (36%)
  Pallas kernels  25.9 us (19%)
  local copies, waits for them, and re-layouts  3.16 us (2%)
    ppermute x12, waiting for transfers between devices, meet(): found.append(lax.ppermute(block, SEQ, pairs))  26.9 us
    all_to_all x1, waiting for transfers between devices, body(): lax.all_to_all(x, SEQ, split_axis=0, concat_axis=0, tiled=True)  11.5 us
    ppermute x12, starting transfers between devices, meet(): found.append(lax.ppermute(block, SEQ, pairs))  10.3 us
    all_to_all x1, starting transfers between devices, body(): home = lax.all_to_all(home, SEQ, split_axis=0, concat_axis=0, tiled=True)  9.33 us
    all_to_all x1, starting transfers between devices, exchange(): return lax.all_to_all(parts, axis, split_axis=0, concat_axis=0, tiled=True)  8.18 us
    ppermute x4, waiting for transfers between devices, shift(): lax.ppermute(x, axis, [(i, (i + step) % count) for i in range(count)])  7.46 us
    pallas_call x1, Pallas kernels, attend(): pl.pallas_call(functools.partial(attend_kernel, patches=patches, heads=he...  7.12 us
    all_to_all x1, starting transfers between devices, body(): lax.all_to_all(x, SEQ, split_axis=0, concat_axis=0, tiled=True)  6.93 us
  transfers between devices with their start and end apart: 26, of which 19 were waited for; matrix products, arithmetic and copies ran while one was open for 2% of the time, Pallas kernels for 6%

profile of v12, /device:TPU:1, one launch (start us, length us, event | category | flops | bytes accessed | tf_op | source)
XLA Modules:
  0.0 138.3 jit_solution(14989608876564540120)
XLA Ops:
  0.6 2.2 %pack.1 = bf16[256,1728]{1,0:T(8,128)(2,1)} custom-call(bf16[256,1152]{1,0:T(8,128)(2,1)} %bitcast.34, bf16[576,256]{1,0:T(8,128)(2,1)} %bitcast.35), custom_call_target="tpu_custom_call" | custom-call | tf_op jit(solution)/shard_map/pack/pallas_call | solution.py:52
  2.9 6.9 %all-to-all-start = ((bf16[16,16,1728]{2,1,0:T(8,128)(2,1)}), bf16[16,16,1728]{2,1,0:T(8,128)(2,1)S(1)}, u32[]{:S(2)}, u32[]{:S(2)}) async-start(bf16[16,16,1728]{2,1,0:T(8,128)(2,1)} %bitcast.33), calls=%async_computation | async-start | bytes 1835008 | tf_op jit(solution)/shard_map/all_to_all | solution.py:612
  12.7 11.5 %all-to-all-done = bf16[16,16,1728]{2,1,0:T(8,128)(2,1)S(1)} async-done(((bf16[16,16,1728]{2,1,0:T(8,128)(2,1)}), bf16[16,16,1728]{2,1,0:T(8,128)(2,1)S(1)}, u32[]{:S(2)}, u32[]{:S(2)}) %all-to-all-start) | async-done | bytes 884768 | tf_op jit(solution)/shard_map/all_to_all | solution.py:612
  25.1 7.1 %attend.1 = (bf16[256,1152]{1,0:T(8,128)(2,1)S(1)}, bf16[864,256]{1,0:T(8,128)(2,1)S(1)}, bf16[864,256]{1,0:T(8,128)(2,1)S(1)}, bf16[576,256]{1,0:T(8,128)(2,1)S(1)}) custom-call(s32[1]{0:T(128)} %bitcast.2.core_ref.half_ref, bf16[256,1728]{1,0:T(8,128)(2,1)} %bitcast.30, f32[2,1152]{1,0:T(2,128)S(1)} %pad_maximum_fusion.affine_ref.affine_hbm, ...), custom_call_target="tpu_custom_call" | custom-call | tf_op jit(solution)/shard_map/attend/pallas_call | solution.py:203
  33.9 2.3 %collective-permute-done.gp_b = bf16[864,256]{1,0:T(8,128)(2,1)S(1)} collective-permute-done((bf16[864,256]{1,0:T(8,128)(2,1)S(1)}, bf16[864,256]{1,0:T(8,128)(2,1)S(1)}, u32[]{:S(2)}, u32[]{:S(2)}) %collective-permute-start) | collective-permute-done | bytes 442400 | tf_op jit(solution)/shard_map/ppermute | solution.py:550
  36.1 2.4 %outer.1 = (bf16[4,41,16,128]{3,2,1,0:T(8,128)(2,1)}, bf16[4,20,16,128]{3,2,1,0:T(8,128)(2,1)}, bf16[4,61,16,128]{3,2,1,0:T(8,128)(2,1)S(1)}) custom-call(s32[1]{0:T(128)} %bitcast.1.where_ref, s32[1]{0:T(128)} %bitcast.2.core_ref.half_ref, bf16[864,256]{1,0:T(8,128)(2,1)S(1)} %get-tuple-element.46.gp_a.gp_keep_hbm, ...), custom_call_target="tpu_custom_call" | custom-call | tf_op jit(solution)/shard_map/outer/pallas_call | solution.py:331
  39.8 6.3 %split.1 = (bf16[256,640]{1,0:T(8,128)(2,1)}, f32[256,1920]{1,0:T(8,128)}) custom-call(s32[1]{0:T(128)} %bitcast.2.core_ref.half_ref, s32[1]{0:T(128)} %bitcast.12.which_ref, bf16[256,1728]{1,0:T(8,128)(2,1)} %bitcast.31, f32[2,1152]{1,0:T(2,128)} %copy-done.4, bf16[1728,1152]{1,0:T(8,128)(2,1)} %bitcast.29, bf16[864,256]{1,0:T(8,128)(2,1)} %copy-done.1, ...), custom_call_target="tpu_custom_call" | custom-call | tf_op jit(solution)/shard_map/split/pallas_call | solution.py:286
  46.1 3.4 %collective-permute-done.3.refs_1_ = bf16[4,20,16,128]{3,2,1,0:T(8,128)(2,1)S(1)} collective-permute-done((bf16[4,20,16,128]{3,2,1,0:T(8,128)(2,1)}, bf16[4,20,16,128]{3,2,1,0:T(8,128)(2,1)S(1)}, u32[]{:S(2)}, u32[]{:S(2)}) %collective-permute-start.3) | collective-permute-done | bytes 327712 | tf_op jit(solution)/shard_map/ppermute | solution.py:566
  52.2 3.2 %collective-permute-done.5.refs_1_ = bf16[2,20,16,128]{3,2,1,0:T(8,128)(2,1)S(1)} collective-permute-done((bf16[2,20,16,128]{3,2,1,0:T(8,128)(2,1)S(1)}, bf16[2,20,16,128]{3,2,1,0:T(8,128)(2,1)S(1)}, u32[]{:S(2)}, u32[]{:S(2)}) %collective-permute-start.5) | collective-permute-done | bytes 163872 | tf_op jit(solution)/shard_map/ppermute | solution.py:566
  59.1 2.6 %collective-permute-done.7.refs_1_ = bf16[1,20,16,128]{3,2,1,0:T(8,128)(2,1)S(1)} collective-permute-done((bf16[1,20,16,128]{3,2,1,0:T(8,128)(2,1)S(1)}, bf16[1,20,16,128]{3,2,1,0:T(8,128)(2,1)S(1)}, u32[]{:S(2)}, u32[]{:S(2)}) %collective-permute-start.7) | collective-permute-done | bytes 81952 | tf_op jit(solution)/shard_map/ppermute | solution.py:566
  63.6 8.2 %all-to-all-start.1 = ((bf16[8,8,16,128]{3,2,1,0:T(8,128)(2,1)}), bf16[8,8,16,128]{3,2,1,0:T(8,128)(2,1)S(1)}, u32[]{:S(2)}, u32[]{:S(2)}) async-start(bf16[8,8,16,128]{3,2,1,0:T(8,128)(2,1)} %bitcast.14), calls=%async_computation.1 | async-start | bytes 524288 | tf_op jit(solution)/shard_map/all_to_all | solution.py:555
  71.8 2.5 %collective-permute-start.8 = (bf16[256,640]{1,0:T(8,128)(2,1)}, bf16[256,640]{1,0:T(8,128)(2,1)S(1)}, u32[]{:S(2)}, u32[]{:S(2)}) collective-permute-start(bf16[256,640]{1,0:T(8,128)(2,1)} %get-tuple-element.64), channel_id=1, source_target_pairs={{0,1},{1,0},{2,3},{3,2},{4,5},{5,4},{6,7},{7,6},{8,9},{9,8},{10,11... | collective-permute-start | bytes 983048 | tf_op jit(solution)/shard_map/ppermute | solution.py:627
  74.3 5.2 %collective-permute-done.8.recv_ref = bf16[256,640]{1,0:T(8,128)(2,1)S(1)} collective-permute-done((bf16[256,640]{1,0:T(8,128)(2,1)}, bf16[256,640]{1,0:T(8,128)(2,1)S(1)}, u32[]{:S(2)}, u32[]{:S(2)}) %collective-permute-start.8) | collective-permute-done | bytes 327712 | tf_op jit(solution)/shard_map/ppermute | solution.py:627
  84.5 2.1 %collective-permute-done.9.below_ref = bf16[8,16,128]{2,1,0:T(8,128)(2,1)S(1)} collective-permute-done((bf16[8,16,128]{2,1,0:T(8,128)(2,1)S(1)}, bf16[8,16,128]{2,1,0:T(8,128)(2,1)S(1)}, u32[]{:S(2)}, u32[]{:S(2)}) %collective-permute-start.9) | collective-permute-done | bytes 32800 | tf_op jit(solution)/shard_map/ppermute | solution.py:580
  86.6 9.3 %all-to-all-start.2 = ((bf16[16,16,1152]{2,1,0:T(8,128)(2,1)}), bf16[16,16,1152]{2,1,0:T(8,128)(2,1)S(1)}, u32[]{:S(2)}, u32[]{:S(2)}) async-start(bf16[16,16,1152]{2,1,0:T(8,128)(2,1)} %bitcast.15), calls=%async_computation.2 | async-start | bytes 1179648 | tf_op jit(solution)/shard_map/all_to_all | solution.py:633
  96.2 4.2 %collective-permute-start.12 = (bf16[16,16,128]{2,1,0:T(8,128)(2,1)S(1)}, bf16[16,16,128]{2,1,0:T(8,128)(2,1)S(1)}, u32[]{:S(2)}, u32[]{:S(2)}) collective-permute-start(bf16[16,16,128]{2,1,0:T(8,128)(2,1)S(1)} %get-tuple-element.71), channel_id=1, source_target_pairs={{0,160},{32,192},{64,224},{96,0},{128,32},{160,64},{192,96},{224,1... | collective-permute-start | bytes 196616 | tf_op jit(solution)/shard_map/ppermute | solution.py:580
  101.7 4.0 %collective-permute-done.11.below_ref = bf16[24,16,128]{2,1,0:T(8,128)(2,1)S(1)} collective-permute-done((bf16[24,16,128]{2,1,0:T(8,128)(2,1)S(1)}, bf16[24,16,128]{2,1,0:T(8,128)(2,1)S(1)}, u32[]{:S(2)}, u32[]{:S(2)}) %collective-permute-start.11) | collective-permute-done | bytes 98336 | tf_op jit(solution)/shard_map/ppermute | solution.py:580
  105.7 2.7 %collective-permute-start.13 = (bf16[1,41,16,128]{3,2,1,0:T(8,128)(2,1)S(1)}, bf16[1,41,16,128]{3,2,1,0:T(8,128)(2,1)S(1)}, u32[]{:S(2)}, u32[]{:S(2)}) collective-permute-start(bf16[1,41,16,128]{3,2,1,0:T(8,128)(2,1)S(1)} %get-tuple-element.72.refs_0_), channel_id=1, source_target_pairs={{0,16},{2,14},{4,20},{6,10},{8,24},{10,6},{12,28},{14,2},{16,0},{1... | collective-permute-start | bytes 503816 | tf_op jit(solution)/shard_map/ppermute | solution.py:566
  108.4 4.5 %collective-permute-done.14.refs_3_ = bf16[1,20,16,128]{3,2,1,0:T(8,128)(2,1)S(1)} collective-permute-done((bf16[1,20,16,128]{3,2,1,0:T(8,128)(2,1)S(1)}, bf16[1,20,16,128]{3,2,1,0:T(8,128)(2,1)S(1)}, u32[]{:S(2)}, u32[]{:S(2)}) %collective-permute-start.14) | collective-permute-done | bytes 81952 | tf_op jit(solution)/shard_map/ppermute | solution.py:566
  113.9 3.4 %collective-permute-done.16.refs_3_ = bf16[2,20,16,128]{3,2,1,0:T(8,128)(2,1)S(1)} collective-permute-done((bf16[2,20,16,128]{3,2,1,0:T(8,128)(2,1)S(1)}, bf16[2,20,16,128]{3,2,1,0:T(8,128)(2,1)S(1)}, u32[]{:S(2)}, u32[]{:S(2)}) %collective-permute-start.16) | collective-permute-done | bytes 163872 | tf_op jit(solution)/shard_map/ppermute | solution.py:566
  119.5 2.1 %collective-permute-start.17 = (bf16[4,20,16,128]{3,2,1,0:T(8,128)(2,1)S(1)}, bf16[4,20,16,128]{3,2,1,0:T(8,128)(2,1)S(1)}, u32[]{:S(2)}, u32[]{:S(2)}) collective-permute-start(bf16[4,20,16,128]{3,2,1,0:T(8,128)(2,1)S(1)} %get-tuple-element.87.refs_1_), channel_id=1, source_target_pairs={{0,12},{2,14},{4,8},{6,10},{8,4},{10,6},{12,0},{14,2},{16,28},{18,... | collective-permute-start | bytes 983048 | tf_op jit(solution)/shard_map/ppermute | solution.py:566
  122.7 4.8 %collective-permute-done.17.refs_3_ = bf16[4,20,16,128]{3,2,1,0:T(8,128)(2,1)S(1)} collective-permute-done((bf16[4,20,16,128]{3,2,1,0:T(8,128)(2,1)S(1)}, bf16[4,20,16,128]{3,2,1,0:T(8,128)(2,1)S(1)}, u32[]{:S(2)}, u32[]{:S(2)}) %collective-permute-start.17) | collective-permute-done | bytes 327712 | tf_op jit(solution)/shard_map/ppermute | solution.py:566
  127.5 3.4 %collective-permute-start.19 = (bf16[4,41,16,128]{3,2,1,0:T(8,128)(2,1)S(1)}, bf16[4,41,16,128]{3,2,1,0:T(8,128)(2,1)S(1)}, u32[]{:S(2)}, u32[]{:S(2)}) collective-permute-start(bf16[4,41,16,128]{3,2,1,0:T(8,128)(2,1)S(1)} %get-tuple-element.86.refs_0_), channel_id=1, source_target_pairs={{0,2},{2,0},{1,3},{3,1},{4,6},{6,4},{5,7},{7,5},{8,10},{10,8},{9,1... | collective-permute-start | bytes 2015240 | tf_op jit(solution)/shard_map/ppermute | solution.py:550
  135.4 2.9 %untile.1 = bf16[1728,1152]{1,0:T(8,128)(2,1)} custom-call(s32[1]{0:T(128)} %bitcast.1.where_ref, s32[1]{0:T(128)} %bitcast.2.core_ref.half_ref, bf16[4,41,16,128]{3,2,1,0:T(8,128)(2,1)S(1)} %get-tuple-element.86.refs_0_, bf16[4,20,16,128]{3,2,1,0:T(8,128)(2,1)S(1)} %get-tuple-element.87.refs_1_, ...), custom_call_target="tpu_custom_call" | custom-call | tf_op jit(solution)/shard_map/untile/pallas_call | solution.py:538
  (59 shorter events, 30.5 us)
Async XLA Ops:
  2.9 21.3 %all-to-all-start = ((bf16[16,16,1728]{2,1,0:T(8,128)(2,1)}), bf16[16,16,1728]{2,1,0:T(8,128)(2,1)S(1)}, u32[]{:S(2)}, u32[]{:S(2)}) async-start(bf16[16,16,1728]{2,1,0:T(8,128)(2,1)} %bitcast.33), calls=%async_computation | async-start | bytes 1835008 | tf_op jit(solution)/shard_map/all_to_all | solution.py:612
  33.0 3.1 %collective-permute-start.1 = (bf16[256,1152]{1,0:T(8,128)(2,1)S(1)}, bf16[256,1152]{1,0:T(8,128)(2,1)S(1)}, u32[]{:S(2)}, u32[]{:S(2)}) collective-permute-start(bf16[256,1152]{1,0:T(8,128)(2,1)S(1)} %get-tuple-element.48.mod_a), channel_id=1, source_target_pairs={{0,2},{2,0},{1,3},{3,1},{4,6},{6,4},{5,7},{7,5},{8,10},{10,8},{9,1... | collective-permute-start | bytes 1769480 | tf_op jit(solution)/shard_map/ppermute | solution.py:550
  38.5 11.0 %collective-permute-start.2 = (bf16[4,41,16,128]{3,2,1,0:T(8,128)(2,1)}, bf16[4,41,16,128]{3,2,1,0:T(8,128)(2,1)}, u32[]{:S(2)}, u32[]{:S(2)}) collective-permute-start(bf16[4,41,16,128]{3,2,1,0:T(8,128)(2,1)} %get-tuple-element.50), channel_id=1, source_target_pairs={{0,4},{2,18},{4,0},{6,22},{8,12},{10,26},{12,8},{14,30},{16,20},{1... | collective-permute-start | bytes 2015240 | tf_op jit(solution)/shard_map/ppermute | solution.py:566
  38.8 10.7 %collective-permute-start.3 = (bf16[4,20,16,128]{3,2,1,0:T(8,128)(2,1)}, bf16[4,20,16,128]{3,2,1,0:T(8,128)(2,1)S(1)}, u32[]{:S(2)}, u32[]{:S(2)}) collective-permute-start(bf16[4,20,16,128]{3,2,1,0:T(8,128)(2,1)} %get-tuple-element.51), channel_id=1, source_target_pairs={{0,12},{2,14},{4,8},{6,10},{8,4},{10,6},{12,0},{14,2},{16,28},{18,... | collective-permute-start | bytes 983048 | tf_op jit(solution)/shard_map/ppermute | solution.py:566
  50.9 6.4 %collective-permute-start.4 = (bf16[2,41,16,128]{3,2,1,0:T(8,128)(2,1)S(1)}, bf16[2,41,16,128]{3,2,1,0:T(8,128)(2,1)S(1)}, u32[]{:S(2)}, u32[]{:S(2)}) collective-permute-start(bf16[2,41,16,128]{3,2,1,0:T(8,128)(2,1)S(1)} %get-tuple-element.57), channel_id=1, source_target_pairs={{0,12},{2,6},{4,8},{6,2},{8,4},{10,14},{12,0},{14,10},{16,28},{18,... | collective-permute-start | bytes 1007624 | tf_op jit(solution)/shard_map/ppermute | solution.py:566
  51.0 4.4 %collective-permute-start.5 = (bf16[2,20,16,128]{3,2,1,0:T(8,128)(2,1)S(1)}, bf16[2,20,16,128]{3,2,1,0:T(8,128)(2,1)S(1)}, u32[]{:S(2)}, u32[]{:S(2)}) collective-permute-start(bf16[2,20,16,128]{3,2,1,0:T(8,128)(2,1)S(1)} %get-tuple-element.58), channel_id=1, source_target_pairs={{0,16},{2,18},{4,20},{6,22},{8,24},{10,26},{12,28},{14,30},{16,0},... | collective-permute-start | bytes 491528 | tf_op jit(solution)/shard_map/ppermute | solution.py:566
  57.4 5.5 %collective-permute-start.6 = (bf16[1,41,16,128]{3,2,1,0:T(8,128)(2,1)S(1)}, bf16[1,41,16,128]{3,2,1,0:T(8,128)(2,1)S(1)}, u32[]{:S(2)}, u32[]{:S(2)}) collective-permute-start(bf16[1,41,16,128]{3,2,1,0:T(8,128)(2,1)S(1)} %get-tuple-element.60), channel_id=1, source_target_pairs={{0,16},{2,14},{4,20},{6,10},{8,24},{10,6},{12,28},{14,2},{16,0},{1... | collective-permute-start | bytes 503816 | tf_op jit(solution)/shard_map/ppermute | solution.py:566
  58.5 3.3 %collective-permute-start.7 = (bf16[1,20,16,128]{3,2,1,0:T(8,128)(2,1)S(1)}, bf16[1,20,16,128]{3,2,1,0:T(8,128)(2,1)S(1)}, u32[]{:S(2)}, u32[]{:S(2)}) collective-permute-start(bf16[1,20,16,128]{3,2,1,0:T(8,128)(2,1)S(1)} %get-tuple-element.61), channel_id=1, source_target_pairs={{0,4},{2,6},{4,0},{6,2},{8,12},{10,14},{12,8},{14,10},{16,20},{18,... | collective-permute-start | bytes 245768 | tf_op jit(solution)/shard_map/ppermute | solution.py:566
  63.6 17.6 %all-to-all-start.1 = ((bf16[8,8,16,128]{3,2,1,0:T(8,128)(2,1)}), bf16[8,8,16,128]{3,2,1,0:T(8,128)(2,1)S(1)}, u32[]{:S(2)}, u32[]{:S(2)}) async-start(bf16[8,8,16,128]{3,2,1,0:T(8,128)(2,1)} %bitcast.14), calls=%async_computation.1 | async-start | bytes 524288 | tf_op jit(solution)/shard_map/all_to_all | solution.py:555
  71.8 7.6 %collective-permute-start.8 = (bf16[256,640]{1,0:T(8,128)(2,1)}, bf16[256,640]{1,0:T(8,128)(2,1)S(1)}, u32[]{:S(2)}, u32[]{:S(2)}) collective-permute-start(bf16[256,640]{1,0:T(8,128)(2,1)} %get-tuple-element.64), channel_id=1, source_target_pairs={{0,1},{1,0},{2,3},{3,2},{4,5},{5,4},{6,7},{7,6},{8,9},{9,8},{10,11... | collective-permute-start | bytes 983048 | tf_op jit(solution)/shard_map/ppermute | solution.py:627
  81.3 3.1 %collective-permute-start.10 = (bf16[8,16,128]{2,1,0:T(8,128)(2,1)S(1)}, bf16[8,16,128]{2,1,0:T(8,128)(2,1)S(1)}, u32[]{:S(2)}, u32[]{:S(2)}) collective-permute-start(bf16[8,16,128]{2,1,0:T(8,128)(2,1)S(1)} %reduce.1.own_ref), channel_id=1, source_target_pairs={{0,224},{32,0},{64,32},{96,64},{128,96},{160,128},{192,160},{224,1... | collective-permute-start | bytes 98312 | tf_op jit(solution)/shard_map/ppermute | solution.py:580
  82.6 4.0 %collective-permute-start.9 = (bf16[8,16,128]{2,1,0:T(8,128)(2,1)S(1)}, bf16[8,16,128]{2,1,0:T(8,128)(2,1)S(1)}, u32[]{:S(2)}, u32[]{:S(2)}) collective-permute-start(bf16[8,16,128]{2,1,0:T(8,128)(2,1)S(1)} %reduce.1.own_ref), channel_id=1, source_target_pairs={{0,32},{32,64},{64,96},{96,128},{128,160},{160,192},{192,224},{224... | collective-permute-start | bytes 98312 | tf_op jit(solution)/shard_map/ppermute | solution.py:580
  86.6 26.3 %all-to-all-start.2 = ((bf16[16,16,1152]{2,1,0:T(8,128)(2,1)}), bf16[16,16,1152]{2,1,0:T(8,128)(2,1)S(1)}, u32[]{:S(2)}, u32[]{:S(2)}) async-start(bf16[16,16,1152]{2,1,0:T(8,128)(2,1)} %bitcast.15), calls=%async_computation.2 | async-start | bytes 1179648 | tf_op jit(solution)/shard_map/all_to_all | solution.py:633
  95.9 9.8 %collective-permute-start.11 = (bf16[24,16,128]{2,1,0:T(8,128)(2,1)S(1)}, bf16[24,16,128]{2,1,0:T(8,128)(2,1)S(1)}, u32[]{:S(2)}, u32[]{:S(2)}) collective-permute-start(bf16[24,16,128]{2,1,0:T(8,128)(2,1)S(1)} %get-tuple-element.70.near_ref), channel_id=1, source_target_pairs={{0,96},{32,128},{64,160},{96,192},{128,224},{160,0},{192,32},{224,... | collective-permute-start | bytes 294920 | tf_op jit(solution)/shard_map/ppermute | solution.py:580
  96.2 5.5 %collective-permute-start.12 = (bf16[16,16,128]{2,1,0:T(8,128)(2,1)S(1)}, bf16[16,16,128]{2,1,0:T(8,128)(2,1)S(1)}, u32[]{:S(2)}, u32[]{:S(2)}) collective-permute-start(bf16[16,16,128]{2,1,0:T(8,128)(2,1)S(1)} %get-tuple-element.71), channel_id=1, source_target_pairs={{0,160},{32,192},{64,224},{96,0},{128,32},{160,64},{192,96},{224,1... | collective-permute-start | bytes 196616 | tf_op jit(solution)/shard_map/ppermute | solution.py:580
  105.7 7.1 %collective-permute-start.13 = (bf16[1,41,16,128]{3,2,1,0:T(8,128)(2,1)S(1)}, bf16[1,41,16,128]{3,2,1,0:T(8,128)(2,1)S(1)}, u32[]{:S(2)}, u32[]{:S(2)}) collective-permute-start(bf16[1,41,16,128]{3,2,1,0:T(8,128)(2,1)S(1)} %get-tuple-element.72.refs_0_), channel_id=1, source_target_pairs={{0,16},{2,14},{4,20},{6,10},{8,24},{10,6},{12,28},{14,2},{16,0},{1... | collective-permute-start | bytes 503816 | tf_op jit(solution)/shard_map/ppermute | solution.py:566
  108.4 4.5 %collective-permute-start.14 = (bf16[1,20,16,128]{3,2,1,0:T(8,128)(2,1)S(1)}, bf16[1,20,16,128]{3,2,1,0:T(8,128)(2,1)S(1)}, u32[]{:S(2)}, u32[]{:S(2)}) collective-permute-start(bf16[1,20,16,128]{3,2,1,0:T(8,128)(2,1)S(1)} %get-tuple-element.73.refs_2_), channel_id=1, source_target_pairs={{0,4},{2,6},{4,0},{6,2},{8,12},{10,14},{12,8},{14,10},{16,20},{18,... | collective-permute-start | bytes 245768 | tf_op jit(solution)/shard_map/ppermute | solution.py:566
  112.9 6.4 %collective-permute-start.15 = (bf16[2,41,16,128]{3,2,1,0:T(8,128)(2,1)S(1)}, bf16[2,41,16,128]{3,2,1,0:T(8,128)(2,1)S(1)}, u32[]{:S(2)}, u32[]{:S(2)}) collective-permute-start(bf16[2,41,16,128]{3,2,1,0:T(8,128)(2,1)S(1)} %get-tuple-element.77.refs_0_), channel_id=1, source_target_pairs={{0,12},{2,6},{4,8},{6,2},{8,4},{10,14},{12,0},{14,10},{16,28},{18,... | collective-permute-start | bytes 1007624 | tf_op jit(solution)/shard_map/ppermute | solution.py:566
  113.0 4.3 %collective-permute-start.16 = (bf16[2,20,16,128]{3,2,1,0:T(8,128)(2,1)S(1)}, bf16[2,20,16,128]{3,2,1,0:T(8,128)(2,1)S(1)}, u32[]{:S(2)}, u32[]{:S(2)}) collective-permute-start(bf16[2,20,16,128]{3,2,1,0:T(8,128)(2,1)S(1)} %get-tuple-element.78.refs_2_), channel_id=1, source_target_pairs={{0,16},{2,18},{4,20},{6,22},{8,24},{10,26},{12,28},{14,30},{16,0},... | collective-permute-start | bytes 491528 | tf_op jit(solution)/shard_map/ppermute | solution.py:566
  119.4 11.5 %collective-permute-start.18 = (bf16[4,41,16,128]{3,2,1,0:T(8,128)(2,1)S(1)}, bf16[4,41,16,128]{3,2,1,0:T(8,128)(2,1)S(1)}, u32[]{:S(2)}, u32[]{:S(2)}) collective-permute-start(bf16[4,41,16,128]{3,2,1,0:T(8,128)(2,1)S(1)} %get-tuple-element.86.refs_0_), channel_id=1, source_target_pairs={{0,4},{2,18},{4,0},{6,22},{8,12},{10,26},{12,8},{14,30},{16,20},{1... | collective-permute-start | bytes 2015240 | tf_op jit(solution)/shard_map/ppermute | solution.py:566
  119.5 8.0 %collective-permute-start.17 = (bf16[4,20,16,128]{3,2,1,0:T(8,128)(2,1)S(1)}, bf16[4,20,16,128]{3,2,1,0:T(8,128)(2,1)S(1)}, u32[]{:S(2)}, u32[]{:S(2)}) collective-permute-start(bf16[4,20,16,128]{3,2,1,0:T(8,128)(2,1)S(1)} %get-tuple-element.87.refs_1_), channel_id=1, source_target_pairs={{0,12},{2,14},{4,8},{6,10},{8,4},{10,6},{12,0},{14,2},{16,28},{18,... | collective-permute-start | bytes 983048 | tf_op jit(solution)/shard_map/ppermute | solution.py:566
  127.5 7.9 %collective-permute-start.19 = (bf16[4,41,16,128]{3,2,1,0:T(8,128)(2,1)S(1)}, bf16[4,41,16,128]{3,2,1,0:T(8,128)(2,1)S(1)}, u32[]{:S(2)}, u32[]{:S(2)}) collective-permute-start(bf16[4,41,16,128]{3,2,1,0:T(8,128)(2,1)S(1)} %get-tuple-element.86.refs_0_), channel_id=1, source_target_pairs={{0,2},{2,0},{1,3},{3,1},{4,6},{6,4},{5,7},{7,5},{8,10},{10,8},{9,1... | collective-permute-start | bytes 2015240 | tf_op jit(solution)/shard_map/ppermute | solution.py:550
  130.9 4.5 %collective-permute-start.21 = (bf16[4,41,16,128]{3,2,1,0:T(8,128)(2,1)S(1)}, bf16[4,41,16,128]{3,2,1,0:T(8,128)(2,1)S(1)}, u32[]{:S(2)}, u32[]{:S(2)}) collective-permute-start(bf16[4,41,16,128]{3,2,1,0:T(8,128)(2,1)S(1)} %collective-permute-done.18.refs_2_), channel_id=1, source_target_pairs={{0,2},{2,0},{1,3},{3,1},{4,6},{6,4},{5,7},{7,5},{8,10},{10,8},{9,1... | collective-permute-start | bytes 2015240 | tf_op jit(solution)/shard_map/ppermute | solution.py:550
  132.7 2.7 %collective-permute-start.22 = (bf16[4,20,16,128]{3,2,1,0:T(8,128)(2,1)S(1)}, bf16[4,20,16,128]{3,2,1,0:T(8,128)(2,1)S(1)}, u32[]{:S(2)}, u32[]{:S(2)}) collective-permute-start(bf16[4,20,16,128]{3,2,1,0:T(8,128)(2,1)S(1)} %collective-permute-done.17.refs_3_), channel_id=1, source_target_pairs={{0,2},{2,0},{1,3},{3,1},{4,6},{6,4},{5,7},{7,5},{8,10},{10,8},{9,1... | collective-permute-start | bytes 983048 | tf_op jit(solution)/shard_map/ppermute | solution.py:550
  (8 other events, 80.0 us)

commit v13 on v12

--- a/solution.py
+++ b/solution.py
@@ -580,16 +580,16 @@
     return lax.ppermute(x, axis, [(i, (i + step) % count) for i in range(count)])
 
 
-def gather_clips(own, home):
+def gather_clips(own, beside):
     near, two = trio(own, shift(own, "dp", 1), shift(own, "dp", -1))
-    near, two, home = lax.optimization_barrier((near, two, home))
-    return near, shift(near, "dp", 3), shift(two, "dp", -3), home
+    near, two, beside = lax.optimization_barrier((near, two, beside))
+    return near, shift(near, "dp", 3), shift(two, "dp", -3), beside
 
 
 def gather_plane(have, where, half, rows, width, beside):
-    got, beside = lax.optimization_barrier((meet(have, 2), beside))
+    have = join(list(zip(have, meet(have, 2))))
+    got, beside = lax.optimization_barrier((meet(have, 1), beside))
     have = join(list(zip(have, got)))
-    have = join(list(zip(have, meet(have, 1))))
     got = meet(have, 0)
     got[-1], have, beside = lax.optimization_barrier((got[-1], have, unpack(beside)))
     pieces = list(have) + got
@@ -626,10 +626,9 @@
     own, send = lax.optimization_barrier((own, send))
     recv = lax.ppermute(send, "tensor", [(0, 1), (1, 0)])
     own = exchange(own.reshape((clips, own.shape[0] // clips) + own.shape[1:]), "dp")
-    own, recv = lax.optimization_barrier((own, recv))
     own = reduce(own, 1.0 / math.sqrt(clips * frames * patches))
+    near, below, above, recv = gather_clips(own, recv)
     home = finish(which, recv, keep, width).reshape(frames, own_patches, width)
-    near, below, above, home = gather_clips(own, home)
     home = lax.all_to_all(home, SEQ, split_axis=0, concat_axis=0, tiled=True)
     clip = lax.axis_index("dp").astype(jnp.int32).reshape(1)
     have = place(clip, near, below, above, clips, size)

time: 139 us -> 141 us (1.014)
  waiting for transfers between devices: 57.3 us -> 60.6 us
    ppermute x12, waiting for transfers between devices: 26.9 us -> 34.1 us  [meet(): found.append(lax.ppermute(block, SEQ, pairs))]
    all_to_all x1, waiting for transfers between devices: 1.8 us -> 6.99 us  [exchange(): return lax.all_to_all(parts, axis, split_axis=0, concat_axis=0, tiled=True)]
    ppermute x1, waiting for transfers between devices: 5.19 us -> 0.01 us  [body(): recv = lax.ppermute(send, 'tensor', [(0, 1), (1, 0)])]
    ppermute x4, waiting for transfers between devices: 7.46 us -> 2.61 us  [shift(): lax.ppermute(x, axis, [(i, (i + step) % count) for i in range(count)])]
    ppermute x6, starting transfers between devices: 6.56 us -> 3.11 us  [swap(): return lax.ppermute(x, axes, [(i, i ^ k) for i in range(count)])]
    all_to_all x1, starting transfers between devices: 9.33 us -> 11.7 us  [body(): home = lax.all_to_all(home, SEQ, split_axis=0, concat_axis=0, tiled=True)]
  transfers between devices with their start and end apart: 26 -> 26, of which waited for: 19 -> 17; matrix products, arithmetic and copies ran while one was open for 2% -> 2% of each run, Pallas kernels for 6% -> 6%
where the time goes in v13:
time: 141 us
  waiting for transfers between devices  60.6 us (43%)
  starting transfers between devices  48.9 us (35%)
  Pallas kernels  26 us (18%)
  local copies, waits for them, and re-layouts  3.16 us (2%)
    ppermute x12, waiting for transfers between devices, meet(): found.append(lax.ppermute(block, SEQ, pairs))  34.1 us
    all_to_all x1, starting transfers between devices, body(): home = lax.all_to_all(home, SEQ, split_axis=0, concat_axis=0, tiled=True)  11.7 us
    all_to_all x1, waiting for transfers between devices, body(): lax.all_to_all(x, SEQ, split_axis=0, concat_axis=0, tiled=True)  11.5 us
    ppermute x12, starting transfers between devices, meet(): found.append(lax.ppermute(block, SEQ, pairs))  10.5 us
    all_to_all x1, starting transfers between devices, exchange(): return lax.all_to_all(parts, axis, split_axis=0, concat_axis=0, tiled=True)  8.18 us
    pallas_call x1, Pallas kernels, attend(): pl.pallas_call(functools.partial(attend_kernel, patches=patches, heads=he...  7.12 us
    all_to_all x1, waiting for transfers between devices, exchange(): return lax.all_to_all(parts, axis, split_axis=0, concat_axis=0, tiled=True)  6.99 us
    all_to_all x1, starting transfers between devices, body(): lax.all_to_all(x, SEQ, split_axis=0, concat_axis=0, tiled=True)  6.93 us
  transfers between devices with their start and end apart: 26, of which 17 were waited for; matrix products, arithmetic and copies ran while one was open for 2% of the time, Pallas kernels for 6%

profile of v13, /device:TPU:1, one launch (start us, length us, event | category | flops | bytes accessed | tf_op | source)
XLA Modules:
  0.0 140.8 jit_solution(16366640262202327441)
XLA Ops:
  0.6 2.2 %pack.1 = bf16[256,1728]{1,0:T(8,128)(2,1)} custom-call(bf16[256,1152]{1,0:T(8,128)(2,1)} %bitcast.34, bf16[576,256]{1,0:T(8,128)(2,1)} %bitcast.35), custom_call_target="tpu_custom_call" | custom-call | tf_op jit(solution)/shard_map/pack/pallas_call | solution.py:52
  2.9 6.9 %all-to-all-start = ((bf16[16,16,1728]{2,1,0:T(8,128)(2,1)}), bf16[16,16,1728]{2,1,0:T(8,128)(2,1)S(1)}, u32[]{:S(2)}, u32[]{:S(2)}) async-start(bf16[16,16,1728]{2,1,0:T(8,128)(2,1)} %bitcast.33), calls=%async_computation | async-start | bytes 1835008 | tf_op jit(solution)/shard_map/all_to_all | solution.py:612
  12.7 11.5 %all-to-all-done = bf16[16,16,1728]{2,1,0:T(8,128)(2,1)S(1)} async-done(((bf16[16,16,1728]{2,1,0:T(8,128)(2,1)}), bf16[16,16,1728]{2,1,0:T(8,128)(2,1)S(1)}, u32[]{:S(2)}, u32[]{:S(2)}) %all-to-all-start) | async-done | bytes 884768 | tf_op jit(solution)/shard_map/all_to_all | solution.py:612
  25.1 7.1 %attend.1 = (bf16[256,1152]{1,0:T(8,128)(2,1)S(1)}, bf16[864,256]{1,0:T(8,128)(2,1)S(1)}, bf16[864,256]{1,0:T(8,128)(2,1)S(1)}, bf16[576,256]{1,0:T(8,128)(2,1)S(1)}) custom-call(s32[1]{0:T(128)} %bitcast.2.core_ref.half_ref, bf16[256,1728]{1,0:T(8,128)(2,1)} %bitcast.30, f32[2,1152]{1,0:T(2,128)S(1)} %pad_maximum_fusion.affine_ref.affine_hbm, ...), custom_call_target="tpu_custom_call" | custom-call | tf_op jit(solution)/shard_map/attend/pallas_call | solution.py:203
  33.9 2.3 %collective-permute-done.gp_b = bf16[864,256]{1,0:T(8,128)(2,1)S(1)} collective-permute-done((bf16[864,256]{1,0:T(8,128)(2,1)S(1)}, bf16[864,256]{1,0:T(8,128)(2,1)S(1)}, u32[]{:S(2)}, u32[]{:S(2)}) %collective-permute-start) | collective-permute-done | bytes 442400 | tf_op jit(solution)/shard_map/ppermute | solution.py:550
  36.1 2.4 %outer.1 = (bf16[4,41,16,128]{3,2,1,0:T(8,128)(2,1)}, bf16[4,20,16,128]{3,2,1,0:T(8,128)(2,1)}, bf16[4,61,16,128]{3,2,1,0:T(8,128)(2,1)S(1)}) custom-call(s32[1]{0:T(128)} %bitcast.1.where_ref, s32[1]{0:T(128)} %bitcast.2.core_ref.half_ref, bf16[864,256]{1,0:T(8,128)(2,1)S(1)} %get-tuple-element.44.gp_a.gp_keep_hbm, ...), custom_call_target="tpu_custom_call" | custom-call | tf_op jit(solution)/shard_map/outer/pallas_call | solution.py:331
  39.8 6.3 %split.1 = (bf16[256,640]{1,0:T(8,128)(2,1)}, f32[256,1920]{1,0:T(8,128)}) custom-call(s32[1]{0:T(128)} %bitcast.2.core_ref.half_ref, s32[1]{0:T(128)} %bitcast.12.which_ref, bf16[256,1728]{1,0:T(8,128)(2,1)} %bitcast.31, f32[2,1152]{1,0:T(2,128)} %copy-done.4, bf16[1728,1152]{1,0:T(8,128)(2,1)} %bitcast.29, bf16[864,256]{1,0:T(8,128)(2,1)} %copy-done.1, ...), custom_call_target="tpu_custom_call" | custom-call | tf_op jit(solution)/shard_map/split/pallas_call | solution.py:286
  46.1 3.4 %collective-permute-done.3.refs_1_ = bf16[4,20,16,128]{3,2,1,0:T(8,128)(2,1)S(1)} collective-permute-done((bf16[4,20,16,128]{3,2,1,0:T(8,128)(2,1)}, bf16[4,20,16,128]{3,2,1,0:T(8,128)(2,1)S(1)}, u32[]{:S(2)}, u32[]{:S(2)}) %collective-permute-start.3) | collective-permute-done | bytes 327712 | tf_op jit(solution)/shard_map/ppermute | solution.py:566
  52.2 3.2 %collective-permute-done.5.refs_1_ = bf16[2,20,16,128]{3,2,1,0:T(8,128)(2,1)S(1)} collective-permute-done((bf16[2,20,16,128]{3,2,1,0:T(8,128)(2,1)S(1)}, bf16[2,20,16,128]{3,2,1,0:T(8,128)(2,1)S(1)}, u32[]{:S(2)}, u32[]{:S(2)}) %collective-permute-start.5) | collective-permute-done | bytes 163872 | tf_op jit(solution)/shard_map/ppermute | solution.py:566
  55.4 1.9 %collective-permute-done.4.refs_0_ = bf16[2,41,16,128]{3,2,1,0:T(8,128)(2,1)S(1)} collective-permute-done((bf16[2,41,16,128]{3,2,1,0:T(8,128)(2,1)S(1)}, bf16[2,41,16,128]{3,2,1,0:T(8,128)(2,1)S(1)}, u32[]{:S(2)}, u32[]{:S(2)}) %collective-permute-start.4) | collective-permute-done | bytes 335904 | tf_op jit(solution)/shard_map/ppermute | solution.py:566
  59.1 2.6 %collective-permute-done.7.refs_1_ = bf16[1,20,16,128]{3,2,1,0:T(8,128)(2,1)S(1)} collective-permute-done((bf16[1,20,16,128]{3,2,1,0:T(8,128)(2,1)S(1)}, bf16[1,20,16,128]{3,2,1,0:T(8,128)(2,1)S(1)}, u32[]{:S(2)}, u32[]{:S(2)}) %collective-permute-start.7) | collective-permute-done | bytes 81952 | tf_op jit(solution)/shard_map/ppermute | solution.py:566
  63.6 8.2 %all-to-all-start.1 = ((bf16[8,8,16,128]{3,2,1,0:T(8,128)(2,1)}), bf16[8,8,16,128]{3,2,1,0:T(8,128)(2,1)S(1)}, u32[]{:S(2)}, u32[]{:S(2)}) async-start(bf16[8,8,16,128]{3,2,1,0:T(8,128)(2,1)} %bitcast.14), calls=%async_computation.1 | async-start | bytes 524288 | tf_op jit(solution)/shard_map/all_to_all | solution.py:555
  71.8 2.5 %collective-permute-start.10 = (bf16[256,640]{1,0:T(8,128)(2,1)}, bf16[256,640]{1,0:T(8,128)(2,1)S(1)}, u32[]{:S(2)}, u32[]{:S(2)}) collective-permute-start(bf16[256,640]{1,0:T(8,128)(2,1)} %get-tuple-element.64), channel_id=1, source_target_pairs={{0,1},{1,0},{2,3},{3,2},{4,5},{5,4},{6,7},{7,6},{8,9},{9,8},{10,11... | collective-permute-start | bytes 983048 | tf_op jit(solution)/shard_map/ppermute | solution.py:627
  74.3 7.0 %all-to-all-done.1.parts_ref = bf16[8,8,16,128]{3,2,1,0:T(8,128)(2,1)S(1)} async-done(((bf16[8,8,16,128]{3,2,1,0:T(8,128)(2,1)}), bf16[8,8,16,128]{3,2,1,0:T(8,128)(2,1)S(1)}, u32[]{:S(2)}, u32[]{:S(2)}) %all-to-all-start.1) | async-done | bytes 262176 | tf_op jit(solution)/shard_map/all_to_all | solution.py:555
  82.9 1.6 %collective-permute-done.9.above_ref = bf16[8,16,128]{2,1,0:T(8,128)(2,1)S(1)} collective-permute-done((bf16[8,16,128]{2,1,0:T(8,128)(2,1)S(1)}, bf16[8,16,128]{2,1,0:T(8,128)(2,1)S(1)}, u32[]{:S(2)}, u32[]{:S(2)}) %collective-permute-start.9) | collective-permute-done | bytes 32800 | tf_op jit(solution)/shard_map/ppermute | solution.py:580
  86.0 4.1 %collective-permute-start.12 = (bf16[16,16,128]{2,1,0:T(8,128)(2,1)S(1)}, bf16[16,16,128]{2,1,0:T(8,128)(2,1)S(1)}, u32[]{:S(2)}, u32[]{:S(2)}) collective-permute-start(bf16[16,16,128]{2,1,0:T(8,128)(2,1)S(1)} %get-tuple-element.66), channel_id=1, source_target_pairs={{0,160},{32,192},{64,224},{96,0},{128,32},{160,64},{192,96},{224,1... | collective-permute-start | bytes 196616 | tf_op jit(solution)/shard_map/ppermute | solution.py:580
  91.6 11.7 %all-to-all-start.2 = ((bf16[16,16,1152]{2,1,0:T(8,128)(2,1)}), bf16[16,16,1152]{2,1,0:T(8,128)(2,1)S(1)}, u32[]{:S(2)}, u32[]{:S(2)}) async-start(bf16[16,16,1152]{2,1,0:T(8,128)(2,1)} %bitcast.15), calls=%async_computation.2 | async-start | bytes 1179648 | tf_op jit(solution)/shard_map/all_to_all | solution.py:632
  103.3 2.7 %collective-permute-start.13 = (bf16[1,41,16,128]{3,2,1,0:T(8,128)(2,1)S(1)}, bf16[1,41,16,128]{3,2,1,0:T(8,128)(2,1)S(1)}, u32[]{:S(2)}, u32[]{:S(2)}) collective-permute-start(bf16[1,41,16,128]{3,2,1,0:T(8,128)(2,1)S(1)} %get-tuple-element.67.refs_0_), channel_id=1, source_target_pairs={{0,16},{2,14},{4,20},{6,10},{8,24},{10,6},{12,28},{14,2},{16,0},{1... | collective-permute-start | bytes 503816 | tf_op jit(solution)/shard_map/ppermute | solution.py:566
  106.0 7.6 %collective-permute-done.14.refs_3_ = bf16[1,20,16,128]{3,2,1,0:T(8,128)(2,1)S(1)} collective-permute-done((bf16[1,20,16,128]{3,2,1,0:T(8,128)(2,1)S(1)}, bf16[1,20,16,128]{3,2,1,0:T(8,128)(2,1)S(1)}, u32[]{:S(2)}, u32[]{:S(2)}) %collective-permute-start.14) | collective-permute-done | bytes 81952 | tf_op jit(solution)/shard_map/ppermute | solution.py:566
  116.6 3.4 %collective-permute-done.16.refs_3_ = bf16[2,20,16,128]{3,2,1,0:T(8,128)(2,1)S(1)} collective-permute-done((bf16[2,20,16,128]{3,2,1,0:T(8,128)(2,1)S(1)}, bf16[2,20,16,128]{3,2,1,0:T(8,128)(2,1)S(1)}, u32[]{:S(2)}, u32[]{:S(2)}) %collective-permute-start.16) | collective-permute-done | bytes 163872 | tf_op jit(solution)/shard_map/ppermute | solution.py:566
  124.7 7.9 %collective-permute-done.17.refs_3_ = bf16[4,20,16,128]{3,2,1,0:T(8,128)(2,1)S(1)} collective-permute-done((bf16[4,20,16,128]{3,2,1,0:T(8,128)(2,1)S(1)}, bf16[4,20,16,128]{3,2,1,0:T(8,128)(2,1)S(1)}, u32[]{:S(2)}, u32[]{:S(2)}) %collective-permute-start.17) | collective-permute-done | bytes 327712 | tf_op jit(solution)/shard_map/ppermute | solution.py:566
  132.6 1.7 %collective-permute-start.19 = (bf16[4,41,16,128]{3,2,1,0:T(8,128)(2,1)S(1)}, bf16[4,41,16,128]{3,2,1,0:T(8,128)(2,1)S(1)}, u32[]{:S(2)}, u32[]{:S(2)}) collective-permute-start(bf16[4,41,16,128]{3,2,1,0:T(8,128)(2,1)S(1)} %get-tuple-element.82.refs_0_), channel_id=1, source_target_pairs={{0,2},{2,0},{1,3},{3,1},{4,6},{6,4},{5,7},{7,5},{8,10},{10,8},{9,1... | collective-permute-start | bytes 2015240 | tf_op jit(solution)/shard_map/ppermute | solution.py:550
  134.8 2.7 %collective-permute-done.20.refs_5_ = bf16[4,20,16,128]{3,2,1,0:T(8,128)(2,1)S(1)} collective-permute-done((bf16[4,20,16,128]{3,2,1,0:T(8,128)(2,1)S(1)}, bf16[4,20,16,128]{3,2,1,0:T(8,128)(2,1)S(1)}, u32[]{:S(2)}, u32[]{:S(2)}) %collective-permute-start.20) | collective-permute-done | bytes 327712 | tf_op jit(solution)/shard_map/ppermute | solution.py:550
  138.0 2.9 %untile.1 = bf16[1728,1152]{1,0:T(8,128)(2,1)} custom-call(s32[1]{0:T(128)} %bitcast.1.where_ref, s32[1]{0:T(128)} %bitcast.2.core_ref.half_ref, bf16[4,41,16,128]{3,2,1,0:T(8,128)(2,1)S(1)} %get-tuple-element.82.refs_0_, bf16[4,20,16,128]{3,2,1,0:T(8,128)(2,1)S(1)} %get-tuple-element.83.refs_1_, ...), custom_call_target="tpu_custom_call" | custom-call | tf_op jit(solution)/shard_map/untile/pallas_call | solution.py:538
  (59 shorter events, 26.4 us)
Async XLA Ops:
  2.9 21.3 %all-to-all-start = ((bf16[16,16,1728]{2,1,0:T(8,128)(2,1)}), bf16[16,16,1728]{2,1,0:T(8,128)(2,1)S(1)}, u32[]{:S(2)}, u32[]{:S(2)}) async-start(bf16[16,16,1728]{2,1,0:T(8,128)(2,1)} %bitcast.33), calls=%async_computation | async-start | bytes 1835008 | tf_op jit(solution)/shard_map/all_to_all | solution.py:612
  33.0 3.1 %collective-permute-start.1 = (bf16[256,1152]{1,0:T(8,128)(2,1)S(1)}, bf16[256,1152]{1,0:T(8,128)(2,1)S(1)}, u32[]{:S(2)}, u32[]{:S(2)}) collective-permute-start(bf16[256,1152]{1,0:T(8,128)(2,1)S(1)} %get-tuple-element.46.mod_a), channel_id=1, source_target_pairs={{0,2},{2,0},{1,3},{3,1},{4,6},{6,4},{5,7},{7,5},{8,10},{10,8},{9,1... | collective-permute-start | bytes 1769480 | tf_op jit(solution)/shard_map/ppermute | solution.py:550
  38.5 11.0 %collective-permute-start.2 = (bf16[4,41,16,128]{3,2,1,0:T(8,128)(2,1)}, bf16[4,41,16,128]{3,2,1,0:T(8,128)(2,1)}, u32[]{:S(2)}, u32[]{:S(2)}) collective-permute-start(bf16[4,41,16,128]{3,2,1,0:T(8,128)(2,1)} %get-tuple-element.48), channel_id=1, source_target_pairs={{0,4},{2,18},{4,0},{6,22},{8,12},{10,26},{12,8},{14,30},{16,20},{1... | collective-permute-start | bytes 2015240 | tf_op jit(solution)/shard_map/ppermute | solution.py:566
  38.8 10.7 %collective-permute-start.3 = (bf16[4,20,16,128]{3,2,1,0:T(8,128)(2,1)}, bf16[4,20,16,128]{3,2,1,0:T(8,128)(2,1)S(1)}, u32[]{:S(2)}, u32[]{:S(2)}) collective-permute-start(bf16[4,20,16,128]{3,2,1,0:T(8,128)(2,1)} %get-tuple-element.49), channel_id=1, source_target_pairs={{0,12},{2,14},{4,8},{6,10},{8,4},{10,6},{12,0},{14,2},{16,28},{18,... | collective-permute-start | bytes 983048 | tf_op jit(solution)/shard_map/ppermute | solution.py:566
  50.9 6.4 %collective-permute-start.4 = (bf16[2,41,16,128]{3,2,1,0:T(8,128)(2,1)S(1)}, bf16[2,41,16,128]{3,2,1,0:T(8,128)(2,1)S(1)}, u32[]{:S(2)}, u32[]{:S(2)}) collective-permute-start(bf16[2,41,16,128]{3,2,1,0:T(8,128)(2,1)S(1)} %get-tuple-element.55), channel_id=1, source_target_pairs={{0,12},{2,6},{4,8},{6,2},{8,4},{10,14},{12,0},{14,10},{16,28},{18,... | collective-permute-start | bytes 1007624 | tf_op jit(solution)/shard_map/ppermute | solution.py:566
  51.0 4.4 %collective-permute-start.5 = (bf16[2,20,16,128]{3,2,1,0:T(8,128)(2,1)S(1)}, bf16[2,20,16,128]{3,2,1,0:T(8,128)(2,1)S(1)}, u32[]{:S(2)}, u32[]{:S(2)}) collective-permute-start(bf16[2,20,16,128]{3,2,1,0:T(8,128)(2,1)S(1)} %get-tuple-element.56), channel_id=1, source_target_pairs={{0,16},{2,18},{4,20},{6,22},{8,24},{10,26},{12,28},{14,30},{16,0},... | collective-permute-start | bytes 491528 | tf_op jit(solution)/shard_map/ppermute | solution.py:566
  57.4 5.5 %collective-permute-start.6 = (bf16[1,41,16,128]{3,2,1,0:T(8,128)(2,1)S(1)}, bf16[1,41,16,128]{3,2,1,0:T(8,128)(2,1)S(1)}, u32[]{:S(2)}, u32[]{:S(2)}) collective-permute-start(bf16[1,41,16,128]{3,2,1,0:T(8,128)(2,1)S(1)} %get-tuple-element.58), channel_id=1, source_target_pairs={{0,16},{2,14},{4,20},{6,10},{8,24},{10,6},{12,28},{14,2},{16,0},{1... | collective-permute-start | bytes 503816 | tf_op jit(solution)/shard_map/ppermute | solution.py:566
  58.5 3.3 %collective-permute-start.7 = (bf16[1,20,16,128]{3,2,1,0:T(8,128)(2,1)S(1)}, bf16[1,20,16,128]{3,2,1,0:T(8,128)(2,1)S(1)}, u32[]{:S(2)}, u32[]{:S(2)}) collective-permute-start(bf16[1,20,16,128]{3,2,1,0:T(8,128)(2,1)S(1)} %get-tuple-element.59), channel_id=1, source_target_pairs={{0,4},{2,6},{4,0},{6,2},{8,12},{10,14},{12,8},{14,10},{16,20},{18,... | collective-permute-start | bytes 245768 | tf_op jit(solution)/shard_map/ppermute | solution.py:566
  63.6 17.6 %all-to-all-start.1 = ((bf16[8,8,16,128]{3,2,1,0:T(8,128)(2,1)}), bf16[8,8,16,128]{3,2,1,0:T(8,128)(2,1)S(1)}, u32[]{:S(2)}, u32[]{:S(2)}) async-start(bf16[8,8,16,128]{3,2,1,0:T(8,128)(2,1)} %bitcast.14), calls=%async_computation.1 | async-start | bytes 524288 | tf_op jit(solution)/shard_map/all_to_all | solution.py:555
  71.8 13.7 %collective-permute-start.10 = (bf16[256,640]{1,0:T(8,128)(2,1)}, bf16[256,640]{1,0:T(8,128)(2,1)S(1)}, u32[]{:S(2)}, u32[]{:S(2)}) collective-permute-start(bf16[256,640]{1,0:T(8,128)(2,1)} %get-tuple-element.64), channel_id=1, source_target_pairs={{0,1},{1,0},{2,3},{3,2},{4,5},{5,4},{6,7},{7,6},{8,9},{9,8},{10,11... | collective-permute-start | bytes 983048 | tf_op jit(solution)/shard_map/ppermute | solution.py:627
  81.3 3.1 %collective-permute-start.9 = (bf16[8,16,128]{2,1,0:T(8,128)(2,1)S(1)}, bf16[8,16,128]{2,1,0:T(8,128)(2,1)S(1)}, u32[]{:S(2)}, u32[]{:S(2)}) collective-permute-start(bf16[8,16,128]{2,1,0:T(8,128)(2,1)S(1)} %reduce.1.own_ref), channel_id=1, source_target_pairs={{0,224},{32,0},{64,32},{96,64},{128,96},{160,128},{192,160},{224,1... | collective-permute-start | bytes 98312 | tf_op jit(solution)/shard_map/ppermute | solution.py:580
  81.4 4.1 %collective-permute-start.8 = (bf16[8,16,128]{2,1,0:T(8,128)(2,1)S(1)}, bf16[8,16,128]{2,1,0:T(8,128)(2,1)S(1)}, u32[]{:S(2)}, u32[]{:S(2)}) collective-permute-start(bf16[8,16,128]{2,1,0:T(8,128)(2,1)S(1)} %reduce.1.own_ref), channel_id=1, source_target_pairs={{0,32},{32,64},{64,96},{96,128},{128,160},{160,192},{192,224},{224... | collective-permute-start | bytes 98312 | tf_op jit(solution)/shard_map/ppermute | solution.py:580
  85.5 17.8 %collective-permute-start.11 = (bf16[24,16,128]{2,1,0:T(8,128)(2,1)S(1)}, bf16[24,16,128]{2,1,0:T(8,128)(2,1)S(1)}, u32[]{:S(2)}, u32[]{:S(2)}) collective-permute-start(bf16[24,16,128]{2,1,0:T(8,128)(2,1)S(1)} %get-tuple-element.65.near_ref), channel_id=1, source_target_pairs={{0,96},{32,128},{64,160},{96,192},{128,224},{160,0},{192,32},{224,... | collective-permute-start | bytes 294920 | tf_op jit(solution)/shard_map/ppermute | solution.py:580
  86.0 17.3 %collective-permute-start.12 = (bf16[16,16,128]{2,1,0:T(8,128)(2,1)S(1)}, bf16[16,16,128]{2,1,0:T(8,128)(2,1)S(1)}, u32[]{:S(2)}, u32[]{:S(2)}) collective-permute-start(bf16[16,16,128]{2,1,0:T(8,128)(2,1)S(1)} %get-tuple-element.66), channel_id=1, source_target_pairs={{0,160},{32,192},{64,224},{96,0},{128,32},{160,64},{192,96},{224,1... | collective-permute-start | bytes 196616 | tf_op jit(solution)/shard_map/ppermute | solution.py:580
  91.6 28.4 %all-to-all-start.2 = ((bf16[16,16,1152]{2,1,0:T(8,128)(2,1)}), bf16[16,16,1152]{2,1,0:T(8,128)(2,1)S(1)}, u32[]{:S(2)}, u32[]{:S(2)}) async-start(bf16[16,16,1152]{2,1,0:T(8,128)(2,1)} %bitcast.15), calls=%async_computation.2 | async-start | bytes 1179648 | tf_op jit(solution)/shard_map/all_to_all | solution.py:632
  103.3 11.8 %collective-permute-start.13 = (bf16[1,41,16,128]{3,2,1,0:T(8,128)(2,1)S(1)}, bf16[1,41,16,128]{3,2,1,0:T(8,128)(2,1)S(1)}, u32[]{:S(2)}, u32[]{:S(2)}) collective-permute-start(bf16[1,41,16,128]{3,2,1,0:T(8,128)(2,1)S(1)} %get-tuple-element.67.refs_0_), channel_id=1, source_target_pairs={{0,16},{2,14},{4,20},{6,10},{8,24},{10,6},{12,28},{14,2},{16,0},{1... | collective-permute-start | bytes 503816 | tf_op jit(solution)/shard_map/ppermute | solution.py:566
  106.0 7.7 %collective-permute-start.14 = (bf16[1,20,16,128]{3,2,1,0:T(8,128)(2,1)S(1)}, bf16[1,20,16,128]{3,2,1,0:T(8,128)(2,1)S(1)}, u32[]{:S(2)}, u32[]{:S(2)}) collective-permute-start(bf16[1,20,16,128]{3,2,1,0:T(8,128)(2,1)S(1)} %get-tuple-element.68.refs_2_), channel_id=1, source_target_pairs={{0,4},{2,6},{4,0},{6,2},{8,12},{10,14},{12,8},{14,10},{16,20},{18,... | collective-permute-start | bytes 245768 | tf_op jit(solution)/shard_map/ppermute | solution.py:566
  115.2 6.4 %collective-permute-start.15 = (bf16[2,41,16,128]{3,2,1,0:T(8,128)(2,1)S(1)}, bf16[2,41,16,128]{3,2,1,0:T(8,128)(2,1)S(1)}, u32[]{:S(2)}, u32[]{:S(2)}) collective-permute-start(bf16[2,41,16,128]{3,2,1,0:T(8,128)(2,1)S(1)} %get-tuple-element.69.refs_0_), channel_id=1, source_target_pairs={{0,12},{2,6},{4,8},{6,2},{8,4},{10,14},{12,0},{14,10},{16,28},{18,... | collective-permute-start | bytes 1007624 | tf_op jit(solution)/shard_map/ppermute | solution.py:566
  115.5 4.5 %collective-permute-start.16 = (bf16[2,20,16,128]{3,2,1,0:T(8,128)(2,1)S(1)}, bf16[2,20,16,128]{3,2,1,0:T(8,128)(2,1)S(1)}, u32[]{:S(2)}, u32[]{:S(2)}) collective-permute-start(bf16[2,20,16,128]{3,2,1,0:T(8,128)(2,1)S(1)} %get-tuple-element.70.refs_2_), channel_id=1, source_target_pairs={{0,16},{2,18},{4,20},{6,22},{8,24},{10,26},{12,28},{14,30},{16,0},... | collective-permute-start | bytes 491528 | tf_op jit(solution)/shard_map/ppermute | solution.py:566
  121.6 12.7 %collective-permute-start.18 = (bf16[4,41,16,128]{3,2,1,0:T(8,128)(2,1)S(1)}, bf16[4,41,16,128]{3,2,1,0:T(8,128)(2,1)S(1)}, u32[]{:S(2)}, u32[]{:S(2)}) collective-permute-start(bf16[4,41,16,128]{3,2,1,0:T(8,128)(2,1)S(1)} %get-tuple-element.82.refs_0_), channel_id=1, source_target_pairs={{0,4},{2,18},{4,0},{6,22},{8,12},{10,26},{12,8},{14,30},{16,20},{1... | collective-permute-start | bytes 2015240 | tf_op jit(solution)/shard_map/ppermute | solution.py:566
  123.0 9.6 %collective-permute-start.17 = (bf16[4,20,16,128]{3,2,1,0:T(8,128)(2,1)S(1)}, bf16[4,20,16,128]{3,2,1,0:T(8,128)(2,1)S(1)}, u32[]{:S(2)}, u32[]{:S(2)}) collective-permute-start(bf16[4,20,16,128]{3,2,1,0:T(8,128)(2,1)S(1)} %get-tuple-element.83.refs_1_), channel_id=1, source_target_pairs={{0,12},{2,14},{4,8},{6,10},{8,4},{10,6},{12,0},{14,2},{16,28},{18,... | collective-permute-start | bytes 983048 | tf_op jit(solution)/shard_map/ppermute | solution.py:566
  132.6 5.4 %collective-permute-start.19 = (bf16[4,41,16,128]{3,2,1,0:T(8,128)(2,1)S(1)}, bf16[4,41,16,128]{3,2,1,0:T(8,128)(2,1)S(1)}, u32[]{:S(2)}, u32[]{:S(2)}) collective-permute-start(bf16[4,41,16,128]{3,2,1,0:T(8,128)(2,1)S(1)} %get-tuple-element.82.refs_0_), channel_id=1, source_target_pairs={{0,2},{2,0},{1,3},{3,1},{4,6},{6,4},{5,7},{7,5},{8,10},{10,8},{9,1... | collective-permute-start | bytes 2015240 | tf_op jit(solution)/shard_map/ppermute | solution.py:550
  134.3 3.6 %collective-permute-start.21 = (bf16[4,41,16,128]{3,2,1,0:T(8,128)(2,1)S(1)}, bf16[4,41,16,128]{3,2,1,0:T(8,128)(2,1)S(1)}, u32[]{:S(2)}, u32[]{:S(2)}) collective-permute-start(bf16[4,41,16,128]{3,2,1,0:T(8,128)(2,1)S(1)} %collective-permute-done.18.refs_2_), channel_id=1, source_target_pairs={{0,2},{2,0},{1,3},{3,1},{4,6},{6,4},{5,7},{7,5},{8,10},{10,8},{9,1... | collective-permute-start | bytes 2015240 | tf_op jit(solution)/shard_map/ppermute | solution.py:550
  134.3 3.2 %collective-permute-start.20 = (bf16[4,20,16,128]{3,2,1,0:T(8,128)(2,1)S(1)}, bf16[4,20,16,128]{3,2,1,0:T(8,128)(2,1)S(1)}, u32[]{:S(2)}, u32[]{:S(2)}) collective-permute-start(bf16[4,20,16,128]{3,2,1,0:T(8,128)(2,1)S(1)} %get-tuple-element.83.refs_1_), channel_id=1, source_target_pairs={{0,2},{2,0},{1,3},{3,1},{4,6},{6,4},{5,7},{7,5},{8,10},{10,8},{9,1... | collective-permute-start | bytes 983048 | tf_op jit(solution)/shard_map/ppermute | solution.py:550
  (8 other events, 88.1 us)
